TPU v7x, 32 devices: a whole 2x2x4 slice. The times are simulated.
32 devices in a mesh: group: 2 (over y), tile: 4 (over z), list: 4 (over x, core).
Axes of the slice: x: 2, y: 2, z: 4, core: 2. Of those that a mesh axis runs over, the one named last changes fastest.
Arguments:
- probes: float32 [8192, 256], P(('group', 'tile', 'list')), parts along dimension 0, may hold values from -6 to 6
- right_bases: bfloat16 [8, 1, 96, 1024], P(('group', 'tile'), None, 'list'), parts along dimension 0, may hold values from -0.1875 to 0.1875
- left_bases: bfloat16 [8, 1, 96, 1024], P(('group', 'tile'), None, 'list'), parts along dimension 0, may hold values from -0.625 to 0.625
- near_tiles: bfloat16 [8, 1024, 3, 1024], P(('group', 'tile'), None, None, 'list'), parts along dimension 0, may hold values from -0.109375 to 0.109375
- tile_ranks: int32 [8, 1], P(('group', 'tile')), parts along dimension 0, may hold values from 32 to 96
- column_rows: int32 [4, 1], P('tile'), may hold values from 0 to 3, as said below
- row_columns: int32 [4, 1], P('tile'), may hold values from 0 to 3, as said below
Outputs:
- product: float32 [8192, 256], P(('group', 'tile', 'list')), parts along dimension 0
There are 2 independent parts, one for each index of `group`. A program takes and returns all parts, laid end to end along the dimension named above; an argument that names none is the same for every part. Nothing has to cross between parts.
Inputs may be any that keep to these rules, and one draw needn't show every extreme that they name: `column_rows`: each row j lists 1 distinct tile rows. Tile (i, j) is listed in row j here exactly when j is listed in row i of row_columns. A listed tile may lie beside the diagonal; its low-rank term then adds to the dense tile. `row_columns`: each row i lists 1 distinct tile columns, matching column_rows.
All inputs are finite; a program needn't handle non-finite values.
Results may differ from a plain program's by a relative error of at most 0.0048.
Values may be sent and summed in bfloat16 or wider, within the bound.
No kernel may reach another device: no remote copies, remote signals or barrier semaphores. Data moves between devices by JAX's collectives and lax.ppermute only.
A program may use at most 64 MiB of HBM per device.

v0:
```python
import jax
import jax.numpy as jnp
from jax import lax
from jax.sharding import PartitionSpec as P


def shifted(block, axis, distance):
    devices = range(lax.axis_size(axis))
    route = [(i - distance, i) for i in devices if i - distance in devices]
    return lax.ppermute(block, axis, route)


def image_part(operand, right_bases, left_bases, near_tiles, tile_ranks, column_rows, row_columns):
    tile_slots = right_bases.shape[1]
    rank_part = right_bases.shape[2]
    tile_rows = right_bases.shape[3]
    probe_count = operand.shape[1]
    tile_count = lax.axis_size("tile")
    right_flat = right_bases.reshape(tile_slots * rank_part, tile_rows)
    left_flat = left_bases.reshape(tile_slots * rank_part, tile_rows)
    dense_flat = near_tiles.reshape(tile_rows, -1)
    values = jnp.dot(
        right_flat,
        lax.all_gather(operand, "list", axis=0, tiled=True),
        preferred_element_type=jnp.float32,
    )
    rank_level = lax.axis_index("list") * rank_part + lax.iota(jnp.int32, rank_part)
    rank_mask = rank_level[None, :] < tile_ranks[0][:, None]
    coefficients = jnp.where(
        rank_mask[:, :, None], values.reshape(tile_slots, rank_part, probe_count), 0.0
    ).astype(jnp.bfloat16)
    targets = (column_rows[0][None, :] == lax.iota(jnp.int32, tile_count)[:, None]).astype(
        jnp.bfloat16
    )
    outgoing = jnp.einsum(
        "dk,krp->drp", targets, coefficients, preferred_element_type=jnp.float32
    ).astype(jnp.bfloat16)
    sources = (row_columns[0][:, None] == lax.iota(jnp.int32, tile_count)[None, :]).astype(
        jnp.bfloat16
    )
    chosen = jnp.einsum(
        "kj,jrp->krp",
        sources,
        lax.all_to_all(outgoing, "tile", split_axis=0, concat_axis=0, tiled=True),
        preferred_element_type=jnp.float32,
    ).astype(jnp.bfloat16)
    chosen = chosen.reshape(tile_slots * rank_part, -1)
    far_sum = lax.dot_general(
        left_flat, chosen, (((0,), (0,)), ((), ())), preferred_element_type=jnp.float32
    )
    arrived = {}
    for offset in (1, -1):
        arrived[offset] = shifted(operand, "tile", offset)
    stacked = jnp.concatenate([arrived[1], operand, arrived[-1]], axis=0)
    near_sum = jnp.dot(dense_flat, stacked, preferred_element_type=jnp.float32)
    partial_image = near_sum + far_sum
    return lax.psum_scatter(partial_image, "list", scatter_dimension=0, tiled=True)


def local(probes, right_bases, left_bases, near_tiles, tile_ranks, column_rows, row_columns):
    probe_bf = probes.astype(jnp.bfloat16)
    first_pass = image_part(
        probe_bf, right_bases, left_bases, near_tiles, tile_ranks, column_rows, row_columns
    ).astype(jnp.bfloat16)
    return image_part(
        first_pass, right_bases, left_bases, near_tiles, tile_ranks, column_rows, row_columns
    )


def solution(mesh):
    placed = (
        P(("group", "tile", "list"), None),
        P(("group", "tile"), None, "list", None),
        P(("group", "tile"), None, "list", None),
        P(("group", "tile"), None, None, "list"),
        P(("group", "tile"), None),
        P("tile", None),
        P("tile", None),
    )
    return jax.shard_map(
        local,
        mesh=mesh,
        in_specs=placed,
        out_specs=P(("group", "tile", "list"), None),
        check_vma=False,
    )
```

profile of v0, /device:TPU:0, one launch (start us, length us, event | category | flops | bytes accessed | tf_op | source)
XLA Modules:
  0.0 120.9 jit_solution(18293655642215492507)
XLA Ops:
  6.5 1.1 convert_element_type.33
  7.6 8.6 %all_gather.6 = bf16[1024,256]{1,0:T(8,128)(2,1)S(1)} all-gather(bf16[256,256]{1,0:T(8,128)(2,1)S(1)} %convert_element_type.33), channel_id=1, replica_groups=mesh['group'=2,'tile'=4,'list'=4] {'list'}, dimensions={0}, use_global_device_ids=true | all-gather | bytes 655360 | tf_op jit(solution)/shard_map/all_gather | solution.py:24
  17.6 1.0 fusion.3
  18.6 0.7 multiply_convert_fusion.1
  19.3 4.9 %all-to-all-start = ((bf16[4,24,256]{2,1,0:T(8,128)(2,1)}), bf16[4,24,256]{2,1,0:T(8,128)(2,1)S(1)}, u32[]{:S(2)}, u32[]{:S(2)}) async-start(bf16[4,24,256]{2,1,0:T(8,128)(2,1)} %multiply_convert_fusion.1), calls=%async_computation | async-start | bytes 98304 | tf_op jit(solution)/shard_map/all_to_all | solution.py:44
  24.1 3.9 %collective-permute-start = (bf16[256,256]{1,0:T(8,128)(2,1)S(1)}, bf16[256,256]{1,0:T(8,128)(2,1)S(1)}, u32[]{:S(2)}, u32[]{:S(2)}) collective-permute-start(bf16[256,256]{1,0:T(8,128)(2,1)S(1)} %convert_element_type.33), channel_id=1, source_target_pairs={{0,4},{4,8},{8,12},{1,5},{5,9},{9,13},{2,6},{6,10},{10,14},{3,7},{... | collective-permute-start | bytes 393224 | tf_op jit(solution)/shard_map/ppermute | solution.py:10
  28.1 1.3 %collective-permute-start.1 = (bf16[256,256]{1,0:T(8,128)(2,1)S(1)}, bf16[256,256]{1,0:T(8,128)(2,1)}, u32[]{:S(2)}, u32[]{:S(2)}) collective-permute-start(bf16[256,256]{1,0:T(8,128)(2,1)S(1)} %convert_element_type.33), channel_id=1, source_target_pairs={{4,0},{8,4},{12,8},{5,1},{9,5},{13,9},{6,2},{10,6},{14,10},{7,3},{... | collective-permute-start | bytes 393224 | tf_op jit(solution)/shard_map/ppermute | solution.py:10
  30.0 0.9 copy.9
  31.1 0.3 fusion.19
  31.4 3.6 %collective-permute-done.1 = bf16[256,256]{1,0:T(8,128)(2,1)} collective-permute-done((bf16[256,256]{1,0:T(8,128)(2,1)S(1)}, bf16[256,256]{1,0:T(8,128)(2,1)}, u32[]{:S(2)}, u32[]{:S(2)}) %collective-permute-start.1) | collective-permute-done | bytes 131104 | tf_op jit(solution)/shard_map/ppermute | solution.py:10
  35.0 2.5 %fusion.1 = f32[1024,256]{0,1:T(8,128)} fusion(f32[256,1024]{1,0:T(8,128)S(1)} %fusion.19, bf16[1024,768]{0,1:T(8,128)(2,1)S(1)} %bitcast.39, bf16[256,256]{1,0:T(8,128)(2,1)} %collective-permute-done.1, bf16[256,256]{1,0:T(8,128)(2,1)S(1)} %convert_element_type.33, bf16[256,256]{1,0:T(8,128)(2,1)S(1)} %collective-permute-done), kind=kOutput, calls=%fused_computation.3 | convolution fusion | flops 404094976 | bytes 4063232 | tf_op jit(solution)/shard_map/dot_general | solution.py:55
  37.5 24.7 %reduce-scatter.3.cloned.1.call-done = f32[256,256]{0,1:T(8,128)} async-done(((f32[1024,256]{0,1:T(8,128)}), f32[256,256]{0,1:T(8,128)}) %reduce-scatter.3.cloned.1.call-update) | async-done | bytes 262160 | tf_op jit(solution)/shard_map/reduce_scatter | solution.py:57
  62.2 1.0 convert_element_type.37
  63.2 6.8 %all_gather.7 = bf16[1024,256]{0,1:T(8,128)(2,1)S(1)} all-gather(bf16[256,256]{0,1:T(8,128)(2,1)S(1)} %convert_element_type.37), channel_id=1, replica_groups=mesh['group'=2,'tile'=4,'list'=4] {'list'}, dimensions={0}, use_global_device_ids=true | all-gather | bytes 655360 | tf_op jit(solution)/shard_map/all_gather | solution.py:24
  70.2 0.7 multiply_convert_fusion
  70.9 4.6 %all-to-all-start.1 = ((bf16[4,24,256]{2,1,0:T(8,128)(2,1)}), bf16[4,24,256]{2,1,0:T(8,128)(2,1)S(1)}, u32[]{:S(2)}, u32[]{:S(2)}) async-start(bf16[4,24,256]{2,1,0:T(8,128)(2,1)} %multiply_convert_fusion), calls=%async_computation.2 | async-start | bytes 98304 | tf_op jit(solution)/shard_map/all_to_all | solution.py:44
  75.5 3.9 %collective-permute-start.2 = (bf16[256,256]{0,1:T(8,128)(2,1)S(1)}, bf16[256,256]{0,1:T(8,128)(2,1)S(1)}, u32[]{:S(2)}, u32[]{:S(2)}) collective-permute-start(bf16[256,256]{0,1:T(8,128)(2,1)S(1)} %convert_element_type.37), channel_id=1, source_target_pairs={{0,4},{4,8},{8,12},{1,5},{5,9},{9,13},{2,6},{6,10},{10,14},{3,7},{... | collective-permute-start | bytes 393224 | tf_op jit(solution)/shard_map/ppermute | solution.py:10
  79.4 1.3 %collective-permute-start.3 = (bf16[256,256]{0,1:T(8,128)(2,1)S(1)}, bf16[256,256]{0,1:T(8,128)(2,1)S(1)}, u32[]{:S(2)}, u32[]{:S(2)}) collective-permute-start(bf16[256,256]{0,1:T(8,128)(2,1)S(1)} %convert_element_type.37), channel_id=1, source_target_pairs={{4,0},{8,4},{12,8},{5,1},{9,5},{13,9},{6,2},{10,6},{14,10},{7,3},{... | collective-permute-start | bytes 393224 | tf_op jit(solution)/shard_map/ppermute | solution.py:10
  80.7 0.5 all-to-all-done.1
  81.7 0.4 collective-permute-done.2
  82.1 4.2 %collective-permute-done.3 = bf16[256,256]{0,1:T(8,128)(2,1)S(1)} collective-permute-done((bf16[256,256]{0,1:T(8,128)(2,1)S(1)}, bf16[256,256]{0,1:T(8,128)(2,1)S(1)}, u32[]{:S(2)}, u32[]{:S(2)}) %collective-permute-start.3) | collective-permute-done | bytes 131104 | tf_op jit(solution)/shard_map/ppermute | solution.py:10
  86.3 1.5 %fusion = f32[1024,256]{0,1:T(8,128)} fusion(f32[256,1024]{1,0:T(8,128)S(1)} %fusion.17, bf16[1024,768]{0,1:T(8,128)(2,1)S(1)} %bitcast.40, bf16[256,256]{0,1:T(8,128)(2,1)S(1)} %collective-permute-done.3, bf16[256,256]{0,1:T(8,128)(2,1)S(1)} %convert_element_type.37, bf16[256,256]{0,1:T(8,128)(2,1)S(1)} %collective-permute-done.2), kind=kOutput, calls=%fused_computation.1 | convolution fusion | flops 404094976 | bytes 4063232 | tf_op jit(solution)/shard_map/dot_general | solution.py:55
  87.9 24.4 %reduce-scatter.5.cloned.1.call-done = f32[256,256]{0,1:T(8,128)} async-done(((f32[1024,256]{0,1:T(8,128)}), f32[256,256]{0,1:T(8,128)}) %reduce-scatter.5.cloned.1.call-update) | async-done | bytes 262160 | tf_op jit(solution)/shard_map/reduce_scatter | solution.py:57
  112.3 1.8 %copy.10 = f32[256,256]{1,0:T(8,128)} copy(f32[256,256]{0,1:T(8,128)} %reduce-scatter.5.cloned.1.call-done) | data formatting | bytes 524288 | tf_op jit(solution)/shard_map/reduce_scatter | solution.py:57
  (18 shorter events, 0.9 us)
Async XLA Ops:
  6.5 24.5 %copy-start = (bf16[1,1,24,1024]{3,2,1,0:T(8,128)(2,1)S(1)}, bf16[1,1,24,1024]{3,2,1,0:T(8,128)(2,1)}, u32[]{:S(2)}) copy-start(bf16[1,1,24,1024]{3,2,1,0:T(8,128)(2,1)} %param.9) | copy-start | bytes 147460
  6.5 23.5 %copy-start.1 = (bf16[1,1024,3,256]{3,1,2,0:T(8,128)(2,1)S(1)}, bf16[1,1024,3,256]{3,1,2,0:T(8,128)(2,1)}, u32[]{:S(2)}) copy-start(bf16[1,1024,3,256]{3,1,2,0:T(8,128)(2,1)} %param.10) | copy-start | bytes 4718596
  19.3 11.6 %all-to-all-start = ((bf16[4,24,256]{2,1,0:T(8,128)(2,1)}), bf16[4,24,256]{2,1,0:T(8,128)(2,1)S(1)}, u32[]{:S(2)}, u32[]{:S(2)}) async-start(bf16[4,24,256]{2,1,0:T(8,128)(2,1)} %multiply_convert_fusion.1), calls=%async_computation | async-start | bytes 98304 | tf_op jit(solution)/shard_map/all_to_all | solution.py:44
  24.1 38.1 %reduce-scatter.3.cloned.1.call-start = ((), (), s32[]{:S(2)}) async-start(), calls=%async_computation.4 | async-start | bytes 1310720 | tf_op jit(solution)/shard_map/reduce_scatter | solution.py:57
  24.1 7.3 %collective-permute-start = (bf16[256,256]{1,0:T(8,128)(2,1)S(1)}, bf16[256,256]{1,0:T(8,128)(2,1)S(1)}, u32[]{:S(2)}, u32[]{:S(2)}) collective-permute-start(bf16[256,256]{1,0:T(8,128)(2,1)S(1)} %convert_element_type.33), channel_id=1, source_target_pairs={{0,4},{4,8},{8,12},{1,5},{5,9},{9,13},{2,6},{6,10},{10,14},{3,7},{... | collective-permute-start | bytes 393224 | tf_op jit(solution)/shard_map/ppermute | solution.py:10
  28.1 7.0 %collective-permute-start.1 = (bf16[256,256]{1,0:T(8,128)(2,1)S(1)}, bf16[256,256]{1,0:T(8,128)(2,1)}, u32[]{:S(2)}, u32[]{:S(2)}) collective-permute-start(bf16[256,256]{1,0:T(8,128)(2,1)S(1)} %convert_element_type.33), channel_id=1, source_target_pairs={{4,0},{8,4},{12,8},{5,1},{9,5},{13,9},{6,2},{10,6},{14,10},{7,3},{... | collective-permute-start | bytes 393224 | tf_op jit(solution)/shard_map/ppermute | solution.py:10
  37.5 32.4 %copy-start.2 = (bf16[1,1,24,1024]{3,2,1,0:T(8,128)(2,1)S(1)}, bf16[1,1,24,1024]{3,2,1,0:T(8,128)(2,1)}, u32[]{:S(2)}) copy-start(bf16[1,1,24,1024]{3,2,1,0:T(8,128)(2,1)} %param.8) | copy-start | bytes 147460
  70.9 10.3 %all-to-all-start.1 = ((bf16[4,24,256]{2,1,0:T(8,128)(2,1)}), bf16[4,24,256]{2,1,0:T(8,128)(2,1)S(1)}, u32[]{:S(2)}, u32[]{:S(2)}) async-start(bf16[4,24,256]{2,1,0:T(8,128)(2,1)} %multiply_convert_fusion), calls=%async_computation.2 | async-start | bytes 98304 | tf_op jit(solution)/shard_map/all_to_all | solution.py:44
  75.5 36.8 %reduce-scatter.5.cloned.1.call-start = ((), (), s32[]{:S(2)}) async-start(), calls=%async_computation.5 | async-start | bytes 1310720 | tf_op jit(solution)/shard_map/reduce_scatter | solution.py:57
  75.5 6.6 %collective-permute-start.2 = (bf16[256,256]{0,1:T(8,128)(2,1)S(1)}, bf16[256,256]{0,1:T(8,128)(2,1)S(1)}, u32[]{:S(2)}, u32[]{:S(2)}) collective-permute-start(bf16[256,256]{0,1:T(8,128)(2,1)S(1)} %convert_element_type.37), channel_id=1, source_target_pairs={{0,4},{4,8},{8,12},{1,5},{5,9},{9,13},{2,6},{6,10},{10,14},{3,7},{... | collective-permute-start | bytes 393224 | tf_op jit(solution)/shard_map/ppermute | solution.py:10
  79.4 6.9 %collective-permute-start.3 = (bf16[256,256]{0,1:T(8,128)(2,1)S(1)}, bf16[256,256]{0,1:T(8,128)(2,1)S(1)}, u32[]{:S(2)}, u32[]{:S(2)}) collective-permute-start(bf16[256,256]{0,1:T(8,128)(2,1)S(1)} %convert_element_type.37), channel_id=1, source_target_pairs={{4,0},{8,4},{12,8},{5,1},{9,5},{13,9},{6,2},{10,6},{14,10},{7,3},{... | collective-permute-start | bytes 393224 | tf_op jit(solution)/shard_map/ppermute | solution.py:10
Sparse Core Ops, SparseCore 0:
  37.6 24.4 reduce-scatter.2
  88.0 24.2 reduce-scatter.4
where the time goes:
time: 121 us
  waiting for transfers between devices  57.8 us (48%)
  starting transfers between devices  19.9 us (16%)
  between operations  15.5 us (13%)
  blocking collectives  15.4 us (13%)
  matrix products  6.17 us (5%)
  other arithmetic  3.48 us (3%)
  local copies, waits for them, and re-layouts  2.67 us (2%)
    reduce_scatter x2, waiting for transfers between devices, image_part(): lax.psum_scatter(partial_image, 'list', scatter_dimension=0, tiled=True)  49.1 us
    all_gather x2, blocking collectives, image_part(): lax.all_gather(operand, 'list', axis=0, tiled=True)  15.4 us
    ppermute x4, starting transfers between devices, shifted(): return lax.ppermute(block, axis, route)  10.4 us
    all_to_all x2, starting transfers between devices, image_part(): lax.all_to_all(outgoing, 'tile', split_axis=0, concat_axis=0, tiled=True)  9.45 us
    ppermute x4, waiting for transfers between devices, shifted(): return lax.ppermute(block, axis, route)  8.24 us
    dot_general x2, matrix products, image_part(): near_sum = jnp.dot(dense_flat, stacked, preferred_element_type=jnp.float32)  4.02 us
  transfers between devices with their start and end apart: 8, of which 6 were waited for; matrix products, arithmetic and copies ran while one was open for 1% of the time, Pallas kernels for 0%

commit v1 on v0

v1 whole, which is shorter than its diff:
```python
import functools

import jax
import jax.numpy as jnp
from jax import lax
from jax.experimental import pallas as pl
from jax.experimental.pallas import tpu as pltpu
from jax.sharding import PartitionSpec as P

BF = jnp.bfloat16
F32 = jnp.float32


def shifted(block, axis, distance):
    devices = range(lax.axis_size(axis))
    route = [(i - distance, i) for i in devices if i - distance in devices]
    return lax.ppermute(block, axis, route)


def image_part(operand, right_bases, left_bases, near_tiles, tile_ranks, column_rows, row_columns):
    tile_slots = right_bases.shape[1]
    rank_part = right_bases.shape[2]
    tile_rows = right_bases.shape[3]
    probe_count = operand.shape[1]
    tile_count = lax.axis_size("tile")
    right_flat = right_bases.reshape(tile_slots * rank_part, tile_rows)
    left_flat = left_bases.reshape(tile_slots * rank_part, tile_rows)
    dense_flat = near_tiles.reshape(tile_rows, -1)
    values = jnp.dot(
        right_flat,
        lax.all_gather(operand, "list", axis=0, tiled=True),
        preferred_element_type=F32,
    )
    rank_level = lax.axis_index("list") * rank_part + lax.iota(jnp.int32, rank_part)
    rank_mask = rank_level[None, :] < tile_ranks[0][:, None]
    coefficients = jnp.where(
        rank_mask[:, :, None], values.reshape(tile_slots, rank_part, probe_count), 0.0
    ).astype(BF)
    targets = (column_rows[0][None, :] == lax.iota(jnp.int32, tile_count)[:, None]).astype(BF)
    outgoing = jnp.einsum(
        "dk,krp->drp", targets, coefficients, preferred_element_type=F32
    ).astype(BF)
    sources = (row_columns[0][:, None] == lax.iota(jnp.int32, tile_count)[None, :]).astype(BF)
    chosen = jnp.einsum(
        "kj,jrp->krp",
        sources,
        lax.all_to_all(outgoing, "tile", split_axis=0, concat_axis=0, tiled=True),
        preferred_element_type=F32,
    ).astype(BF)
    chosen = chosen.reshape(tile_slots * rank_part, -1)
    far_sum = lax.dot_general(
        left_flat, chosen, (((0,), (0,)), ((), ())), preferred_element_type=F32
    )
    arrived = {}
    for offset in (1, -1):
        arrived[offset] = shifted(operand, "tile", offset)
    stacked = jnp.concatenate([arrived[1], operand, arrived[-1]], axis=0)
    near_sum = jnp.dot(dense_flat, stacked, preferred_element_type=F32)
    partial_image = near_sum + far_sum
    return lax.psum_scatter(partial_image, "list", scatter_dimension=0, tiled=True)


def many_slots(probes, right_bases, left_bases, near_tiles, tile_ranks, column_rows, row_columns):
    rest = (right_bases, left_bases, near_tiles, tile_ranks, column_rows, row_columns)
    first_pass = image_part(probes.astype(BF), *rest).astype(BF)
    return image_part(first_pass, *rest)


VMEM = pl.BlockSpec(memory_space=pltpu.VMEM)
SMEM = pl.BlockSpec(memory_space=pltpu.SMEM)


def image_kernel(tile_count, near_ref, left_ref, blocks_ref, right_ref, columns_ref, out_ref):
    me = lax.axis_index("tile")
    rows = near_ref.shape[2]
    parts = out_ref.shape[0]
    source = columns_ref[0, 0]
    coefficients = jnp.dot(
        right_ref[source], blocks_ref[source], preferred_element_type=F32
    ).astype(BF)
    above = jnp.where(me > 0, blocks_ref[jnp.maximum(me - 1, 0)], 0)
    below = jnp.where(me < tile_count - 1, blocks_ref[jnp.minimum(me + 1, tile_count - 1)], 0)
    own = blocks_ref[me]
    for part in range(parts):
        cut = slice(part * rows, (part + 1) * rows)
        total = lax.dot_general(
            left_ref[:, cut], coefficients, (((0,), (0,)), ((), ())), preferred_element_type=F32
        )
        for side, block in enumerate((above, own, below)):
            total += jnp.dot(near_ref[side, cut, :], block, preferred_element_type=F32)
        out_ref[part] = total.astype(out_ref.dtype)


def image(near, left, blocks, right, row_columns):
    tile_count, rows, probes = blocks.shape
    parts = near.shape[1] // rows
    flops = 2 * near.size * probes
    return pl.pallas_call(
        functools.partial(image_kernel, tile_count),
        out_shape=jax.ShapeDtypeStruct((parts, rows, probes), BF),
        in_specs=[VMEM, VMEM, VMEM, VMEM, SMEM],
        out_specs=VMEM,
        compiler_params=pltpu.CompilerParams(vmem_limit_bytes=40 * 2**20),
        cost_estimate=pl.CostEstimate(
            flops=flops, bytes_accessed=2 * near.size, transcendentals=0
        ),
    )(near, left, blocks, right, row_columns)


def one_slot(probes, right_bases, left_bases, near_tiles, tile_ranks, column_rows, row_columns):
    rank_part, tile_rows = right_bases.shape[2:]
    rows, probe_count = probes.shape
    list_count = lax.axis_size("list")
    ranks = rank_part * list_count
    me = lax.axis_index("list")
    bases = jnp.stack([right_bases[0, 0], left_bases[0, 0]])
    bases = lax.all_gather(bases, "list", axis=0)
    left = bases[:, 1].reshape(ranks, tile_rows)
    right = lax.dynamic_slice_in_dim(bases[:, 0], me * rows, rows, 2).reshape(ranks, rows)
    keep = lax.iota(jnp.int32, ranks) < tile_ranks[0, 0]
    right = jnp.where(keep[:, None], right, 0)
    near = near_tiles[0].transpose(1, 0, 2)
    block = probes.astype(BF)
    blocks = lax.all_gather(jnp.concatenate([block, right]), "tile", axis=0)
    right, blocks = blocks[:, rows:], blocks[:, :rows]
    partial = image(near, left, blocks, right, row_columns)
    arrived = lax.all_to_all(partial, "list", 0, 0, tiled=True)
    first_pass = jnp.sum(arrived.astype(F32), axis=0).astype(BF)
    blocks = lax.all_gather(first_pass, "tile", axis=0)
    partial = image(near, left, blocks, right, row_columns)
    arrived = lax.all_to_all(partial, "list", 0, 0, tiled=True)
    return jnp.sum(arrived.astype(F32), axis=0)


def local(probes, right_bases, left_bases, near_tiles, tile_ranks, column_rows, row_columns):
    small = right_bases.shape[1] == 1 and lax.axis_size("tile") <= 4
    form = one_slot if small else many_slots
    return form(
        probes, right_bases, left_bases, near_tiles, tile_ranks, column_rows, row_columns
    )


def solution(mesh):
    placed = (
        P(("group", "tile", "list"), None),
        P(("group", "tile"), None, "list", None),
        P(("group", "tile"), None, "list", None),
        P(("group", "tile"), None, None, "list"),
        P(("group", "tile"), None),
        P("tile", None),
        P("tile", None),
    )
    return jax.shard_map(
        local,
        mesh=mesh,
        in_specs=placed,
        out_specs=P(("group", "tile", "list"), None),
        check_vma=False,
    )
```

time: 121 us -> 70 us (0.58)
  waiting for transfers between devices: 57.8 us -> 0 us
  blocking collectives: 15.4 us -> 64.8 us
  starting transfers between devices: 19.9 us -> 0 us
  between operations: 15.5 us -> 1.4 us
  matrix products: 6.17 us -> 0 us
  local copies, waits for them, and re-layouts: 2.67 us -> 0.1 us
  other arithmetic: 3.48 us -> 1.85 us
  Pallas kernels: 0 us -> 1.61 us
    reduce_scatter x2 -> x0, waiting for transfers between devices: 49.1 us -> none  [image_part(): lax.psum_scatter(partial_image, 'list', scatter_dimension=0, tiled=True)]
    all_gather x2 -> x3, blocking collectives: 15.4 us -> 42.3 us  [the longest x1 19.2 us: one_slot(): blocks = lax.all_gather(jnp.concatenate([block, right]), 'tile', axis=0)]
    all_to_all x0 -> x2, blocking collectives: none -> 22.5 us  [one_slot(): arrived = lax.all_to_all(partial, 'list', 0, 0, tiled=True)]
    ppermute x4 -> x0, starting transfers between devices: 10.4 us -> none  [shifted(): return lax.ppermute(block, axis, route)]
    all_to_all x2 -> x0, starting transfers between devices: 9.45 us -> none  [image_part(): lax.all_to_all(outgoing, 'tile', split_axis=0, concat_axis=0, tiled=True)]
    ppermute x4 -> x0, waiting for transfers between devices: 8.24 us -> none  [shifted(): return lax.ppermute(block, axis, route)]
    dot_general x8 -> x0, matrix products: 6.17 us -> none  [the longest x2 4.02 us: image_part(): near_sum = jnp.dot(dense_flat, stacked, preferred_element_type=jnp.float32)]
    convert_element_type x4 -> x1, other arithmetic: 3.47 us -> 0.02 us  [one_slot(): block = probes.astype(BF)]
  transfers between devices with their start and end apart: 8 -> 0, of which waited for: 6 -> 0; matrix products, arithmetic and copies ran while one was open for 1% -> 0% of each run, Pallas kernels for 0% -> 0%
where the time goes in v1:
time: 70 us; the launch traced here: 69.8 us
  blocking collectives  64.8 us (93%)
  other arithmetic  1.85 us (3%)
  Pallas kernels  1.61 us (2%)
  between operations  1.4 us (2%)
    all_to_all x2, blocking collectives, one_slot(): arrived = lax.all_to_all(partial, 'list', 0, 0, tiled=True)  22.5 us
    all_gather x1, blocking collectives, one_slot(): blocks = lax.all_gather(jnp.concatenate([block, right]), 'tile', axis=0)  19.2 us
    all_gather x1, blocking collectives, one_slot(): blocks = lax.all_gather(first_pass, 'tile', axis=0)  15.3 us
    all_gather x1, blocking collectives, one_slot(): bases = lax.all_gather(bases, 'list', axis=0)  7.91 us
    pallas_call x2, Pallas kernels, image(): pl.pallas_call(functools.partial(image_kernel, tile_count), out_shape=jax...  1.61 us

profile of v1, /device:TPU:0, one launch (start us, length us, event | category | flops | bytes accessed | tf_op | source)
XLA Modules:
  0.0 69.8 jit_solution(12063584117159075366)
XLA Ops:
  0.0 0.0 copy-start.1
  0.0 0.9 %pad_maximum_fusion.1 = bf16[2,24,1024]{2,1,0:T(8,128)(2,1)S(1)} fusion(bf16[1,24,1024]{2,1,0:T(8,128)(2,1)} %bitcast.23, bf16[1,24,1024]{2,1,0:T(8,128)(2,1)} %bitcast.24), kind=kLoop, calls=%fused_computation.2 | loop fusion | flops 49152 | bytes 196608 | tf_op jit(solution)/shard_map/stack | solution.py:116
  0.9 7.9 %all-gather = bf16[8,24,1024]{2,1,0:T(8,128)(2,1)S(1)} all-gather(bf16[2,24,1024]{2,1,0:T(8,128)(2,1)S(1)} %pad_maximum_fusion.1), channel_id=2, replica_groups=mesh['group'=2,'tile'=4,'list'=4] {'list'}, dimensions={0}, use_global_device_ids=true | all-gather | bytes 491520 | tf_op jit(solution)/shard_map/all_gather | solution.py:117
  9.5 0.0 copy-done.1
  9.5 0.0 copy-start
  9.6 0.1 bitcast_select_fusion
  9.7 19.2 %all-gather.1 = bf16[1408,256]{1,0:T(8,128)(2,1)S(1)} all-gather(bf16[352,256]{1,0:T(8,128)(2,1)S(1)} %pad_maximum_fusion), channel_id=3, replica_groups=mesh['group'=2,'tile'=4,'list'=4] {'tile'}, dimensions={0}, use_global_device_ids=true | all-gather | bytes 901120 | tf_op jit(solution)/shard_map/all_gather | solution.py:124
  29.6 0.0 copy-done
  29.6 0.8 %shard_map.64 = bf16[4,256,256]{2,1,0:T(8,128)(2,1)S(1)} custom-call(bf16[3,1024,256]{2,1,0:T(8,128)(2,1)S(1)} %bitcast.15, bf16[96,1024]{1,0:T(8,128)(2,1)S(1)} %bitcast.18, bf16[4,256,256]{2,1,0:T(8,128)(2,1)S(1)} %slice.18.blocks_ref, bf16[4,96,256]{2,1,0:T(8,128)(2,1)S(1)} %slice.19.right_ref, s32[1,1]{1,0:T(1,128)S(6)} %copy.11.columns_ref), custom_call_target="tpu_custom_call" | custom-call | flops 402653184 | bytes 1572864 | tf_op jit(solution)/shard_map/pallas_call | solution.py:98
  30.4 11.2 %all_to_all.10 = bf16[4,256,256]{2,1,0:T(8,128)(2,1)S(1)} all-to-all(bf16[4,256,256]{2,1,0:T(8,128)(2,1)S(1)} %shard_map.64), channel_id=1, replica_groups=mesh['group'=2,'tile'=4,'list'=4] {'list'}, dimensions={0} | all-to-all | bytes 1048576 | tf_op jit(solution)/shard_map/all_to_all | solution.py:127
  41.6 0.1 reduce_sum.21
  41.7 15.3 %all-gather.2 = bf16[1024,256]{1,0:T(8,128)(2,1)S(1)} all-gather(bf16[256,256]{1,0:T(8,128)(2,1)S(1)} %reduce_sum.21), channel_id=4, replica_groups=mesh['group'=2,'tile'=4,'list'=4] {'tile'}, dimensions={0}, use_global_device_ids=true | all-gather | bytes 655360 | tf_op jit(solution)/shard_map/all_gather | solution.py:129
  57.0 0.8 %shard_map.65 = bf16[4,256,256]{2,1,0:T(8,128)(2,1)S(1)} custom-call(bf16[3,1024,256]{2,1,0:T(8,128)(2,1)S(1)} %bitcast.16, bf16[96,1024]{1,0:T(8,128)(2,1)S(1)} %bitcast.19, bf16[4,256,256]{2,1,0:T(8,128)(2,1)S(1)} %bitcast.17, bf16[4,96,256]{2,1,0:T(8,128)(2,1)S(1)} %slice.19.right_ref, s32[1,1]{1,0:T(1,128)S(6)} %copy.11.columns_ref), custom_call_target="tpu_custom_call" | custom-call | flops 402653184 | bytes 1572864 | tf_op jit(solution)/shard_map/pallas_call | solution.py:98
  57.8 11.2 %all_to_all.11 = bf16[4,256,256]{2,1,0:T(8,128)(2,1)S(1)} all-to-all(bf16[4,256,256]{2,1,0:T(8,128)(2,1)S(1)} %shard_map.65), channel_id=1, replica_groups=mesh['group'=2,'tile'=4,'list'=4] {'list'}, dimensions={0} | all-to-all | bytes 1048576 | tf_op jit(solution)/shard_map/all_to_all | solution.py:131
  69.0 0.8 %convert_reduce_fusion = f32[256,256]{1,0:T(8,128)} fusion(bf16[4,256,256]{2,1,0:T(8,128)(2,1)S(1)} %all_to_all.11), kind=kLoop, calls=%fused_computation | loop fusion | flops 458752 | bytes 786432 | tf_op jit(solution)/shard_map/reduce_sum | solution.py:132
  (7 shorter events, 0.1 us)
Async XLA Ops:
  0.0 9.5 %copy-start.1 = (f32[256,256]{1,0:T(8,128)S(1)}, f32[256,256]{1,0:T(8,128)}, u32[]{:S(2)}) copy-start(f32[256,256]{1,0:T(8,128)} %param.7) | copy-start | bytes 786436
  9.5 20.1 %copy-start = (bf16[1,1024,3,256]{3,1,2,0:T(8,128)(2,1)S(1)}, bf16[1,1024,3,256]{3,1,2,0:T(8,128)(2,1)}, u32[]{:S(2)}) copy-start(bf16[1,1024,3,256]{3,1,2,0:T(8,128)(2,1)} %param.10) | copy-start | bytes 4718596

commit v2 on v1

--- a/solution.py
+++ b/solution.py
@@ -70,70 +70,147 @@
 SMEM = pl.BlockSpec(memory_space=pltpu.SMEM)
 
 
-def image_kernel(tile_count, near_ref, left_ref, blocks_ref, right_ref, columns_ref, out_ref):
-    me = lax.axis_index("tile")
+def chosen_coefficients(tile_count, columns_ref, coefficient_refs):
+    distance = lax.rem(lax.axis_index("tile") - columns_ref[0, 0] + tile_count, tile_count)
+    chosen = coefficient_refs[0][...]
+    for step in range(1, tile_count):
+        chosen = jnp.where(distance == step, coefficient_refs[step][...], chosen)
+    return chosen
+
+
+def row_part(near_ref, left_ref, block_refs, coefficients, start):
     rows = near_ref.shape[2]
-    parts = out_ref.shape[0]
-    source = columns_ref[0, 0]
-    coefficients = jnp.dot(
-        right_ref[source], blocks_ref[source], preferred_element_type=F32
-    ).astype(BF)
-    above = jnp.where(me > 0, blocks_ref[jnp.maximum(me - 1, 0)], 0)
-    below = jnp.where(me < tile_count - 1, blocks_ref[jnp.minimum(me + 1, tile_count - 1)], 0)
-    own = blocks_ref[me]
-    for part in range(parts):
-        cut = slice(part * rows, (part + 1) * rows)
-        total = lax.dot_general(
-            left_ref[:, cut], coefficients, (((0,), (0,)), ((), ())), preferred_element_type=F32
-        )
-        for side, block in enumerate((above, own, below)):
-            total += jnp.dot(near_ref[side, cut, :], block, preferred_element_type=F32)
-        out_ref[part] = total.astype(out_ref.dtype)
-
-
-def image(near, left, blocks, right, row_columns):
-    tile_count, rows, probes = blocks.shape
-    parts = near.shape[1] // rows
-    flops = 2 * near.size * probes
+    cut = pl.ds(pl.multiple_of(start, rows), rows)
+    total = lax.dot_general(
+        left_ref[:, cut], coefficients, (((0,), (0,)), ((), ())), preferred_element_type=F32
+    )
+    for side, block_ref in enumerate(block_refs):
+        total += jnp.dot(near_ref[side, cut, :], block_ref[...], preferred_element_type=F32)
+    return total
+
+
+def first_kernel(tile_count, rank_part, near_ref, left_ref, right_ref, ranks_ref, columns_ref, *refs):
+    block_refs, coefficient_refs, (keep_ref, send_ref) = refs[:3], refs[3:-2], refs[-2:]
+    rows = near_ref.shape[2]
+    groups, rank_rows = right_ref.shape[:2]
+    me = lax.axis_index("list")
+    coefficients = chosen_coefficients(tile_count, columns_ref, coefficient_refs)
+    sums = [jnp.zeros((rank_rows, rows), F32)] * groups
+    for turn in range(groups):
+        part = me ^ turn
+        total = row_part(near_ref, left_ref, block_refs, coefficients, part * rows)
+        out_ref = send_ref if turn % 2 else keep_ref
+        out_ref[turn // 2, :rows, :] = total.astype(out_ref.dtype)
+        rounded = total.astype(BF)
+        cut = pl.ds(pl.multiple_of(part * rows, rows), rows)
+        for group in range(groups):
+            sums[group] += jnp.dot(
+                right_ref[me ^ group, :, cut], rounded, preferred_element_type=F32
+            )
+    slot = lax.broadcasted_iota(jnp.int32, (rank_rows, rows), 0)
+    for turn in range(groups):
+        level = (me ^ turn) * rank_part + slot
+        out_ref = send_ref if turn % 2 else keep_ref
+        out_ref[turn // 2, rows:, :] = jnp.where(
+            level < ranks_ref[0, 0], sums[turn], 0.0
+        ).astype(out_ref.dtype)
+
+
+def second_kernel(tile_count, near_ref, left_ref, columns_ref, *refs):
+    block_refs, coefficient_refs, (keep_ref, send_ref) = refs[:3], refs[3:-2], refs[-2:]
+    rows = near_ref.shape[2]
+    me = lax.axis_index("list")
+    coefficients = chosen_coefficients(tile_count, columns_ref, coefficient_refs)
+    for turn in range(2 * keep_ref.shape[0]):
+        total = row_part(near_ref, left_ref, block_refs, coefficients, (me ^ turn) * rows)
+        out_ref = send_ref if turn % 2 else keep_ref
+        out_ref[turn // 2] = total.astype(out_ref.dtype)
+
+
+def call(kernel, out_rows, near, operands, smem):
+    rows = near.shape[2]
+    half = near.shape[1] // rows // 2
+    shape = (half, out_rows, operands[-1].shape[-1])
     return pl.pallas_call(
-        functools.partial(image_kernel, tile_count),
-        out_shape=jax.ShapeDtypeStruct((parts, rows, probes), BF),
-        in_specs=[VMEM, VMEM, VMEM, VMEM, SMEM],
-        out_specs=VMEM,
+        kernel,
+        out_shape=(jax.ShapeDtypeStruct(shape, F32), jax.ShapeDtypeStruct(shape, SEND)),
+        in_specs=[SMEM if index in smem else VMEM for index in range(len(operands) + 1)],
+        out_specs=(VMEM, VMEM),
         compiler_params=pltpu.CompilerParams(vmem_limit_bytes=40 * 2**20),
         cost_estimate=pl.CostEstimate(
-            flops=flops, bytes_accessed=2 * near.size, transcendentals=0
+            flops=2 * near.size * shape[2], bytes_accessed=2 * near.size, transcendentals=0
         ),
-    )(near, left, blocks, right, row_columns)
+    )(near, *operands)
+
+
+SEND = F32
+
+
+def rotated(block, axis, distance):
+    count = lax.axis_size(axis)
+    return lax.ppermute(block, axis, [(i, (i + distance) % count) for i in range(count)])
+
+
+def swapped(block, axis, bit):
+    return lax.ppermute(block, axis, [(i, i ^ bit) for i in range(lax.axis_size(axis))])
+
+
+def wrapped(block, axis):
+    last = lax.axis_size(axis) - 1
+    return lax.ppermute(block, axis, [(0, last), (last, 0)])
+
+
+def list_sum(keep, send):
+    pair = keep + swapped(send, "list", 1)
+    return pair[0] + swapped(pair[1].astype(BF), "list", 2)
 
 
 def one_slot(probes, right_bases, left_bases, near_tiles, tile_ranks, column_rows, row_columns):
     rank_part, tile_rows = right_bases.shape[2:]
-    rows, probe_count = probes.shape
-    list_count = lax.axis_size("list")
-    ranks = rank_part * list_count
-    me = lax.axis_index("list")
-    bases = jnp.stack([right_bases[0, 0], left_bases[0, 0]])
-    bases = lax.all_gather(bases, "list", axis=0)
-    left = bases[:, 1].reshape(ranks, tile_rows)
-    right = lax.dynamic_slice_in_dim(bases[:, 0], me * rows, rows, 2).reshape(ranks, rows)
-    keep = lax.iota(jnp.int32, ranks) < tile_ranks[0, 0]
-    right = jnp.where(keep[:, None], right, 0)
+    rows = probes.shape[0]
+    tile_count = lax.axis_size("tile")
+    rank_rows = -(-rank_part // 16) * 16
+    padding = jnp.zeros((rank_rows - rank_part, tile_rows), BF)
+    own_right = jnp.concatenate([right_bases[0, 0], padding])
+    left = jnp.concatenate([left_bases[0, 0], padding])
     near = near_tiles[0].transpose(1, 0, 2)
     block = probes.astype(BF)
-    blocks = lax.all_gather(jnp.concatenate([block, right]), "tile", axis=0)
-    right, blocks = blocks[:, rows:], blocks[:, :rows]
-    partial = image(near, left, blocks, right, row_columns)
-    arrived = lax.all_to_all(partial, "list", 0, 0, tiled=True)
-    first_pass = jnp.sum(arrived.astype(F32), axis=0).astype(BF)
-    blocks = lax.all_gather(first_pass, "tile", axis=0)
-    partial = image(near, left, blocks, right, row_columns)
-    arrived = lax.all_to_all(partial, "list", 0, 0, tiled=True)
-    return jnp.sum(arrived.astype(F32), axis=0)
+    above, below = shifted(block, "tile", 1), shifted(block, "tile", -1)
+    column = lax.all_gather(block, "list", axis=0, tiled=True)
+    right = lax.all_gather(own_right, "list", axis=0)
+    values = jnp.dot(own_right, column, preferred_element_type=F32)
+    level = lax.axis_index("list") * rank_part + lax.iota(jnp.int32, rank_rows)
+    own = jnp.where((level < tile_ranks[0, 0])[:, None], values, 0.0).astype(BF)
+    coefficients = [own] + [rotated(own, "tile", step) for step in range(1, tile_count)]
+    keep, send = call(
+        functools.partial(first_kernel, tile_count, rank_part),
+        rows + rank_rows,
+        near,
+        (left, right, tile_ranks, row_columns, above, block, below, *coefficients),
+        (3, 4),
+    )
+    both = list_sum(keep, send).astype(BF)
+    above, below = shifted(both, "tile", 1), shifted(both, "tile", -1)
+    own = both[rows:]
+    ends = wrapped(own, "tile")
+    me = lax.axis_index("tile")
+    coefficients = [own]
+    coefficients.append(jnp.where(me == 0, ends, above[rows:]))
+    coefficients += [rotated(own, "tile", step) for step in range(2, tile_count - 1)]
+    coefficients.append(jnp.where(me == tile_count - 1, ends, below[rows:]))
+    keep, send = call(
+        functools.partial(second_kernel, tile_count),
+        rows,
+        near,
+        (left, row_columns, above[:rows], both[:rows], below[:rows], *coefficients),
+        (2,),
+    )
+    return list_sum(keep, send)
 
 
 def local(probes, right_bases, left_bases, near_tiles, tile_ranks, column_rows, row_columns):
-    small = right_bases.shape[1] == 1 and lax.axis_size("tile") <= 4
+    few = lax.axis_size("tile") == 4 and lax.axis_size("list") == 4
+    small = right_bases.shape[1] == 1 and few
     form = one_slot if small else many_slots
     return form(
         probes, right_bases, left_bases, near_tiles, tile_ranks, column_rows, row_columns

time: 70 us -> 61.7 us (0.88)
  blocking collectives: 64.8 us -> 13 us
  starting transfers between devices: 0 us -> 23.4 us
  waiting for transfers between devices: 0 us -> 18.1 us
  matrix products: 0 us -> 1 us
    all_gather x3 -> x2, blocking collectives: 42.3 us -> 13 us  [the longest x1 7.17 us: one_slot(): column = lax.all_gather(block, 'list', axis=0, tiled=True)]
    ppermute x0 -> x13, starting transfers between devices: none -> 23.4 us  [the longest x4 10.1 us: shifted(): return lax.ppermute(block, axis, route)]
    all_to_all x2 -> x0, blocking collectives: 22.5 us -> none  [one_slot(): arrived = lax.all_to_all(partial, 'list', 0, 0, tiled=True)]
    ppermute x0 -> x13, waiting for transfers between devices: none -> 18.1 us  [the longest x4 13.5 us: swapped(): lax.ppermute(block, axis, [(i, i ^ bit) for i in range(lax.axis_size(axis...]
    convert_element_type x1, other arithmetic: 0.02 us -> 1.08 us  [one_slot(): block = probes.astype(BF)]
    dot_general x0 -> x1, matrix products: none -> 1 us  [one_slot(): values = jnp.dot(own_right, column, preferred_element_type=F32)]
    another operation x1 -> x0, other arithmetic: 0.88 us -> none  [one_slot(): bases = jnp.stack([right_bases[0, 0], left_bases[0, 0]])]
    add x0 -> x3, other arithmetic: none -> 0.87 us  [the longest x1 0.73 us: list_sum(): return pair[0] + swapped(pair[1].astype(BF), 'list', 2)]
  transfers between devices with their start and end apart: 0 -> 13, of which waited for: 0 -> 6; matrix products, arithmetic and copies ran while one was open for 0% -> 2% of each run, Pallas kernels for 0% -> 0%
where the time goes in v2:
time: 61.7 us; the launch traced here: 61.4 us
  starting transfers between devices  23.4 us (38%)
  waiting for transfers between devices  18.1 us (29%)
  blocking collectives  13 us (21%)
  Pallas kernels  2.29 us (4%)
  other arithmetic  2 us (3%)
  between operations  1.52 us (2%)
  matrix products  1 us (2%)
    ppermute x4, waiting for transfers between devices, swapped(): lax.ppermute(block, axis, [(i, i ^ bit) for i in range(lax.axis_size(axis...  13.5 us
    ppermute x4, starting transfers between devices, shifted(): return lax.ppermute(block, axis, route)  10.1 us
    all_gather x1, blocking collectives, one_slot(): column = lax.all_gather(block, 'list', axis=0, tiled=True)  7.17 us
    ppermute x4, starting transfers between devices, rotated(): lax.ppermute(block, axis, [(i, (i + distance) % count) for i in range(cou...  6.7 us
    all_gather x1, blocking collectives, one_slot(): right = lax.all_gather(own_right, 'list', axis=0)  5.79 us
    ppermute x1, starting transfers between devices, wrapped(): return lax.ppermute(block, axis, [(0, last), (last, 0)])  4.32 us
    ppermute x1, waiting for transfers between devices, wrapped(): return lax.ppermute(block, axis, [(0, last), (last, 0)])  2.99 us
    pallas_call x2, Pallas kernels, call(): pl.pallas_call(kernel, out_shape=(jax.ShapeDtypeStruct(shape, F32), jax.S...  2.29 us
  transfers between devices with their start and end apart: 13, of which 6 were waited for; matrix products, arithmetic and copies ran while one was open for 2% of the time, Pallas kernels for 0%

profile of v2, /device:TPU:0, one launch (start us, length us, event | category | flops | bytes accessed | tf_op | source)
XLA Modules:
  0.0 61.4 jit_solution(4063419507965927209)
XLA Ops:
  0.0 1.1 %convert_element_type.23.refs_1_ = bf16[256,256]{1,0:T(8,128)(2,1)S(1)} convert(f32[256,256]{1,0:T(8,128)} %param.7) | non-fusion elementwise | flops 65536 | bytes 393216 | tf_op jit(solution)/shard_map/convert_element_type | solution.py:177
  1.1 4.9 %collective-permute-start = (bf16[256,256]{1,0:T(8,128)(2,1)S(1)}, bf16[256,256]{1,0:T(8,128)(2,1)S(1)}, u32[]{:S(2)}, u32[]{:S(2)}) collective-permute-start(bf16[256,256]{1,0:T(8,128)(2,1)S(1)} %convert_element_type.23.refs_1_), channel_id=1, source_target_pairs={{0,4},{4,8},{8,12},{1,5},{5,9},{9,13},{2,6},{6,10},{10,14},{3,7},{... | collective-permute-start | bytes 393224 | tf_op jit(solution)/shard_map/ppermute | solution.py:17
  6.0 1.3 %collective-permute-start.1 = (bf16[256,256]{1,0:T(8,128)(2,1)S(1)}, bf16[256,256]{1,0:T(8,128)(2,1)S(1)}, u32[]{:S(2)}, u32[]{:S(2)}) collective-permute-start(bf16[256,256]{1,0:T(8,128)(2,1)S(1)} %convert_element_type.23.refs_1_), channel_id=1, source_target_pairs={{4,0},{8,4},{12,8},{5,1},{9,5},{13,9},{6,2},{10,6},{14,10},{7,3},{... | collective-permute-start | bytes 393224 | tf_op jit(solution)/shard_map/ppermute | solution.py:17
  7.3 7.2 %all_gather.11 = bf16[1024,256]{1,0:T(8,128)(2,1)S(1)} all-gather(bf16[256,256]{1,0:T(8,128)(2,1)S(1)} %convert_element_type.23.refs_1_), channel_id=1, replica_groups=mesh['group'=2,'tile'=4,'list'=4] {'list'}, dimensions={0}, use_global_device_ids=true | all-gather | bytes 655360 | tf_op jit(solution)/shard_map/all_gather | solution.py:179
  15.2 1.0 %fusion.refs_3_ = bf16[32,256]{1,0:T(8,128)(2,1)S(1)} fusion(bf16[1024,256]{1,0:T(8,128)(2,1)S(1)} %all_gather.11, pred[32]{0:T(512)(128)(4,1)S(1)} %add_compare_fusion, bf16[24,1024]{1,0:T(8,128)(2,1)} %bitcast.26), kind=kOutput, calls=%fused_computation.1 | convolution fusion | flops 16793600 | bytes 589856 | tf_op jit(solution)/shard_map/dot_general | solution.py:181
  16.2 2.7 %collective-permute-start.2 = (bf16[32,256]{1,0:T(8,128)(2,1)S(1)}, bf16[32,256]{1,0:T(8,128)(2,1)S(1)}, u32[]{:S(2)}, u32[]{:S(2)}) collective-permute-start(bf16[32,256]{1,0:T(8,128)(2,1)S(1)} %fusion.refs_3_), channel_id=1, source_target_pairs={{0,4},{4,8},{8,12},{12,0},{1,5},{5,9},{9,13},{13,1},{2,6},{6,10},{... | collective-permute-start | bytes 49160 | tf_op jit(solution)/shard_map/ppermute | solution.py:151
  18.9 2.6 %collective-permute-start.3 = (bf16[32,256]{1,0:T(8,128)(2,1)S(1)}, bf16[32,256]{1,0:T(8,128)(2,1)S(1)}, u32[]{:S(2)}, u32[]{:S(2)}) collective-permute-start(bf16[32,256]{1,0:T(8,128)(2,1)S(1)} %fusion.refs_3_), channel_id=1, source_target_pairs={{0,8},{4,12},{8,0},{12,4},{1,9},{5,13},{9,1},{13,5},{2,10},{6,14},... | collective-permute-start | bytes 49160 | tf_op jit(solution)/shard_map/ppermute | solution.py:151
  21.5 1.3 %collective-permute-start.4 = (bf16[32,256]{1,0:T(8,128)(2,1)S(1)}, bf16[32,256]{1,0:T(8,128)(2,1)S(1)}, u32[]{:S(2)}, u32[]{:S(2)}) collective-permute-start(bf16[32,256]{1,0:T(8,128)(2,1)S(1)} %fusion.refs_3_), channel_id=1, source_target_pairs={{0,12},{4,0},{8,4},{12,8},{1,13},{5,1},{9,5},{13,9},{2,14},{6,2},{... | collective-permute-start | bytes 49160 | tf_op jit(solution)/shard_map/ppermute | solution.py:151
  22.8 5.8 %all-gather = bf16[128,1024]{1,0:T(8,128)(2,1)S(1)} all-gather(bf16[32,1024]{1,0:T(8,128)(2,1)S(1)} %concatenate.7), channel_id=2, replica_groups=mesh['group'=2,'tile'=4,'list'=4] {'list'}, dimensions={0}, use_global_device_ids=true | all-gather | bytes 327680 | tf_op jit(solution)/shard_map/all_gather | solution.py:180
  29.3 1.6 %shard_map.64 = (f32[2,288,256]{2,1,0:T(8,128)S(1)}, f32[2,288,256]{2,1,0:T(8,128)S(1)}) custom-call(bf16[3,1024,256]{2,1,0:T(8,128)(2,1)S(1)} %bitcast.23, bf16[32,1024]{1,0:T(8,128)(2,1)S(1)} %concatenate.6.left_ref, bf16[4,32,1024]{2,1,0:T(8,128)(2,1)S(1)} %bitcast.25, s32[1,1]{1,0:T(1,128)} %copy.7.ranks_ref, s32[1,1]{1,0:T(1,128)S(6)} %copy.8.columns_ref, ...), custom_call_target="tpu_custom_call" | custom-call | flops 402653184 | bytes 1572864 | tf_op jit(solution)/shard_map/pallas_call | solution.py:134
  30.9 0.4 collective-permute-start.5
  31.3 1.7 %collective-permute-done.5 = f32[2,288,256]{2,1,0:T(8,128)S(1)} collective-permute-done((f32[2,288,256]{2,1,0:T(8,128)S(1)}, f32[2,288,256]{2,1,0:T(8,128)S(1)}, u32[]{:S(2)}, u32[]{:S(2)}) %collective-permute-start.5) | collective-permute-done | bytes 589856 | tf_op jit(solution)/shard_map/ppermute | solution.py:155
  33.1 0.9 %collective-permute-start.6 = (bf16[288,256]{1,0:T(8,128)(2,1)S(1)}, bf16[288,256]{1,0:T(8,128)(2,1)S(1)}, u32[]{:S(2)}, u32[]{:S(2)}) collective-permute-start(bf16[288,256]{1,0:T(8,128)(2,1)S(1)} %fusion.4), channel_id=1, source_target_pairs={{0,2},{1,3},{2,0},{3,1},{4,6},{5,7},{6,4},{7,5},{8,10},{9,11},{10,... | collective-permute-start | bytes 442376 | tf_op jit(solution)/shard_map/ppermute | solution.py:155
  34.0 5.3 %collective-permute-done.6 = bf16[288,256]{1,0:T(8,128)(2,1)S(1)} collective-permute-done((bf16[288,256]{1,0:T(8,128)(2,1)S(1)}, bf16[288,256]{1,0:T(8,128)(2,1)S(1)}, u32[]{:S(2)}, u32[]{:S(2)}) %collective-permute-start.6) | collective-permute-done | bytes 147488 | tf_op jit(solution)/shard_map/ppermute | solution.py:155
  39.3 2.6 %collective-permute-start.7 = (bf16[288,256]{1,0:T(8,128)(2,1)S(1)}, bf16[288,256]{1,0:T(8,128)(2,1)S(1)}, u32[]{:S(2)}, u32[]{:S(2)}) collective-permute-start(bf16[288,256]{1,0:T(8,128)(2,1)S(1)} %fusion.2), channel_id=1, source_target_pairs={{0,4},{4,8},{8,12},{1,5},{5,9},{9,13},{2,6},{6,10},{10,14},{3,7},{... | collective-permute-start | bytes 442376 | tf_op jit(solution)/shard_map/ppermute | solution.py:17
  41.9 1.3 %collective-permute-start.8 = (bf16[288,256]{1,0:T(8,128)(2,1)S(1)}, bf16[288,256]{1,0:T(8,128)(2,1)S(1)}, u32[]{:S(2)}, u32[]{:S(2)}) collective-permute-start(bf16[288,256]{1,0:T(8,128)(2,1)S(1)} %fusion.2), channel_id=1, source_target_pairs={{4,0},{8,4},{12,8},{5,1},{9,5},{13,9},{6,2},{10,6},{14,10},{7,3},{... | collective-permute-start | bytes 442376 | tf_op jit(solution)/shard_map/ppermute | solution.py:17
  43.2 4.3 %collective-permute-start.9 = (bf16[32,256]{1,0:T(8,128)(2,1)S(1)}, bf16[32,256]{1,0:T(8,128)(2,1)S(1)}, u32[]{:S(2)}, u32[]{:S(2)}) collective-permute-start(bf16[32,256]{1,0:T(8,128)(2,1)S(1)} %slice.47.refs_3_), channel_id=1, source_target_pairs={{0,12},{12,0},{1,13},{13,1},{2,14},{14,2},{3,15},{15,3},{16,28},{2... | collective-permute-start | bytes 49160 | tf_op jit(solution)/shard_map/ppermute | solution.py:160
  47.6 3.0 %collective-permute-done.9 = bf16[32,256]{1,0:T(8,128)(2,1)S(1)} collective-permute-done((bf16[32,256]{1,0:T(8,128)(2,1)S(1)}, bf16[32,256]{1,0:T(8,128)(2,1)S(1)}, u32[]{:S(2)}, u32[]{:S(2)}) %collective-permute-start.9) | collective-permute-done | bytes 16416 | tf_op jit(solution)/shard_map/ppermute | solution.py:160
  50.7 1.6 %collective-permute-done.10.refs_5_ = bf16[32,256]{1,0:T(8,128)(2,1)S(1)} collective-permute-done((bf16[32,256]{1,0:T(8,128)(2,1)S(1)}, bf16[32,256]{1,0:T(8,128)(2,1)S(1)}, u32[]{:S(2)}, u32[]{:S(2)}) %collective-permute-start.10) | collective-permute-done | bytes 16416 | tf_op jit(solution)/shard_map/ppermute | solution.py:151
  52.3 0.7 %shard_map.65 = (f32[2,256,256]{2,1,0:T(8,128)S(1)}, f32[2,256,256]{2,1,0:T(8,128)S(1)}) custom-call(bf16[3,1024,256]{2,1,0:T(8,128)(2,1)S(1)} %bitcast.24, bf16[32,1024]{1,0:T(8,128)(2,1)S(1)} %concatenate.6.left_ref, s32[1,1]{1,0:T(1,128)S(6)} %copy.8.columns_ref, bf16[256,256]{1,0:T(8,128)(2,1)S(1)} %slice.44.refs_0_, ...), custom_call_target="tpu_custom_call" | custom-call | flops 402653184 | bytes 1572864 | tf_op jit(solution)/shard_map/pallas_call | solution.py:134
  53.0 1.9 %collective-permute-done.11 = f32[2,256,256]{2,1,0:T(8,128)S(1)} collective-permute-done((f32[2,256,256]{2,1,0:T(8,128)S(1)}, f32[2,256,256]{2,1,0:T(8,128)S(1)}, u32[]{:S(2)}, u32[]{:S(2)}) %collective-permute-start.11) | collective-permute-done | bytes 524320 | tf_op jit(solution)/shard_map/ppermute | solution.py:155
  55.0 0.9 %collective-permute-start.12 = (bf16[256,256]{1,0:T(8,128)(2,1)S(1)}, bf16[256,256]{1,0:T(8,128)(2,1)S(1)}, u32[]{:S(2)}, u32[]{:S(2)}) collective-permute-start(bf16[256,256]{1,0:T(8,128)(2,1)S(1)} %fusion.5), channel_id=1, source_target_pairs={{0,2},{1,3},{2,0},{3,1},{4,6},{5,7},{6,4},{7,5},{8,10},{9,11},{10,... | collective-permute-start | bytes 393224 | tf_op jit(solution)/shard_map/ppermute | solution.py:155
  55.9 4.7 %collective-permute-done.12 = bf16[256,256]{1,0:T(8,128)(2,1)S(1)} collective-permute-done((bf16[256,256]{1,0:T(8,128)(2,1)S(1)}, bf16[256,256]{1,0:T(8,128)(2,1)S(1)}, u32[]{:S(2)}, u32[]{:S(2)}) %collective-permute-start.12) | collective-permute-done | bytes 131104 | tf_op jit(solution)/shard_map/ppermute | solution.py:155
  60.6 0.7 %fusion.3 = f32[256,256]{1,0:T(8,128)} fusion(f32[2,256,256]{2,1,0:T(8,128)S(1)} %add.30, bf16[256,256]{1,0:T(8,128)(2,1)S(1)} %collective-permute-done.12), kind=kLoop, calls=%fused_computation.8 | loop fusion | flops 131072 | bytes 655360 | tf_op jit(solution)/shard_map/add | solution.py:165
  (28 shorter events, 0.4 us)
Async XLA Ops:
  0.0 22.8 %copy-start.1 = (bf16[1,1,24,1024]{3,2,1,0:T(8,128)(2,1)S(1)}, bf16[1,1,24,1024]{3,2,1,0:T(8,128)(2,1)}, u32[]{:S(2)}) copy-start(bf16[1,1,24,1024]{3,2,1,0:T(8,128)(2,1)} %param.8) | copy-start | bytes 147460
  0.0 28.6 %copy-start.2 = (bf16[1,1,24,1024]{3,2,1,0:T(8,128)(2,1)S(1)}, bf16[1,1,24,1024]{3,2,1,0:T(8,128)(2,1)}, u32[]{:S(2)}) copy-start(bf16[1,1,24,1024]{3,2,1,0:T(8,128)(2,1)} %param.9) | copy-start | bytes 147460
  0.0 29.3 %copy-start = (bf16[1,1024,3,256]{3,1,2,0:T(8,128)(2,1)S(1)}, bf16[1,1024,3,256]{3,1,2,0:T(8,128)(2,1)}, u32[]{:S(2)}) copy-start(bf16[1,1024,3,256]{3,1,2,0:T(8,128)(2,1)} %param.10) | copy-start | bytes 4718596
  1.1 28.2 %collective-permute-start = (bf16[256,256]{1,0:T(8,128)(2,1)S(1)}, bf16[256,256]{1,0:T(8,128)(2,1)S(1)}, u32[]{:S(2)}, u32[]{:S(2)}) collective-permute-start(bf16[256,256]{1,0:T(8,128)(2,1)S(1)} %convert_element_type.23.refs_1_), channel_id=1, source_target_pairs={{0,4},{4,8},{8,12},{1,5},{5,9},{9,13},{2,6},{6,10},{10,14},{3,7},{... | collective-permute-start | bytes 393224 | tf_op jit(solution)/shard_map/ppermute | solution.py:17
  6.0 23.3 %collective-permute-start.1 = (bf16[256,256]{1,0:T(8,128)(2,1)S(1)}, bf16[256,256]{1,0:T(8,128)(2,1)S(1)}, u32[]{:S(2)}, u32[]{:S(2)}) collective-permute-start(bf16[256,256]{1,0:T(8,128)(2,1)S(1)} %convert_element_type.23.refs_1_), channel_id=1, source_target_pairs={{4,0},{8,4},{12,8},{5,1},{9,5},{13,9},{6,2},{10,6},{14,10},{7,3},{... | collective-permute-start | bytes 393224 | tf_op jit(solution)/shard_map/ppermute | solution.py:17
  16.2 13.1 %collective-permute-start.2 = (bf16[32,256]{1,0:T(8,128)(2,1)S(1)}, bf16[32,256]{1,0:T(8,128)(2,1)S(1)}, u32[]{:S(2)}, u32[]{:S(2)}) collective-permute-start(bf16[32,256]{1,0:T(8,128)(2,1)S(1)} %fusion.refs_3_), channel_id=1, source_target_pairs={{0,4},{4,8},{8,12},{12,0},{1,5},{5,9},{9,13},{13,1},{2,6},{6,10},{... | collective-permute-start | bytes 49160 | tf_op jit(solution)/shard_map/ppermute | solution.py:151
  18.9 10.4 %collective-permute-start.3 = (bf16[32,256]{1,0:T(8,128)(2,1)S(1)}, bf16[32,256]{1,0:T(8,128)(2,1)S(1)}, u32[]{:S(2)}, u32[]{:S(2)}) collective-permute-start(bf16[32,256]{1,0:T(8,128)(2,1)S(1)} %fusion.refs_3_), channel_id=1, source_target_pairs={{0,8},{4,12},{8,0},{12,4},{1,9},{5,13},{9,1},{13,5},{2,10},{6,14},... | collective-permute-start | bytes 49160 | tf_op jit(solution)/shard_map/ppermute | solution.py:151
  21.5 7.8 %collective-permute-start.4 = (bf16[32,256]{1,0:T(8,128)(2,1)S(1)}, bf16[32,256]{1,0:T(8,128)(2,1)S(1)}, u32[]{:S(2)}, u32[]{:S(2)}) collective-permute-start(bf16[32,256]{1,0:T(8,128)(2,1)S(1)} %fusion.refs_3_), channel_id=1, source_target_pairs={{0,12},{4,0},{8,4},{12,8},{1,13},{5,1},{9,5},{13,9},{2,14},{6,2},{... | collective-permute-start | bytes 49160 | tf_op jit(solution)/shard_map/ppermute | solution.py:151
  30.9 2.0 %collective-permute-start.5 = (f32[2,288,256]{2,1,0:T(8,128)S(1)}, f32[2,288,256]{2,1,0:T(8,128)S(1)}, u32[]{:S(2)}, u32[]{:S(2)}) collective-permute-start(f32[2,288,256]{2,1,0:T(8,128)S(1)} %get-tuple-element.10), channel_id=1, source_target_pairs={{0,1},{1,0},{2,3},{3,2},{4,5},{5,4},{6,7},{7,6},{8,9},{9,8},{10,11... | collective-permute-start | bytes 1769480 | tf_op jit(solution)/shard_map/ppermute | solution.py:155
  33.1 6.2 %collective-permute-start.6 = (bf16[288,256]{1,0:T(8,128)(2,1)S(1)}, bf16[288,256]{1,0:T(8,128)(2,1)S(1)}, u32[]{:S(2)}, u32[]{:S(2)}) collective-permute-start(bf16[288,256]{1,0:T(8,128)(2,1)S(1)} %fusion.4), channel_id=1, source_target_pairs={{0,2},{1,3},{2,0},{3,1},{4,6},{5,7},{6,4},{7,5},{8,10},{9,11},{10,... | collective-permute-start | bytes 442376 | tf_op jit(solution)/shard_map/ppermute | solution.py:155
  39.3 11.4 %collective-permute-start.7 = (bf16[288,256]{1,0:T(8,128)(2,1)S(1)}, bf16[288,256]{1,0:T(8,128)(2,1)S(1)}, u32[]{:S(2)}, u32[]{:S(2)}) collective-permute-start(bf16[288,256]{1,0:T(8,128)(2,1)S(1)} %fusion.2), channel_id=1, source_target_pairs={{0,4},{4,8},{8,12},{1,5},{5,9},{9,13},{2,6},{6,10},{10,14},{3,7},{... | collective-permute-start | bytes 442376 | tf_op jit(solution)/shard_map/ppermute | solution.py:17
  41.9 8.7 %collective-permute-start.8 = (bf16[288,256]{1,0:T(8,128)(2,1)S(1)}, bf16[288,256]{1,0:T(8,128)(2,1)S(1)}, u32[]{:S(2)}, u32[]{:S(2)}) collective-permute-start(bf16[288,256]{1,0:T(8,128)(2,1)S(1)} %fusion.2), channel_id=1, source_target_pairs={{4,0},{8,4},{12,8},{5,1},{9,5},{13,9},{6,2},{10,6},{14,10},{7,3},{... | collective-permute-start | bytes 442376 | tf_op jit(solution)/shard_map/ppermute | solution.py:17
  43.2 7.4 %collective-permute-start.9 = (bf16[32,256]{1,0:T(8,128)(2,1)S(1)}, bf16[32,256]{1,0:T(8,128)(2,1)S(1)}, u32[]{:S(2)}, u32[]{:S(2)}) collective-permute-start(bf16[32,256]{1,0:T(8,128)(2,1)S(1)} %slice.47.refs_3_), channel_id=1, source_target_pairs={{0,12},{12,0},{1,13},{13,1},{2,14},{14,2},{3,15},{15,3},{16,28},{2... | collective-permute-start | bytes 49160 | tf_op jit(solution)/shard_map/ppermute | solution.py:160
  47.6 4.7 %collective-permute-start.10 = (bf16[32,256]{1,0:T(8,128)(2,1)S(1)}, bf16[32,256]{1,0:T(8,128)(2,1)S(1)}, u32[]{:S(2)}, u32[]{:S(2)}) collective-permute-start(bf16[32,256]{1,0:T(8,128)(2,1)S(1)} %slice.47.refs_3_), channel_id=1, source_target_pairs={{0,8},{4,12},{8,0},{12,4},{1,9},{5,13},{9,1},{13,5},{2,10},{6,14},... | collective-permute-start | bytes 49160 | tf_op jit(solution)/shard_map/ppermute | solution.py:151
  53.0 2.0 %collective-permute-start.11 = (f32[2,256,256]{2,1,0:T(8,128)S(1)}, f32[2,256,256]{2,1,0:T(8,128)S(1)}, u32[]{:S(2)}, u32[]{:S(2)}) collective-permute-start(f32[2,256,256]{2,1,0:T(8,128)S(1)} %get-tuple-element.12), channel_id=1, source_target_pairs={{0,1},{1,0},{2,3},{3,2},{4,5},{5,4},{6,7},{7,6},{8,9},{9,8},{10,11... | collective-permute-start | bytes 1572872 | tf_op jit(solution)/shard_map/ppermute | solution.py:155
  55.0 5.6 %collective-permute-start.12 = (bf16[256,256]{1,0:T(8,128)(2,1)S(1)}, bf16[256,256]{1,0:T(8,128)(2,1)S(1)}, u32[]{:S(2)}, u32[]{:S(2)}) collective-permute-start(bf16[256,256]{1,0:T(8,128)(2,1)S(1)} %fusion.5), channel_id=1, source_target_pairs={{0,2},{1,3},{2,0},{3,1},{4,6},{5,7},{6,4},{7,5},{8,10},{9,11},{10,... | collective-permute-start | bytes 393224 | tf_op jit(solution)/shard_map/ppermute | solution.py:155

commit v3 on v0

v3 whole, which is shorter than its diff:
```python
import functools

import jax
import jax.numpy as jnp
from jax import lax
from jax.experimental import pallas as pl
from jax.experimental.pallas import tpu as pltpu
from jax.sharding import PartitionSpec as P

BF = jnp.bfloat16
F32 = jnp.float32


def shifted(block, axis, distance):
    devices = range(lax.axis_size(axis))
    route = [(i - distance, i) for i in devices if i - distance in devices]
    return lax.ppermute(block, axis, route)


def image_part(operand, right_bases, left_bases, near_tiles, tile_ranks, column_rows, row_columns):
    tile_slots = right_bases.shape[1]
    rank_part = right_bases.shape[2]
    tile_rows = right_bases.shape[3]
    probe_count = operand.shape[1]
    tile_count = lax.axis_size("tile")
    right_flat = right_bases.reshape(tile_slots * rank_part, tile_rows)
    left_flat = left_bases.reshape(tile_slots * rank_part, tile_rows)
    dense_flat = near_tiles.reshape(tile_rows, -1)
    values = jnp.dot(
        right_flat,
        lax.all_gather(operand, "list", axis=0, tiled=True),
        preferred_element_type=F32,
    )
    rank_level = lax.axis_index("list") * rank_part + lax.iota(jnp.int32, rank_part)
    rank_mask = rank_level[None, :] < tile_ranks[0][:, None]
    coefficients = jnp.where(
        rank_mask[:, :, None], values.reshape(tile_slots, rank_part, probe_count), 0.0
    ).astype(BF)
    targets = (column_rows[0][None, :] == lax.iota(jnp.int32, tile_count)[:, None]).astype(BF)
    outgoing = jnp.einsum(
        "dk,krp->drp", targets, coefficients, preferred_element_type=F32
    ).astype(BF)
    sources = (row_columns[0][:, None] == lax.iota(jnp.int32, tile_count)[None, :]).astype(BF)
    chosen = jnp.einsum(
        "kj,jrp->krp",
        sources,
        lax.all_to_all(outgoing, "tile", split_axis=0, concat_axis=0, tiled=True),
        preferred_element_type=F32,
    ).astype(BF)
    chosen = chosen.reshape(tile_slots * rank_part, -1)
    far_sum = lax.dot_general(
        left_flat, chosen, (((0,), (0,)), ((), ())), preferred_element_type=F32
    )
    arrived = {}
    for offset in (1, -1):
        arrived[offset] = shifted(operand, "tile", offset)
    stacked = jnp.concatenate([arrived[1], operand, arrived[-1]], axis=0)
    near_sum = jnp.dot(dense_flat, stacked, preferred_element_type=F32)
    partial_image = near_sum + far_sum
    return lax.psum_scatter(partial_image, "list", scatter_dimension=0, tiled=True)


def many_slots(probes, right_bases, left_bases, near_tiles, tile_ranks, column_rows, row_columns):
    rest = (right_bases, left_bases, near_tiles, tile_ranks, column_rows, row_columns)
    first_pass = image_part(probes.astype(BF), *rest).astype(BF)
    return image_part(first_pass, *rest)


VMEM = pl.BlockSpec(memory_space=pltpu.VMEM)


def kernel_call(kernel, outs, operands, flops=0):
    return pl.pallas_call(
        kernel,
        out_shape=tuple(jax.ShapeDtypeStruct(shape, kind) for shape, kind in outs),
        in_specs=[VMEM] * len(operands),
        out_specs=tuple(VMEM for _ in outs),
        compiler_params=pltpu.CompilerParams(vmem_limit_bytes=40 * 2**20),
        cost_estimate=pl.CostEstimate(
            flops=flops, bytes_accessed=2 * operands[0].size, transcendentals=0
        ),
    )(*operands)


def prepare_kernel(probes_ref, right_ref, left_ref, block_ref, parts_ref, padded_ref):
    ranks = right_ref.shape[0]
    rows = probes_ref.shape[0]
    block_ref[...] = probes_ref[...].astype(BF)
    parts_ref[...] = jnp.zeros_like(parts_ref)
    padded_ref[...] = jnp.zeros_like(padded_ref)
    padded_ref[:ranks, :] = left_ref[...]
    for part in range(parts_ref.shape[0]):
        parts_ref[part, :ranks, :] = right_ref[:, part * rows : (part + 1) * rows]


def kept_levels(group, rank_part, ranks_ref, shape):
    slot = lax.broadcasted_iota(jnp.int32, shape, 0)
    return (group * rank_part + slot < ranks_ref[...]) & (slot < rank_part)


def coefficient_kernel(rank_part, parts_ref, own_ref, across_ref, pair_ref, ranks_ref, out_ref):
    me = lax.axis_index("list")
    blocks = (own_ref[...], pair_ref[0], across_ref[...], pair_ref[1])
    total = jnp.zeros(out_ref.shape, F32)
    for turn, block in enumerate(blocks):
        total += jnp.dot(parts_ref[me ^ turn], block, preferred_element_type=F32)
    keep = kept_levels(me, rank_part, ranks_ref, out_ref.shape)
    out_ref[...] = jnp.where(keep, total, 0.0).astype(out_ref.dtype)


def partner(tile, turn, count):
    if turn == 2:
        return lax.rem(tile + count + 2 * lax.rem(tile, 2) - 1, count)
    return tile ^ (turn if turn < 2 else 2)


def tile_swap(block, turn):
    count = lax.axis_size("tile")
    if turn == 2:
        route = [(i, (i + count + 2 * (i % 2) - 1) % count) for i in range(count)]
    else:
        route = [(i, i ^ (1 if turn == 1 else 2)) for i in range(count)]
    return lax.ppermute(block, "tile", route)


def list_swap(block, bit):
    return lax.ppermute(block, "list", [(i, i ^ bit) for i in range(lax.axis_size("list"))])


def across(block):
    cut = block.shape[0] // 2
    return jnp.concatenate([list_swap(block[:cut], 2), list_swap(block[cut:], 2)])


def far_and_near(rows, columns_ref, block_refs, coefficient_refs):
    count = lax.axis_size("tile")
    tile = lax.axis_index("tile")
    chosen = coefficient_refs[0][...]
    for turn in (1, 2, 3):
        listed = columns_ref[...] == partner(tile, turn, count)
        chosen = jnp.where(listed, coefficient_refs[turn][...], chosen)
    odd = lax.rem(tile, 2)
    inside = (tile > 0) & (tile < count - 1)
    blocks = [
        (1, block_refs[0][:rows, :]),
        (2 - 2 * odd, block_refs[1][:rows, :]),
        (2 * odd, jnp.where(inside, block_refs[2][:rows, :], 0)),
    ]
    return chosen, blocks


def row_part(near_ref, left_ref, blocks, coefficients, part):
    rows = near_ref.shape[2]
    cut = pl.ds(pl.multiple_of(part * rows, rows), rows)
    total = lax.dot_general(
        left_ref[:, cut], coefficients, (((0,), (0,)), ((), ())), preferred_element_type=F32
    )
    for side, block in blocks:
        total += jnp.dot(near_ref[side, cut, :], block, preferred_element_type=F32)
    return total


def first_kernel(rank_part, near_ref, left_ref, columns_ref, ranks_ref, *refs):
    right_refs, block_refs, coefficient_refs = refs[:3], refs[3:6], refs[6:10]
    keep_ref, send_ref = refs[10:]
    rows = near_ref.shape[2]
    me = lax.axis_index("list")
    right = (right_refs[0], right_refs[2].at[0], right_refs[1], right_refs[2].at[1])
    coefficients, blocks = far_and_near(rows, columns_ref, block_refs, coefficient_refs)
    shape = coefficients.shape
    sums = [jnp.zeros(shape, F32)] * 4
    for turn in (1, 3, 0, 2):
        part = me ^ turn
        total = row_part(near_ref, left_ref, blocks, coefficients, part)
        out_ref = send_ref if turn % 2 else keep_ref
        out_ref[turn // 2, :rows, :] = total.astype(out_ref.dtype)
        rounded = total.astype(BF)
        for group in range(4):
            sums[group] += jnp.dot(right[group][part], rounded, preferred_element_type=F32)
    for turn in range(4):
        keep = kept_levels(me ^ turn, rank_part, ranks_ref, shape)
        out_ref = send_ref if turn % 2 else keep_ref
        out_ref[turn // 2, rows:, :] = jnp.where(keep, sums[turn], 0.0).astype(out_ref.dtype)


def second_kernel(near_ref, left_ref, columns_ref, *refs):
    block_refs, coefficient_refs, (keep_ref, send_ref) = refs[:3], refs[3:7], refs[7:]
    rows = near_ref.shape[2]
    me = lax.axis_index("list")
    coefficients, blocks = far_and_near(rows, columns_ref, block_refs, coefficient_refs)
    for turn in (1, 3, 0, 2):
        out_ref = send_ref if turn % 2 else keep_ref
        total = row_part(near_ref, left_ref, blocks, coefficients, me ^ turn)
        out_ref[turn // 2] = total.astype(out_ref.dtype)


def list_sum(keep, send):
    pair = keep + list_swap(send, 1)
    return pair[0] + across(pair[1].astype(BF))


def one_slot(probes, right_bases, left_bases, near_tiles, tile_ranks, column_rows, row_columns):
    rank_part, tile_rows = right_bases.shape[2:]
    rows, probe_count = probes.shape
    slots = -(-rank_part // 16) * 16
    near = near_tiles[0].transpose(1, 0, 2)
    flops = 2 * near.size * probe_count
    block, right, left = kernel_call(
        prepare_kernel,
        [
            ((rows, probe_count), BF),
            ((tile_rows // rows, slots, rows), BF),
            ((slots, tile_rows), BF),
        ],
        (probes, right_bases[0, 0], left_bases[0, 0]),
    )
    block_across = across(block)
    right_across = list_swap(right, 2)
    beside = [block, tile_swap(block, 1), tile_swap(block, 2)]
    block_pair = list_swap(jnp.stack([block, block_across]), 1)
    (own,) = kernel_call(
        functools.partial(coefficient_kernel, rank_part),
        [((slots, probe_count), BF)],
        (right, block, block_across, block_pair, tile_ranks),
    )
    coefficients = [own] + [tile_swap(own, turn) for turn in (1, 2, 3)]
    right_pair = list_swap(jnp.stack([right, right_across]), 1)
    shape = (2, rows + slots, probe_count)
    keep, send = kernel_call(
        functools.partial(first_kernel, rank_part),
        [(shape, F32), (shape, F32)],
        (
            near,
            left,
            row_columns,
            tile_ranks,
            right,
            right_across,
            right_pair,
            *beside,
            *coefficients,
        ),
        flops,
    )
    both = list_sum(keep, send).astype(BF)
    beside = [both, tile_swap(both, 1), tile_swap(both, 2)]
    coefficients = [message[rows:] for message in beside] + [tile_swap(both[rows:], 3)]
    shape = (2, rows, probe_count)
    keep, send = kernel_call(
        second_kernel,
        [(shape, F32), (shape, F32)],
        (near, left, row_columns, *beside, *coefficients),
        flops,
    )
    return list_sum(keep, send)


def local(probes, right_bases, left_bases, near_tiles, tile_ranks, column_rows, row_columns):
    few = lax.axis_size("tile") == 4 and lax.axis_size("list") == 4
    small = right_bases.shape[1] == 1 and few
    form = one_slot if small else many_slots
    return form(
        probes, right_bases, left_bases, near_tiles, tile_ranks, column_rows, row_columns
    )


def solution(mesh):
    placed = (
        P(("group", "tile", "list"), None),
        P(("group", "tile"), None, "list", None),
        P(("group", "tile"), None, "list", None),
        P(("group", "tile"), None, None, "list"),
        P(("group", "tile"), None),
        P("tile", None),
        P("tile", None),
    )
    return jax.shard_map(
        local,
        mesh=mesh,
        in_specs=placed,
        out_specs=P(("group", "tile", "list"), None),
        check_vma=False,
    )
```

time: 121 us -> 53.9 us (0.45)
  waiting for transfers between devices: 57.8 us -> 21.9 us
  blocking collectives: 15.4 us -> 0 us
  between operations: 15.5 us -> 1.42 us
  matrix products: 6.17 us -> 0 us
  starting transfers between devices: 19.9 us -> 24.2 us
  other arithmetic: 3.48 us -> 0.96 us
  Pallas kernels: 0 us -> 2.5 us
    reduce_scatter x2 -> x0, waiting for transfers between devices: 49.1 us -> none  [image_part(): lax.psum_scatter(partial_image, 'list', scatter_dimension=0, tiled=True)]
    all_gather x2 -> x0, blocking collectives: 15.4 us -> none  [image_part(): lax.all_gather(operand, 'list', axis=0, tiled=True)]
    ppermute x4 -> x19, starting transfers between devices: 10.4 us -> 24.2 us  [the longest x8 14.5 us: tile_swap(): return lax.ppermute(block, 'tile', route)]
    ppermute x4 -> x19, waiting for transfers between devices: 8.24 us -> 21.9 us  [the longest x11 14.4 us: list_swap(): lax.ppermute(block, 'list', [(i, i ^ bit) for i in range(lax.axis_size('l...]
    all_to_all x2 -> x0, starting transfers between devices: 9.45 us -> none  [image_part(): lax.all_to_all(outgoing, 'tile', split_axis=0, concat_axis=0, tiled=True)]
    dot_general x8 -> x0, matrix products: 6.17 us -> none  [the longest x2 4.02 us: image_part(): near_sum = jnp.dot(dense_flat, stacked, preferred_element_type=jnp.float32)]
    convert_element_type x4 -> x1, other arithmetic: 3.47 us -> 0.04 us  [one_slot(): both = list_sum(keep, send).astype(BF)]
    pallas_call x0 -> x4, Pallas kernels: none -> 2.5 us  [kernel_call(): pl.pallas_call(kernel, out_shape=tuple((jax.ShapeDtypeStruct(shape, kind)...]
  transfers between devices with their start and end apart: 8 -> 19, of which waited for: 6 -> 12; matrix products, arithmetic and copies ran while one was open for 1% -> 0% of each run, Pallas kernels for 0% -> 0%
where the time goes in v3:
time: 53.9 us; the launch traced here: 53.7 us
  starting transfers between devices  24.2 us (45%)
  waiting for transfers between devices  21.9 us (41%)
  local copies, waits for them, and re-layouts  2.72 us (5%)
  Pallas kernels  2.5 us (5%)
  between operations  1.42 us (3%)
  other arithmetic  0.96 us (2%)
    ppermute x8, starting transfers between devices, tile_swap(): return lax.ppermute(block, 'tile', route)  14.5 us
    ppermute x11, waiting for transfers between devices, list_swap(): lax.ppermute(block, 'list', [(i, i ^ bit) for i in range(lax.axis_size('l...  14.4 us
    ppermute x11, starting transfers between devices, list_swap(): lax.ppermute(block, 'list', [(i, i ^ bit) for i in range(lax.axis_size('l...  9.63 us
    ppermute x8, waiting for transfers between devices, tile_swap(): return lax.ppermute(block, 'tile', route)  7.55 us
    unnamed x9, local copies, waits for them, and re-layouts  2.67 us
    pallas_call x4, Pallas kernels, kernel_call(): pl.pallas_call(kernel, out_shape=tuple((jax.ShapeDtypeStruct(shape, kind)...  2.5 us
  transfers between devices with their start and end apart: 19, of which 12 were waited for; matrix products, arithmetic and copies ran while one was open for 0% of the time, Pallas kernels for 0%

profile of v3, /device:TPU:0, one launch (start us, length us, event | category | flops | bytes accessed | tf_op | source)
XLA Modules:
  0.0 53.7 jit_solution(7300377975723934962)
XLA Ops:
  0.0 1.1 %copy-done.1 = f32[256,256]{1,0:T(8,128)S(1)} copy-done((f32[256,256]{1,0:T(8,128)S(1)}, f32[256,256]{1,0:T(8,128)}, u32[]{:S(2)}) %copy-start.1) | copy-done | bytes 262168
  1.1 0.8 %copy-done.2 = bf16[1,1,24,1024]{3,2,1,0:T(8,128)(2,1)S(1)} copy-done((bf16[1,1,24,1024]{3,2,1,0:T(8,128)(2,1)S(1)}, bf16[1,1,24,1024]{3,2,1,0:T(8,128)(2,1)}, u32[]{:S(2)}) %copy-start.2) | copy-done | bytes 49176
  1.9 0.8 %copy-done.3 = bf16[1,1,24,1024]{3,2,1,0:T(8,128)(2,1)S(1)} copy-done((bf16[1,1,24,1024]{3,2,1,0:T(8,128)(2,1)S(1)}, bf16[1,1,24,1024]{3,2,1,0:T(8,128)(2,1)}, u32[]{:S(2)}) %copy-start.3) | copy-done | bytes 49176
  2.7 3.0 %collective-permute-start.4 = (bf16[128,256]{1,0:T(8,128)(2,1)S(1)}, bf16[128,256]{1,0:T(8,128)(2,1)S(1)}, u32[]{:S(2)}, u32[]{:S(2)}) collective-permute-start(bf16[128,256]{1,0:T(8,128)(2,1)S(1)} %get-tuple-element.28), channel_id=1, source_target_pairs={{0,2},{1,3},{2,0},{3,1},{4,6},{5,7},{6,4},{7,5},{8,10},{9,11},{10,... | collective-permute-start | bytes 196616 | tf_op jit(solution)/shard_map/ppermute | solution.py:127
  5.8 1.9 %collective-permute-start.5 = (bf16[128,256]{1,0:T(8,128)(2,1)S(1)}, bf16[128,256]{1,0:T(8,128)(2,1)S(1)}, u32[]{:S(2)}, u32[]{:S(2)}) collective-permute-start(bf16[128,256]{1,0:T(8,128)(2,1)S(1)} %get-tuple-element.27), channel_id=1, source_target_pairs={{0,2},{1,3},{2,0},{3,1},{4,6},{5,7},{6,4},{7,5},{8,10},{9,11},{10,... | collective-permute-start | bytes 196616 | tf_op jit(solution)/shard_map/ppermute | solution.py:127
  8.2 2.6 %collective-permute-done.5 = bf16[128,256]{1,0:T(8,128)(2,1)S(1)} collective-permute-done((bf16[128,256]{1,0:T(8,128)(2,1)S(1)}, bf16[128,256]{1,0:T(8,128)(2,1)S(1)}, u32[]{:S(2)}, u32[]{:S(2)}) %collective-permute-start.5) | collective-permute-done | bytes 65568 | tf_op jit(solution)/shard_map/ppermute | solution.py:127
  10.9 4.2 %collective-permute-start.3 = (bf16[256,256]{1,0:T(8,128)(2,1)S(1)}, bf16[256,256]{1,0:T(8,128)(2,1)S(1)}, u32[]{:S(2)}, u32[]{:S(2)}) collective-permute-start(bf16[256,256]{1,0:T(8,128)(2,1)S(1)} %get-tuple-element.14.own_ref.refs_3_), channel_id=1, source_target_pairs={{0,12},{4,8},{8,4},{12,0},{1,13},{5,9},{9,5},{13,1},{2,14},{6,10},... | collective-permute-start | bytes 393224 | tf_op jit(solution)/shard_map/ppermute | solution.py:123
  16.8 3.7 %collective-permute-start.8 = (bf16[32,256]{1,0:T(8,128)(2,1)S(1)}, bf16[32,256]{1,0:T(8,128)(2,1)S(1)}, u32[]{:S(2)}, u32[]{:S(2)}) collective-permute-start(bf16[32,256]{1,0:T(8,128)(2,1)S(1)} %shard_map.65.refs_6_), channel_id=1, source_target_pairs={{0,12},{4,8},{8,4},{12,0},{1,13},{5,9},{9,5},{13,1},{2,14},{6,10},... | collective-permute-start | bytes 49160 | tf_op jit(solution)/shard_map/ppermute | solution.py:123
  20.4 1.6 %collective-permute-start.7 = (bf16[32,256]{1,0:T(8,128)(2,1)S(1)}, bf16[32,256]{1,0:T(8,128)(2,1)S(1)}, u32[]{:S(2)}, u32[]{:S(2)}) collective-permute-start(bf16[32,256]{1,0:T(8,128)(2,1)S(1)} %shard_map.65.refs_6_), channel_id=1, source_target_pairs={{0,4},{4,0},{8,12},{12,8},{1,5},{5,1},{9,13},{13,9},{2,6},{6,2},{1... | collective-permute-start | bytes 49160 | tf_op jit(solution)/shard_map/ppermute | solution.py:123
  22.8 1.4 %collective-permute-done.7.refs_7_ = bf16[32,256]{1,0:T(8,128)(2,1)S(1)} collective-permute-done((bf16[32,256]{1,0:T(8,128)(2,1)S(1)}, bf16[32,256]{1,0:T(8,128)(2,1)S(1)}, u32[]{:S(2)}, u32[]{:S(2)}) %collective-permute-start.7) | collective-permute-done | bytes 16416 | tf_op jit(solution)/shard_map/ppermute | solution.py:123
  24.2 1.6 %shard_map.66 = (f32[2,288,256]{2,1,0:T(8,128)S(1)}, f32[2,288,256]{2,1,0:T(8,128)S(1)}) custom-call(bf16[3,1024,256]{2,1,0:T(8,128)(2,1)S(1)} %bitcast.27, bf16[32,1024]{1,0:T(8,128)(2,1)S(1)} %get-tuple-element.12.left_ref, s32[1,1]{1,0:T(1,128)S(6)} %copy.9.columns_ref, s32[1,1]{1,0:T(1,128)S(6)} %copy.8.ranks_ref, ...), custom_call_target="tpu_custom_call" | custom-call | flops 402653184 | bytes 1572864 | tf_op jit(solution)/shard_map/pallas_call | solution.py:73
  25.8 2.0 %collective-permute-done.10 = f32[2,288,256]{2,1,0:T(8,128)S(1)} collective-permute-done((f32[2,288,256]{2,1,0:T(8,128)S(1)}, f32[2,288,256]{2,1,0:T(8,128)S(1)}, u32[]{:S(2)}, u32[]{:S(2)}) %collective-permute-start.10) | collective-permute-done | bytes 589856 | tf_op jit(solution)/shard_map/ppermute | solution.py:127
  27.9 1.1 %collective-permute-start.11 = (bf16[144,256]{1,0:T(8,128)(2,1)S(1)}, bf16[144,256]{1,0:T(8,128)(2,1)S(1)}, u32[]{:S(2)}, u32[]{:S(2)}) collective-permute-start(bf16[144,256]{1,0:T(8,128)(2,1)S(1)} %get-tuple-element.23), channel_id=1, source_target_pairs={{0,2},{1,3},{2,0},{3,1},{4,6},{5,7},{6,4},{7,5},{8,10},{9,11},{10,... | collective-permute-start | bytes 221192 | tf_op jit(solution)/shard_map/ppermute | solution.py:127
  29.1 1.0 %collective-permute-start.12 = (bf16[144,256]{1,0:T(8,128)(2,1)S(1)}, bf16[144,256]{1,0:T(8,128)(2,1)S(1)}, u32[]{:S(2)}, u32[]{:S(2)}) collective-permute-start(bf16[144,256]{1,0:T(8,128)(2,1)S(1)} %get-tuple-element.24), channel_id=1, source_target_pairs={{0,2},{1,3},{2,0},{3,1},{4,6},{5,7},{6,4},{7,5},{8,10},{9,11},{10,... | collective-permute-start | bytes 221192 | tf_op jit(solution)/shard_map/ppermute | solution.py:127
  30.0 3.1 %collective-permute-done.11 = bf16[144,256]{1,0:T(8,128)(2,1)S(1)} collective-permute-done((bf16[144,256]{1,0:T(8,128)(2,1)S(1)}, bf16[144,256]{1,0:T(8,128)(2,1)S(1)}, u32[]{:S(2)}, u32[]{:S(2)}) %collective-permute-start.11) | collective-permute-done | bytes 73760 | tf_op jit(solution)/shard_map/ppermute | solution.py:127
  33.1 0.8 %collective-permute-done.12 = bf16[144,256]{1,0:T(8,128)(2,1)S(1)} collective-permute-done((bf16[144,256]{1,0:T(8,128)(2,1)S(1)}, bf16[144,256]{1,0:T(8,128)(2,1)S(1)}, u32[]{:S(2)}, u32[]{:S(2)}) %collective-permute-start.12) | collective-permute-done | bytes 73760 | tf_op jit(solution)/shard_map/ppermute | solution.py:127
  33.9 2.9 %collective-permute-start.14 = (bf16[288,256]{1,0:T(8,128)(2,1)S(1)}, bf16[288,256]{1,0:T(8,128)(2,1)S(1)}, u32[]{:S(2)}, u32[]{:S(2)}) collective-permute-start(bf16[288,256]{1,0:T(8,128)(2,1)S(1)} %fusion.1.refs_0_), channel_id=1, source_target_pairs={{0,12},{4,8},{8,4},{12,0},{1,13},{5,9},{9,5},{13,1},{2,14},{6,10},... | collective-permute-start | bytes 442376 | tf_op jit(solution)/shard_map/ppermute | solution.py:123
  37.2 1.2 %collective-permute-start.15 = (bf16[32,256]{1,0:T(8,128)(2,1)S(1)}, bf16[32,256]{1,0:T(8,128)(2,1)S(1)}, u32[]{:S(2)}, u32[]{:S(2)}) collective-permute-start(bf16[32,256]{1,0:T(8,128)(2,1)S(1)} %slice.72.refs_3_), channel_id=1, source_target_pairs={{0,8},{4,12},{8,0},{12,4},{1,9},{5,13},{9,1},{13,5},{2,10},{6,14},... | collective-permute-start | bytes 49160 | tf_op jit(solution)/shard_map/ppermute | solution.py:123
  38.4 4.2 %collective-permute-done.14.refs_2_ = bf16[288,256]{1,0:T(8,128)(2,1)S(1)} collective-permute-done((bf16[288,256]{1,0:T(8,128)(2,1)S(1)}, bf16[288,256]{1,0:T(8,128)(2,1)S(1)}, u32[]{:S(2)}, u32[]{:S(2)}) %collective-permute-start.14) | collective-permute-done | bytes 147488 | tf_op jit(solution)/shard_map/ppermute | solution.py:123
  42.6 1.9 %collective-permute-done.13.refs_1_ = bf16[288,256]{1,0:T(8,128)(2,1)S(1)} collective-permute-done((bf16[288,256]{1,0:T(8,128)(2,1)S(1)}, bf16[288,256]{1,0:T(8,128)(2,1)S(1)}, u32[]{:S(2)}, u32[]{:S(2)}) %collective-permute-start.13) | collective-permute-done | bytes 147488 | tf_op jit(solution)/shard_map/ppermute | solution.py:123
  45.3 1.9 %collective-permute-done.16 = f32[2,256,256]{2,1,0:T(8,128)S(1)} collective-permute-done((f32[2,256,256]{2,1,0:T(8,128)S(1)}, f32[2,256,256]{2,1,0:T(8,128)S(1)}, u32[]{:S(2)}, u32[]{:S(2)}) %collective-permute-start.16) | collective-permute-done | bytes 524320 | tf_op jit(solution)/shard_map/ppermute | solution.py:127
  47.3 1.1 %collective-permute-start.17 = (bf16[128,256]{1,0:T(8,128)(2,1)S(1)}, bf16[128,256]{1,0:T(8,128)(2,1)S(1)}, u32[]{:S(2)}, u32[]{:S(2)}) collective-permute-start(bf16[128,256]{1,0:T(8,128)(2,1)S(1)} %get-tuple-element.25), channel_id=1, source_target_pairs={{0,2},{1,3},{2,0},{3,1},{4,6},{5,7},{6,4},{7,5},{8,10},{9,11},{10,... | collective-permute-start | bytes 196616 | tf_op jit(solution)/shard_map/ppermute | solution.py:127
  48.4 1.0 %collective-permute-start.18 = (bf16[128,256]{1,0:T(8,128)(2,1)S(1)}, bf16[128,256]{1,0:T(8,128)(2,1)S(1)}, u32[]{:S(2)}, u32[]{:S(2)}) collective-permute-start(bf16[128,256]{1,0:T(8,128)(2,1)S(1)} %get-tuple-element.26), channel_id=1, source_target_pairs={{0,2},{1,3},{2,0},{3,1},{4,6},{5,7},{6,4},{7,5},{8,10},{9,11},{10,... | collective-permute-start | bytes 196616 | tf_op jit(solution)/shard_map/ppermute | solution.py:127
  49.3 2.9 %collective-permute-done.17 = bf16[128,256]{1,0:T(8,128)(2,1)S(1)} collective-permute-done((bf16[128,256]{1,0:T(8,128)(2,1)S(1)}, bf16[128,256]{1,0:T(8,128)(2,1)S(1)}, u32[]{:S(2)}, u32[]{:S(2)}) %collective-permute-start.17) | collective-permute-done | bytes 65568 | tf_op jit(solution)/shard_map/ppermute | solution.py:127
  (40 shorter events, 4.7 us)
Async XLA Ops:
  0.0 24.2 %copy-start = (bf16[1,1024,3,256]{3,1,2,0:T(8,128)(2,1)S(1)}, bf16[1,1024,3,256]{3,1,2,0:T(8,128)(2,1)}, u32[]{:S(2)}) copy-start(bf16[1,1024,3,256]{3,1,2,0:T(8,128)(2,1)} %param.10) | copy-start | bytes 4718596
  0.0 1.1 %copy-start.1 = (f32[256,256]{1,0:T(8,128)S(1)}, f32[256,256]{1,0:T(8,128)}, u32[]{:S(2)}) copy-start(f32[256,256]{1,0:T(8,128)} %probes_ref.1) | copy-start | bytes 786436
  1.1 0.8 %copy-start.2 = (bf16[1,1,24,1024]{3,2,1,0:T(8,128)(2,1)S(1)}, bf16[1,1,24,1024]{3,2,1,0:T(8,128)(2,1)}, u32[]{:S(2)}) copy-start(bf16[1,1,24,1024]{3,2,1,0:T(8,128)(2,1)} %param.8) | copy-start | bytes 147460
  1.9 0.8 %copy-start.3 = (bf16[1,1,24,1024]{3,2,1,0:T(8,128)(2,1)S(1)}, bf16[1,1,24,1024]{3,2,1,0:T(8,128)(2,1)}, u32[]{:S(2)}) copy-start(bf16[1,1,24,1024]{3,2,1,0:T(8,128)(2,1)} %param.9) | copy-start | bytes 147460
  2.7 5.5 %collective-permute-start.4 = (bf16[128,256]{1,0:T(8,128)(2,1)S(1)}, bf16[128,256]{1,0:T(8,128)(2,1)S(1)}, u32[]{:S(2)}, u32[]{:S(2)}) collective-permute-start(bf16[128,256]{1,0:T(8,128)(2,1)S(1)} %get-tuple-element.28), channel_id=1, source_target_pairs={{0,2},{1,3},{2,0},{3,1},{4,6},{5,7},{6,4},{7,5},{8,10},{9,11},{10,... | collective-permute-start | bytes 196616 | tf_op jit(solution)/shard_map/ppermute | solution.py:127
  5.7 9.4 %collective-permute-start = (bf16[4,32,256]{2,1,0:T(8,128)(2,1)S(1)}, bf16[4,32,256]{2,1,0:T(8,128)(2,1)S(1)}, u32[]{:S(2)}, u32[]{:S(2)}) collective-permute-start(bf16[4,32,256]{2,1,0:T(8,128)(2,1)S(1)} %get-tuple-element.13.parts_ref.refs_0_), channel_id=1, source_target_pairs={{0,2},{1,3},{2,0},{3,1},{4,6},{5,7},{6,4},{7,5},{8,10},{9,11},{10,... | collective-permute-start | bytes 196616 | tf_op jit(solution)/shard_map/ppermute | solution.py:127
  5.8 5.0 %collective-permute-start.5 = (bf16[128,256]{1,0:T(8,128)(2,1)S(1)}, bf16[128,256]{1,0:T(8,128)(2,1)S(1)}, u32[]{:S(2)}, u32[]{:S(2)}) collective-permute-start(bf16[128,256]{1,0:T(8,128)(2,1)S(1)} %get-tuple-element.27), channel_id=1, source_target_pairs={{0,2},{1,3},{2,0},{3,1},{4,6},{5,7},{6,4},{7,5},{8,10},{9,11},{10,... | collective-permute-start | bytes 196616 | tf_op jit(solution)/shard_map/ppermute | solution.py:127
  10.8 5.2 %collective-permute-start.6 = (bf16[2,256,256]{2,1,0:T(8,128)(2,1)S(1)}, bf16[2,256,256]{2,1,0:T(8,128)(2,1)S(1)}, u32[]{:S(2)}, u32[]{:S(2)}) collective-permute-start(bf16[2,256,256]{2,1,0:T(8,128)(2,1)S(1)} %pad_maximum_fusion), channel_id=1, source_target_pairs={{0,1},{1,0},{2,3},{3,2},{4,5},{5,4},{6,7},{7,6},{8,9},{9,8},{10,11... | collective-permute-start | bytes 786440 | tf_op jit(solution)/shard_map/ppermute | solution.py:127
  10.9 9.6 %collective-permute-start.3 = (bf16[256,256]{1,0:T(8,128)(2,1)S(1)}, bf16[256,256]{1,0:T(8,128)(2,1)S(1)}, u32[]{:S(2)}, u32[]{:S(2)}) collective-permute-start(bf16[256,256]{1,0:T(8,128)(2,1)S(1)} %get-tuple-element.14.own_ref.refs_3_), channel_id=1, source_target_pairs={{0,12},{4,8},{8,4},{12,0},{1,13},{5,9},{9,5},{13,1},{2,14},{6,10},... | collective-permute-start | bytes 393224 | tf_op jit(solution)/shard_map/ppermute | solution.py:123
  15.1 7.7 %collective-permute-start.2 = (bf16[256,256]{1,0:T(8,128)(2,1)S(1)}, bf16[256,256]{1,0:T(8,128)(2,1)S(1)}, u32[]{:S(2)}, u32[]{:S(2)}) collective-permute-start(bf16[256,256]{1,0:T(8,128)(2,1)S(1)} %get-tuple-element.14.own_ref.refs_3_), channel_id=1, source_target_pairs={{0,4},{4,0},{8,12},{12,8},{1,5},{5,1},{9,13},{13,9},{2,6},{6,2},{1... | collective-permute-start | bytes 393224 | tf_op jit(solution)/shard_map/ppermute | solution.py:123
  15.1 7.7 %collective-permute-start.1 = (bf16[2,4,32,256]{3,2,1,0:T(8,128)(2,1)S(1)}, bf16[2,4,32,256]{3,2,1,0:T(8,128)(2,1)S(1)}, u32[]{:S(2)}, u32[]{:S(2)}) collective-permute-start(bf16[2,4,32,256]{3,2,1,0:T(8,128)(2,1)S(1)} %pad_maximum_fusion.1), channel_id=1, source_target_pairs={{0,1},{1,0},{2,3},{3,2},{4,5},{5,4},{6,7},{7,6},{8,9},{9,8},{10,11... | collective-permute-start | bytes 393224 | tf_op jit(solution)/shard_map/ppermute | solution.py:127
  16.2 6.6 %collective-permute-start.9 = (bf16[32,256]{1,0:T(8,128)(2,1)S(1)}, bf16[32,256]{1,0:T(8,128)(2,1)S(1)}, u32[]{:S(2)}, u32[]{:S(2)}) collective-permute-start(bf16[32,256]{1,0:T(8,128)(2,1)S(1)} %shard_map.65.refs_6_), channel_id=1, source_target_pairs={{0,8},{4,12},{8,0},{12,4},{1,9},{5,13},{9,1},{13,5},{2,10},{6,14},... | collective-permute-start | bytes 49160 | tf_op jit(solution)/shard_map/ppermute | solution.py:123
  16.8 6.0 %collective-permute-start.8 = (bf16[32,256]{1,0:T(8,128)(2,1)S(1)}, bf16[32,256]{1,0:T(8,128)(2,1)S(1)}, u32[]{:S(2)}, u32[]{:S(2)}) collective-permute-start(bf16[32,256]{1,0:T(8,128)(2,1)S(1)} %shard_map.65.refs_6_), channel_id=1, source_target_pairs={{0,12},{4,8},{8,4},{12,0},{1,13},{5,9},{9,5},{13,1},{2,14},{6,10},... | collective-permute-start | bytes 49160 | tf_op jit(solution)/shard_map/ppermute | solution.py:123
  20.4 3.7 %collective-permute-start.7 = (bf16[32,256]{1,0:T(8,128)(2,1)S(1)}, bf16[32,256]{1,0:T(8,128)(2,1)S(1)}, u32[]{:S(2)}, u32[]{:S(2)}) collective-permute-start(bf16[32,256]{1,0:T(8,128)(2,1)S(1)} %shard_map.65.refs_6_), channel_id=1, source_target_pairs={{0,4},{4,0},{8,12},{12,8},{1,5},{5,1},{9,13},{13,9},{2,6},{6,2},{1... | collective-permute-start | bytes 49160 | tf_op jit(solution)/shard_map/ppermute | solution.py:123
  25.8 2.0 %collective-permute-start.10 = (f32[2,288,256]{2,1,0:T(8,128)S(1)}, f32[2,288,256]{2,1,0:T(8,128)S(1)}, u32[]{:S(2)}, u32[]{:S(2)}) collective-permute-start(f32[2,288,256]{2,1,0:T(8,128)S(1)} %get-tuple-element.16), channel_id=1, source_target_pairs={{0,1},{1,0},{2,3},{3,2},{4,5},{5,4},{6,7},{7,6},{8,9},{9,8},{10,11... | collective-permute-start | bytes 1769480 | tf_op jit(solution)/shard_map/ppermute | solution.py:127
  27.9 5.2 %collective-permute-start.11 = (bf16[144,256]{1,0:T(8,128)(2,1)S(1)}, bf16[144,256]{1,0:T(8,128)(2,1)S(1)}, u32[]{:S(2)}, u32[]{:S(2)}) collective-permute-start(bf16[144,256]{1,0:T(8,128)(2,1)S(1)} %get-tuple-element.23), channel_id=1, source_target_pairs={{0,2},{1,3},{2,0},{3,1},{4,6},{5,7},{6,4},{7,5},{8,10},{9,11},{10,... | collective-permute-start | bytes 221192 | tf_op jit(solution)/shard_map/ppermute | solution.py:127
  29.1 4.8 %collective-permute-start.12 = (bf16[144,256]{1,0:T(8,128)(2,1)S(1)}, bf16[144,256]{1,0:T(8,128)(2,1)S(1)}, u32[]{:S(2)}, u32[]{:S(2)}) collective-permute-start(bf16[144,256]{1,0:T(8,128)(2,1)S(1)} %get-tuple-element.24), channel_id=1, source_target_pairs={{0,2},{1,3},{2,0},{3,1},{4,6},{5,7},{6,4},{7,5},{8,10},{9,11},{10,... | collective-permute-start | bytes 221192 | tf_op jit(solution)/shard_map/ppermute | solution.py:127
  33.9 8.7 %collective-permute-start.14 = (bf16[288,256]{1,0:T(8,128)(2,1)S(1)}, bf16[288,256]{1,0:T(8,128)(2,1)S(1)}, u32[]{:S(2)}, u32[]{:S(2)}) collective-permute-start(bf16[288,256]{1,0:T(8,128)(2,1)S(1)} %fusion.1.refs_0_), channel_id=1, source_target_pairs={{0,12},{4,8},{8,4},{12,0},{1,13},{5,9},{9,5},{13,1},{2,14},{6,10},... | collective-permute-start | bytes 442376 | tf_op jit(solution)/shard_map/ppermute | solution.py:123
  36.8 7.7 %collective-permute-start.13 = (bf16[288,256]{1,0:T(8,128)(2,1)S(1)}, bf16[288,256]{1,0:T(8,128)(2,1)S(1)}, u32[]{:S(2)}, u32[]{:S(2)}) collective-permute-start(bf16[288,256]{1,0:T(8,128)(2,1)S(1)} %fusion.1.refs_0_), channel_id=1, source_target_pairs={{0,4},{4,0},{8,12},{12,8},{1,5},{5,1},{9,13},{13,9},{2,6},{6,2},{1... | collective-permute-start | bytes 442376 | tf_op jit(solution)/shard_map/ppermute | solution.py:123
  37.2 7.3 %collective-permute-start.15 = (bf16[32,256]{1,0:T(8,128)(2,1)S(1)}, bf16[32,256]{1,0:T(8,128)(2,1)S(1)}, u32[]{:S(2)}, u32[]{:S(2)}) collective-permute-start(bf16[32,256]{1,0:T(8,128)(2,1)S(1)} %slice.72.refs_3_), channel_id=1, source_target_pairs={{0,8},{4,12},{8,0},{12,4},{1,9},{5,13},{9,1},{13,5},{2,10},{6,14},... | collective-permute-start | bytes 49160 | tf_op jit(solution)/shard_map/ppermute | solution.py:123
  45.2 2.0 %collective-permute-start.16 = (f32[2,256,256]{2,1,0:T(8,128)S(1)}, f32[2,256,256]{2,1,0:T(8,128)S(1)}, u32[]{:S(2)}, u32[]{:S(2)}) collective-permute-start(f32[2,256,256]{2,1,0:T(8,128)S(1)} %get-tuple-element.18), channel_id=1, source_target_pairs={{0,1},{1,0},{2,3},{3,2},{4,5},{5,4},{6,7},{7,6},{8,9},{9,8},{10,11... | collective-permute-start | bytes 1572872 | tf_op jit(solution)/shard_map/ppermute | solution.py:127
  47.3 5.0 %collective-permute-start.17 = (bf16[128,256]{1,0:T(8,128)(2,1)S(1)}, bf16[128,256]{1,0:T(8,128)(2,1)S(1)}, u32[]{:S(2)}, u32[]{:S(2)}) collective-permute-start(bf16[128,256]{1,0:T(8,128)(2,1)S(1)} %get-tuple-element.25), channel_id=1, source_target_pairs={{0,2},{1,3},{2,0},{3,1},{4,6},{5,7},{6,4},{7,5},{8,10},{9,11},{10,... | collective-permute-start | bytes 196616 | tf_op jit(solution)/shard_map/ppermute | solution.py:127
  48.4 4.6 %collective-permute-start.18 = (bf16[128,256]{1,0:T(8,128)(2,1)S(1)}, bf16[128,256]{1,0:T(8,128)(2,1)S(1)}, u32[]{:S(2)}, u32[]{:S(2)}) collective-permute-start(bf16[128,256]{1,0:T(8,128)(2,1)S(1)} %get-tuple-element.26), channel_id=1, source_target_pairs={{0,2},{1,3},{2,0},{3,1},{4,6},{5,7},{6,4},{7,5},{8,10},{9,11},{10,... | collective-permute-start | bytes 196616 | tf_op jit(solution)/shard_map/ppermute | solution.py:127

commit v4 on v3

--- a/solution.py
+++ b/solution.py
@@ -82,10 +82,9 @@
     )(*operands)
 
 
-def prepare_kernel(probes_ref, right_ref, left_ref, block_ref, parts_ref, padded_ref):
+def bases_kernel(right_ref, left_ref, parts_ref, padded_ref):
     ranks = right_ref.shape[0]
-    rows = probes_ref.shape[0]
-    block_ref[...] = probes_ref[...].astype(BF)
+    rows = parts_ref.shape[2]
     parts_ref[...] = jnp.zeros_like(parts_ref)
     padded_ref[...] = jnp.zeros_like(padded_ref)
     padded_ref[:ranks, :] = left_ref[...]
@@ -108,28 +107,16 @@
     out_ref[...] = jnp.where(keep, total, 0.0).astype(out_ref.dtype)
 
 
-def partner(tile, turn, count):
-    if turn == 2:
-        return lax.rem(tile + count + 2 * lax.rem(tile, 2) - 1, count)
-    return tile ^ (turn if turn < 2 else 2)
-
-
 def tile_swap(block, turn):
     count = lax.axis_size("tile")
-    if turn == 2:
-        route = [(i, (i + count + 2 * (i % 2) - 1) % count) for i in range(count)]
-    else:
-        route = [(i, i ^ (1 if turn == 1 else 2)) for i in range(count)]
+    route = [(i, i ^ turn) for i in range(count)]
+    if turn == 0:
+        route = [(i, min(max(i - 1 + 2 * (i % 2), 0), count - 1)) for i in range(count)]
     return lax.ppermute(block, "tile", route)
 
 
 def list_swap(block, bit):
     return lax.ppermute(block, "list", [(i, i ^ bit) for i in range(lax.axis_size("list"))])
-
-
-def across(block):
-    cut = block.shape[0] // 2
-    return jnp.concatenate([list_swap(block[:cut], 2), list_swap(block[cut:], 2)])
 
 
 def far_and_near(rows, columns_ref, block_refs, coefficient_refs):
@@ -137,7 +124,7 @@
     tile = lax.axis_index("tile")
     chosen = coefficient_refs[0][...]
     for turn in (1, 2, 3):
-        listed = columns_ref[...] == partner(tile, turn, count)
+        listed = columns_ref[...] == tile ^ turn
         chosen = jnp.where(listed, coefficient_refs[turn][...], chosen)
     odd = lax.rem(tile, 2)
     inside = (tile > 0) & (tile < count - 1)
@@ -168,19 +155,20 @@
     right = (right_refs[0], right_refs[2].at[0], right_refs[1], right_refs[2].at[1])
     coefficients, blocks = far_and_near(rows, columns_ref, block_refs, coefficient_refs)
     shape = coefficients.shape
-    sums = [jnp.zeros(shape, F32)] * 4
+    sums = jnp.zeros((4 * shape[0], shape[1]), F32)
     for turn in (1, 3, 0, 2):
         part = me ^ turn
         total = row_part(near_ref, left_ref, blocks, coefficients, part)
         out_ref = send_ref if turn % 2 else keep_ref
         out_ref[turn // 2, :rows, :] = total.astype(out_ref.dtype)
         rounded = total.astype(BF)
-        for group in range(4):
-            sums[group] += jnp.dot(right[group][part], rounded, preferred_element_type=F32)
+        stacked = jnp.concatenate([group_ref[part] for group_ref in right])
+        sums += jnp.dot(stacked, rounded, preferred_element_type=F32)
     for turn in range(4):
         keep = kept_levels(me ^ turn, rank_part, ranks_ref, shape)
         out_ref = send_ref if turn % 2 else keep_ref
-        out_ref[turn // 2, rows:, :] = jnp.where(keep, sums[turn], 0.0).astype(out_ref.dtype)
+        group_sum = sums[turn * shape[0] : (turn + 1) * shape[0]]
+        out_ref[turn // 2, rows:, :] = jnp.where(keep, group_sum, 0.0).astype(out_ref.dtype)
 
 
 def second_kernel(near_ref, left_ref, columns_ref, *refs):
@@ -196,7 +184,7 @@
 
 def list_sum(keep, send):
     pair = keep + list_swap(send, 1)
-    return pair[0] + across(pair[1].astype(BF))
+    return pair[0] + list_swap(pair[1].astype(BF), 2)
 
 
 def one_slot(probes, right_bases, left_bases, near_tiles, tile_ranks, column_rows, row_columns):
@@ -205,18 +193,15 @@
     slots = -(-rank_part // 16) * 16
     near = near_tiles[0].transpose(1, 0, 2)
     flops = 2 * near.size * probe_count
-    block, right, left = kernel_call(
-        prepare_kernel,
-        [
-            ((rows, probe_count), BF),
-            ((tile_rows // rows, slots, rows), BF),
-            ((slots, tile_rows), BF),
-        ],
-        (probes, right_bases[0, 0], left_bases[0, 0]),
-    )
-    block_across = across(block)
-    right_across = list_swap(right, 2)
-    beside = [block, tile_swap(block, 1), tile_swap(block, 2)]
+    right, left = kernel_call(
+        bases_kernel,
+        [((tile_rows // rows, slots, rows), BF), ((slots, tile_rows), BF)],
+        (right_bases[0, 0], left_bases[0, 0]),
+    )
+    block = probes.astype(BF)
+    block_across = list_swap(block, 2)
+    beside = [block, tile_swap(block, 1), tile_swap(block, 0)]
+    block_across, beside[1] = lax.optimization_barrier((block_across, beside[1]))
     block_pair = list_swap(jnp.stack([block, block_across]), 1)
     (own,) = kernel_call(
         functools.partial(coefficient_kernel, rank_part),
@@ -224,6 +209,8 @@
         (right, block, block_across, block_pair, tile_ranks),
     )
     coefficients = [own] + [tile_swap(own, turn) for turn in (1, 2, 3)]
+    right, _ = lax.optimization_barrier((right, block_across))
+    right_across = list_swap(right, 2)
     right_pair = list_swap(jnp.stack([right, right_across]), 1)
     shape = (2, rows + slots, probe_count)
     keep, send = kernel_call(
@@ -243,8 +230,9 @@
         flops,
     )
     both = list_sum(keep, send).astype(BF)
-    beside = [both, tile_swap(both, 1), tile_swap(both, 2)]
-    coefficients = [message[rows:] for message in beside] + [tile_swap(both[rows:], 3)]
+    beside = [both, tile_swap(both, 1), tile_swap(both[:rows], 0)]
+    coefficients = [message[rows:] for message in beside[:2]]
+    coefficients += [tile_swap(both[rows:], turn) for turn in (2, 3)]
     shape = (2, rows, probe_count)
     keep, send = kernel_call(
         second_kernel,

time: 53.9 us -> 50.1 us (0.929)
  starting transfers between devices: 24.2 us -> 19.4 us
  other arithmetic: 0.96 us -> 2.99 us
  local copies, waits for them, and re-layouts: 2.72 us -> 1.65 us
    ppermute x11 -> x8, starting transfers between devices: 9.63 us -> 5.19 us  [list_swap(): lax.ppermute(block, 'list', [(i, i ^ bit) for i in range(lax.axis_size('l...]
    ppermute x11 -> x8, waiting for transfers between devices: 14.4 us -> 16.4 us  [list_swap(): lax.ppermute(block, 'list', [(i, i ^ bit) for i in range(lax.axis_size('l...]
    ppermute x8 -> x9, waiting for transfers between devices: 7.55 us -> 5.59 us  [tile_swap(): return lax.ppermute(block, 'tile', route)]
    convert_element_type x0 -> x1, other arithmetic: none -> 1.08 us  [one_slot(): block = probes.astype(BF)]
    unnamed x9 -> x6, local copies, waits for them, and re-layouts: 2.67 us -> 1.6 us
    another operation x1 -> x2, other arithmetic: 0.03 us -> 0.99 us  [one_slot(): block_pair = list_swap(jnp.stack([block, block_across]), 1)]
    ppermute x8 -> x9, starting transfers between devices: 14.5 us -> 14.2 us  [tile_swap(): return lax.ppermute(block, 'tile', route)]
  transfers between devices with their start and end apart: 19 -> 17, of which waited for: 12 -> 11; matrix products, arithmetic and copies ran while one was open for 0% -> 2% of each run, Pallas kernels for 0% -> 0%
where the time goes in v4:
time: 50.1 us; the launch traced here: 49.7 us
  waiting for transfers between devices  22 us (44%)
  starting transfers between devices  19.4 us (39%)
  other arithmetic  2.99 us (6%)
  Pallas kernels  2.23 us (4%)
  local copies, waits for them, and re-layouts  1.65 us (3%)
  between operations  1.46 us (3%)
    ppermute x8, waiting for transfers between devices, list_swap(): lax.ppermute(block, 'list', [(i, i ^ bit) for i in range(lax.axis_size('l...  16.4 us
    ppermute x9, starting transfers between devices, tile_swap(): return lax.ppermute(block, 'tile', route)  14.2 us
    ppermute x9, waiting for transfers between devices, tile_swap(): return lax.ppermute(block, 'tile', route)  5.59 us
    ppermute x8, starting transfers between devices, list_swap(): lax.ppermute(block, 'list', [(i, i ^ bit) for i in range(lax.axis_size('l...  5.19 us
    pallas_call x4, Pallas kernels, kernel_call(): pl.pallas_call(kernel, out_shape=tuple((jax.ShapeDtypeStruct(shape, kind)...  2.23 us
    unnamed x6, local copies, waits for them, and re-layouts  1.6 us
    convert_element_type x1, other arithmetic, one_slot(): block = probes.astype(BF)  1.08 us
  transfers between devices with their start and end apart: 17, of which 11 were waited for; matrix products, arithmetic and copies ran while one was open for 2% of the time, Pallas kernels for 0%

profile of v4, /device:TPU:0, one launch (start us, length us, event | category | flops | bytes accessed | tf_op | source)
XLA Modules:
  0.0 49.7 jit_solution(15484275229991637899)
XLA Ops:
  0.0 1.1 %convert_element_type.20.own_ref.refs_3_ = bf16[256,256]{1,0:T(8,128)(2,1)S(1)} convert(f32[256,256]{1,0:T(8,128)} %param.7) | non-fusion elementwise | flops 65536 | bytes 393216 | tf_op jit(solution)/shard_map/convert_element_type | solution.py:201
  1.1 3.1 %collective-permute-start.1 = (bf16[256,256]{1,0:T(8,128)(2,1)S(1)}, bf16[256,256]{1,0:T(8,128)(2,1)S(1)}, u32[]{:S(2)}, u32[]{:S(2)}) collective-permute-start(bf16[256,256]{1,0:T(8,128)(2,1)S(1)} %convert_element_type.20.own_ref.refs_3_), channel_id=1, source_target_pairs={{0,4},{4,0},{8,12},{12,8},{1,5},{5,1},{9,13},{13,9},{2,6},{6,2},{1... | collective-permute-start | bytes 393224 | tf_op jit(solution)/shard_map/ppermute | solution.py:115
  4.2 1.5 %collective-permute-start = (bf16[256,256]{1,0:T(8,128)(2,1)S(1)}, bf16[256,256]{1,0:T(8,128)(2,1)S(1)}, u32[]{:S(2)}, u32[]{:S(2)}) collective-permute-start(bf16[256,256]{1,0:T(8,128)(2,1)S(1)} %convert_element_type.20.own_ref.refs_3_), channel_id=1, source_target_pairs={{0,2},{1,3},{2,0},{3,1},{4,6},{5,7},{6,4},{7,5},{8,10},{9,11},{10,... | collective-permute-start | bytes 393224 | tf_op jit(solution)/shard_map/ppermute | solution.py:119
  5.7 0.8 %copy-done.1 = bf16[1,1,24,1024]{3,2,1,0:T(8,128)(2,1)S(1)} copy-done((bf16[1,1,24,1024]{3,2,1,0:T(8,128)(2,1)S(1)}, bf16[1,1,24,1024]{3,2,1,0:T(8,128)(2,1)}, u32[]{:S(2)}) %copy-start.1) | copy-done | bytes 49176
  6.5 0.8 %copy-done.2 = bf16[1,1,24,1024]{3,2,1,0:T(8,128)(2,1)S(1)} copy-done((bf16[1,1,24,1024]{3,2,1,0:T(8,128)(2,1)S(1)}, bf16[1,1,24,1024]{3,2,1,0:T(8,128)(2,1)}, u32[]{:S(2)}) %copy-start.2) | copy-done | bytes 49176
  7.3 1.0 %convert_bitcast_fusion = bf16[1,256,256]{2,1,0:T(8,128)(2,1)S(1)} fusion(f32[256,256]{1,0:T(8,128)} %param.7), kind=kLoop, calls=%fused_computation.11 | loop fusion | flops 65536 | bytes 393216 | tf_op jit(solution)/shard_map/stack | solution.py:205
  8.3 0.9 %collective-permute-done.across_ref = bf16[256,256]{1,0:T(8,128)(2,1)S(1)} collective-permute-done((bf16[256,256]{1,0:T(8,128)(2,1)S(1)}, bf16[256,256]{1,0:T(8,128)(2,1)S(1)}, u32[]{:S(2)}, u32[]{:S(2)}) %collective-permute-start) | collective-permute-done | bytes 131104 | tf_op jit(solution)/shard_map/ppermute | solution.py:119
  9.1 1.5 %collective-permute-start.2 = (bf16[4,32,256]{2,1,0:T(8,128)(2,1)S(1)}, bf16[4,32,256]{2,1,0:T(8,128)(2,1)S(1)}, u32[]{:S(2)}, u32[]{:S(2)}) collective-permute-start(bf16[4,32,256]{2,1,0:T(8,128)(2,1)S(1)} %get-tuple-element.17.parts_ref.refs_0_), channel_id=1, source_target_pairs={{0,2},{1,3},{2,0},{3,1},{4,6},{5,7},{6,4},{7,5},{8,10},{9,11},{10,... | collective-permute-start | bytes 196616 | tf_op jit(solution)/shard_map/ppermute | solution.py:119
  11.4 2.0 %collective-permute-done.2.refs_1_ = bf16[4,32,256]{2,1,0:T(8,128)(2,1)S(1)} collective-permute-done((bf16[4,32,256]{2,1,0:T(8,128)(2,1)S(1)}, bf16[4,32,256]{2,1,0:T(8,128)(2,1)S(1)}, u32[]{:S(2)}, u32[]{:S(2)}) %collective-permute-start.2) | collective-permute-done | bytes 65568 | tf_op jit(solution)/shard_map/ppermute | solution.py:119
  14.4 2.5 %collective-permute-start.8 = (bf16[32,256]{1,0:T(8,128)(2,1)S(1)}, bf16[32,256]{1,0:T(8,128)(2,1)S(1)}, u32[]{:S(2)}, u32[]{:S(2)}) collective-permute-start(bf16[32,256]{1,0:T(8,128)(2,1)S(1)} %shard_map.65.refs_6_), channel_id=1, source_target_pairs={{0,12},{4,8},{8,4},{12,0},{1,13},{5,9},{9,5},{13,1},{2,14},{6,10},... | collective-permute-start | bytes 49160 | tf_op jit(solution)/shard_map/ppermute | solution.py:115
  16.9 1.6 %collective-permute-start.7 = (bf16[32,256]{1,0:T(8,128)(2,1)S(1)}, bf16[32,256]{1,0:T(8,128)(2,1)S(1)}, u32[]{:S(2)}, u32[]{:S(2)}) collective-permute-start(bf16[32,256]{1,0:T(8,128)(2,1)S(1)} %shard_map.65.refs_6_), channel_id=1, source_target_pairs={{0,8},{4,12},{8,0},{12,4},{1,9},{5,13},{9,1},{13,5},{2,10},{6,14},... | collective-permute-start | bytes 49160 | tf_op jit(solution)/shard_map/ppermute | solution.py:115
  19.9 1.6 %collective-permute-done.7.refs_8_ = bf16[32,256]{1,0:T(8,128)(2,1)S(1)} collective-permute-done((bf16[32,256]{1,0:T(8,128)(2,1)S(1)}, bf16[32,256]{1,0:T(8,128)(2,1)S(1)}, u32[]{:S(2)}, u32[]{:S(2)}) %collective-permute-start.7) | collective-permute-done | bytes 16416 | tf_op jit(solution)/shard_map/ppermute | solution.py:115
  22.2 1.3 %shard_map.66 = (f32[2,288,256]{2,1,0:T(8,128)S(1)}, f32[2,288,256]{2,1,0:T(8,128)S(1)}) custom-call(bf16[3,1024,256]{2,1,0:T(8,128)(2,1)S(1)} %bitcast.24, bf16[32,1024]{1,0:T(8,128)(2,1)S(1)} %get-tuple-element.14.left_ref, s32[1,1]{1,0:T(1,128)S(6)} %copy.8.columns_ref, s32[1,1]{1,0:T(1,128)S(6)} %copy.7.ranks_ref, ...), custom_call_target="tpu_custom_call" | custom-call | flops 402653184 | bytes 1572864 | tf_op jit(solution)/shard_map/pallas_call | solution.py:73
  23.6 2.0 %collective-permute-done.9 = f32[2,288,256]{2,1,0:T(8,128)S(1)} collective-permute-done((f32[2,288,256]{2,1,0:T(8,128)S(1)}, f32[2,288,256]{2,1,0:T(8,128)S(1)}, u32[]{:S(2)}, u32[]{:S(2)}) %collective-permute-start.9) | collective-permute-done | bytes 589856 | tf_op jit(solution)/shard_map/ppermute | solution.py:119
  25.7 0.9 %collective-permute-start.10 = (bf16[288,256]{1,0:T(8,128)(2,1)S(1)}, bf16[288,256]{1,0:T(8,128)(2,1)S(1)}, u32[]{:S(2)}, u32[]{:S(2)}) collective-permute-start(bf16[288,256]{1,0:T(8,128)(2,1)S(1)} %fusion.3), channel_id=1, source_target_pairs={{0,2},{1,3},{2,0},{3,1},{4,6},{5,7},{6,4},{7,5},{8,10},{9,11},{10,... | collective-permute-start | bytes 442376 | tf_op jit(solution)/shard_map/ppermute | solution.py:119
  26.6 5.1 %collective-permute-done.10 = bf16[288,256]{1,0:T(8,128)(2,1)S(1)} collective-permute-done((bf16[288,256]{1,0:T(8,128)(2,1)S(1)}, bf16[288,256]{1,0:T(8,128)(2,1)S(1)}, u32[]{:S(2)}, u32[]{:S(2)}) %collective-permute-start.10) | collective-permute-done | bytes 147488 | tf_op jit(solution)/shard_map/ppermute | solution.py:119
  32.8 2.5 %collective-permute-start.14 = (bf16[32,256]{1,0:T(8,128)(2,1)S(1)}, bf16[32,256]{1,0:T(8,128)(2,1)S(1)}, u32[]{:S(2)}, u32[]{:S(2)}) collective-permute-start(bf16[32,256]{1,0:T(8,128)(2,1)S(1)} %slice.35.refs_3_), channel_id=1, source_target_pairs={{0,12},{4,8},{8,4},{12,0},{1,13},{5,9},{9,5},{13,1},{2,14},{6,10},... | collective-permute-start | bytes 49160 | tf_op jit(solution)/shard_map/ppermute | solution.py:115
  35.3 2.5 %collective-permute-start.13 = (bf16[32,256]{1,0:T(8,128)(2,1)S(1)}, bf16[32,256]{1,0:T(8,128)(2,1)S(1)}, u32[]{:S(2)}, u32[]{:S(2)}) collective-permute-start(bf16[32,256]{1,0:T(8,128)(2,1)S(1)} %slice.35.refs_3_), channel_id=1, source_target_pairs={{0,8},{4,12},{8,0},{12,4},{1,9},{5,13},{9,1},{13,5},{2,10},{6,14},... | collective-permute-start | bytes 49160 | tf_op jit(solution)/shard_map/ppermute | solution.py:115
  38.5 2.1 %collective-permute-done.13.refs_5_ = bf16[32,256]{1,0:T(8,128)(2,1)S(1)} collective-permute-done((bf16[32,256]{1,0:T(8,128)(2,1)S(1)}, bf16[32,256]{1,0:T(8,128)(2,1)S(1)}, u32[]{:S(2)}, u32[]{:S(2)}) %collective-permute-start.13) | collective-permute-done | bytes 16416 | tf_op jit(solution)/shard_map/ppermute | solution.py:115
  40.6 0.7 %shard_map.67 = (f32[2,256,256]{2,1,0:T(8,128)S(1)}, f32[2,256,256]{2,1,0:T(8,128)S(1)}) custom-call(bf16[3,1024,256]{2,1,0:T(8,128)(2,1)S(1)} %bitcast.25, bf16[32,1024]{1,0:T(8,128)(2,1)S(1)} %get-tuple-element.14.left_ref, s32[1,1]{1,0:T(1,128)S(6)} %copy.8.columns_ref, bf16[288,256]{1,0:T(8,128)(2,1)S(1)} %fusion.1.refs_0_, ...), custom_call_target="tpu_custom_call" | custom-call | flops 402653184 | bytes 1572864 | tf_op jit(solution)/shard_map/pallas_call | solution.py:73
  41.4 1.9 %collective-permute-done.15 = f32[2,256,256]{2,1,0:T(8,128)S(1)} collective-permute-done((f32[2,256,256]{2,1,0:T(8,128)S(1)}, f32[2,256,256]{2,1,0:T(8,128)S(1)}, u32[]{:S(2)}, u32[]{:S(2)}) %collective-permute-start.15) | collective-permute-done | bytes 524320 | tf_op jit(solution)/shard_map/ppermute | solution.py:119
  43.4 1.1 %collective-permute-start.16 = (bf16[256,256]{1,0:T(8,128)(2,1)S(1)}, bf16[256,256]{1,0:T(8,128)(2,1)S(1)}, u32[]{:S(2)}, u32[]{:S(2)}) collective-permute-start(bf16[256,256]{1,0:T(8,128)(2,1)S(1)} %fusion.4), channel_id=1, source_target_pairs={{0,2},{1,3},{2,0},{3,1},{4,6},{5,7},{6,4},{7,5},{8,10},{9,11},{10,... | collective-permute-start | bytes 393224 | tf_op jit(solution)/shard_map/ppermute | solution.py:119
  44.5 4.5 %collective-permute-done.16 = bf16[256,256]{1,0:T(8,128)(2,1)S(1)} collective-permute-done((bf16[256,256]{1,0:T(8,128)(2,1)S(1)}, bf16[256,256]{1,0:T(8,128)(2,1)S(1)}, u32[]{:S(2)}, u32[]{:S(2)}) %collective-permute-start.16) | collective-permute-done | bytes 131104 | tf_op jit(solution)/shard_map/ppermute | solution.py:119
  49.0 0.7 %fusion.2 = f32[256,256]{1,0:T(8,128)} fusion(f32[2,256,256]{2,1,0:T(8,128)S(1)} %add.14, bf16[256,256]{1,0:T(8,128)(2,1)S(1)} %collective-permute-done.16), kind=kLoop, calls=%fused_computation.6 | loop fusion | flops 131072 | bytes 655360 | tf_op jit(solution)/shard_map/add | solution.py:187
  (33 shorter events, 4.6 us)
Async XLA Ops:
  0.0 22.2 %copy-start = (bf16[1,1024,3,256]{3,1,2,0:T(8,128)(2,1)S(1)}, bf16[1,1024,3,256]{3,1,2,0:T(8,128)(2,1)}, u32[]{:S(2)}) copy-start(bf16[1,1024,3,256]{3,1,2,0:T(8,128)(2,1)} %param.10) | copy-start | bytes 4718596
  1.1 7.2 %collective-permute-start.1 = (bf16[256,256]{1,0:T(8,128)(2,1)S(1)}, bf16[256,256]{1,0:T(8,128)(2,1)S(1)}, u32[]{:S(2)}, u32[]{:S(2)}) collective-permute-start(bf16[256,256]{1,0:T(8,128)(2,1)S(1)} %convert_element_type.20.own_ref.refs_3_), channel_id=1, source_target_pairs={{0,4},{4,0},{8,12},{12,8},{1,5},{5,1},{9,13},{13,9},{2,6},{6,2},{1... | collective-permute-start | bytes 393224 | tf_op jit(solution)/shard_map/ppermute | solution.py:115
  4.2 5.0 %collective-permute-start = (bf16[256,256]{1,0:T(8,128)(2,1)S(1)}, bf16[256,256]{1,0:T(8,128)(2,1)S(1)}, u32[]{:S(2)}, u32[]{:S(2)}) collective-permute-start(bf16[256,256]{1,0:T(8,128)(2,1)S(1)} %convert_element_type.20.own_ref.refs_3_), channel_id=1, source_target_pairs={{0,2},{1,3},{2,0},{3,1},{4,6},{5,7},{6,4},{7,5},{8,10},{9,11},{10,... | collective-permute-start | bytes 393224 | tf_op jit(solution)/shard_map/ppermute | solution.py:119
  5.7 0.8 %copy-start.1 = (bf16[1,1,24,1024]{3,2,1,0:T(8,128)(2,1)S(1)}, bf16[1,1,24,1024]{3,2,1,0:T(8,128)(2,1)}, u32[]{:S(2)}) copy-start(bf16[1,1,24,1024]{3,2,1,0:T(8,128)(2,1)} %param.8) | copy-start | bytes 147460
  6.5 0.8 %copy-start.2 = (bf16[1,1,24,1024]{3,2,1,0:T(8,128)(2,1)S(1)}, bf16[1,1,24,1024]{3,2,1,0:T(8,128)(2,1)}, u32[]{:S(2)}) copy-start(bf16[1,1,24,1024]{3,2,1,0:T(8,128)(2,1)} %param.9) | copy-start | bytes 147460
  9.1 4.3 %collective-permute-start.2 = (bf16[4,32,256]{2,1,0:T(8,128)(2,1)S(1)}, bf16[4,32,256]{2,1,0:T(8,128)(2,1)S(1)}, u32[]{:S(2)}, u32[]{:S(2)}) collective-permute-start(bf16[4,32,256]{2,1,0:T(8,128)(2,1)S(1)} %get-tuple-element.17.parts_ref.refs_0_), channel_id=1, source_target_pairs={{0,2},{1,3},{2,0},{3,1},{4,6},{5,7},{6,4},{7,5},{8,10},{9,11},{10,... | collective-permute-start | bytes 196616 | tf_op jit(solution)/shard_map/ppermute | solution.py:119
  10.7 3.5 %collective-permute-start.5 = (bf16[2,256,256]{2,1,0:T(8,128)(2,1)S(1)}, bf16[2,256,256]{2,1,0:T(8,128)(2,1)S(1)}, u32[]{:S(2)}, u32[]{:S(2)}) collective-permute-start(bf16[2,256,256]{2,1,0:T(8,128)(2,1)S(1)} %pad_maximum_fusion), channel_id=1, source_target_pairs={{0,1},{1,0},{2,3},{3,2},{4,5},{5,4},{6,7},{7,6},{8,9},{9,8},{10,11... | collective-permute-start | bytes 786440 | tf_op jit(solution)/shard_map/ppermute | solution.py:119
  10.7 8.7 %collective-permute-start.4 = (bf16[256,256]{1,0:T(8,128)(2,1)S(1)}, bf16[256,256]{1,0:T(8,128)(2,1)S(1)}, u32[]{:S(2)}, u32[]{:S(2)}) collective-permute-start(bf16[256,256]{1,0:T(8,128)(2,1)S(1)} %convert_element_type.20.own_ref.refs_3_), channel_id=1, source_target_pairs={{0,0},{4,8},{8,4},{12,12},{1,1},{5,9},{9,5},{13,13},{2,2},{6,10},{... | collective-permute-start | bytes 393224 | tf_op jit(solution)/shard_map/ppermute | solution.py:115
  13.4 6.0 %collective-permute-start.3 = (bf16[2,4,32,256]{3,2,1,0:T(8,128)(2,1)S(1)}, bf16[2,4,32,256]{3,2,1,0:T(8,128)(2,1)S(1)}, u32[]{:S(2)}, u32[]{:S(2)}) collective-permute-start(bf16[2,4,32,256]{3,2,1,0:T(8,128)(2,1)S(1)} %pad_maximum_fusion.1), channel_id=1, source_target_pairs={{0,1},{1,0},{2,3},{3,2},{4,5},{5,4},{6,7},{7,6},{8,9},{9,8},{10,11... | collective-permute-start | bytes 393224 | tf_op jit(solution)/shard_map/ppermute | solution.py:119
  14.4 5.6 %collective-permute-start.8 = (bf16[32,256]{1,0:T(8,128)(2,1)S(1)}, bf16[32,256]{1,0:T(8,128)(2,1)S(1)}, u32[]{:S(2)}, u32[]{:S(2)}) collective-permute-start(bf16[32,256]{1,0:T(8,128)(2,1)S(1)} %shard_map.65.refs_6_), channel_id=1, source_target_pairs={{0,12},{4,8},{8,4},{12,0},{1,13},{5,9},{9,5},{13,1},{2,14},{6,10},... | collective-permute-start | bytes 49160 | tf_op jit(solution)/shard_map/ppermute | solution.py:115
  16.9 4.6 %collective-permute-start.7 = (bf16[32,256]{1,0:T(8,128)(2,1)S(1)}, bf16[32,256]{1,0:T(8,128)(2,1)S(1)}, u32[]{:S(2)}, u32[]{:S(2)}) collective-permute-start(bf16[32,256]{1,0:T(8,128)(2,1)S(1)} %shard_map.65.refs_6_), channel_id=1, source_target_pairs={{0,8},{4,12},{8,0},{12,4},{1,9},{5,13},{9,1},{13,5},{2,10},{6,14},... | collective-permute-start | bytes 49160 | tf_op jit(solution)/shard_map/ppermute | solution.py:115
  18.5 3.7 %collective-permute-start.6 = (bf16[32,256]{1,0:T(8,128)(2,1)S(1)}, bf16[32,256]{1,0:T(8,128)(2,1)S(1)}, u32[]{:S(2)}, u32[]{:S(2)}) collective-permute-start(bf16[32,256]{1,0:T(8,128)(2,1)S(1)} %shard_map.65.refs_6_), channel_id=1, source_target_pairs={{0,4},{4,0},{8,12},{12,8},{1,5},{5,1},{9,13},{13,9},{2,6},{6,2},{1... | collective-permute-start | bytes 49160 | tf_op jit(solution)/shard_map/ppermute | solution.py:115
  23.5 2.1 %collective-permute-start.9 = (f32[2,288,256]{2,1,0:T(8,128)S(1)}, f32[2,288,256]{2,1,0:T(8,128)S(1)}, u32[]{:S(2)}, u32[]{:S(2)}) collective-permute-start(f32[2,288,256]{2,1,0:T(8,128)S(1)} %get-tuple-element.20), channel_id=1, source_target_pairs={{0,1},{1,0},{2,3},{3,2},{4,5},{5,4},{6,7},{7,6},{8,9},{9,8},{10,11... | collective-permute-start | bytes 1769480 | tf_op jit(solution)/shard_map/ppermute | solution.py:119
  25.7 6.0 %collective-permute-start.10 = (bf16[288,256]{1,0:T(8,128)(2,1)S(1)}, bf16[288,256]{1,0:T(8,128)(2,1)S(1)}, u32[]{:S(2)}, u32[]{:S(2)}) collective-permute-start(bf16[288,256]{1,0:T(8,128)(2,1)S(1)} %fusion.3), channel_id=1, source_target_pairs={{0,2},{1,3},{2,0},{3,1},{4,6},{5,7},{6,4},{7,5},{8,10},{9,11},{10,... | collective-permute-start | bytes 442376 | tf_op jit(solution)/shard_map/ppermute | solution.py:119
  31.7 6.1 %collective-permute-start.11 = (bf16[288,256]{1,0:T(8,128)(2,1)S(1)}, bf16[288,256]{1,0:T(8,128)(2,1)S(1)}, u32[]{:S(2)}, u32[]{:S(2)}) collective-permute-start(bf16[288,256]{1,0:T(8,128)(2,1)S(1)} %fusion.1.refs_0_), channel_id=1, source_target_pairs={{0,4},{4,0},{8,12},{12,8},{1,5},{5,1},{9,13},{13,9},{2,6},{6,2},{1... | collective-permute-start | bytes 442376 | tf_op jit(solution)/shard_map/ppermute | solution.py:115
  32.1 8.5 %collective-permute-start.12 = (bf16[256,256]{1,0:T(8,128)(2,1)S(1)}, bf16[256,256]{1,0:T(8,128)(2,1)S(1)}, u32[]{:S(2)}, u32[]{:S(2)}) collective-permute-start(bf16[256,256]{1,0:T(8,128)(2,1)S(1)} %slice.34), channel_id=1, source_target_pairs={{0,0},{4,8},{8,4},{12,12},{1,1},{5,9},{9,5},{13,13},{2,2},{6,10},{... | collective-permute-start | bytes 393224 | tf_op jit(solution)/shard_map/ppermute | solution.py:115
  32.8 5.7 %collective-permute-start.14 = (bf16[32,256]{1,0:T(8,128)(2,1)S(1)}, bf16[32,256]{1,0:T(8,128)(2,1)S(1)}, u32[]{:S(2)}, u32[]{:S(2)}) collective-permute-start(bf16[32,256]{1,0:T(8,128)(2,1)S(1)} %slice.35.refs_3_), channel_id=1, source_target_pairs={{0,12},{4,8},{8,4},{12,0},{1,13},{5,9},{9,5},{13,1},{2,14},{6,10},... | collective-permute-start | bytes 49160 | tf_op jit(solution)/shard_map/ppermute | solution.py:115
  35.3 5.3 %collective-permute-start.13 = (bf16[32,256]{1,0:T(8,128)(2,1)S(1)}, bf16[32,256]{1,0:T(8,128)(2,1)S(1)}, u32[]{:S(2)}, u32[]{:S(2)}) collective-permute-start(bf16[32,256]{1,0:T(8,128)(2,1)S(1)} %slice.35.refs_3_), channel_id=1, source_target_pairs={{0,8},{4,12},{8,0},{12,4},{1,9},{5,13},{9,1},{13,5},{2,10},{6,14},... | collective-permute-start | bytes 49160 | tf_op jit(solution)/shard_map/ppermute | solution.py:115
  41.3 2.0 %collective-permute-start.15 = (f32[2,256,256]{2,1,0:T(8,128)S(1)}, f32[2,256,256]{2,1,0:T(8,128)S(1)}, u32[]{:S(2)}, u32[]{:S(2)}) collective-permute-start(f32[2,256,256]{2,1,0:T(8,128)S(1)} %get-tuple-element.22), channel_id=1, source_target_pairs={{0,1},{1,0},{2,3},{3,2},{4,5},{5,4},{6,7},{7,6},{8,9},{9,8},{10,11... | collective-permute-start | bytes 1572872 | tf_op jit(solution)/shard_map/ppermute | solution.py:119
  43.4 5.6 %collective-permute-start.16 = (bf16[256,256]{1,0:T(8,128)(2,1)S(1)}, bf16[256,256]{1,0:T(8,128)(2,1)S(1)}, u32[]{:S(2)}, u32[]{:S(2)}) collective-permute-start(bf16[256,256]{1,0:T(8,128)(2,1)S(1)} %fusion.4), channel_id=1, source_target_pairs={{0,2},{1,3},{2,0},{3,1},{4,6},{5,7},{6,4},{7,5},{8,10},{9,11},{10,... | collective-permute-start | bytes 393224 | tf_op jit(solution)/shard_map/ppermute | solution.py:119

commit v5 on v4

v5 whole, which is shorter than its diff:
```python
import functools

import jax
import jax.numpy as jnp
from jax import lax
from jax.experimental import pallas as pl
from jax.experimental.pallas import tpu as pltpu
from jax.sharding import PartitionSpec as P

BF = jnp.bfloat16
F32 = jnp.float32


def shifted(block, axis, distance):
    devices = range(lax.axis_size(axis))
    route = [(i - distance, i) for i in devices if i - distance in devices]
    return lax.ppermute(block, axis, route)


def image_part(operand, right_bases, left_bases, near_tiles, tile_ranks, column_rows, row_columns):
    tile_slots = right_bases.shape[1]
    rank_part = right_bases.shape[2]
    tile_rows = right_bases.shape[3]
    probe_count = operand.shape[1]
    tile_count = lax.axis_size("tile")
    right_flat = right_bases.reshape(tile_slots * rank_part, tile_rows)
    left_flat = left_bases.reshape(tile_slots * rank_part, tile_rows)
    dense_flat = near_tiles.reshape(tile_rows, -1)
    values = jnp.dot(
        right_flat,
        lax.all_gather(operand, "list", axis=0, tiled=True),
        preferred_element_type=F32,
    )
    rank_level = lax.axis_index("list") * rank_part + lax.iota(jnp.int32, rank_part)
    rank_mask = rank_level[None, :] < tile_ranks[0][:, None]
    coefficients = jnp.where(
        rank_mask[:, :, None], values.reshape(tile_slots, rank_part, probe_count), 0.0
    ).astype(BF)
    targets = (column_rows[0][None, :] == lax.iota(jnp.int32, tile_count)[:, None]).astype(BF)
    outgoing = jnp.einsum(
        "dk,krp->drp", targets, coefficients, preferred_element_type=F32
    ).astype(BF)
    sources = (row_columns[0][:, None] == lax.iota(jnp.int32, tile_count)[None, :]).astype(BF)
    chosen = jnp.einsum(
        "kj,jrp->krp",
        sources,
        lax.all_to_all(outgoing, "tile", split_axis=0, concat_axis=0, tiled=True),
        preferred_element_type=F32,
    ).astype(BF)
    chosen = chosen.reshape(tile_slots * rank_part, -1)
    far_sum = lax.dot_general(
        left_flat, chosen, (((0,), (0,)), ((), ())), preferred_element_type=F32
    )
    arrived = {}
    for offset in (1, -1):
        arrived[offset] = shifted(operand, "tile", offset)
    stacked = jnp.concatenate([arrived[1], operand, arrived[-1]], axis=0)
    near_sum = jnp.dot(dense_flat, stacked, preferred_element_type=F32)
    partial_image = near_sum + far_sum
    return lax.psum_scatter(partial_image, "list", scatter_dimension=0, tiled=True)


def many_slots(probes, right_bases, left_bases, near_tiles, tile_ranks, column_rows, row_columns):
    rest = (right_bases, left_bases, near_tiles, tile_ranks, column_rows, row_columns)
    first_pass = image_part(probes.astype(BF), *rest).astype(BF)
    return image_part(first_pass, *rest)


VMEM = pl.BlockSpec(memory_space=pltpu.VMEM)


def kernel_call(kernel, outs, operands, flops=0):
    return pl.pallas_call(
        kernel,
        out_shape=tuple(jax.ShapeDtypeStruct(shape, kind) for shape, kind in outs),
        in_specs=[VMEM] * len(operands),
        out_specs=tuple(VMEM for _ in outs),
        compiler_params=pltpu.CompilerParams(vmem_limit_bytes=16 * 2**20),
        cost_estimate=pl.CostEstimate(
            flops=flops, bytes_accessed=2 * operands[0].size, transcendentals=0
        ),
    )(*operands)


def coefficient_sums(right_parts, operands, group_rows, rank_part, ranks_ref, keep_ref, send_ref):
    me = lax.axis_index("list")
    total = jnp.zeros((4 * group_rows, operands[0].shape[1]), F32)
    for right, operand in zip(right_parts, operands):
        total += jnp.dot(right, operand, preferred_element_type=F32)
    slot = lax.broadcasted_iota(jnp.int32, (group_rows, total.shape[1]), 0)
    for turn in range(4):
        level = (me ^ turn) * rank_part + slot
        keep = (level < ranks_ref[...]) & (slot < rank_part)
        out_ref = send_ref if turn % 2 else keep_ref
        out_ref[turn // 2] = jnp.where(
            keep, total[turn * group_rows : (turn + 1) * group_rows], 0.0
        )


def coefficient_kernel(even_ref, odd_ref, block_ref, ranks_ref, parts_ref, keep_ref, send_ref):
    me = lax.axis_index("list")
    ranks = even_ref.shape[1]
    rows = block_ref.shape[0]
    slots = keep_ref.shape[1]
    parts_ref[...] = jnp.zeros_like(parts_ref)
    groups = (even_ref.at[0], odd_ref.at[0], even_ref.at[1], odd_ref.at[1])
    for part in range(parts_ref.shape[0]):
        for turn, group_ref in enumerate(groups):
            parts_ref[part, turn * slots : turn * slots + ranks, :] = group_ref[
                :, part * rows : (part + 1) * rows
            ]
    coefficient_sums(
        [parts_ref[me]], [block_ref[...]], slots, ranks, ranks_ref, keep_ref, send_ref
    )


def tile_swap(block, turn):
    count = lax.axis_size("tile")
    route = [(i, i ^ turn) for i in range(count)]
    if turn == 0:
        route = [(i, min(max(i - 1 + 2 * (i % 2), 0), count - 1)) for i in range(count)]
    return lax.ppermute(block, "tile", route)


def list_swap(block, bit):
    return lax.ppermute(block, "list", [(i, i ^ bit) for i in range(lax.axis_size("list"))])


def far_and_near(columns_ref, block_refs, coefficient_refs):
    count = lax.axis_size("tile")
    tile = lax.axis_index("tile")
    own_ref, second_ref, pair_ref = coefficient_refs
    slots = own_ref.shape[0]
    chosen = own_ref[...]
    others = (pair_ref[:slots, :], second_ref[...], pair_ref[slots:, :])
    for turn, other in enumerate(others):
        chosen = jnp.where(columns_ref[...] == tile ^ (turn + 1), other, chosen)
    odd = lax.rem(tile, 2)
    inside = (tile > 0) & (tile < count - 1)
    blocks = [
        (1, block_refs[0][...]),
        (2 - 2 * odd, block_refs[1][...]),
        (2 * odd, jnp.where(inside, block_refs[2][...], 0)),
    ]
    return chosen, blocks


def row_part(near_ref, left_ref, blocks, coefficients, part):
    rows = near_ref.shape[2]
    cut = pl.ds(pl.multiple_of(part * rows, rows), rows)
    total = lax.dot_general(
        left_ref[:, cut], coefficients, (((0,), (0,)), ((), ())), preferred_element_type=F32
    )
    for side, block in blocks:
        total += jnp.dot(near_ref[side, cut, :], block, preferred_element_type=F32)
    return total


def image_kernel(near_ref, left_ref, columns_ref, *refs):
    block_refs, coefficient_refs, (keep_ref, send_ref) = refs[:3], refs[3:6], refs[6:]
    me = lax.axis_index("list")
    coefficients, blocks = far_and_near(columns_ref, block_refs, coefficient_refs)
    totals = []
    for turn in (1, 3, 0, 2):
        out_ref = send_ref if turn % 2 else keep_ref
        total = row_part(near_ref, left_ref, blocks, coefficients, me ^ turn)
        out_ref[turn // 2] = total
        totals.append((me ^ turn, total.astype(BF)))
    return totals


def first_kernel(rank_part, near_ref, left_ref, columns_ref, ranks_ref, parts_ref, *refs):
    totals = image_kernel(near_ref, left_ref, columns_ref, *refs[:8])
    coefficient_sums(
        [parts_ref[part] for part, _ in totals],
        [total for _, total in totals],
        parts_ref.shape[1] // 4,
        rank_part,
        ranks_ref,
        *refs[8:],
    )


def second_kernel(*refs):
    image_kernel(*refs)


def list_sum(keep, send, kind=F32, after=()):
    pair = keep + list_swap(send, 1)
    pair, *_ = lax.optimization_barrier((pair, *after))
    return pair[0] + list_swap(pair[1].astype(kind), 2)


def one_slot(probes, right_bases, left_bases, near_tiles, tile_ranks, column_rows, row_columns):
    rank_part, tile_rows = right_bases.shape[2:]
    rows, probe_count = probes.shape
    slots = -(-rank_part // 16) * 16
    near = near_tiles[0].transpose(1, 0, 2)
    flops = 2 * near.size * probe_count
    right = right_bases[0, 0]
    right = jnp.stack([right, list_swap(right, 2)])
    right_pair = list_swap(right, 1)
    left = jnp.pad(left_bases[0, 0], ((0, slots - rank_part), (0, 0)))
    block = probes.astype(BF)
    beside = [block, tile_swap(block, 1), tile_swap(block, 0)]
    image_sums = [((2, rows, probe_count), F32)] * 2
    small_sums = [((2, slots, probe_count), F32)] * 2
    parts, keep, send = kernel_call(
        coefficient_kernel,
        [((tile_rows // rows, 4 * slots, rows), BF), *small_sums],
        (right, right_pair, block, tile_ranks),
        8 * flops,
    )
    own = list_sum(keep, send, after=beside).astype(BF)
    second = tile_swap(own, 2)
    coefficients = own, second, tile_swap(jnp.concatenate([own, second]), 1)
    keep, send, small_keep, small_send = kernel_call(
        functools.partial(first_kernel, rank_part),
        image_sums + small_sums,
        (near, left, row_columns, tile_ranks, parts, *beside, *coefficients),
        flops,
    )
    own = list_sum(small_keep, small_send).astype(BF)
    second = tile_swap(own, 2)
    block = list_sum(keep, send, BF).astype(BF)
    message = tile_swap(jnp.concatenate([block, own, second]), 1)
    beside = [block, message[:rows], tile_swap(block, 0)]
    coefficients = own, second, message[rows:]
    keep, send = kernel_call(
        second_kernel,
        image_sums,
        (near, left, row_columns, *beside, *coefficients),
        flops,
    )
    return list_sum(keep, send, BF)


def local(probes, right_bases, left_bases, near_tiles, tile_ranks, column_rows, row_columns):
    few = lax.axis_size("tile") == 4 and lax.axis_size("list") == 4
    small = right_bases.shape[1] == 1 and few
    form = one_slot if small else many_slots
    return form(
        probes, right_bases, left_bases, near_tiles, tile_ranks, column_rows, row_columns
    )


def solution(mesh):
    placed = (
        P(("group", "tile", "list"), None),
        P(("group", "tile"), None, "list", None),
        P(("group", "tile"), None, "list", None),
        P(("group", "tile"), None, None, "list"),
        P(("group", "tile"), None),
        P("tile", None),
        P("tile", None),
    )
    return jax.shard_map(
        local,
        mesh=mesh,
        in_specs=placed,
        out_specs=P(("group", "tile", "list"), None),
        check_vma=False,
    )
```

time: 50.1 us -> 56.3 us (1.12); the launches traced: 49.7 us -> 55.3 us
  waiting for transfers between devices: 22 us -> 26.6 us
  starting transfers between devices: 19.4 us -> 22.7 us
  local copies, waits for them, and re-layouts: 1.65 us -> 0.07 us
    ppermute x9 -> x7, waiting for transfers between devices: 5.59 us -> 10.4 us  [tile_swap(): return lax.ppermute(block, 'tile', route)]
    ppermute x8 -> x10, starting transfers between devices: 5.19 us -> 9.2 us  [list_swap(): lax.ppermute(block, 'list', [(i, i ^ bit) for i in range(lax.axis_size('l...]
    unnamed x6 -> x4, local copies, waits for them, and re-layouts: 1.6 us -> 0.01 us
    ppermute x9 -> x7, starting transfers between devices: 14.2 us -> 13.5 us  [tile_swap(): return lax.ppermute(block, 'tile', route)]
    pallas_call x4 -> x3, Pallas kernels: 2.23 us -> 1.77 us  [kernel_call(): pl.pallas_call(kernel, out_shape=tuple((jax.ShapeDtypeStruct(shape, kind)...]
    ppermute x8 -> x10, waiting for transfers between devices: 16.4 us -> 16.2 us  [list_swap(): lax.ppermute(block, 'list', [(i, i ^ bit) for i in range(lax.axis_size('l...]
  transfers between devices with their start and end apart: 17 -> 17, of which waited for: 11 -> 13; matrix products, arithmetic and copies ran while one was open for 2% -> 2% of each run, Pallas kernels for 0% -> 0%
where the time goes in v5:
time: 56.3 us; the launch traced here: 55.3 us
  waiting for transfers between devices  26.6 us (47%)
  starting transfers between devices  22.7 us (40%)
  other arithmetic  2.72 us (5%)
  Pallas kernels  1.77 us (3%)
  between operations  1.5 us (3%)
    ppermute x10, waiting for transfers between devices, list_swap(): lax.ppermute(block, 'list', [(i, i ^ bit) for i in range(lax.axis_size('l...  16.2 us
    ppermute x7, starting transfers between devices, tile_swap(): return lax.ppermute(block, 'tile', route)  13.5 us
    ppermute x7, waiting for transfers between devices, tile_swap(): return lax.ppermute(block, 'tile', route)  10.4 us
    ppermute x10, starting transfers between devices, list_swap(): lax.ppermute(block, 'list', [(i, i ^ bit) for i in range(lax.axis_size('l...  9.2 us
    pallas_call x3, Pallas kernels, kernel_call(): pl.pallas_call(kernel, out_shape=tuple((jax.ShapeDtypeStruct(shape, kind)...  1.77 us
  transfers between devices with their start and end apart: 17, of which 13 were waited for; matrix products, arithmetic and copies ran while one was open for 2% of the time, Pallas kernels for 0%

profile of v5, /device:TPU:0, one launch (start us, length us, event | category | flops | bytes accessed | tf_op | source)
XLA Modules:
  0.0 55.3 jit_solution(17332861243661293598)
XLA Ops:
  0.0 2.9 %collective-permute-start = (bf16[24,1024]{1,0:T(8,128)(2,1)}, bf16[24,1024]{1,0:T(8,128)(2,1)S(1)}, u32[]{:S(2)}, u32[]{:S(2)}) collective-permute-start(bf16[24,1024]{1,0:T(8,128)(2,1)} %bitcast.38), channel_id=1, source_target_pairs={{0,2},{1,3},{2,0},{3,1},{4,6},{5,7},{6,4},{7,5},{8,10},{9,11},{10,... | collective-permute-start | bytes 147464 | tf_op jit(solution)/shard_map/ppermute | solution.py:126
  2.9 2.3 %collective-permute-done = bf16[24,1024]{1,0:T(8,128)(2,1)S(1)} collective-permute-done((bf16[24,1024]{1,0:T(8,128)(2,1)}, bf16[24,1024]{1,0:T(8,128)(2,1)S(1)}, u32[]{:S(2)}, u32[]{:S(2)}) %collective-permute-start) | collective-permute-done | bytes 49184 | tf_op jit(solution)/shard_map/ppermute | solution.py:126
  6.1 1.0 %convert_element_type.28.block_ref.refs_0_ = bf16[256,256]{1,0:T(8,128)(2,1)S(1)} convert(f32[256,256]{1,0:T(8,128)} %param.7) | non-fusion elementwise | flops 65536 | bytes 393216 | tf_op jit(solution)/shard_map/convert_element_type | solution.py:204
  7.8 5.0 %collective-permute-start.2 = (bf16[256,256]{1,0:T(8,128)(2,1)S(1)}, bf16[256,256]{1,0:T(8,128)(2,1)S(1)}, u32[]{:S(2)}, u32[]{:S(2)}) collective-permute-start(bf16[256,256]{1,0:T(8,128)(2,1)S(1)} %convert_element_type.28.block_ref.refs_0_), channel_id=1, source_target_pairs={{0,4},{4,0},{8,12},{12,8},{1,5},{5,1},{9,13},{13,9},{2,6},{6,2},{1... | collective-permute-start | bytes 393224 | tf_op jit(solution)/shard_map/ppermute | solution.py:122
  13.7 1.2 %collective-permute-done.4 = f32[2,32,256]{2,1,0:T(8,128)S(1)} collective-permute-done((f32[2,32,256]{2,1,0:T(8,128)S(1)}, f32[2,32,256]{2,1,0:T(8,128)S(1)}, u32[]{:S(2)}, u32[]{:S(2)}) %collective-permute-start.4) | collective-permute-done | bytes 65568 | tf_op jit(solution)/shard_map/ppermute | solution.py:126
  14.9 1.7 %collective-permute-done.2.refs_1_ = bf16[256,256]{1,0:T(8,128)(2,1)S(1)} collective-permute-done((bf16[256,256]{1,0:T(8,128)(2,1)S(1)}, bf16[256,256]{1,0:T(8,128)(2,1)S(1)}, u32[]{:S(2)}, u32[]{:S(2)}) %collective-permute-start.2) | collective-permute-done | bytes 131104 | tf_op jit(solution)/shard_map/ppermute | solution.py:122
  16.6 1.5 %collective-permute-start.5 = (f32[32,256]{1,0:T(8,128)S(1)}, f32[32,256]{1,0:T(8,128)S(1)}, u32[]{:S(2)}, u32[]{:S(2)}) collective-permute-start(f32[32,256]{1,0:T(8,128)S(1)} %slice_bitcast_fusion.4), channel_id=1, source_target_pairs={{0,2},{1,3},{2,0},{3,1},{4,6},{5,7},{6,4},{7,5},{8,10},{9,11},{10,... | collective-permute-start | bytes 98312 | tf_op jit(solution)/shard_map/ppermute | solution.py:126
  18.1 2.4 %collective-permute-done.5 = f32[32,256]{1,0:T(8,128)S(1)} collective-permute-done((f32[32,256]{1,0:T(8,128)S(1)}, f32[32,256]{1,0:T(8,128)S(1)}, u32[]{:S(2)}, u32[]{:S(2)}) %collective-permute-start.5) | collective-permute-done | bytes 32800 | tf_op jit(solution)/shard_map/ppermute | solution.py:126
  20.5 1.6 %collective-permute-start.6 = (bf16[32,256]{1,0:T(8,128)(2,1)S(1)}, bf16[32,256]{1,0:T(8,128)(2,1)S(1)}, u32[]{:S(2)}, u32[]{:S(2)}) collective-permute-start(bf16[32,256]{1,0:T(8,128)(2,1)S(1)} %fusion.7.refs_3_), channel_id=1, source_target_pairs={{0,8},{4,12},{8,0},{12,4},{1,9},{5,13},{9,1},{13,5},{2,10},{6,14},... | collective-permute-start | bytes 49160 | tf_op jit(solution)/shard_map/ppermute | solution.py:122
  22.2 3.0 %collective-permute-done.6.refs_4_ = bf16[32,256]{1,0:T(8,128)(2,1)S(1)} collective-permute-done((bf16[32,256]{1,0:T(8,128)(2,1)S(1)}, bf16[32,256]{1,0:T(8,128)(2,1)S(1)}, u32[]{:S(2)}, u32[]{:S(2)}) %collective-permute-start.6) | collective-permute-done | bytes 16416 | tf_op jit(solution)/shard_map/ppermute | solution.py:122
  25.2 1.9 %collective-permute-start.7 = (bf16[64,256]{1,0:T(8,128)(2,1)S(1)}, bf16[64,256]{1,0:T(8,128)(2,1)S(1)}, u32[]{:S(2)}, u32[]{:S(2)}) collective-permute-start(bf16[64,256]{1,0:T(8,128)(2,1)S(1)} %pad_maximum_fusion.2), channel_id=1, source_target_pairs={{0,4},{4,0},{8,12},{12,8},{1,5},{5,1},{9,13},{13,9},{2,6},{6,2},{1... | collective-permute-start | bytes 98312 | tf_op jit(solution)/shard_map/ppermute | solution.py:122
  27.8 1.3 %collective-permute-done.7.refs_5_ = bf16[64,256]{1,0:T(8,128)(2,1)S(1)} collective-permute-done((bf16[64,256]{1,0:T(8,128)(2,1)S(1)}, bf16[64,256]{1,0:T(8,128)(2,1)S(1)}, u32[]{:S(2)}, u32[]{:S(2)}) %collective-permute-start.7) | collective-permute-done | bytes 32800 | tf_op jit(solution)/shard_map/ppermute | solution.py:122
  29.1 0.9 %shard_map.65 = (f32[2,256,256]{2,1,0:T(8,128)S(1)}, f32[2,256,256]{2,1,0:T(8,128)S(1)}, f32[2,32,256]{2,1,0:T(8,128)S(1)}, f32[2,32,256]{2,1,0:T(8,128)S(1)}) custom-call(bf16[3,1024,256]{2,1,0:T(8,128)(2,1)S(1)} %bitcast.35, bf16[32,1024]{1,0:T(8,128)(2,1)S(1)} %pad.4.left_ref.refs_1_, s32[1,1]{1,0:T(1,128)S(6)} %copy.8.columns_ref.refs_2_, ...), custom_call_target="tpu_custom_call" | custom-call | flops 402653184 | bytes 1572864 | tf_op jit(solution)/shard_map/pallas_call | solution.py:73
  30.6 1.5 %collective-permute-done.10 = f32[2,32,256]{2,1,0:T(8,128)S(1)} collective-permute-done((f32[2,32,256]{2,1,0:T(8,128)S(1)}, f32[2,32,256]{2,1,0:T(8,128)S(1)}, u32[]{:S(2)}, u32[]{:S(2)}) %collective-permute-start.10) | collective-permute-done | bytes 65568 | tf_op jit(solution)/shard_map/ppermute | solution.py:126
  32.1 1.6 %collective-permute-start.11 = (f32[32,256]{1,0:T(8,128)S(1)}, f32[32,256]{1,0:T(8,128)S(1)}, u32[]{:S(2)}, u32[]{:S(2)}) collective-permute-start(f32[32,256]{1,0:T(8,128)S(1)} %slice_bitcast_fusion.2), channel_id=1, source_target_pairs={{0,2},{1,3},{2,0},{3,1},{4,6},{5,7},{6,4},{7,5},{8,10},{9,11},{10,... | collective-permute-start | bytes 98312 | tf_op jit(solution)/shard_map/ppermute | solution.py:126
  34.4 1.7 %collective-permute-done.11 = f32[32,256]{1,0:T(8,128)S(1)} collective-permute-done((f32[32,256]{1,0:T(8,128)S(1)}, f32[32,256]{1,0:T(8,128)S(1)}, u32[]{:S(2)}, u32[]{:S(2)}) %collective-permute-start.11) | collective-permute-done | bytes 32800 | tf_op jit(solution)/shard_map/ppermute | solution.py:126
  36.1 1.6 %collective-permute-start.12 = (bf16[32,256]{1,0:T(8,128)(2,1)S(1)}, bf16[32,256]{1,0:T(8,128)(2,1)S(1)}, u32[]{:S(2)}, u32[]{:S(2)}) collective-permute-start(bf16[32,256]{1,0:T(8,128)(2,1)S(1)} %fusion.6.refs_6_), channel_id=1, source_target_pairs={{0,8},{4,12},{8,0},{12,4},{1,9},{5,13},{9,1},{13,5},{2,10},{6,14},... | collective-permute-start | bytes 49160 | tf_op jit(solution)/shard_map/ppermute | solution.py:122
  37.7 1.4 %collective-permute-done.9 = bf16[256,256]{1,0:T(8,128)(2,1)S(1)} collective-permute-done((bf16[256,256]{1,0:T(8,128)(2,1)S(1)}, bf16[256,256]{1,0:T(8,128)(2,1)S(1)}, u32[]{:S(2)}, u32[]{:S(2)}) %collective-permute-start.9) | collective-permute-done | bytes 131104 | tf_op jit(solution)/shard_map/ppermute | solution.py:126
  39.1 1.6 %collective-permute-done.12.refs_7_ = bf16[32,256]{1,0:T(8,128)(2,1)S(1)} collective-permute-done((bf16[32,256]{1,0:T(8,128)(2,1)S(1)}, bf16[32,256]{1,0:T(8,128)(2,1)S(1)}, u32[]{:S(2)}, u32[]{:S(2)}) %collective-permute-start.12) | collective-permute-done | bytes 16416 | tf_op jit(solution)/shard_map/ppermute | solution.py:122
  40.8 2.0 %collective-permute-start.13 = (bf16[320,256]{1,0:T(8,128)(2,1)S(1)}, bf16[320,256]{1,0:T(8,128)(2,1)S(1)}, u32[]{:S(2)}, u32[]{:S(2)}) collective-permute-start(bf16[320,256]{1,0:T(8,128)(2,1)S(1)} %pad_maximum_fusion), channel_id=1, source_target_pairs={{0,4},{4,0},{8,12},{12,8},{1,5},{5,1},{9,13},{13,9},{2,6},{6,2},{1... | collective-permute-start | bytes 491528 | tf_op jit(solution)/shard_map/ppermute | solution.py:122
  43.4 2.7 %collective-permute-done.13 = bf16[320,256]{1,0:T(8,128)(2,1)S(1)} collective-permute-done((bf16[320,256]{1,0:T(8,128)(2,1)S(1)}, bf16[320,256]{1,0:T(8,128)(2,1)S(1)}, u32[]{:S(2)}, u32[]{:S(2)}) %collective-permute-start.13) | collective-permute-done | bytes 163872 | tf_op jit(solution)/shard_map/ppermute | solution.py:122
  47.0 1.9 %collective-permute-done.15 = f32[2,256,256]{2,1,0:T(8,128)S(1)} collective-permute-done((f32[2,256,256]{2,1,0:T(8,128)S(1)}, f32[2,256,256]{2,1,0:T(8,128)S(1)}, u32[]{:S(2)}, u32[]{:S(2)}) %collective-permute-start.15) | collective-permute-done | bytes 524320 | tf_op jit(solution)/shard_map/ppermute | solution.py:126
  48.9 1.8 %collective-permute-start.16 = (bf16[256,256]{1,0:T(8,128)(2,1)S(1)}, bf16[256,256]{1,0:T(8,128)(2,1)S(1)}, u32[]{:S(2)}, u32[]{:S(2)}) collective-permute-start(bf16[256,256]{1,0:T(8,128)(2,1)S(1)} %fusion.4), channel_id=1, source_target_pairs={{0,2},{1,3},{2,0},{3,1},{4,6},{5,7},{6,4},{7,5},{8,10},{9,11},{10,... | collective-permute-start | bytes 393224 | tf_op jit(solution)/shard_map/ppermute | solution.py:126
  50.8 3.8 %collective-permute-done.16 = bf16[256,256]{1,0:T(8,128)(2,1)S(1)} collective-permute-done((bf16[256,256]{1,0:T(8,128)(2,1)S(1)}, bf16[256,256]{1,0:T(8,128)(2,1)S(1)}, u32[]{:S(2)}, u32[]{:S(2)}) %collective-permute-start.16) | collective-permute-done | bytes 131104 | tf_op jit(solution)/shard_map/ppermute | solution.py:126
  (36 shorter events, 5.4 us)
Async XLA Ops:
  0.0 5.2 %collective-permute-start = (bf16[24,1024]{1,0:T(8,128)(2,1)}, bf16[24,1024]{1,0:T(8,128)(2,1)S(1)}, u32[]{:S(2)}, u32[]{:S(2)}) collective-permute-start(bf16[24,1024]{1,0:T(8,128)(2,1)} %bitcast.38), channel_id=1, source_target_pairs={{0,2},{1,3},{2,0},{3,1},{4,6},{5,7},{6,4},{7,5},{8,10},{9,11},{10,... | collective-permute-start | bytes 147464 | tf_op jit(solution)/shard_map/ppermute | solution.py:126
  6.0 7.4 %collective-permute-start.1 = (bf16[2,24,1024]{2,1,0:T(8,128)(2,1)S(1)}, bf16[2,24,1024]{2,1,0:T(8,128)(2,1)S(1)}, u32[]{:S(2)}, u32[]{:S(2)}) collective-permute-start(bf16[2,24,1024]{2,1,0:T(8,128)(2,1)S(1)} %pad_maximum_fusion.1.even_ref), channel_id=1, source_target_pairs={{0,1},{1,0},{2,3},{3,2},{4,5},{5,4},{6,7},{7,6},{8,9},{9,8},{10,11... | collective-permute-start | bytes 294920 | tf_op jit(solution)/shard_map/ppermute | solution.py:126
  7.1 7.9 %collective-permute-start.3 = (bf16[256,256]{1,0:T(8,128)(2,1)S(1)}, bf16[256,256]{1,0:T(8,128)(2,1)S(1)}, u32[]{:S(2)}, u32[]{:S(2)}) collective-permute-start(bf16[256,256]{1,0:T(8,128)(2,1)S(1)} %convert_element_type.28.block_ref.refs_0_), channel_id=1, source_target_pairs={{0,0},{4,8},{8,4},{12,12},{1,1},{5,9},{9,5},{13,13},{2,2},{6,10},{... | collective-permute-start | bytes 393224 | tf_op jit(solution)/shard_map/ppermute | solution.py:122
  7.8 8.9 %collective-permute-start.2 = (bf16[256,256]{1,0:T(8,128)(2,1)S(1)}, bf16[256,256]{1,0:T(8,128)(2,1)S(1)}, u32[]{:S(2)}, u32[]{:S(2)}) collective-permute-start(bf16[256,256]{1,0:T(8,128)(2,1)S(1)} %convert_element_type.28.block_ref.refs_0_), channel_id=1, source_target_pairs={{0,4},{4,0},{8,12},{12,8},{1,5},{5,1},{9,13},{13,9},{2,6},{6,2},{1... | collective-permute-start | bytes 393224 | tf_op jit(solution)/shard_map/ppermute | solution.py:122
  13.4 14.4 %copy-start.1 = (bf16[1,1,24,1024]{3,2,1,0:T(8,128)(2,1)S(1)}, bf16[1,1,24,1024]{3,2,1,0:T(8,128)(2,1)}, u32[]{:S(2)}) copy-start(bf16[1,1,24,1024]{3,2,1,0:T(8,128)(2,1)} %param.9) | copy-start | bytes 147460
  13.4 15.7 %copy-start = (bf16[1,1024,3,256]{3,1,2,0:T(8,128)(2,1)S(1)}, bf16[1,1024,3,256]{3,1,2,0:T(8,128)(2,1)}, u32[]{:S(2)}) copy-start(bf16[1,1024,3,256]{3,1,2,0:T(8,128)(2,1)} %param.10) | copy-start | bytes 4718596
  13.6 1.3 %collective-permute-start.4 = (f32[2,32,256]{2,1,0:T(8,128)S(1)}, f32[2,32,256]{2,1,0:T(8,128)S(1)}, u32[]{:S(2)}, u32[]{:S(2)}) collective-permute-start(f32[2,32,256]{2,1,0:T(8,128)S(1)} %get-tuple-element.17), channel_id=1, source_target_pairs={{0,1},{1,0},{2,3},{3,2},{4,5},{5,4},{6,7},{7,6},{8,9},{9,8},{10,11... | collective-permute-start | bytes 196616 | tf_op jit(solution)/shard_map/ppermute | solution.py:126
  16.6 3.9 %collective-permute-start.5 = (f32[32,256]{1,0:T(8,128)S(1)}, f32[32,256]{1,0:T(8,128)S(1)}, u32[]{:S(2)}, u32[]{:S(2)}) collective-permute-start(f32[32,256]{1,0:T(8,128)S(1)} %slice_bitcast_fusion.4), channel_id=1, source_target_pairs={{0,2},{1,3},{2,0},{3,1},{4,6},{5,7},{6,4},{7,5},{8,10},{9,11},{10,... | collective-permute-start | bytes 98312 | tf_op jit(solution)/shard_map/ppermute | solution.py:126
  20.5 4.6 %collective-permute-start.6 = (bf16[32,256]{1,0:T(8,128)(2,1)S(1)}, bf16[32,256]{1,0:T(8,128)(2,1)S(1)}, u32[]{:S(2)}, u32[]{:S(2)}) collective-permute-start(bf16[32,256]{1,0:T(8,128)(2,1)S(1)} %fusion.7.refs_3_), channel_id=1, source_target_pairs={{0,8},{4,12},{8,0},{12,4},{1,9},{5,13},{9,1},{13,5},{2,10},{6,14},... | collective-permute-start | bytes 49160 | tf_op jit(solution)/shard_map/ppermute | solution.py:122
  25.2 3.9 %collective-permute-start.7 = (bf16[64,256]{1,0:T(8,128)(2,1)S(1)}, bf16[64,256]{1,0:T(8,128)(2,1)S(1)}, u32[]{:S(2)}, u32[]{:S(2)}) collective-permute-start(bf16[64,256]{1,0:T(8,128)(2,1)S(1)} %pad_maximum_fusion.2), channel_id=1, source_target_pairs={{0,4},{4,0},{8,12},{12,8},{1,5},{5,1},{9,13},{13,9},{2,6},{6,2},{1... | collective-permute-start | bytes 98312 | tf_op jit(solution)/shard_map/ppermute | solution.py:122
  30.0 3.7 %collective-permute-start.8 = (f32[2,256,256]{2,1,0:T(8,128)S(1)}, f32[2,256,256]{2,1,0:T(8,128)S(1)}, u32[]{:S(2)}, u32[]{:S(2)}) collective-permute-start(f32[2,256,256]{2,1,0:T(8,128)S(1)} %get-tuple-element.20), channel_id=1, source_target_pairs={{0,1},{1,0},{2,3},{3,2},{4,5},{5,4},{6,7},{7,6},{8,9},{9,8},{10,11... | collective-permute-start | bytes 1572872 | tf_op jit(solution)/shard_map/ppermute | solution.py:126
  30.1 2.0 %collective-permute-start.10 = (f32[2,32,256]{2,1,0:T(8,128)S(1)}, f32[2,32,256]{2,1,0:T(8,128)S(1)}, u32[]{:S(2)}, u32[]{:S(2)}) collective-permute-start(f32[2,32,256]{2,1,0:T(8,128)S(1)} %get-tuple-element.22), channel_id=1, source_target_pairs={{0,1},{1,0},{2,3},{3,2},{4,5},{5,4},{6,7},{7,6},{8,9},{9,8},{10,11... | collective-permute-start | bytes 196616 | tf_op jit(solution)/shard_map/ppermute | solution.py:126
  32.1 4.0 %collective-permute-start.11 = (f32[32,256]{1,0:T(8,128)S(1)}, f32[32,256]{1,0:T(8,128)S(1)}, u32[]{:S(2)}, u32[]{:S(2)}) collective-permute-start(f32[32,256]{1,0:T(8,128)S(1)} %slice_bitcast_fusion.2), channel_id=1, source_target_pairs={{0,2},{1,3},{2,0},{3,1},{4,6},{5,7},{6,4},{7,5},{8,10},{9,11},{10,... | collective-permute-start | bytes 98312 | tf_op jit(solution)/shard_map/ppermute | solution.py:126
  33.8 5.3 %collective-permute-start.9 = (bf16[256,256]{1,0:T(8,128)(2,1)S(1)}, bf16[256,256]{1,0:T(8,128)(2,1)S(1)}, u32[]{:S(2)}, u32[]{:S(2)}) collective-permute-start(bf16[256,256]{1,0:T(8,128)(2,1)S(1)} %fusion.3), channel_id=1, source_target_pairs={{0,2},{1,3},{2,0},{3,1},{4,6},{5,7},{6,4},{7,5},{8,10},{9,11},{10,... | collective-permute-start | bytes 393224 | tf_op jit(solution)/shard_map/ppermute | solution.py:126
  36.1 4.6 %collective-permute-start.12 = (bf16[32,256]{1,0:T(8,128)(2,1)S(1)}, bf16[32,256]{1,0:T(8,128)(2,1)S(1)}, u32[]{:S(2)}, u32[]{:S(2)}) collective-permute-start(bf16[32,256]{1,0:T(8,128)(2,1)S(1)} %fusion.6.refs_6_), channel_id=1, source_target_pairs={{0,8},{4,12},{8,0},{12,4},{1,9},{5,13},{9,1},{13,5},{2,10},{6,14},... | collective-permute-start | bytes 49160 | tf_op jit(solution)/shard_map/ppermute | solution.py:122
  40.8 5.4 %collective-permute-start.13 = (bf16[320,256]{1,0:T(8,128)(2,1)S(1)}, bf16[320,256]{1,0:T(8,128)(2,1)S(1)}, u32[]{:S(2)}, u32[]{:S(2)}) collective-permute-start(bf16[320,256]{1,0:T(8,128)(2,1)S(1)} %pad_maximum_fusion), channel_id=1, source_target_pairs={{0,4},{4,0},{8,12},{12,8},{1,5},{5,1},{9,13},{13,9},{2,6},{6,2},{1... | collective-permute-start | bytes 491528 | tf_op jit(solution)/shard_map/ppermute | solution.py:122
  42.7 3.4 %collective-permute-start.14 = (bf16[256,256]{1,0:T(8,128)(2,1)S(1)}, bf16[256,256]{1,0:T(8,128)(2,1)S(1)}, u32[]{:S(2)}, u32[]{:S(2)}) collective-permute-start(bf16[256,256]{1,0:T(8,128)(2,1)S(1)} %fusion.2.refs_3_), channel_id=1, source_target_pairs={{0,0},{4,8},{8,4},{12,12},{1,1},{5,9},{9,5},{13,13},{2,2},{6,10},{... | collective-permute-start | bytes 393224 | tf_op jit(solution)/shard_map/ppermute | solution.py:122
  46.9 2.0 %collective-permute-start.15 = (f32[2,256,256]{2,1,0:T(8,128)S(1)}, f32[2,256,256]{2,1,0:T(8,128)S(1)}, u32[]{:S(2)}, u32[]{:S(2)}) collective-permute-start(f32[2,256,256]{2,1,0:T(8,128)S(1)} %get-tuple-element.24), channel_id=1, source_target_pairs={{0,1},{1,0},{2,3},{3,2},{4,5},{5,4},{6,7},{7,6},{8,9},{9,8},{10,11... | collective-permute-start | bytes 1572872 | tf_op jit(solution)/shard_map/ppermute | solution.py:126
  48.9 5.6 %collective-permute-start.16 = (bf16[256,256]{1,0:T(8,128)(2,1)S(1)}, bf16[256,256]{1,0:T(8,128)(2,1)S(1)}, u32[]{:S(2)}, u32[]{:S(2)}) collective-permute-start(bf16[256,256]{1,0:T(8,128)(2,1)S(1)} %fusion.4), channel_id=1, source_target_pairs={{0,2},{1,3},{2,0},{3,1},{4,6},{5,7},{6,4},{7,5},{8,10},{9,11},{10,... | collective-permute-start | bytes 393224 | tf_op jit(solution)/shard_map/ppermute | solution.py:126

commit v6 on v5

v6 whole, which is shorter than its diff:
```python
import functools

import jax
import jax.numpy as jnp
from jax import lax
from jax.experimental import pallas as pl
from jax.experimental.pallas import tpu as pltpu
from jax.sharding import PartitionSpec as P

BF = jnp.bfloat16
F32 = jnp.float32


def shifted(block, axis, distance):
    devices = range(lax.axis_size(axis))
    route = [(i - distance, i) for i in devices if i - distance in devices]
    return lax.ppermute(block, axis, route)


def image_part(operand, right_bases, left_bases, near_tiles, tile_ranks, column_rows, row_columns):
    tile_slots = right_bases.shape[1]
    rank_part = right_bases.shape[2]
    tile_rows = right_bases.shape[3]
    probe_count = operand.shape[1]
    tile_count = lax.axis_size("tile")
    right_flat = right_bases.reshape(tile_slots * rank_part, tile_rows)
    left_flat = left_bases.reshape(tile_slots * rank_part, tile_rows)
    dense_flat = near_tiles.reshape(tile_rows, -1)
    values = jnp.dot(
        right_flat,
        lax.all_gather(operand, "list", axis=0, tiled=True),
        preferred_element_type=F32,
    )
    rank_level = lax.axis_index("list") * rank_part + lax.iota(jnp.int32, rank_part)
    rank_mask = rank_level[None, :] < tile_ranks[0][:, None]
    coefficients = jnp.where(
        rank_mask[:, :, None], values.reshape(tile_slots, rank_part, probe_count), 0.0
    ).astype(BF)
    targets = (column_rows[0][None, :] == lax.iota(jnp.int32, tile_count)[:, None]).astype(BF)
    outgoing = jnp.einsum(
        "dk,krp->drp", targets, coefficients, preferred_element_type=F32
    ).astype(BF)
    sources = (row_columns[0][:, None] == lax.iota(jnp.int32, tile_count)[None, :]).astype(BF)
    chosen = jnp.einsum(
        "kj,jrp->krp",
        sources,
        lax.all_to_all(outgoing, "tile", split_axis=0, concat_axis=0, tiled=True),
        preferred_element_type=F32,
    ).astype(BF)
    chosen = chosen.reshape(tile_slots * rank_part, -1)
    far_sum = lax.dot_general(
        left_flat, chosen, (((0,), (0,)), ((), ())), preferred_element_type=F32
    )
    arrived = {}
    for offset in (1, -1):
        arrived[offset] = shifted(operand, "tile", offset)
    stacked = jnp.concatenate([arrived[1], operand, arrived[-1]], axis=0)
    near_sum = jnp.dot(dense_flat, stacked, preferred_element_type=F32)
    partial_image = near_sum + far_sum
    return lax.psum_scatter(partial_image, "list", scatter_dimension=0, tiled=True)


def many_slots(probes, right_bases, left_bases, near_tiles, tile_ranks, column_rows, row_columns):
    rest = (right_bases, left_bases, near_tiles, tile_ranks, column_rows, row_columns)
    first_pass = image_part(probes.astype(BF), *rest).astype(BF)
    return image_part(first_pass, *rest)


VMEM = pl.BlockSpec(memory_space=pltpu.VMEM)


def kernel_call(kernel, outs, operands, flops=0):
    return pl.pallas_call(
        kernel,
        out_shape=tuple(jax.ShapeDtypeStruct(shape, kind) for shape, kind in outs),
        in_specs=[VMEM] * len(operands),
        out_specs=tuple(VMEM for _ in outs),
        compiler_params=pltpu.CompilerParams(vmem_limit_bytes=16 * 2**20),
        cost_estimate=pl.CostEstimate(
            flops=flops, bytes_accessed=2 * operands[0].size, transcendentals=0
        ),
    )(*operands)


def stacked(pieces):
    return jnp.concatenate([piece.astype(F32) for piece in pieces]).astype(BF)


def under_rank(values, group, rank_part, ranks_ref):
    level = group * rank_part + lax.broadcasted_iota(jnp.int32, values.shape, 0)
    return jnp.where(level < ranks_ref[...], values, 0.0)


def coefficient_kernel(own_ref, across_ref, block_ref, other_ref, ranks_ref, out_ref):
    me = lax.axis_index("list")
    ranks = own_ref.shape[0]
    rows = block_ref.shape[0]
    total = 0.0
    for part, operand_ref in ((me, block_ref), (me ^ 1, other_ref)):
        cut = pl.ds(pl.multiple_of(part * rows, rows), rows)
        bases = stacked([own_ref[:, cut], across_ref[:, cut]])
        total += jnp.dot(bases, operand_ref[...], preferred_element_type=F32)
    halves = [
        under_rank(total[index * ranks : (index + 1) * ranks], group, ranks, ranks_ref)
        for index, group in enumerate((me, me ^ 2))
    ]
    out_ref[...] = jnp.concatenate(halves).astype(out_ref.dtype)


def tile_swap(block, turn):
    count = lax.axis_size("tile")
    route = [(i, i ^ turn) for i in range(count)]
    if turn == 0:
        route = [(i, min(max(i - 1 + 2 * (i % 2), 0), count - 1)) for i in range(count)]
    return lax.ppermute(block, "tile", route)


def list_swap(block, bit):
    return lax.ppermute(block, "list", [(i, i ^ bit) for i in range(lax.axis_size("list"))])


def image_kernel(near_ref, left_ref, across_ref, columns_ref, *refs):
    block_refs, coefficient_refs, (keep_ref, send_ref) = refs[:3], refs[3:7], refs[7:]
    count = lax.axis_size("tile")
    tile = lax.axis_index("tile")
    me = lax.axis_index("list")
    rows = near_ref.shape[2]
    chosen = coefficient_refs[0][...]
    for turn in (1, 2, 3):
        listed = columns_ref[...] == tile ^ turn
        chosen = jnp.where(listed, coefficient_refs[turn][...], chosen)
    odd = lax.rem(tile, 2)
    inside = (tile > 0) & (tile < count - 1)
    blocks = [
        (1, block_refs[0][...]),
        (2 - 2 * odd, block_refs[1][...]),
        (2 * odd, jnp.where(inside, block_refs[2][...], 0)),
    ]
    totals = []
    for turn in (1, 3, 0, 2):
        part = me ^ turn
        cut = pl.ds(pl.multiple_of(part * rows, rows), rows)
        left = stacked([left_ref[:, cut], across_ref[:, cut]])
        total = lax.dot_general(
            left, chosen, (((0,), (0,)), ((), ())), preferred_element_type=F32
        )
        for side, block in blocks:
            total += jnp.dot(near_ref[side, cut, :], block, preferred_element_type=F32)
        out_ref = send_ref if turn % 2 else keep_ref
        out_ref[turn // 2, :rows, :] = total
        totals.append((cut, total.astype(BF)))
    return totals


def first_kernel(near_ref, left_ref, across_ref, columns_ref, ranks_ref, even_ref, odd_ref, *refs):
    totals = image_kernel(near_ref, left_ref, across_ref, columns_ref, *refs)
    keep_ref, send_ref = refs[7:]
    me = lax.axis_index("list")
    ranks = even_ref.shape[1]
    rows = near_ref.shape[2]
    sums = 0.0
    for cut, total in totals:
        bases = stacked([ref[index, :, cut] for ref in (even_ref, odd_ref) for index in range(2)])
        sums += jnp.dot(bases, total, preferred_element_type=F32)
    for index, turn in enumerate((0, 2, 1, 3)):
        values = sums[index * ranks : (index + 1) * ranks]
        out_ref = send_ref if turn % 2 else keep_ref
        out_ref[turn // 2, rows:, :] = under_rank(values, me ^ turn, ranks, ranks_ref)


def second_kernel(*refs):
    image_kernel(*refs)


def tile_swaps(own):
    return [own] + [tile_swap(own, turn) for turn in (1, 2, 3)]


def one_slot(probes, right_bases, left_bases, near_tiles, tile_ranks, column_rows, row_columns):
    rows, probe_count = probes.shape
    rank_part = right_bases.shape[2]
    near = near_tiles[0].transpose(1, 0, 2)
    flops = 2 * near.size * probe_count
    right, left = right_bases[0, 0], left_bases[0, 0]
    right_across = list_swap(right, 2)
    block = probes.astype(BF)
    beside = [block, tile_swap(block, 1), tile_swap(block, 0)]
    (own,) = kernel_call(
        coefficient_kernel,
        [((2 * rank_part, probe_count), BF)],
        (right, right_across, block, list_swap(block, 1), tile_ranks),
        8 * flops,
    )
    coefficients = tile_swaps(own)
    right = jnp.stack([right, right_across])
    bases = (near, left, list_swap(left, 2), row_columns)
    keep, send = kernel_call(
        first_kernel,
        [((2, rows + rank_part, probe_count), F32)] * 2,
        (*bases, tile_ranks, right, list_swap(right, 1), *beside, *coefficients),
        flops,
    )
    pair = keep + list_swap(send, 1)
    coefficients = tile_swaps(pair[:, rows:].reshape(-1, probe_count).astype(BF))
    block = (pair[0, :rows] + list_swap(pair[1, :rows].astype(BF), 2)).astype(BF)
    block, *coefficients[2:] = lax.optimization_barrier((block, *coefficients[2:]))
    beside = [block, tile_swap(block, 1), tile_swap(block, 0)]
    keep, send = kernel_call(
        second_kernel,
        [((2, rows, probe_count), F32)] * 2,
        (*bases, *beside, *coefficients),
        flops,
    )
    pair = keep + list_swap(send, 1)
    return pair[0] + list_swap(pair[1].astype(BF), 2)


def local(probes, right_bases, left_bases, near_tiles, tile_ranks, column_rows, row_columns):
    few = lax.axis_size("tile") == 4 and lax.axis_size("list") == 4
    small = right_bases.shape[1] == 1 and few
    form = one_slot if small else many_slots
    return form(
        probes, right_bases, left_bases, near_tiles, tile_ranks, column_rows, row_columns
    )


def solution(mesh):
    placed = (
        P(("group", "tile", "list"), None),
        P(("group", "tile"), None, "list", None),
        P(("group", "tile"), None, "list", None),
        P(("group", "tile"), None, None, "list"),
        P(("group", "tile"), None),
        P("tile", None),
        P("tile", None),
    )
    return jax.shard_map(
        local,
        mesh=mesh,
        in_specs=placed,
        out_specs=P(("group", "tile", "list"), None),
        check_vma=False,
    )
```

time: 56.3 us -> 47.3 us (0.84); the launches traced: 55.3 us -> 47.1 us
  waiting for transfers between devices: 26.6 us -> 17.7 us
  local copies, waits for them, and re-layouts: 0.07 us -> 0.93 us
    ppermute x10 -> x8, waiting for transfers between devices: 16.2 us -> 9.82 us  [list_swap(): lax.ppermute(block, 'list', [(i, i ^ bit) for i in range(lax.axis_size('l...]
    ppermute x10 -> x8, starting transfers between devices: 9.2 us -> 5.91 us  [list_swap(): lax.ppermute(block, 'list', [(i, i ^ bit) for i in range(lax.axis_size('l...]
    ppermute x7 -> x10, starting transfers between devices: 13.5 us -> 16.5 us  [tile_swap(): return lax.ppermute(block, 'tile', route)]
    ppermute x7 -> x10, waiting for transfers between devices: 10.4 us -> 7.9 us  [tile_swap(): return lax.ppermute(block, 'tile', route)]
    unnamed x4 -> x6, local copies, waits for them, and re-layouts: 0.01 us -> 0.9 us
  transfers between devices with their start and end apart: 17 -> 18, of which waited for: 13 -> 10; matrix products, arithmetic and copies ran while one was open for 2% -> 4% of each run, Pallas kernels for 0% -> 0%
where the time goes in v6:
time: 47.3 us; the launch traced here: 47.1 us
  starting transfers between devices  22.4 us (47%)
  waiting for transfers between devices  17.7 us (37%)
  other arithmetic  2.68 us (6%)
  Pallas kernels  1.85 us (4%)
  between operations  1.47 us (3%)
  local copies, waits for them, and re-layouts  0.93 us (2%)
    ppermute x10, starting transfers between devices, tile_swap(): return lax.ppermute(block, 'tile', route)  16.5 us
    ppermute x8, waiting for transfers between devices, list_swap(): lax.ppermute(block, 'list', [(i, i ^ bit) for i in range(lax.axis_size('l...  9.82 us
    ppermute x10, waiting for transfers between devices, tile_swap(): return lax.ppermute(block, 'tile', route)  7.9 us
    ppermute x8, starting transfers between devices, list_swap(): lax.ppermute(block, 'list', [(i, i ^ bit) for i in range(lax.axis_size('l...  5.91 us
    pallas_call x3, Pallas kernels, kernel_call(): pl.pallas_call(kernel, out_shape=tuple((jax.ShapeDtypeStruct(shape, kind)...  1.85 us
    convert_element_type x1, other arithmetic, one_slot(): block = probes.astype(BF)  0.96 us
  transfers between devices with their start and end apart: 18, of which 10 were waited for; matrix products, arithmetic and copies ran while one was open for 4% of the time, Pallas kernels for 0%

profile of v6, /device:TPU:0, one launch (start us, length us, event | category | flops | bytes accessed | tf_op | source)
XLA Modules:
  0.0 47.1 jit_solution(18186970248855015044)
XLA Ops:
  0.0 2.9 %collective-permute-start.1 = (bf16[24,1024]{1,0:T(8,128)(2,1)}, bf16[24,1024]{1,0:T(8,128)(2,1)S(1)}, u32[]{:S(2)}, u32[]{:S(2)}) collective-permute-start(bf16[24,1024]{1,0:T(8,128)(2,1)} %bitcast.31), channel_id=1, source_target_pairs={{0,2},{1,3},{2,0},{3,1},{4,6},{5,7},{6,4},{7,5},{8,10},{9,11},{10,... | collective-permute-start | bytes 147464 | tf_op jit(solution)/shard_map/ppermute | solution.py:119
  2.9 1.0 %convert_element_type.23.block_ref.refs_0_ = bf16[256,256]{1,0:T(8,128)(2,1)S(1)} convert(f32[256,256]{1,0:T(8,128)} %param.7) | non-fusion elementwise | flops 65536 | bytes 393216 | tf_op jit(solution)/shard_map/convert_element_type | solution.py:186
  4.0 0.7 %collective-permute-start.4 = (bf16[256,256]{1,0:T(8,128)(2,1)S(1)}, bf16[256,256]{1,0:T(8,128)(2,1)S(1)}, u32[]{:S(2)}, u32[]{:S(2)}) collective-permute-start(bf16[256,256]{1,0:T(8,128)(2,1)S(1)} %convert_element_type.23.block_ref.refs_0_), channel_id=1, source_target_pairs={{0,0},{4,8},{8,4},{12,12},{1,1},{5,9},{9,5},{13,13},{2,2},{6,10},{... | collective-permute-start | bytes 393224 | tf_op jit(solution)/shard_map/ppermute | solution.py:115
  4.7 4.5 %collective-permute-start.3 = (bf16[256,256]{1,0:T(8,128)(2,1)S(1)}, bf16[256,256]{1,0:T(8,128)(2,1)S(1)}, u32[]{:S(2)}, u32[]{:S(2)}) collective-permute-start(bf16[256,256]{1,0:T(8,128)(2,1)S(1)} %convert_element_type.23.block_ref.refs_0_), channel_id=1, source_target_pairs={{0,4},{4,0},{8,12},{12,8},{1,5},{5,1},{9,13},{13,9},{2,6},{6,2},{1... | collective-permute-start | bytes 393224 | tf_op jit(solution)/shard_map/ppermute | solution.py:115
  10.3 0.8 %pad_maximum_fusion.even_ref = bf16[2,24,1024]{2,1,0:T(8,128)(2,1)S(1)} fusion(bf16[1,24,1024]{2,1,0:T(8,128)(2,1)S(1)} %bitcast.34, bf16[1,24,1024]{2,1,0:T(8,128)(2,1)} %bitcast.32), kind=kLoop, calls=%fused_computation.8 | loop fusion | flops 49152 | bytes 196608 | tf_op jit(solution)/shard_map/stack | solution.py:195
  11.3 0.9 %copy-done.2 = bf16[1,1,24,1024]{3,2,1,0:T(8,128)(2,1)S(1)} copy-done((bf16[1,1,24,1024]{3,2,1,0:T(8,128)(2,1)S(1)}, bf16[1,1,24,1024]{3,2,1,0:T(8,128)(2,1)}, u32[]{:S(2)}) %copy-start.2) | copy-done | bytes 49176
  12.3 1.4 %collective-permute-start.8 = (bf16[48,256]{1,0:T(8,128)(2,1)S(1)}, bf16[48,256]{1,0:T(8,128)(2,1)S(1)}, u32[]{:S(2)}, u32[]{:S(2)}) collective-permute-start(bf16[48,256]{1,0:T(8,128)(2,1)S(1)} %shard_map.64.refs_3_), channel_id=1, source_target_pairs={{0,12},{4,8},{8,4},{12,0},{1,13},{5,9},{9,5},{13,1},{2,14},{6,10},... | collective-permute-start | bytes 73736 | tf_op jit(solution)/shard_map/ppermute | solution.py:115
  14.0 2.8 %collective-permute-start.6 = (bf16[48,256]{1,0:T(8,128)(2,1)S(1)}, bf16[48,256]{1,0:T(8,128)(2,1)S(1)}, u32[]{:S(2)}, u32[]{:S(2)}) collective-permute-start(bf16[48,256]{1,0:T(8,128)(2,1)S(1)} %shard_map.64.refs_3_), channel_id=1, source_target_pairs={{0,4},{4,0},{8,12},{12,8},{1,5},{5,1},{9,13},{13,9},{2,6},{6,2},{1... | collective-permute-start | bytes 73736 | tf_op jit(solution)/shard_map/ppermute | solution.py:115
  18.1 0.7 %collective-permute-done.7.refs_5_ = bf16[48,256]{1,0:T(8,128)(2,1)S(1)} collective-permute-done((bf16[48,256]{1,0:T(8,128)(2,1)S(1)}, bf16[48,256]{1,0:T(8,128)(2,1)S(1)}, u32[]{:S(2)}, u32[]{:S(2)}) %collective-permute-start.7) | collective-permute-done | bytes 24608 | tf_op jit(solution)/shard_map/ppermute | solution.py:115
  19.0 1.0 %shard_map.65 = (f32[2,280,256]{2,1,0:T(8,128)S(1)}, f32[2,280,256]{2,1,0:T(8,128)S(1)}) custom-call(bf16[3,1024,256]{2,1,0:T(8,128)(2,1)S(1)} %bitcast.22, bf16[24,1024]{1,0:T(8,128)(2,1)S(1)} %bitcast.25, bf16[24,1024]{1,0:T(8,128)(2,1)S(1)} %collective-permute-done.across_ref.refs_2_, s32[1,1]{1,0:T(1,128)S(6)} %copy.8.columns_ref.refs_3_, ...), custom_call_target="tpu_custom_call" | custom-call | flops 402653184 | bytes 1572864 | tf_op jit(solution)/shard_map/pallas_call | solution.py:73
  20.1 2.0 %collective-permute-done.9 = f32[2,280,256]{2,1,0:T(8,128)S(1)} collective-permute-done((f32[2,280,256]{2,1,0:T(8,128)S(1)}, f32[2,280,256]{2,1,0:T(8,128)S(1)}, u32[]{:S(2)}, u32[]{:S(2)}) %collective-permute-start.9) | collective-permute-done | bytes 573472 | tf_op jit(solution)/shard_map/ppermute | solution.py:119
  22.1 1.6 %collective-permute-start.10 = (bf16[256,256]{1,0:T(8,128)(2,1)S(1)}, bf16[256,256]{1,0:T(8,128)(2,1)S(1)}, u32[]{:S(2)}, u32[]{:S(2)}) collective-permute-start(bf16[256,256]{1,0:T(8,128)(2,1)S(1)} %slice_bitcast_fusion.2), channel_id=1, source_target_pairs={{0,2},{1,3},{2,0},{3,1},{4,6},{5,7},{6,4},{7,5},{8,10},{9,11},{10,... | collective-permute-start | bytes 393224 | tf_op jit(solution)/shard_map/ppermute | solution.py:119
  23.7 2.0 %collective-permute-start.12 = (bf16[48,256]{1,0:T(8,128)(2,1)S(1)}, bf16[48,256]{1,0:T(8,128)(2,1)S(1)}, u32[]{:S(2)}, u32[]{:S(2)}) collective-permute-start(bf16[48,256]{1,0:T(8,128)(2,1)S(1)} %bitcast.27), channel_id=1, source_target_pairs={{0,12},{4,8},{8,4},{12,0},{1,13},{5,9},{9,5},{13,1},{2,14},{6,10},... | collective-permute-start | bytes 73736 | tf_op jit(solution)/shard_map/ppermute | solution.py:115
  25.7 1.1 %collective-permute-start.11 = (bf16[48,256]{1,0:T(8,128)(2,1)S(1)}, bf16[48,256]{1,0:T(8,128)(2,1)S(1)}, u32[]{:S(2)}, u32[]{:S(2)}) collective-permute-start(bf16[48,256]{1,0:T(8,128)(2,1)S(1)} %bitcast.28), channel_id=1, source_target_pairs={{0,8},{4,12},{8,0},{12,4},{1,9},{5,13},{9,1},{13,5},{2,10},{6,14},... | collective-permute-start | bytes 73736 | tf_op jit(solution)/shard_map/ppermute | solution.py:115
  26.8 1.0 %collective-permute-done.10 = bf16[256,256]{1,0:T(8,128)(2,1)S(1)} collective-permute-done((bf16[256,256]{1,0:T(8,128)(2,1)S(1)}, bf16[256,256]{1,0:T(8,128)(2,1)S(1)}, u32[]{:S(2)}, u32[]{:S(2)}) %collective-permute-start.10) | collective-permute-done | bytes 131104 | tf_op jit(solution)/shard_map/ppermute | solution.py:119
  27.8 1.6 %collective-permute-done.12.refs_10_ = bf16[48,256]{1,0:T(8,128)(2,1)S(1)} collective-permute-done((bf16[48,256]{1,0:T(8,128)(2,1)S(1)}, bf16[48,256]{1,0:T(8,128)(2,1)S(1)}, u32[]{:S(2)}, u32[]{:S(2)}) %collective-permute-start.12) | collective-permute-done | bytes 24608 | tf_op jit(solution)/shard_map/ppermute | solution.py:115
  29.3 1.1 %collective-permute-done.11.refs_9_ = bf16[48,256]{1,0:T(8,128)(2,1)S(1)} collective-permute-done((bf16[48,256]{1,0:T(8,128)(2,1)S(1)}, bf16[48,256]{1,0:T(8,128)(2,1)S(1)}, u32[]{:S(2)}, u32[]{:S(2)}) %collective-permute-start.11) | collective-permute-done | bytes 24608 | tf_op jit(solution)/shard_map/ppermute | solution.py:115
  30.4 0.7 %collective-permute-start.14 = (bf16[256,256]{1,0:T(8,128)(2,1)S(1)}, bf16[256,256]{1,0:T(8,128)(2,1)S(1)}, u32[]{:S(2)}, u32[]{:S(2)}) collective-permute-start(bf16[256,256]{1,0:T(8,128)(2,1)S(1)} %fusion.2.refs_4_), channel_id=1, source_target_pairs={{0,0},{4,8},{8,4},{12,12},{1,1},{5,9},{9,5},{13,13},{2,2},{6,10},{... | collective-permute-start | bytes 393224 | tf_op jit(solution)/shard_map/ppermute | solution.py:115
  31.1 3.1 %collective-permute-start.13 = (bf16[256,256]{1,0:T(8,128)(2,1)S(1)}, bf16[256,256]{1,0:T(8,128)(2,1)S(1)}, u32[]{:S(2)}, u32[]{:S(2)}) collective-permute-start(bf16[256,256]{1,0:T(8,128)(2,1)S(1)} %fusion.2.refs_4_), channel_id=1, source_target_pairs={{0,4},{4,0},{8,12},{12,8},{1,5},{5,1},{9,13},{13,9},{2,6},{6,2},{1... | collective-permute-start | bytes 393224 | tf_op jit(solution)/shard_map/ppermute | solution.py:115
  34.2 3.7 %collective-permute-done.15.refs_8_ = bf16[48,256]{1,0:T(8,128)(2,1)S(1)} collective-permute-done((bf16[48,256]{1,0:T(8,128)(2,1)S(1)}, bf16[48,256]{1,0:T(8,128)(2,1)S(1)}, u32[]{:S(2)}, u32[]{:S(2)}) %collective-permute-start.15) | collective-permute-done | bytes 24608 | tf_op jit(solution)/shard_map/ppermute | solution.py:115
  38.0 0.7 %shard_map.66 = (f32[2,256,256]{2,1,0:T(8,128)S(1)}, f32[2,256,256]{2,1,0:T(8,128)S(1)}) custom-call(bf16[3,1024,256]{2,1,0:T(8,128)(2,1)S(1)} %bitcast.23, bf16[24,1024]{1,0:T(8,128)(2,1)S(1)} %bitcast.26, bf16[24,1024]{1,0:T(8,128)(2,1)S(1)} %collective-permute-done.across_ref.refs_2_, s32[1,1]{1,0:T(1,128)S(6)} %copy.8.columns_ref.refs_3_, ...), custom_call_target="tpu_custom_call" | custom-call | flops 402653184 | bytes 1572864 | tf_op jit(solution)/shard_map/pallas_call | solution.py:73
  38.8 1.9 %collective-permute-done.16 = f32[2,256,256]{2,1,0:T(8,128)S(1)} collective-permute-done((f32[2,256,256]{2,1,0:T(8,128)S(1)}, f32[2,256,256]{2,1,0:T(8,128)S(1)}, u32[]{:S(2)}, u32[]{:S(2)}) %collective-permute-start.16) | collective-permute-done | bytes 524320 | tf_op jit(solution)/shard_map/ppermute | solution.py:119
  41.4 5.0 %collective-permute-done.17 = bf16[256,256]{1,0:T(8,128)(2,1)S(1)} collective-permute-done((bf16[256,256]{1,0:T(8,128)(2,1)S(1)}, bf16[256,256]{1,0:T(8,128)(2,1)S(1)}, u32[]{:S(2)}, u32[]{:S(2)}) %collective-permute-start.17) | collective-permute-done | bytes 131104 | tf_op jit(solution)/shard_map/ppermute | solution.py:119
  46.4 0.7 %fusion = f32[256,256]{1,0:T(8,128)} fusion(f32[2,256,256]{2,1,0:T(8,128)S(1)} %add.14, bf16[256,256]{1,0:T(8,128)(2,1)S(1)} %collective-permute-done.17), kind=kLoop, calls=%fused_computation.2 | loop fusion | flops 131072 | bytes 655360 | tf_op jit(solution)/shard_map/add | solution.py:215
  (30 shorter events, 2.9 us)
Async XLA Ops:
  0.0 10.3 %collective-permute-start.1 = (bf16[24,1024]{1,0:T(8,128)(2,1)}, bf16[24,1024]{1,0:T(8,128)(2,1)S(1)}, u32[]{:S(2)}, u32[]{:S(2)}) collective-permute-start(bf16[24,1024]{1,0:T(8,128)(2,1)} %bitcast.31), channel_id=1, source_target_pairs={{0,2},{1,3},{2,0},{3,1},{4,6},{5,7},{6,4},{7,5},{8,10},{9,11},{10,... | collective-permute-start | bytes 147464 | tf_op jit(solution)/shard_map/ppermute | solution.py:119
  3.9 7.3 %collective-permute-start.5 = (bf16[256,256]{1,0:T(8,128)(2,1)S(1)}, bf16[256,256]{1,0:T(8,128)(2,1)S(1)}, u32[]{:S(2)}, u32[]{:S(2)}) collective-permute-start(bf16[256,256]{1,0:T(8,128)(2,1)S(1)} %convert_element_type.23.block_ref.refs_0_), channel_id=1, source_target_pairs={{0,1},{1,0},{2,3},{3,2},{4,5},{5,4},{6,7},{7,6},{8,9},{9,8},{10,11... | collective-permute-start | bytes 393224 | tf_op jit(solution)/shard_map/ppermute | solution.py:119
  4.0 10.0 %collective-permute-start.4 = (bf16[256,256]{1,0:T(8,128)(2,1)S(1)}, bf16[256,256]{1,0:T(8,128)(2,1)S(1)}, u32[]{:S(2)}, u32[]{:S(2)}) collective-permute-start(bf16[256,256]{1,0:T(8,128)(2,1)S(1)} %convert_element_type.23.block_ref.refs_0_), channel_id=1, source_target_pairs={{0,0},{4,8},{8,4},{12,12},{1,1},{5,9},{9,5},{13,13},{2,2},{6,10},{... | collective-permute-start | bytes 393224 | tf_op jit(solution)/shard_map/ppermute | solution.py:115
  4.7 12.8 %collective-permute-start.3 = (bf16[256,256]{1,0:T(8,128)(2,1)S(1)}, bf16[256,256]{1,0:T(8,128)(2,1)S(1)}, u32[]{:S(2)}, u32[]{:S(2)}) collective-permute-start(bf16[256,256]{1,0:T(8,128)(2,1)S(1)} %convert_element_type.23.block_ref.refs_0_), channel_id=1, source_target_pairs={{0,4},{4,0},{8,12},{12,8},{1,5},{5,1},{9,13},{13,9},{2,6},{6,2},{1... | collective-permute-start | bytes 393224 | tf_op jit(solution)/shard_map/ppermute | solution.py:115
  9.1 4.6 %collective-permute-start = (bf16[24,1024]{1,0:T(8,128)(2,1)}, bf16[24,1024]{1,0:T(8,128)(2,1)S(1)}, u32[]{:S(2)}, u32[]{:S(2)}) collective-permute-start(bf16[24,1024]{1,0:T(8,128)(2,1)} %bitcast.24), channel_id=1, source_target_pairs={{0,2},{1,3},{2,0},{3,1},{4,6},{5,7},{6,4},{7,5},{8,10},{9,11},{10,... | collective-permute-start | bytes 147464 | tf_op jit(solution)/shard_map/ppermute | solution.py:119
  11.1 7.9 %copy-start = (bf16[1,1024,3,256]{3,1,2,0:T(8,128)(2,1)S(1)}, bf16[1,1024,3,256]{3,1,2,0:T(8,128)(2,1)}, u32[]{:S(2)}) copy-start(bf16[1,1024,3,256]{3,1,2,0:T(8,128)(2,1)} %param.10) | copy-start | bytes 4718596
  11.1 7.9 %copy-start.1 = (bf16[1,1,24,1024]{3,2,1,0:T(8,128)(2,1)S(1)}, bf16[1,1,24,1024]{3,2,1,0:T(8,128)(2,1)}, u32[]{:S(2)}) copy-start(bf16[1,1,24,1024]{3,2,1,0:T(8,128)(2,1)} %param.9) | copy-start | bytes 147460
  11.2 6.3 %collective-permute-start.2 = (bf16[2,24,1024]{2,1,0:T(8,128)(2,1)S(1)}, bf16[2,24,1024]{2,1,0:T(8,128)(2,1)S(1)}, u32[]{:S(2)}, u32[]{:S(2)}) collective-permute-start(bf16[2,24,1024]{2,1,0:T(8,128)(2,1)S(1)} %pad_maximum_fusion.even_ref), channel_id=1, source_target_pairs={{0,1},{1,0},{2,3},{3,2},{4,5},{5,4},{6,7},{7,6},{8,9},{9,8},{10,11... | collective-permute-start | bytes 294920 | tf_op jit(solution)/shard_map/ppermute | solution.py:119
  11.2 0.9 %copy-start.2 = (bf16[1,1,24,1024]{3,2,1,0:T(8,128)(2,1)S(1)}, bf16[1,1,24,1024]{3,2,1,0:T(8,128)(2,1)}, u32[]{:S(2)}) copy-start(bf16[1,1,24,1024]{3,2,1,0:T(8,128)(2,1)} %param.8) | copy-start | bytes 147460
  12.3 5.8 %collective-permute-start.8 = (bf16[48,256]{1,0:T(8,128)(2,1)S(1)}, bf16[48,256]{1,0:T(8,128)(2,1)S(1)}, u32[]{:S(2)}, u32[]{:S(2)}) collective-permute-start(bf16[48,256]{1,0:T(8,128)(2,1)S(1)} %shard_map.64.refs_3_), channel_id=1, source_target_pairs={{0,12},{4,8},{8,4},{12,0},{1,13},{5,9},{9,5},{13,1},{2,14},{6,10},... | collective-permute-start | bytes 73736 | tf_op jit(solution)/shard_map/ppermute | solution.py:115
  13.8 5.0 %collective-permute-start.7 = (bf16[48,256]{1,0:T(8,128)(2,1)S(1)}, bf16[48,256]{1,0:T(8,128)(2,1)S(1)}, u32[]{:S(2)}, u32[]{:S(2)}) collective-permute-start(bf16[48,256]{1,0:T(8,128)(2,1)S(1)} %shard_map.64.refs_3_), channel_id=1, source_target_pairs={{0,8},{4,12},{8,0},{12,4},{1,9},{5,13},{9,1},{13,5},{2,10},{6,14},... | collective-permute-start | bytes 73736 | tf_op jit(solution)/shard_map/ppermute | solution.py:115
  14.0 5.0 %collective-permute-start.6 = (bf16[48,256]{1,0:T(8,128)(2,1)S(1)}, bf16[48,256]{1,0:T(8,128)(2,1)S(1)}, u32[]{:S(2)}, u32[]{:S(2)}) collective-permute-start(bf16[48,256]{1,0:T(8,128)(2,1)S(1)} %shard_map.64.refs_3_), channel_id=1, source_target_pairs={{0,4},{4,0},{8,12},{12,8},{1,5},{5,1},{9,13},{13,9},{2,6},{6,2},{1... | collective-permute-start | bytes 73736 | tf_op jit(solution)/shard_map/ppermute | solution.py:115
  20.0 2.0 %collective-permute-start.9 = (f32[2,280,256]{2,1,0:T(8,128)S(1)}, f32[2,280,256]{2,1,0:T(8,128)S(1)}, u32[]{:S(2)}, u32[]{:S(2)}) collective-permute-start(f32[2,280,256]{2,1,0:T(8,128)S(1)} %get-tuple-element.13), channel_id=1, source_target_pairs={{0,1},{1,0},{2,3},{3,2},{4,5},{5,4},{6,7},{7,6},{8,9},{9,8},{10,11... | collective-permute-start | bytes 1720328 | tf_op jit(solution)/shard_map/ppermute | solution.py:119
  22.1 5.6 %collective-permute-start.10 = (bf16[256,256]{1,0:T(8,128)(2,1)S(1)}, bf16[256,256]{1,0:T(8,128)(2,1)S(1)}, u32[]{:S(2)}, u32[]{:S(2)}) collective-permute-start(bf16[256,256]{1,0:T(8,128)(2,1)S(1)} %slice_bitcast_fusion.2), channel_id=1, source_target_pairs={{0,2},{1,3},{2,0},{3,1},{4,6},{5,7},{6,4},{7,5},{8,10},{9,11},{10,... | collective-permute-start | bytes 393224 | tf_op jit(solution)/shard_map/ppermute | solution.py:119
  23.7 5.6 %collective-permute-start.12 = (bf16[48,256]{1,0:T(8,128)(2,1)S(1)}, bf16[48,256]{1,0:T(8,128)(2,1)S(1)}, u32[]{:S(2)}, u32[]{:S(2)}) collective-permute-start(bf16[48,256]{1,0:T(8,128)(2,1)S(1)} %bitcast.27), channel_id=1, source_target_pairs={{0,12},{4,8},{8,4},{12,0},{1,13},{5,9},{9,5},{13,1},{2,14},{6,10},... | collective-permute-start | bytes 73736 | tf_op jit(solution)/shard_map/ppermute | solution.py:115
  25.7 4.7 %collective-permute-start.11 = (bf16[48,256]{1,0:T(8,128)(2,1)S(1)}, bf16[48,256]{1,0:T(8,128)(2,1)S(1)}, u32[]{:S(2)}, u32[]{:S(2)}) collective-permute-start(bf16[48,256]{1,0:T(8,128)(2,1)S(1)} %bitcast.28), channel_id=1, source_target_pairs={{0,8},{4,12},{8,0},{12,4},{1,9},{5,13},{9,1},{13,5},{2,10},{6,14},... | collective-permute-start | bytes 73736 | tf_op jit(solution)/shard_map/ppermute | solution.py:115
  30.4 7.6 %collective-permute-start.14 = (bf16[256,256]{1,0:T(8,128)(2,1)S(1)}, bf16[256,256]{1,0:T(8,128)(2,1)S(1)}, u32[]{:S(2)}, u32[]{:S(2)}) collective-permute-start(bf16[256,256]{1,0:T(8,128)(2,1)S(1)} %fusion.2.refs_4_), channel_id=1, source_target_pairs={{0,0},{4,8},{8,4},{12,12},{1,1},{5,9},{9,5},{13,13},{2,2},{6,10},{... | collective-permute-start | bytes 393224 | tf_op jit(solution)/shard_map/ppermute | solution.py:115
  31.1 6.9 %collective-permute-start.13 = (bf16[256,256]{1,0:T(8,128)(2,1)S(1)}, bf16[256,256]{1,0:T(8,128)(2,1)S(1)}, u32[]{:S(2)}, u32[]{:S(2)}) collective-permute-start(bf16[256,256]{1,0:T(8,128)(2,1)S(1)} %fusion.2.refs_4_), channel_id=1, source_target_pairs={{0,4},{4,0},{8,12},{12,8},{1,5},{5,1},{9,13},{13,9},{2,6},{6,2},{1... | collective-permute-start | bytes 393224 | tf_op jit(solution)/shard_map/ppermute | solution.py:115
  34.1 3.8 %collective-permute-start.15 = (bf16[48,256]{1,0:T(8,128)(2,1)S(1)}, bf16[48,256]{1,0:T(8,128)(2,1)S(1)}, u32[]{:S(2)}, u32[]{:S(2)}) collective-permute-start(bf16[48,256]{1,0:T(8,128)(2,1)S(1)} %bitcast.29), channel_id=1, source_target_pairs={{0,4},{4,0},{8,12},{12,8},{1,5},{5,1},{9,13},{13,9},{2,6},{6,2},{1... | collective-permute-start | bytes 73736 | tf_op jit(solution)/shard_map/ppermute | solution.py:115
  38.7 2.0 %collective-permute-start.16 = (f32[2,256,256]{2,1,0:T(8,128)S(1)}, f32[2,256,256]{2,1,0:T(8,128)S(1)}, u32[]{:S(2)}, u32[]{:S(2)}) collective-permute-start(f32[2,256,256]{2,1,0:T(8,128)S(1)} %get-tuple-element.18), channel_id=1, source_target_pairs={{0,1},{1,0},{2,3},{3,2},{4,5},{5,4},{6,7},{7,6},{8,9},{9,8},{10,11... | collective-permute-start | bytes 1572872 | tf_op jit(solution)/shard_map/ppermute | solution.py:119
  40.8 5.6 %collective-permute-start.17 = (bf16[256,256]{1,0:T(8,128)(2,1)S(1)}, bf16[256,256]{1,0:T(8,128)(2,1)S(1)}, u32[]{:S(2)}, u32[]{:S(2)}) collective-permute-start(bf16[256,256]{1,0:T(8,128)(2,1)S(1)} %fusion.3), channel_id=1, source_target_pairs={{0,2},{1,3},{2,0},{3,1},{4,6},{5,7},{6,4},{7,5},{8,10},{9,11},{10,... | collective-permute-start | bytes 393224 | tf_op jit(solution)/shard_map/ppermute | solution.py:119

commit v7 on v6

--- a/solution.py
+++ b/solution.py
@@ -91,14 +91,14 @@
     return jnp.where(level < ranks_ref[...], values, 0.0)
 
 
-def coefficient_kernel(own_ref, across_ref, block_ref, other_ref, ranks_ref, out_ref):
+def coefficient_kernel(bases_ref, across_ref, block_ref, other_ref, ranks_ref, out_ref):
     me = lax.axis_index("list")
-    ranks = own_ref.shape[0]
+    ranks = bases_ref.shape[1]
     rows = block_ref.shape[0]
     total = 0.0
     for part, operand_ref in ((me, block_ref), (me ^ 1, other_ref)):
         cut = pl.ds(pl.multiple_of(part * rows, rows), rows)
-        bases = stacked([own_ref[:, cut], across_ref[:, cut]])
+        bases = stacked([bases_ref[0, :, cut], across_ref[0, :, cut]])
         total += jnp.dot(bases, operand_ref[...], preferred_element_type=F32)
     halves = [
         under_rank(total[index * ranks : (index + 1) * ranks], group, ranks, ranks_ref)
@@ -119,8 +119,8 @@
     return lax.ppermute(block, "list", [(i, i ^ bit) for i in range(lax.axis_size("list"))])
 
 
-def image_kernel(near_ref, left_ref, across_ref, columns_ref, *refs):
-    block_refs, coefficient_refs, (keep_ref, send_ref) = refs[:3], refs[3:7], refs[7:]
+def image_kernel(turns, near_ref, bases_ref, across_ref, columns_ref, *refs):
+    block_refs, coefficient_refs, out_ref = refs[:3], refs[3:7], refs[7]
     count = lax.axis_size("tile")
     tile = lax.axis_index("tile")
     me = lax.axis_index("list")
@@ -137,43 +137,54 @@
         (2 * odd, jnp.where(inside, block_refs[2][...], 0)),
     ]
     totals = []
-    for turn in (1, 3, 0, 2):
+    for index, turn in enumerate(turns):
         part = me ^ turn
         cut = pl.ds(pl.multiple_of(part * rows, rows), rows)
-        left = stacked([left_ref[:, cut], across_ref[:, cut]])
+        left = stacked([bases_ref[1, :, cut], across_ref[1, :, cut]])
         total = lax.dot_general(
             left, chosen, (((0,), (0,)), ((), ())), preferred_element_type=F32
         )
         for side, block in blocks:
             total += jnp.dot(near_ref[side, cut, :], block, preferred_element_type=F32)
-        out_ref = send_ref if turn % 2 else keep_ref
-        out_ref[turn // 2, :rows, :] = total
+        out_ref[index] = total
         totals.append((cut, total.astype(BF)))
     return totals
 
 
-def first_kernel(near_ref, left_ref, across_ref, columns_ref, ranks_ref, even_ref, odd_ref, *refs):
-    totals = image_kernel(near_ref, left_ref, across_ref, columns_ref, *refs)
-    keep_ref, send_ref = refs[7:]
-    me = lax.axis_index("list")
-    ranks = even_ref.shape[1]
-    rows = near_ref.shape[2]
+def right_products(totals, bases_ref, across_ref, pair_ref):
     sums = 0.0
     for cut, total in totals:
-        bases = stacked([ref[index, :, cut] for ref in (even_ref, odd_ref) for index in range(2)])
-        sums += jnp.dot(bases, total, preferred_element_type=F32)
+        groups = [bases_ref[0, :, cut], across_ref[0, :, cut], pair_ref[0, :, cut], pair_ref[1, :, cut]]
+        sums += jnp.dot(stacked(groups), total, preferred_element_type=F32)
+    return sums
+
+
+def sent_kernel(near_ref, bases_ref, across_ref, columns_ref, *refs):
+    operands, pair_ref, out_ref, sums_ref = refs[:7], *refs[7:]
+    totals = image_kernel(
+        (1, 3), near_ref, bases_ref, across_ref, columns_ref, *operands, out_ref
+    )
+    sums_ref[...] = right_products(totals, bases_ref, across_ref, pair_ref)
+
+
+def kept_kernel(near_ref, bases_ref, across_ref, columns_ref, *refs):
+    operands, (pair_ref, ranks_ref, sums_ref), outs = refs[:7], refs[7:10], refs[10:]
+    totals = image_kernel(
+        (0, 2), near_ref, bases_ref, across_ref, columns_ref, *operands, outs[0]
+    )
+    sums = sums_ref[...] + right_products(totals, bases_ref, across_ref, pair_ref)
+    me = lax.axis_index("list")
+    ranks = bases_ref.shape[1]
     for index, turn in enumerate((0, 2, 1, 3)):
         values = sums[index * ranks : (index + 1) * ranks]
-        out_ref = send_ref if turn % 2 else keep_ref
-        out_ref[turn // 2, rows:, :] = under_rank(values, me ^ turn, ranks, ranks_ref)
-
-
-def second_kernel(*refs):
-    image_kernel(*refs)
-
-
-def tile_swaps(own):
-    return [own] + [tile_swap(own, turn) for turn in (1, 2, 3)]
+        start = index % 2 * ranks
+        outs[1 + index // 2][start : start + ranks, :] = under_rank(
+            values, me ^ turn, ranks, ranks_ref
+        )
+
+
+def second_kernel(turns, *refs):
+    image_kernel(turns, *refs)
 
 
 def one_slot(probes, right_bases, left_bases, near_tiles, tile_ranks, column_rows, row_columns):
@@ -181,37 +192,52 @@
     rank_part = right_bases.shape[2]
     near = near_tiles[0].transpose(1, 0, 2)
     flops = 2 * near.size * probe_count
-    right, left = right_bases[0, 0], left_bases[0, 0]
-    right_across = list_swap(right, 2)
+    halves = ((2, rows, probe_count), F32)
+    small = ((2 * rank_part, probe_count), F32)
+
+    bases = jnp.stack([right_bases[0, 0], left_bases[0, 0]])
+    bases_across = list_swap(bases, 2)
     block = probes.astype(BF)
     beside = [block, tile_swap(block, 1), tile_swap(block, 0)]
     (own,) = kernel_call(
         coefficient_kernel,
         [((2 * rank_part, probe_count), BF)],
-        (right, right_across, block, list_swap(block, 1), tile_ranks),
+        (bases, bases_across, block, list_swap(block, 1), tile_ranks),
         8 * flops,
     )
-    coefficients = tile_swaps(own)
-    right = jnp.stack([right, right_across])
-    bases = (near, left, list_swap(left, 2), row_columns)
-    keep, send = kernel_call(
-        first_kernel,
-        [((2, rows + rank_part, probe_count), F32)] * 2,
-        (*bases, tile_ranks, right, list_swap(right, 1), *beside, *coefficients),
-        flops,
-    )
-    pair = keep + list_swap(send, 1)
-    coefficients = tile_swaps(pair[:, rows:].reshape(-1, probe_count).astype(BF))
-    block = (pair[0, :rows] + list_swap(pair[1, :rows].astype(BF), 2)).astype(BF)
-    block, *coefficients[2:] = lax.optimization_barrier((block, *coefficients[2:]))
-    beside = [block, tile_swap(block, 1), tile_swap(block, 0)]
-    keep, send = kernel_call(
-        second_kernel,
-        [((2, rows, probe_count), F32)] * 2,
-        (*bases, *beside, *coefficients),
-        flops,
-    )
-    pair = keep + list_swap(send, 1)
+    coefficients = [own] + [tile_swap(own, turn) for turn in (1, 2, 3)]
+    right = jnp.stack([bases[0], bases_across[0]])
+    right, _ = lax.optimization_barrier((right, own))
+    right_pair = list_swap(right, 1)
+
+    fixed = (near, bases, bases_across, row_columns)
+    operands = (*fixed, *beside, *coefficients, right_pair)
+    send, sums = kernel_call(
+        sent_kernel, [halves, ((4 * rank_part, probe_count), F32)], operands, flops
+    )
+    arrived = list_swap(send, 1)
+    keep, small_keep, small_send = kernel_call(
+        kept_kernel, [halves, small, small], (*operands, tile_ranks, sums), flops
+    )
+    own = (small_keep + list_swap(small_send, 1)).astype(BF)
+    pair = keep + arrived
+    second, third = tile_swap(own, 2), tile_swap(own, 3)
+    block = (pair[0] + list_swap(pair[1].astype(BF), 2)).astype(BF)
+    message = jnp.concatenate([block, own])
+    message, second, third = lax.optimization_barrier((message, second, third))
+    message = tile_swap(message, 1)
+    beside = [block, message[:rows], tile_swap(block, 0)]
+    coefficients = [own, message[rows:], second, third]
+
+    operands = (*fixed, *beside, *coefficients)
+    (send,) = kernel_call(
+        functools.partial(second_kernel, (1, 3)), [halves], operands, flops
+    )
+    arrived = list_swap(send, 1)
+    (keep,) = kernel_call(
+        functools.partial(second_kernel, (0, 2)), [halves], operands, flops
+    )
+    pair = keep + arrived
     return pair[0] + list_swap(pair[1].astype(BF), 2)
 
 

time: 47.3 us -> 43.6 us (0.922)
  the two profiles are of different devices: /device:TPU:0 before, /device:TPU:12 now
where the time goes in v7:
time: 43.6 us; the launch traced here: 43.3 us
  starting transfers between devices  20.5 us (47%)
  waiting for transfers between devices  15.3 us (35%)
  other arithmetic  3.58 us (8%)
  Pallas kernels  2.4 us (6%)
  between operations  1.49 us (3%)
    ppermute x9, starting transfers between devices, tile_swap(): return lax.ppermute(block, 'tile', route)  15.8 us
    ppermute x8, waiting for transfers between devices, list_swap(): lax.ppermute(block, 'list', [(i, i ^ bit) for i in range(lax.axis_size('l...  8.3 us
    ppermute x9, waiting for transfers between devices, tile_swap(): return lax.ppermute(block, 'tile', route)  7.02 us
    ppermute x8, starting transfers between devices, list_swap(): lax.ppermute(block, 'list', [(i, i ^ bit) for i in range(lax.axis_size('l...  4.74 us
    pallas_call x5, Pallas kernels, kernel_call(): pl.pallas_call(kernel, out_shape=tuple((jax.ShapeDtypeStruct(shape, kind)...  2.4 us
    convert_element_type x1, other arithmetic, one_slot(): block = probes.astype(BF)  0.96 us
  transfers between devices with their start and end apart: 17, of which 9 were waited for; matrix products, arithmetic and copies ran while one was open for 5% of the time, Pallas kernels for 3%

profile of v7, /device:TPU:12, one launch (start us, length us, event | category | flops | bytes accessed | tf_op | source)
XLA Modules:
  0.0 43.3 jit_solution(4850772051984953391)
XLA Ops:
  0.0 0.8 %pad_maximum_fusion.2.bases_ref.refs_1_ = bf16[2,24,1024]{2,1,0:T(8,128)(2,1)S(1)} fusion(bf16[1,24,1024]{2,1,0:T(8,128)(2,1)} %bitcast.23, bf16[1,24,1024]{2,1,0:T(8,128)(2,1)} %bitcast.25), kind=kLoop, calls=%fused_computation.11 | loop fusion | flops 49152 | bytes 196608 | tf_op jit(solution)/shard_map/stack | solution.py:198
  0.8 1.6 %collective-permute-start = (bf16[2,24,1024]{2,1,0:T(8,128)(2,1)S(1)}, bf16[2,24,1024]{2,1,0:T(8,128)(2,1)S(1)}, u32[]{:S(2)}, u32[]{:S(2)}) collective-permute-start(bf16[2,24,1024]{2,1,0:T(8,128)(2,1)S(1)} %pad_maximum_fusion.2.bases_ref.refs_1_), channel_id=1, source_target_pairs={{0,2},{1,3},{2,0},{3,1},{4,6},{5,7},{6,4},{7,5},{8,10},{9,11},{10,... | collective-permute-start | bytes 294920 | tf_op jit(solution)/shard_map/ppermute | solution.py:119
  2.4 1.0 %convert_element_type.23.block_ref.refs_0_ = bf16[256,256]{1,0:T(8,128)(2,1)S(1)} convert(f32[256,256]{1,0:T(8,128)} %param.7) | non-fusion elementwise | flops 65536 | bytes 393216 | tf_op jit(solution)/shard_map/convert_element_type | solution.py:200
  3.4 3.5 %collective-permute-start.2 = (bf16[256,256]{1,0:T(8,128)(2,1)S(1)}, bf16[256,256]{1,0:T(8,128)(2,1)S(1)}, u32[]{:S(2)}, u32[]{:S(2)}) collective-permute-start(bf16[256,256]{1,0:T(8,128)(2,1)S(1)} %convert_element_type.23.block_ref.refs_0_), channel_id=1, source_target_pairs={{0,0},{4,8},{8,4},{12,12},{1,1},{5,9},{9,5},{13,13},{2,2},{6,10},{... | collective-permute-start | bytes 393224 | tf_op jit(solution)/shard_map/ppermute | solution.py:115
  7.7 0.8 %pad_maximum_fusion.1 = bf16[2,24,1024]{2,1,0:T(8,128)(2,1)S(1)} fusion(bf16[1,24,1024]{2,1,0:T(8,128)(2,1)} %bitcast.24, bf16[1,24,1024]{2,1,0:T(8,128)(2,1)S(1)} %slice.30), kind=kLoop, calls=%fused_computation.10 | loop fusion | flops 49152 | bytes 196608 | tf_op jit(solution)/shard_map/stack | solution.py:209
  9.0 0.4 %collective-permute-start.6 = (bf16[48,256]{1,0:T(8,128)(2,1)S(1)}, bf16[48,256]{1,0:T(8,128)(2,1)S(1)}, u32[]{:S(2)}, u32[]{:S(2)}) collective-permute-start(bf16[48,256]{1,0:T(8,128)(2,1)S(1)} %shard_map.64.refs_3_), channel_id=1, source_target_pairs={{0,12},{4,8},{8,4},{12,0},{1,13},{5,9},{9,5},{13,1},{2,14},{6,10},... | collective-permute-start | bytes 73736 | tf_op jit(solution)/shard_map/ppermute | solution.py:115
  9.4 3.8 %collective-permute-start.5 = (bf16[48,256]{1,0:T(8,128)(2,1)S(1)}, bf16[48,256]{1,0:T(8,128)(2,1)S(1)}, u32[]{:S(2)}, u32[]{:S(2)}) collective-permute-start(bf16[48,256]{1,0:T(8,128)(2,1)S(1)} %shard_map.64.refs_3_), channel_id=1, source_target_pairs={{0,8},{4,12},{8,0},{12,4},{1,9},{5,13},{9,1},{13,5},{2,10},{6,14},... | collective-permute-start | bytes 73736 | tf_op jit(solution)/shard_map/ppermute | solution.py:115
  13.9 1.5 %collective-permute-done.5.refs_5_ = bf16[48,256]{1,0:T(8,128)(2,1)S(1)} collective-permute-done((bf16[48,256]{1,0:T(8,128)(2,1)S(1)}, bf16[48,256]{1,0:T(8,128)(2,1)S(1)}, u32[]{:S(2)}, u32[]{:S(2)}) %collective-permute-start.5) | collective-permute-done | bytes 24608 | tf_op jit(solution)/shard_map/ppermute | solution.py:115
  15.4 1.7 %collective-permute-done.4.refs_4_ = bf16[48,256]{1,0:T(8,128)(2,1)S(1)} collective-permute-done((bf16[48,256]{1,0:T(8,128)(2,1)S(1)}, bf16[48,256]{1,0:T(8,128)(2,1)S(1)}, u32[]{:S(2)}, u32[]{:S(2)}) %collective-permute-start.4) | collective-permute-done | bytes 24608 | tf_op jit(solution)/shard_map/ppermute | solution.py:115
  17.0 0.7 %shard_map.65 = (f32[2,256,256]{2,1,0:T(8,128)S(1)}, f32[96,256]{1,0:T(8,128)S(1)}) custom-call(bf16[3,1024,256]{2,1,0:T(8,128)(2,1)S(1)} %bitcast.19, bf16[2,24,1024]{2,1,0:T(8,128)(2,1)S(1)} %pad_maximum_fusion.2.bases_ref.refs_1_, bf16[2,24,1024]{2,1,0:T(8,128)(2,1)S(1)} %collective-permute-done.across_ref.refs_2_, s32[1,1]{1,0:T(1,128)S(6)} %copy.8.columns_ref.refs_3_, ...), custom_call_target="tpu_custom_call" | custom-call | flops 402653184 | bytes 1572864 | tf_op jit(solution)/shard_map/pallas_call | solution.py:73
  17.8 0.7 %shard_map.66 = (f32[2,256,256]{2,1,0:T(8,128)S(1)}, f32[48,256]{1,0:T(8,128)S(1)}, f32[48,256]{1,0:T(8,128)S(1)}) custom-call(bf16[3,1024,256]{2,1,0:T(8,128)(2,1)S(1)} %bitcast.20, bf16[2,24,1024]{2,1,0:T(8,128)(2,1)S(1)} %pad_maximum_fusion.2.bases_ref.refs_1_, bf16[2,24,1024]{2,1,0:T(8,128)(2,1)S(1)} %collective-permute-done.across_ref.refs_2_, ...), custom_call_target="tpu_custom_call" | custom-call | flops 402653184 | bytes 1572864 | tf_op jit(solution)/shard_map/pallas_call | solution.py:73
  18.5 0.6 %collective-permute-start.10 = (f32[48,256]{1,0:T(8,128)S(1)}, f32[48,256]{1,0:T(8,128)S(1)}, u32[]{:S(2)}, u32[]{:S(2)}) collective-permute-start(f32[48,256]{1,0:T(8,128)S(1)} %get-tuple-element.19), channel_id=1, source_target_pairs={{0,1},{1,0},{2,3},{3,2},{4,5},{5,4},{6,7},{7,6},{8,9},{9,8},{10,11... | collective-permute-start | bytes 147464 | tf_op jit(solution)/shard_map/ppermute | solution.py:119
  19.1 0.6 %collective-permute-done.8 = f32[2,256,256]{2,1,0:T(8,128)S(1)} collective-permute-done((f32[2,256,256]{2,1,0:T(8,128)S(1)}, f32[2,256,256]{2,1,0:T(8,128)S(1)}, u32[]{:S(2)}, u32[]{:S(2)}) %collective-permute-start.8) | collective-permute-done | bytes 524320 | tf_op jit(solution)/shard_map/ppermute | solution.py:119
  19.8 0.6 %collective-permute-start.9 = (bf16[256,256]{1,0:T(8,128)(2,1)S(1)}, bf16[256,256]{1,0:T(8,128)(2,1)S(1)}, u32[]{:S(2)}, u32[]{:S(2)}) collective-permute-start(bf16[256,256]{1,0:T(8,128)(2,1)S(1)} %fusion.3), channel_id=1, source_target_pairs={{0,2},{1,3},{2,0},{3,1},{4,6},{5,7},{6,4},{7,5},{8,10},{9,11},{10,... | collective-permute-start | bytes 393224 | tf_op jit(solution)/shard_map/ppermute | solution.py:119
  20.4 0.5 %collective-permute-start.12 = (bf16[48,256]{1,0:T(8,128)(2,1)S(1)}, bf16[48,256]{1,0:T(8,128)(2,1)S(1)}, u32[]{:S(2)}, u32[]{:S(2)}) collective-permute-start(bf16[48,256]{1,0:T(8,128)(2,1)S(1)} %add_convert_fusion.refs_7_), channel_id=1, source_target_pairs={{0,12},{4,8},{8,4},{12,0},{1,13},{5,9},{9,5},{13,1},{2,14},{6,10},... | collective-permute-start | bytes 73736 | tf_op jit(solution)/shard_map/ppermute | solution.py:115
  21.0 2.4 %collective-permute-start.11 = (bf16[48,256]{1,0:T(8,128)(2,1)S(1)}, bf16[48,256]{1,0:T(8,128)(2,1)S(1)}, u32[]{:S(2)}, u32[]{:S(2)}) collective-permute-start(bf16[48,256]{1,0:T(8,128)(2,1)S(1)} %add_convert_fusion.refs_7_), channel_id=1, source_target_pairs={{0,8},{4,12},{8,0},{12,4},{1,9},{5,13},{9,1},{13,5},{2,10},{6,14},... | collective-permute-start | bytes 73736 | tf_op jit(solution)/shard_map/ppermute | solution.py:115
  23.3 2.1 %collective-permute-done.9 = bf16[256,256]{1,0:T(8,128)(2,1)S(1)} collective-permute-done((bf16[256,256]{1,0:T(8,128)(2,1)S(1)}, bf16[256,256]{1,0:T(8,128)(2,1)S(1)}, u32[]{:S(2)}, u32[]{:S(2)}) %collective-permute-start.9) | collective-permute-done | bytes 131104 | tf_op jit(solution)/shard_map/ppermute | solution.py:119
  25.7 1.9 %collective-permute-start.13 = (bf16[304,256]{1,0:T(8,128)(2,1)S(1)}, bf16[304,256]{1,0:T(8,128)(2,1)S(1)}, u32[]{:S(2)}, u32[]{:S(2)}) collective-permute-start(bf16[304,256]{1,0:T(8,128)(2,1)S(1)} %pad_maximum_fusion), channel_id=1, source_target_pairs={{0,4},{4,0},{8,12},{12,8},{1,5},{5,1},{9,13},{13,9},{2,6},{6,2},{1... | collective-permute-start | bytes 466952 | tf_op jit(solution)/shard_map/ppermute | solution.py:115
  27.6 3.2 %collective-permute-start.14 = (bf16[256,256]{1,0:T(8,128)(2,1)S(1)}, bf16[256,256]{1,0:T(8,128)(2,1)S(1)}, u32[]{:S(2)}, u32[]{:S(2)}) collective-permute-start(bf16[256,256]{1,0:T(8,128)(2,1)S(1)} %fusion.2.refs_4_), channel_id=1, source_target_pairs={{0,0},{4,8},{8,4},{12,12},{1,1},{5,9},{9,5},{13,13},{2,2},{6,10},{... | collective-permute-start | bytes 393224 | tf_op jit(solution)/shard_map/ppermute | solution.py:115
  30.9 3.5 %collective-permute-done.14.refs_6_ = bf16[256,256]{1,0:T(8,128)(2,1)S(1)} collective-permute-done((bf16[256,256]{1,0:T(8,128)(2,1)S(1)}, bf16[256,256]{1,0:T(8,128)(2,1)S(1)}, u32[]{:S(2)}, u32[]{:S(2)}) %collective-permute-start.14) | collective-permute-done | bytes 131104 | tf_op jit(solution)/shard_map/ppermute | solution.py:115
  35.4 1.5 %collective-permute-done.15 = f32[2,256,256]{2,1,0:T(8,128)S(1)} collective-permute-done((f32[2,256,256]{2,1,0:T(8,128)S(1)}, f32[2,256,256]{2,1,0:T(8,128)S(1)}, u32[]{:S(2)}, u32[]{:S(2)}) %collective-permute-start.15) | collective-permute-done | bytes 524320 | tf_op jit(solution)/shard_map/ppermute | solution.py:119
  37.0 1.5 %collective-permute-start.16 = (bf16[256,256]{1,0:T(8,128)(2,1)S(1)}, bf16[256,256]{1,0:T(8,128)(2,1)S(1)}, u32[]{:S(2)}, u32[]{:S(2)}) collective-permute-start(bf16[256,256]{1,0:T(8,128)(2,1)S(1)} %fusion.4), channel_id=1, source_target_pairs={{0,2},{1,3},{2,0},{3,1},{4,6},{5,7},{6,4},{7,5},{8,10},{9,11},{10,... | collective-permute-start | bytes 393224 | tf_op jit(solution)/shard_map/ppermute | solution.py:119
  38.5 4.1 %collective-permute-done.16 = bf16[256,256]{1,0:T(8,128)(2,1)S(1)} collective-permute-done((bf16[256,256]{1,0:T(8,128)(2,1)S(1)}, bf16[256,256]{1,0:T(8,128)(2,1)S(1)}, u32[]{:S(2)}, u32[]{:S(2)}) %collective-permute-start.16) | collective-permute-done | bytes 131104 | tf_op jit(solution)/shard_map/ppermute | solution.py:119
  42.6 0.7 %fusion = f32[256,256]{1,0:T(8,128)} fusion(f32[2,256,256]{2,1,0:T(8,128)S(1)} %add.18, bf16[256,256]{1,0:T(8,128)(2,1)S(1)} %collective-permute-done.16), kind=kLoop, calls=%fused_computation.2 | loop fusion | flops 131072 | bytes 655360 | tf_op jit(solution)/shard_map/add | solution.py:241
  (31 shorter events, 2.2 us)
Async XLA Ops:
  0.8 6.8 %collective-permute-start = (bf16[2,24,1024]{2,1,0:T(8,128)(2,1)S(1)}, bf16[2,24,1024]{2,1,0:T(8,128)(2,1)S(1)}, u32[]{:S(2)}, u32[]{:S(2)}) collective-permute-start(bf16[2,24,1024]{2,1,0:T(8,128)(2,1)S(1)} %pad_maximum_fusion.2.bases_ref.refs_1_), channel_id=1, source_target_pairs={{0,2},{1,3},{2,0},{3,1},{4,6},{5,7},{6,4},{7,5},{8,10},{9,11},{10,... | collective-permute-start | bytes 294920 | tf_op jit(solution)/shard_map/ppermute | solution.py:119
  3.4 5.2 %collective-permute-start.3 = (bf16[256,256]{1,0:T(8,128)(2,1)S(1)}, bf16[256,256]{1,0:T(8,128)(2,1)S(1)}, u32[]{:S(2)}, u32[]{:S(2)}) collective-permute-start(bf16[256,256]{1,0:T(8,128)(2,1)S(1)} %convert_element_type.23.block_ref.refs_0_), channel_id=1, source_target_pairs={{0,1},{1,0},{2,3},{3,2},{4,5},{5,4},{6,7},{7,6},{8,9},{9,8},{10,11... | collective-permute-start | bytes 393224 | tf_op jit(solution)/shard_map/ppermute | solution.py:119
  3.4 9.8 %collective-permute-start.2 = (bf16[256,256]{1,0:T(8,128)(2,1)S(1)}, bf16[256,256]{1,0:T(8,128)(2,1)S(1)}, u32[]{:S(2)}, u32[]{:S(2)}) collective-permute-start(bf16[256,256]{1,0:T(8,128)(2,1)S(1)} %convert_element_type.23.block_ref.refs_0_), channel_id=1, source_target_pairs={{0,0},{4,8},{8,4},{12,12},{1,1},{5,9},{9,5},{13,13},{2,2},{6,10},{... | collective-permute-start | bytes 393224 | tf_op jit(solution)/shard_map/ppermute | solution.py:115
  6.9 6.9 %collective-permute-start.1 = (bf16[256,256]{1,0:T(8,128)(2,1)S(1)}, bf16[256,256]{1,0:T(8,128)(2,1)S(1)}, u32[]{:S(2)}, u32[]{:S(2)}) collective-permute-start(bf16[256,256]{1,0:T(8,128)(2,1)S(1)} %convert_element_type.23.block_ref.refs_0_), channel_id=1, source_target_pairs={{0,4},{4,0},{8,12},{12,8},{1,5},{5,1},{9,13},{13,9},{2,6},{6,2},{1... | collective-permute-start | bytes 393224 | tf_op jit(solution)/shard_map/ppermute | solution.py:115
  8.5 8.5 %copy-start = (bf16[1,1024,3,256]{3,1,2,0:T(8,128)(2,1)S(1)}, bf16[1,1024,3,256]{3,1,2,0:T(8,128)(2,1)}, u32[]{:S(2)}) copy-start(bf16[1,1024,3,256]{3,1,2,0:T(8,128)(2,1)} %param.10) | copy-start | bytes 4718596
  8.7 8.4 %collective-permute-start.7 = (bf16[2,24,1024]{2,1,0:T(8,128)(2,1)S(1)}, bf16[2,24,1024]{2,1,0:T(8,128)(2,1)S(1)}, u32[]{:S(2)}, u32[]{:S(2)}) collective-permute-start(bf16[2,24,1024]{2,1,0:T(8,128)(2,1)S(1)} %pad_maximum_fusion.1), channel_id=1, source_target_pairs={{0,1},{1,0},{2,3},{3,2},{4,5},{5,4},{6,7},{7,6},{8,9},{9,8},{10,11... | collective-permute-start | bytes 294920 | tf_op jit(solution)/shard_map/ppermute | solution.py:119
  9.0 4.9 %collective-permute-start.6 = (bf16[48,256]{1,0:T(8,128)(2,1)S(1)}, bf16[48,256]{1,0:T(8,128)(2,1)S(1)}, u32[]{:S(2)}, u32[]{:S(2)}) collective-permute-start(bf16[48,256]{1,0:T(8,128)(2,1)S(1)} %shard_map.64.refs_3_), channel_id=1, source_target_pairs={{0,12},{4,8},{8,4},{12,0},{1,13},{5,9},{9,5},{13,1},{2,14},{6,10},... | collective-permute-start | bytes 73736 | tf_op jit(solution)/shard_map/ppermute | solution.py:115
  9.4 6.0 %collective-permute-start.5 = (bf16[48,256]{1,0:T(8,128)(2,1)S(1)}, bf16[48,256]{1,0:T(8,128)(2,1)S(1)}, u32[]{:S(2)}, u32[]{:S(2)}) collective-permute-start(bf16[48,256]{1,0:T(8,128)(2,1)S(1)} %shard_map.64.refs_3_), channel_id=1, source_target_pairs={{0,8},{4,12},{8,0},{12,4},{1,9},{5,13},{9,1},{13,5},{2,10},{6,14},... | collective-permute-start | bytes 73736 | tf_op jit(solution)/shard_map/ppermute | solution.py:115
  13.2 3.8 %collective-permute-start.4 = (bf16[48,256]{1,0:T(8,128)(2,1)S(1)}, bf16[48,256]{1,0:T(8,128)(2,1)S(1)}, u32[]{:S(2)}, u32[]{:S(2)}) collective-permute-start(bf16[48,256]{1,0:T(8,128)(2,1)S(1)} %shard_map.64.refs_3_), channel_id=1, source_target_pairs={{0,4},{4,0},{8,12},{12,8},{1,5},{5,1},{9,13},{13,9},{2,6},{6,2},{1... | collective-permute-start | bytes 73736 | tf_op jit(solution)/shard_map/ppermute | solution.py:115
  17.7 2.0 %collective-permute-start.8 = (f32[2,256,256]{2,1,0:T(8,128)S(1)}, f32[2,256,256]{2,1,0:T(8,128)S(1)}, u32[]{:S(2)}, u32[]{:S(2)}) collective-permute-start(f32[2,256,256]{2,1,0:T(8,128)S(1)} %get-tuple-element.17), channel_id=1, source_target_pairs={{0,1},{1,0},{2,3},{3,2},{4,5},{5,4},{6,7},{7,6},{8,9},{9,8},{10,11... | collective-permute-start | bytes 1572872 | tf_op jit(solution)/shard_map/ppermute | solution.py:119
  18.5 1.9 %collective-permute-start.10 = (f32[48,256]{1,0:T(8,128)S(1)}, f32[48,256]{1,0:T(8,128)S(1)}, u32[]{:S(2)}, u32[]{:S(2)}) collective-permute-start(f32[48,256]{1,0:T(8,128)S(1)} %get-tuple-element.19), channel_id=1, source_target_pairs={{0,1},{1,0},{2,3},{3,2},{4,5},{5,4},{6,7},{7,6},{8,9},{9,8},{10,11... | collective-permute-start | bytes 147464 | tf_op jit(solution)/shard_map/ppermute | solution.py:119
  19.8 5.6 %collective-permute-start.9 = (bf16[256,256]{1,0:T(8,128)(2,1)S(1)}, bf16[256,256]{1,0:T(8,128)(2,1)S(1)}, u32[]{:S(2)}, u32[]{:S(2)}) collective-permute-start(bf16[256,256]{1,0:T(8,128)(2,1)S(1)} %fusion.3), channel_id=1, source_target_pairs={{0,2},{1,3},{2,0},{3,1},{4,6},{5,7},{6,4},{7,5},{8,10},{9,11},{10,... | collective-permute-start | bytes 393224 | tf_op jit(solution)/shard_map/ppermute | solution.py:119
  20.4 5.0 %collective-permute-start.12 = (bf16[48,256]{1,0:T(8,128)(2,1)S(1)}, bf16[48,256]{1,0:T(8,128)(2,1)S(1)}, u32[]{:S(2)}, u32[]{:S(2)}) collective-permute-start(bf16[48,256]{1,0:T(8,128)(2,1)S(1)} %add_convert_fusion.refs_7_), channel_id=1, source_target_pairs={{0,12},{4,8},{8,4},{12,0},{1,13},{5,9},{9,5},{13,1},{2,14},{6,10},... | collective-permute-start | bytes 73736 | tf_op jit(solution)/shard_map/ppermute | solution.py:115
  21.0 4.7 %collective-permute-start.11 = (bf16[48,256]{1,0:T(8,128)(2,1)S(1)}, bf16[48,256]{1,0:T(8,128)(2,1)S(1)}, u32[]{:S(2)}, u32[]{:S(2)}) collective-permute-start(bf16[48,256]{1,0:T(8,128)(2,1)S(1)} %add_convert_fusion.refs_7_), channel_id=1, source_target_pairs={{0,8},{4,12},{8,0},{12,4},{1,9},{5,13},{9,1},{13,5},{2,10},{6,14},... | collective-permute-start | bytes 73736 | tf_op jit(solution)/shard_map/ppermute | solution.py:115
  25.7 5.2 %collective-permute-start.13 = (bf16[304,256]{1,0:T(8,128)(2,1)S(1)}, bf16[304,256]{1,0:T(8,128)(2,1)S(1)}, u32[]{:S(2)}, u32[]{:S(2)}) collective-permute-start(bf16[304,256]{1,0:T(8,128)(2,1)S(1)} %pad_maximum_fusion), channel_id=1, source_target_pairs={{0,4},{4,0},{8,12},{12,8},{1,5},{5,1},{9,13},{13,9},{2,6},{6,2},{1... | collective-permute-start | bytes 466952 | tf_op jit(solution)/shard_map/ppermute | solution.py:115
  27.6 6.8 %collective-permute-start.14 = (bf16[256,256]{1,0:T(8,128)(2,1)S(1)}, bf16[256,256]{1,0:T(8,128)(2,1)S(1)}, u32[]{:S(2)}, u32[]{:S(2)}) collective-permute-start(bf16[256,256]{1,0:T(8,128)(2,1)S(1)} %fusion.2.refs_4_), channel_id=1, source_target_pairs={{0,0},{4,8},{8,4},{12,12},{1,1},{5,9},{9,5},{13,13},{2,2},{6,10},{... | collective-permute-start | bytes 393224 | tf_op jit(solution)/shard_map/ppermute | solution.py:115
  34.9 2.0 %collective-permute-start.15 = (f32[2,256,256]{2,1,0:T(8,128)S(1)}, f32[2,256,256]{2,1,0:T(8,128)S(1)}, u32[]{:S(2)}, u32[]{:S(2)}) collective-permute-start(f32[2,256,256]{2,1,0:T(8,128)S(1)} %shard_map.68), channel_id=1, source_target_pairs={{0,1},{1,0},{2,3},{3,2},{4,5},{5,4},{6,7},{7,6},{8,9},{9,8},{10,11... | collective-permute-start | bytes 1572872 | tf_op jit(solution)/shard_map/ppermute | solution.py:119
  37.0 5.6 %collective-permute-start.16 = (bf16[256,256]{1,0:T(8,128)(2,1)S(1)}, bf16[256,256]{1,0:T(8,128)(2,1)S(1)}, u32[]{:S(2)}, u32[]{:S(2)}) collective-permute-start(bf16[256,256]{1,0:T(8,128)(2,1)S(1)} %fusion.4), channel_id=1, source_target_pairs={{0,2},{1,3},{2,0},{3,1},{4,6},{5,7},{6,4},{7,5},{8,10},{9,11},{10,... | collective-permute-start | bytes 393224 | tf_op jit(solution)/shard_map/ppermute | solution.py:119

commit v8 on v7

--- a/solution.py
+++ b/solution.py
@@ -108,11 +108,19 @@
 
 
 def tile_swap(block, turn):
-    count = lax.axis_size("tile")
-    route = [(i, i ^ turn) for i in range(count)]
-    if turn == 0:
-        route = [(i, min(max(i - 1 + 2 * (i % 2), 0), count - 1)) for i in range(count)]
-    return lax.ppermute(block, "tile", route)
+    return lax.ppermute(block, "tile", [(i, i ^ turn) for i in range(lax.axis_size("tile"))])
+
+
+def middle_swap(block):
+    tiles, parts = lax.axis_size("tile"), lax.axis_size("list")
+    route = []
+    for tile in range(tiles):
+        for part in range(parts):
+            to = (tile - 1 + 2 * (tile % 2), part)
+            if tile in (0, tiles - 1):
+                to = (tile, part ^ 1)
+            route.append((tile * parts + part, to[0] * parts + to[1]))
+    return lax.ppermute(block, ("tile", "list"), route)
 
 
 def list_swap(block, bit):
@@ -126,14 +134,16 @@
     me = lax.axis_index("list")
     rows = near_ref.shape[2]
     chosen = coefficient_refs[0][...]
+    slots = chosen.shape[0]
     for turn in (1, 2, 3):
-        listed = columns_ref[...] == tile ^ turn
-        chosen = jnp.where(listed, coefficient_refs[turn][...], chosen)
+        other_ref = coefficient_refs[turn]
+        other = other_ref[other_ref.shape[0] - slots :, :]
+        chosen = jnp.where(columns_ref[...] == tile ^ turn, other, chosen)
     odd = lax.rem(tile, 2)
     inside = (tile > 0) & (tile < count - 1)
     blocks = [
         (1, block_refs[0][...]),
-        (2 - 2 * odd, block_refs[1][...]),
+        (2 - 2 * odd, block_refs[1][:rows, :]),
         (2 * odd, jnp.where(inside, block_refs[2][...], 0)),
     ]
     totals = []
@@ -196,9 +206,10 @@
     small = ((2 * rank_part, probe_count), F32)
 
     bases = jnp.stack([right_bases[0, 0], left_bases[0, 0]])
+    bases, probes = lax.optimization_barrier((bases, probes))
     bases_across = list_swap(bases, 2)
     block = probes.astype(BF)
-    beside = [block, tile_swap(block, 1), tile_swap(block, 0)]
+    beside = [block, tile_swap(block, 1), middle_swap(block)]
     (own,) = kernel_call(
         coefficient_kernel,
         [((2 * rank_part, probe_count), BF)],
@@ -226,8 +237,8 @@
     message = jnp.concatenate([block, own])
     message, second, third = lax.optimization_barrier((message, second, third))
     message = tile_swap(message, 1)
-    beside = [block, message[:rows], tile_swap(block, 0)]
-    coefficients = [own, message[rows:], second, third]
+    beside = [block, message, middle_swap(block)]
+    coefficients = [own, message, second, third]
 
     operands = (*fixed, *beside, *coefficients)
     (send,) = kernel_call(

time: 43.6 us -> 40.9 us (0.938)
  the two profiles are of different devices: /device:TPU:12 before, /device:TPU:0 now
where the time goes in v8:
time: 40.9 us; the launch traced here: 40.7 us
  starting transfers between devices  17.2 us (42%)
  waiting for transfers between devices  16.8 us (41%)
  other arithmetic  2.78 us (7%)
  Pallas kernels  2.41 us (6%)
  between operations  1.47 us (4%)
    ppermute x7, starting transfers between devices, tile_swap(): lax.ppermute(block, 'tile', [(i, i ^ turn) for i in range(lax.axis_size('...  10.3 us
    ppermute x8, waiting for transfers between devices, list_swap(): lax.ppermute(block, 'list', [(i, i ^ bit) for i in range(lax.axis_size('l...  8.38 us
    ppermute x7, waiting for transfers between devices, tile_swap(): lax.ppermute(block, 'tile', [(i, i ^ turn) for i in range(lax.axis_size('...  7.04 us
    ppermute x8, starting transfers between devices, list_swap(): lax.ppermute(block, 'list', [(i, i ^ bit) for i in range(lax.axis_size('l...  6.48 us
    pallas_call x5, Pallas kernels, kernel_call(): pl.pallas_call(kernel, out_shape=tuple((jax.ShapeDtypeStruct(shape, kind)...  2.41 us
    ppermute x2, waiting for transfers between devices, middle_swap(): return lax.ppermute(block, ('tile', 'list'), route)  1.35 us
    convert_element_type x1, other arithmetic, one_slot(): block = probes.astype(BF)  0.96 us
    another operation x1, other arithmetic, one_slot(): bases = jnp.stack([right_bases[0, 0], left_bases[0, 0]])  0.83 us
  transfers between devices with their start and end apart: 17, of which 10 were waited for; matrix products, arithmetic and copies ran while one was open for 3% of the time, Pallas kernels for 3%

profile of v8, /device:TPU:0, one launch (start us, length us, event | category | flops | bytes accessed | tf_op | source)
XLA Modules:
  0.0 40.7 jit_solution(12430701558184082160)
XLA Ops:
  0.0 0.8 %pad_maximum_fusion.1.bases_ref.refs_1_ = bf16[2,24,1024]{2,1,0:T(8,128)(2,1)S(1)} fusion(bf16[1,24,1024]{2,1,0:T(8,128)(2,1)} %bitcast.23, bf16[1,24,1024]{2,1,0:T(8,128)(2,1)} %bitcast.24), kind=kLoop, calls=%fused_computation.10 | loop fusion | flops 49152 | bytes 196608 | tf_op jit(solution)/shard_map/stack | solution.py:208
  0.8 3.0 %collective-permute-start = (bf16[2,24,1024]{2,1,0:T(8,128)(2,1)S(1)}, bf16[2,24,1024]{2,1,0:T(8,128)(2,1)S(1)}, u32[]{:S(2)}, u32[]{:S(2)}) collective-permute-start(bf16[2,24,1024]{2,1,0:T(8,128)(2,1)S(1)} %pad_maximum_fusion.1.bases_ref.refs_1_), channel_id=1, source_target_pairs={{0,2},{1,3},{2,0},{3,1},{4,6},{5,7},{6,4},{7,5},{8,10},{9,11},{10,... | collective-permute-start | bytes 294920 | tf_op jit(solution)/shard_map/ppermute | solution.py:127
  3.8 1.0 %convert_element_type.23.block_ref.refs_0_ = bf16[256,256]{1,0:T(8,128)(2,1)S(1)} convert(f32[256,256]{1,0:T(8,128)} %param.7) | non-fusion elementwise | flops 65536 | bytes 393216 | tf_op jit(solution)/shard_map/convert_element_type | solution.py:211
  5.4 2.7 %collective-permute-start.1 = (bf16[256,256]{1,0:T(8,128)(2,1)S(1)}, bf16[256,256]{1,0:T(8,128)(2,1)S(1)}, u32[]{:S(2)}, u32[]{:S(2)}) collective-permute-start(bf16[256,256]{1,0:T(8,128)(2,1)S(1)} %convert_element_type.23.block_ref.refs_0_), channel_id=1, source_target_pairs={{0,4},{4,0},{8,12},{12,8},{1,5},{5,1},{9,13},{13,9},{2,6},{6,2},{1... | collective-permute-start | bytes 393224 | tf_op jit(solution)/shard_map/ppermute | solution.py:111
  9.1 1.8 %collective-permute-start.6 = (bf16[48,256]{1,0:T(8,128)(2,1)S(1)}, bf16[48,256]{1,0:T(8,128)(2,1)S(1)}, u32[]{:S(2)}, u32[]{:S(2)}) collective-permute-start(bf16[48,256]{1,0:T(8,128)(2,1)S(1)} %shard_map.64.refs_3_), channel_id=1, source_target_pairs={{0,12},{4,8},{8,4},{12,0},{1,13},{5,9},{9,5},{13,1},{2,14},{6,10},... | collective-permute-start | bytes 73736 | tf_op jit(solution)/shard_map/ppermute | solution.py:111
  10.9 2.6 %collective-permute-start.4 = (bf16[48,256]{1,0:T(8,128)(2,1)S(1)}, bf16[48,256]{1,0:T(8,128)(2,1)S(1)}, u32[]{:S(2)}, u32[]{:S(2)}) collective-permute-start(bf16[48,256]{1,0:T(8,128)(2,1)S(1)} %shard_map.64.refs_3_), channel_id=1, source_target_pairs={{0,4},{4,0},{8,12},{12,8},{1,5},{5,1},{9,13},{13,9},{2,6},{6,2},{1... | collective-permute-start | bytes 73736 | tf_op jit(solution)/shard_map/ppermute | solution.py:111
  14.2 0.6 %collective-permute-done.6.refs_6_ = bf16[48,256]{1,0:T(8,128)(2,1)S(1)} collective-permute-done((bf16[48,256]{1,0:T(8,128)(2,1)S(1)}, bf16[48,256]{1,0:T(8,128)(2,1)S(1)}, u32[]{:S(2)}, u32[]{:S(2)}) %collective-permute-start.6) | collective-permute-done | bytes 24608 | tf_op jit(solution)/shard_map/ppermute | solution.py:111
  14.8 0.8 %collective-permute-done.5.refs_5_ = bf16[48,256]{1,0:T(8,128)(2,1)S(1)} collective-permute-done((bf16[48,256]{1,0:T(8,128)(2,1)S(1)}, bf16[48,256]{1,0:T(8,128)(2,1)S(1)}, u32[]{:S(2)}, u32[]{:S(2)}) %collective-permute-start.5) | collective-permute-done | bytes 24608 | tf_op jit(solution)/shard_map/ppermute | solution.py:111
  15.7 0.7 %shard_map.65 = (f32[2,256,256]{2,1,0:T(8,128)S(1)}, f32[96,256]{1,0:T(8,128)S(1)}) custom-call(bf16[3,1024,256]{2,1,0:T(8,128)(2,1)S(1)} %bitcast.19, bf16[2,24,1024]{2,1,0:T(8,128)(2,1)S(1)} %pad_maximum_fusion.1.bases_ref.refs_1_, bf16[2,24,1024]{2,1,0:T(8,128)(2,1)S(1)} %collective-permute-done.across_ref.refs_2_, s32[1,1]{1,0:T(1,128)S(6)} %copy.8.columns_ref.refs_3_, ...), custom_call_target="tpu_custom_call" | custom-call | flops 402653184 | bytes 1572864 | tf_op jit(solution)/shard_map/pallas_call | solution.py:73
  16.4 0.7 %shard_map.66 = (f32[2,256,256]{2,1,0:T(8,128)S(1)}, f32[48,256]{1,0:T(8,128)S(1)}, f32[48,256]{1,0:T(8,128)S(1)}) custom-call(bf16[3,1024,256]{2,1,0:T(8,128)(2,1)S(1)} %bitcast.20, bf16[2,24,1024]{2,1,0:T(8,128)(2,1)S(1)} %pad_maximum_fusion.1.bases_ref.refs_1_, bf16[2,24,1024]{2,1,0:T(8,128)(2,1)S(1)} %collective-permute-done.across_ref.refs_2_, ...), custom_call_target="tpu_custom_call" | custom-call | flops 402653184 | bytes 1572864 | tf_op jit(solution)/shard_map/pallas_call | solution.py:73
  17.1 0.6 %collective-permute-start.10 = (f32[48,256]{1,0:T(8,128)S(1)}, f32[48,256]{1,0:T(8,128)S(1)}, u32[]{:S(2)}, u32[]{:S(2)}) collective-permute-start(f32[48,256]{1,0:T(8,128)S(1)} %get-tuple-element.23), channel_id=1, source_target_pairs={{0,1},{1,0},{2,3},{3,2},{4,5},{5,4},{6,7},{7,6},{8,9},{9,8},{10,11... | collective-permute-start | bytes 147464 | tf_op jit(solution)/shard_map/ppermute | solution.py:127
  17.7 0.6 %collective-permute-done.8 = f32[2,256,256]{2,1,0:T(8,128)S(1)} collective-permute-done((f32[2,256,256]{2,1,0:T(8,128)S(1)}, f32[2,256,256]{2,1,0:T(8,128)S(1)}, u32[]{:S(2)}, u32[]{:S(2)}) %collective-permute-start.8) | collective-permute-done | bytes 524320 | tf_op jit(solution)/shard_map/ppermute | solution.py:127
  18.4 1.6 %collective-permute-start.9 = (bf16[256,256]{1,0:T(8,128)(2,1)S(1)}, bf16[256,256]{1,0:T(8,128)(2,1)S(1)}, u32[]{:S(2)}, u32[]{:S(2)}) collective-permute-start(bf16[256,256]{1,0:T(8,128)(2,1)S(1)} %fusion.3), channel_id=1, source_target_pairs={{0,2},{1,3},{2,0},{3,1},{4,6},{5,7},{6,4},{7,5},{8,10},{9,11},{10,... | collective-permute-start | bytes 393224 | tf_op jit(solution)/shard_map/ppermute | solution.py:127
  20.0 1.9 %collective-permute-start.12 = (bf16[48,256]{1,0:T(8,128)(2,1)S(1)}, bf16[48,256]{1,0:T(8,128)(2,1)S(1)}, u32[]{:S(2)}, u32[]{:S(2)}) collective-permute-start(bf16[48,256]{1,0:T(8,128)(2,1)S(1)} %add_convert_fusion.refs_7_), channel_id=1, source_target_pairs={{0,12},{4,8},{8,4},{12,0},{1,13},{5,9},{9,5},{13,1},{2,14},{6,10},... | collective-permute-start | bytes 73736 | tf_op jit(solution)/shard_map/ppermute | solution.py:111
  22.3 1.8 %collective-permute-done.9 = bf16[256,256]{1,0:T(8,128)(2,1)S(1)} collective-permute-done((bf16[256,256]{1,0:T(8,128)(2,1)S(1)}, bf16[256,256]{1,0:T(8,128)(2,1)S(1)}, u32[]{:S(2)}, u32[]{:S(2)}) %collective-permute-start.9) | collective-permute-done | bytes 131104 | tf_op jit(solution)/shard_map/ppermute | solution.py:127
  24.1 1.6 %collective-permute-done.12.refs_10_ = bf16[48,256]{1,0:T(8,128)(2,1)S(1)} collective-permute-done((bf16[48,256]{1,0:T(8,128)(2,1)S(1)}, bf16[48,256]{1,0:T(8,128)(2,1)S(1)}, u32[]{:S(2)}, u32[]{:S(2)}) %collective-permute-start.12) | collective-permute-done | bytes 24608 | tf_op jit(solution)/shard_map/ppermute | solution.py:111
  25.7 0.9 %collective-permute-done.11.refs_9_ = bf16[48,256]{1,0:T(8,128)(2,1)S(1)} collective-permute-done((bf16[48,256]{1,0:T(8,128)(2,1)S(1)}, bf16[48,256]{1,0:T(8,128)(2,1)S(1)}, u32[]{:S(2)}, u32[]{:S(2)}) %collective-permute-start.11) | collective-permute-done | bytes 24608 | tf_op jit(solution)/shard_map/ppermute | solution.py:111
  26.6 0.8 %collective-permute-start.13 = (bf16[304,256]{1,0:T(8,128)(2,1)S(1)}, bf16[304,256]{1,0:T(8,128)(2,1)S(1)}, u32[]{:S(2)}, u32[]{:S(2)}) collective-permute-start(bf16[304,256]{1,0:T(8,128)(2,1)S(1)} %pad_maximum_fusion), channel_id=1, source_target_pairs={{0,4},{4,0},{8,12},{12,8},{1,5},{5,1},{9,13},{13,9},{2,6},{6,2},{1... | collective-permute-start | bytes 466952 | tf_op jit(solution)/shard_map/ppermute | solution.py:111
  27.4 1.3 %collective-permute-done.14.refs_6_ = bf16[256,256]{1,0:T(8,128)(2,1)S(1)} collective-permute-done((bf16[256,256]{1,0:T(8,128)(2,1)S(1)}, bf16[256,256]{1,0:T(8,128)(2,1)S(1)}, u32[]{:S(2)}, u32[]{:S(2)}) %collective-permute-start.14) | collective-permute-done | bytes 131104 | tf_op jit(solution)/shard_map/ppermute | solution.py:123
  28.8 3.1 %collective-permute-done.13.refs_5_.refs_8_ = bf16[304,256]{1,0:T(8,128)(2,1)S(1)} collective-permute-done((bf16[304,256]{1,0:T(8,128)(2,1)S(1)}, bf16[304,256]{1,0:T(8,128)(2,1)S(1)}, u32[]{:S(2)}, u32[]{:S(2)}) %collective-permute-start.13) | collective-permute-done | bytes 155680 | tf_op jit(solution)/shard_map/ppermute | solution.py:111
  32.8 1.5 %collective-permute-done.15 = f32[2,256,256]{2,1,0:T(8,128)S(1)} collective-permute-done((f32[2,256,256]{2,1,0:T(8,128)S(1)}, f32[2,256,256]{2,1,0:T(8,128)S(1)}, u32[]{:S(2)}, u32[]{:S(2)}) %collective-permute-start.15) | collective-permute-done | bytes 524320 | tf_op jit(solution)/shard_map/ppermute | solution.py:127
  34.4 1.1 %collective-permute-start.16 = (bf16[256,256]{1,0:T(8,128)(2,1)S(1)}, bf16[256,256]{1,0:T(8,128)(2,1)S(1)}, u32[]{:S(2)}, u32[]{:S(2)}) collective-permute-start(bf16[256,256]{1,0:T(8,128)(2,1)S(1)} %fusion.4), channel_id=1, source_target_pairs={{0,2},{1,3},{2,0},{3,1},{4,6},{5,7},{6,4},{7,5},{8,10},{9,11},{10,... | collective-permute-start | bytes 393224 | tf_op jit(solution)/shard_map/ppermute | solution.py:127
  35.5 4.5 %collective-permute-done.16 = bf16[256,256]{1,0:T(8,128)(2,1)S(1)} collective-permute-done((bf16[256,256]{1,0:T(8,128)(2,1)S(1)}, bf16[256,256]{1,0:T(8,128)(2,1)S(1)}, u32[]{:S(2)}, u32[]{:S(2)}) %collective-permute-start.16) | collective-permute-done | bytes 131104 | tf_op jit(solution)/shard_map/ppermute | solution.py:127
  40.0 0.7 %fusion = f32[256,256]{1,0:T(8,128)} fusion(f32[2,256,256]{2,1,0:T(8,128)S(1)} %add.18, bf16[256,256]{1,0:T(8,128)(2,1)S(1)} %collective-permute-done.16), kind=kLoop, calls=%fused_computation.2 | loop fusion | flops 131072 | bytes 655360 | tf_op jit(solution)/shard_map/add | solution.py:252
  (30 shorter events, 2.5 us)
Async XLA Ops:
  0.8 7.9 %collective-permute-start = (bf16[2,24,1024]{2,1,0:T(8,128)(2,1)S(1)}, bf16[2,24,1024]{2,1,0:T(8,128)(2,1)S(1)}, u32[]{:S(2)}, u32[]{:S(2)}) collective-permute-start(bf16[2,24,1024]{2,1,0:T(8,128)(2,1)S(1)} %pad_maximum_fusion.1.bases_ref.refs_1_), channel_id=1, source_target_pairs={{0,2},{1,3},{2,0},{3,1},{4,6},{5,7},{6,4},{7,5},{8,10},{9,11},{10,... | collective-permute-start | bytes 294920 | tf_op jit(solution)/shard_map/ppermute | solution.py:127
  4.8 4.0 %collective-permute-start.3 = (bf16[256,256]{1,0:T(8,128)(2,1)S(1)}, bf16[256,256]{1,0:T(8,128)(2,1)S(1)}, u32[]{:S(2)}, u32[]{:S(2)}) collective-permute-start(bf16[256,256]{1,0:T(8,128)(2,1)S(1)} %convert_element_type.23.block_ref.refs_0_), channel_id=1, source_target_pairs={{0,1},{1,0},{2,3},{3,2},{4,5},{5,4},{6,7},{7,6},{8,9},{9,8},{10,11... | collective-permute-start | bytes 393224 | tf_op jit(solution)/shard_map/ppermute | solution.py:127
  4.9 6.0 %collective-permute-start.2 = (bf16[256,256]{1,0:T(8,128)(2,1)S(1)}, bf16[256,256]{1,0:T(8,128)(2,1)S(1)}, u32[]{:S(2)}, u32[]{:S(2)}) collective-permute-start(bf16[256,256]{1,0:T(8,128)(2,1)S(1)} %convert_element_type.23.block_ref.refs_0_), channel_id=1, source_target_pairs={{0,1},{1,0},{2,3},{3,2},{4,8},{5,9},{6,10},{7,11},{8,4},{9,5},{10,... | collective-permute-start | bytes 393224 | tf_op jit(solution)/shard_map/ppermute | solution.py:123
  5.4 8.8 %collective-permute-start.1 = (bf16[256,256]{1,0:T(8,128)(2,1)S(1)}, bf16[256,256]{1,0:T(8,128)(2,1)S(1)}, u32[]{:S(2)}, u32[]{:S(2)}) collective-permute-start(bf16[256,256]{1,0:T(8,128)(2,1)S(1)} %convert_element_type.23.block_ref.refs_0_), channel_id=1, source_target_pairs={{0,4},{4,0},{8,12},{12,8},{1,5},{5,1},{9,13},{13,9},{2,6},{6,2},{1... | collective-permute-start | bytes 393224 | tf_op jit(solution)/shard_map/ppermute | solution.py:111
  8.8 6.9 %copy-start = (bf16[1,1024,3,256]{3,1,2,0:T(8,128)(2,1)S(1)}, bf16[1,1024,3,256]{3,1,2,0:T(8,128)(2,1)}, u32[]{:S(2)}) copy-start(bf16[1,1024,3,256]{3,1,2,0:T(8,128)(2,1)} %param.10) | copy-start | bytes 4718596
  9.0 6.7 %collective-permute-start.7 = (bf16[2,24,1024]{2,1,0:T(8,128)(2,1)S(1)}, bf16[2,24,1024]{2,1,0:T(8,128)(2,1)S(1)}, u32[]{:S(2)}, u32[]{:S(2)}) collective-permute-start(bf16[2,24,1024]{2,1,0:T(8,128)(2,1)S(1)} %pad_maximum_fusion.2), channel_id=1, source_target_pairs={{0,1},{1,0},{2,3},{3,2},{4,5},{5,4},{6,7},{7,6},{8,9},{9,8},{10,11... | collective-permute-start | bytes 294920 | tf_op jit(solution)/shard_map/ppermute | solution.py:127
  9.1 5.7 %collective-permute-start.6 = (bf16[48,256]{1,0:T(8,128)(2,1)S(1)}, bf16[48,256]{1,0:T(8,128)(2,1)S(1)}, u32[]{:S(2)}, u32[]{:S(2)}) collective-permute-start(bf16[48,256]{1,0:T(8,128)(2,1)S(1)} %shard_map.64.refs_3_), channel_id=1, source_target_pairs={{0,12},{4,8},{8,4},{12,0},{1,13},{5,9},{9,5},{13,1},{2,14},{6,10},... | collective-permute-start | bytes 73736 | tf_op jit(solution)/shard_map/ppermute | solution.py:111
  10.9 4.7 %collective-permute-start.5 = (bf16[48,256]{1,0:T(8,128)(2,1)S(1)}, bf16[48,256]{1,0:T(8,128)(2,1)S(1)}, u32[]{:S(2)}, u32[]{:S(2)}) collective-permute-start(bf16[48,256]{1,0:T(8,128)(2,1)S(1)} %shard_map.64.refs_3_), channel_id=1, source_target_pairs={{0,8},{4,12},{8,0},{12,4},{1,9},{5,13},{9,1},{13,5},{2,10},{6,14},... | collective-permute-start | bytes 73736 | tf_op jit(solution)/shard_map/ppermute | solution.py:111
  10.9 4.7 %collective-permute-start.4 = (bf16[48,256]{1,0:T(8,128)(2,1)S(1)}, bf16[48,256]{1,0:T(8,128)(2,1)S(1)}, u32[]{:S(2)}, u32[]{:S(2)}) collective-permute-start(bf16[48,256]{1,0:T(8,128)(2,1)S(1)} %shard_map.64.refs_3_), channel_id=1, source_target_pairs={{0,4},{4,0},{8,12},{12,8},{1,5},{5,1},{9,13},{13,9},{2,6},{6,2},{1... | collective-permute-start | bytes 73736 | tf_op jit(solution)/shard_map/ppermute | solution.py:111
  16.4 2.0 %collective-permute-start.8 = (f32[2,256,256]{2,1,0:T(8,128)S(1)}, f32[2,256,256]{2,1,0:T(8,128)S(1)}, u32[]{:S(2)}, u32[]{:S(2)}) collective-permute-start(f32[2,256,256]{2,1,0:T(8,128)S(1)} %get-tuple-element.21), channel_id=1, source_target_pairs={{0,1},{1,0},{2,3},{3,2},{4,5},{5,4},{6,7},{7,6},{8,9},{9,8},{10,11... | collective-permute-start | bytes 1572872 | tf_op jit(solution)/shard_map/ppermute | solution.py:127
  17.1 2.9 %collective-permute-start.10 = (f32[48,256]{1,0:T(8,128)S(1)}, f32[48,256]{1,0:T(8,128)S(1)}, u32[]{:S(2)}, u32[]{:S(2)}) collective-permute-start(f32[48,256]{1,0:T(8,128)S(1)} %get-tuple-element.23), channel_id=1, source_target_pairs={{0,1},{1,0},{2,3},{3,2},{4,5},{5,4},{6,7},{7,6},{8,9},{9,8},{10,11... | collective-permute-start | bytes 147464 | tf_op jit(solution)/shard_map/ppermute | solution.py:127
  18.4 5.6 %collective-permute-start.9 = (bf16[256,256]{1,0:T(8,128)(2,1)S(1)}, bf16[256,256]{1,0:T(8,128)(2,1)S(1)}, u32[]{:S(2)}, u32[]{:S(2)}) collective-permute-start(bf16[256,256]{1,0:T(8,128)(2,1)S(1)} %fusion.3), channel_id=1, source_target_pairs={{0,2},{1,3},{2,0},{3,1},{4,6},{5,7},{6,4},{7,5},{8,10},{9,11},{10,... | collective-permute-start | bytes 393224 | tf_op jit(solution)/shard_map/ppermute | solution.py:127
  20.0 5.7 %collective-permute-start.12 = (bf16[48,256]{1,0:T(8,128)(2,1)S(1)}, bf16[48,256]{1,0:T(8,128)(2,1)S(1)}, u32[]{:S(2)}, u32[]{:S(2)}) collective-permute-start(bf16[48,256]{1,0:T(8,128)(2,1)S(1)} %add_convert_fusion.refs_7_), channel_id=1, source_target_pairs={{0,12},{4,8},{8,4},{12,0},{1,13},{5,9},{9,5},{13,1},{2,14},{6,10},... | collective-permute-start | bytes 73736 | tf_op jit(solution)/shard_map/ppermute | solution.py:111
  21.9 4.7 %collective-permute-start.11 = (bf16[48,256]{1,0:T(8,128)(2,1)S(1)}, bf16[48,256]{1,0:T(8,128)(2,1)S(1)}, u32[]{:S(2)}, u32[]{:S(2)}) collective-permute-start(bf16[48,256]{1,0:T(8,128)(2,1)S(1)} %add_convert_fusion.refs_7_), channel_id=1, source_target_pairs={{0,8},{4,12},{8,0},{12,4},{1,9},{5,13},{9,1},{13,5},{2,10},{6,14},... | collective-permute-start | bytes 73736 | tf_op jit(solution)/shard_map/ppermute | solution.py:111
  26.6 5.2 %collective-permute-start.13 = (bf16[304,256]{1,0:T(8,128)(2,1)S(1)}, bf16[304,256]{1,0:T(8,128)(2,1)S(1)}, u32[]{:S(2)}, u32[]{:S(2)}) collective-permute-start(bf16[304,256]{1,0:T(8,128)(2,1)S(1)} %pad_maximum_fusion), channel_id=1, source_target_pairs={{0,4},{4,0},{8,12},{12,8},{1,5},{5,1},{9,13},{13,9},{2,6},{6,2},{1... | collective-permute-start | bytes 466952 | tf_op jit(solution)/shard_map/ppermute | solution.py:111
  27.4 1.3 %collective-permute-start.14 = (bf16[256,256]{1,0:T(8,128)(2,1)S(1)}, bf16[256,256]{1,0:T(8,128)(2,1)S(1)}, u32[]{:S(2)}, u32[]{:S(2)}) collective-permute-start(bf16[256,256]{1,0:T(8,128)(2,1)S(1)} %fusion.2.refs_4_), channel_id=1, source_target_pairs={{0,1},{1,0},{2,3},{3,2},{4,8},{5,9},{6,10},{7,11},{8,4},{9,5},{10,... | collective-permute-start | bytes 393224 | tf_op jit(solution)/shard_map/ppermute | solution.py:123
  32.3 2.0 %collective-permute-start.15 = (f32[2,256,256]{2,1,0:T(8,128)S(1)}, f32[2,256,256]{2,1,0:T(8,128)S(1)}, u32[]{:S(2)}, u32[]{:S(2)}) collective-permute-start(f32[2,256,256]{2,1,0:T(8,128)S(1)} %shard_map.68), channel_id=1, source_target_pairs={{0,1},{1,0},{2,3},{3,2},{4,5},{5,4},{6,7},{7,6},{8,9},{9,8},{10,11... | collective-permute-start | bytes 1572872 | tf_op jit(solution)/shard_map/ppermute | solution.py:127
  34.4 5.6 %collective-permute-start.16 = (bf16[256,256]{1,0:T(8,128)(2,1)S(1)}, bf16[256,256]{1,0:T(8,128)(2,1)S(1)}, u32[]{:S(2)}, u32[]{:S(2)}) collective-permute-start(bf16[256,256]{1,0:T(8,128)(2,1)S(1)} %fusion.4), channel_id=1, source_target_pairs={{0,2},{1,3},{2,0},{3,1},{4,6},{5,7},{6,4},{7,5},{8,10},{9,11},{10,... | collective-permute-start | bytes 393224 | tf_op jit(solution)/shard_map/ppermute | solution.py:127

commit v9 on v8

--- a/solution.py
+++ b/solution.py
@@ -128,22 +128,19 @@
 
 
 def image_kernel(turns, near_ref, bases_ref, across_ref, columns_ref, *refs):
-    block_refs, coefficient_refs, out_ref = refs[:3], refs[3:7], refs[7]
+    block_refs, coefficients_ref, out_ref = refs[:3], refs[3], refs[4]
     count = lax.axis_size("tile")
     tile = lax.axis_index("tile")
     me = lax.axis_index("list")
     rows = near_ref.shape[2]
-    chosen = coefficient_refs[0][...]
-    slots = chosen.shape[0]
-    for turn in (1, 2, 3):
-        other_ref = coefficient_refs[turn]
-        other = other_ref[other_ref.shape[0] - slots :, :]
-        chosen = jnp.where(columns_ref[...] == tile ^ turn, other, chosen)
+    chosen = coefficients_ref[0]
+    for column in range(1, count):
+        chosen = jnp.where(columns_ref[...] == column, coefficients_ref[column], chosen)
     odd = lax.rem(tile, 2)
     inside = (tile > 0) & (tile < count - 1)
     blocks = [
         (1, block_refs[0][...]),
-        (2 - 2 * odd, block_refs[1][:rows, :]),
+        (2 - 2 * odd, block_refs[1][...]),
         (2 * odd, jnp.where(inside, block_refs[2][...], 0)),
     ]
     totals = []
@@ -170,7 +167,7 @@
 
 
 def sent_kernel(near_ref, bases_ref, across_ref, columns_ref, *refs):
-    operands, pair_ref, out_ref, sums_ref = refs[:7], *refs[7:]
+    operands, pair_ref, out_ref, sums_ref = refs[:4], *refs[4:]
     totals = image_kernel(
         (1, 3), near_ref, bases_ref, across_ref, columns_ref, *operands, out_ref
     )
@@ -178,7 +175,7 @@
 
 
 def kept_kernel(near_ref, bases_ref, across_ref, columns_ref, *refs):
-    operands, (pair_ref, ranks_ref, sums_ref), outs = refs[:7], refs[7:10], refs[10:]
+    operands, (pair_ref, ranks_ref, sums_ref), outs = refs[:4], refs[4:7], refs[7:]
     totals = image_kernel(
         (0, 2), near_ref, bases_ref, across_ref, columns_ref, *operands, outs[0]
     )
@@ -195,6 +192,11 @@
 
 def second_kernel(turns, *refs):
     image_kernel(turns, *refs)
+
+
+def over_tiles(own):
+    copies = jnp.broadcast_to(own, (lax.axis_size("tile"), *own.shape))
+    return lax.all_to_all(copies, "tile", 0, 0, tiled=True)
 
 
 def one_slot(probes, right_bases, left_bases, near_tiles, tile_ranks, column_rows, row_columns):
@@ -216,13 +218,13 @@
         (bases, bases_across, block, list_swap(block, 1), tile_ranks),
         8 * flops,
     )
-    coefficients = [own] + [tile_swap(own, turn) for turn in (1, 2, 3)]
+    coefficients = over_tiles(own)
     right = jnp.stack([bases[0], bases_across[0]])
     right, _ = lax.optimization_barrier((right, own))
     right_pair = list_swap(right, 1)
 
     fixed = (near, bases, bases_across, row_columns)
-    operands = (*fixed, *beside, *coefficients, right_pair)
+    operands = (*fixed, *beside, coefficients, right_pair)
     send, sums = kernel_call(
         sent_kernel, [halves, ((4 * rank_part, probe_count), F32)], operands, flops
     )
@@ -232,15 +234,13 @@
     )
     own = (small_keep + list_swap(small_send, 1)).astype(BF)
     pair = keep + arrived
-    second, third = tile_swap(own, 2), tile_swap(own, 3)
+    own, pair = lax.optimization_barrier((own, pair))
+    coefficients = over_tiles(own)
     block = (pair[0] + list_swap(pair[1].astype(BF), 2)).astype(BF)
-    message = jnp.concatenate([block, own])
-    message, second, third = lax.optimization_barrier((message, second, third))
-    message = tile_swap(message, 1)
-    beside = [block, message, middle_swap(block)]
-    coefficients = [own, message, second, third]
-
-    operands = (*fixed, *beside, *coefficients)
+    block, coefficients = lax.optimization_barrier((block, coefficients))
+    beside = [block, tile_swap(block, 1), middle_swap(block)]
+
+    operands = (*fixed, *beside, coefficients)
     (send,) = kernel_call(
         functools.partial(second_kernel, (1, 3)), [halves], operands, flops
     )

time: 40.9 us -> 49.7 us (1.22)
  waiting for transfers between devices: 16.8 us -> 23 us
  local copies, waits for them, and re-layouts: 0.05 us -> 1.34 us
  starting transfers between devices: 17.2 us -> 18.4 us
    all_to_all x0 -> x2, waiting for transfers between devices: none -> 10.1 us  [over_tiles(): return lax.all_to_all(copies, 'tile', 0, 0, tiled=True)]
    all_to_all x0 -> x2, starting transfers between devices: none -> 7.99 us  [over_tiles(): return lax.all_to_all(copies, 'tile', 0, 0, tiled=True)]
    ppermute x7 -> x2, starting transfers between devices: 10.3 us -> 4.23 us  [tile_swap(): lax.ppermute(block, 'tile', [(i, i ^ turn) for i in range(lax.axis_size('...]
    ppermute x7 -> x2, waiting for transfers between devices: 7.04 us -> 4.57 us  [tile_swap(): lax.ppermute(block, 'tile', [(i, i ^ turn) for i in range(lax.axis_size('...]
    broadcast_in_dim x0 -> x2, local copies, waits for them, and re-layouts: none -> 1.29 us  [over_tiles(): copies = jnp.broadcast_to(own, (lax.axis_size('tile'), *own.shape))]
    ppermute x2, waiting for transfers between devices: 1.35 us -> 0.11 us  [middle_swap(): return lax.ppermute(block, ('tile', 'list'), route)]
  transfers between devices with their start and end apart: 17 -> 14, of which waited for: 10 -> 9; matrix products, arithmetic and copies ran while one was open for 3% -> 3% of each run, Pallas kernels for 3% -> 3%
where the time goes in v9:
time: 49.7 us; the launch traced here: 49.3 us
  waiting for transfers between devices  23 us (46%)
  starting transfers between devices  18.4 us (37%)
  other arithmetic  2.71 us (5%)
  Pallas kernels  2.36 us (5%)
  between operations  1.47 us (3%)
  local copies, waits for them, and re-layouts  1.34 us (3%)
    all_to_all x2, waiting for transfers between devices, over_tiles(): return lax.all_to_all(copies, 'tile', 0, 0, tiled=True)  10.1 us
    ppermute x8, waiting for transfers between devices, list_swap(): lax.ppermute(block, 'list', [(i, i ^ bit) for i in range(lax.axis_size('l...  8.27 us
    all_to_all x2, starting transfers between devices, over_tiles(): return lax.all_to_all(copies, 'tile', 0, 0, tiled=True)  7.99 us
    ppermute x8, starting transfers between devices, list_swap(): lax.ppermute(block, 'list', [(i, i ^ bit) for i in range(lax.axis_size('l...  6.02 us
    ppermute x2, waiting for transfers between devices, tile_swap(): lax.ppermute(block, 'tile', [(i, i ^ turn) for i in range(lax.axis_size('...  4.57 us
    ppermute x2, starting transfers between devices, tile_swap(): lax.ppermute(block, 'tile', [(i, i ^ turn) for i in range(lax.axis_size('...  4.23 us
    pallas_call x5, Pallas kernels, kernel_call(): pl.pallas_call(kernel, out_shape=tuple((jax.ShapeDtypeStruct(shape, kind)...  2.36 us
    broadcast_in_dim x2, local copies, waits for them, and re-layouts, over_tiles(): copies = jnp.broadcast_to(own, (lax.axis_size('tile'), *own.shape))  1.29 us
  transfers between devices with their start and end apart: 14, of which 9 were waited for; matrix products, arithmetic and copies ran while one was open for 3% of the time, Pallas kernels for 3%

profile of v9, /device:TPU:0, one launch (start us, length us, event | category | flops | bytes accessed | tf_op | source)
XLA Modules:
  0.0 49.3 jit_solution(9158217825157112365)
XLA Ops:
  0.0 0.8 %pad_maximum_fusion.bases_ref.refs_1_ = bf16[2,24,1024]{2,1,0:T(8,128)(2,1)S(1)} fusion(bf16[1,24,1024]{2,1,0:T(8,128)(2,1)} %bitcast.21, bf16[1,24,1024]{2,1,0:T(8,128)(2,1)} %bitcast.22), kind=kLoop, calls=%fused_computation.8 | loop fusion | flops 49152 | bytes 196608 | tf_op jit(solution)/shard_map/stack | solution.py:210
  0.8 1.0 %convert_element_type.23.block_ref.refs_0_ = bf16[256,256]{1,0:T(8,128)(2,1)S(1)} convert(f32[256,256]{1,0:T(8,128)} %param.7) | non-fusion elementwise | flops 65536 | bytes 393216 | tf_op jit(solution)/shard_map/convert_element_type | solution.py:213
  1.8 0.5 %collective-permute-start.3 = (bf16[256,256]{1,0:T(8,128)(2,1)S(1)}, bf16[256,256]{1,0:T(8,128)(2,1)S(1)}, u32[]{:S(2)}, u32[]{:S(2)}) collective-permute-start(bf16[256,256]{1,0:T(8,128)(2,1)S(1)} %convert_element_type.23.block_ref.refs_0_), channel_id=1, source_target_pairs={{0,1},{1,0},{2,3},{3,2},{4,5},{5,4},{6,7},{7,6},{8,9},{9,8},{10,11... | collective-permute-start | bytes 393224 | tf_op jit(solution)/shard_map/ppermute | solution.py:127
  2.3 2.6 %collective-permute-start = (bf16[2,24,1024]{2,1,0:T(8,128)(2,1)S(1)}, bf16[2,24,1024]{2,1,0:T(8,128)(2,1)S(1)}, u32[]{:S(2)}, u32[]{:S(2)}) collective-permute-start(bf16[2,24,1024]{2,1,0:T(8,128)(2,1)S(1)} %pad_maximum_fusion.bases_ref.refs_1_), channel_id=1, source_target_pairs={{0,2},{1,3},{2,0},{3,1},{4,6},{5,7},{6,4},{7,5},{8,10},{9,11},{10,... | collective-permute-start | bytes 294920 | tf_op jit(solution)/shard_map/ppermute | solution.py:127
  5.1 3.0 %collective-permute-start.1 = (bf16[256,256]{1,0:T(8,128)(2,1)S(1)}, bf16[256,256]{1,0:T(8,128)(2,1)S(1)}, u32[]{:S(2)}, u32[]{:S(2)}) collective-permute-start(bf16[256,256]{1,0:T(8,128)(2,1)S(1)} %convert_element_type.23.block_ref.refs_0_), channel_id=1, source_target_pairs={{0,4},{4,0},{8,12},{12,8},{1,5},{5,1},{9,13},{13,9},{2,6},{6,2},{1... | collective-permute-start | bytes 393224 | tf_op jit(solution)/shard_map/ppermute | solution.py:111
  8.9 0.6 %broadcast_in_dim.6 = bf16[4,48,256]{2,1,0:T(8,128)(2,1)} broadcast(bf16[48,256]{1,0:T(8,128)(2,1)S(1)} %shard_map.64), dimensions={1,2} | broadcast | bytes 122880 | tf_op jit(solution)/shard_map/broadcast_in_dim | solution.py:198
  9.6 4.7 %all-to-all-start = ((bf16[4,48,256]{2,1,0:T(8,128)(2,1)}), bf16[4,48,256]{2,1,0:T(8,128)(2,1)S(1)}, u32[]{:S(2)}, u32[]{:S(2)}) async-start(bf16[4,48,256]{2,1,0:T(8,128)(2,1)} %broadcast_in_dim.6), calls=%async_computation | async-start | bytes 196608 | tf_op jit(solution)/shard_map/all_to_all | solution.py:199
  15.0 0.6 %collective-permute-done.4.refs_4_ = bf16[2,24,1024]{2,1,0:T(8,128)(2,1)S(1)} collective-permute-done((bf16[2,24,1024]{2,1,0:T(8,128)(2,1)S(1)}, bf16[2,24,1024]{2,1,0:T(8,128)(2,1)S(1)}, u32[]{:S(2)}, u32[]{:S(2)}) %collective-permute-start.4) | collective-permute-done | bytes 98336 | tf_op jit(solution)/shard_map/ppermute | solution.py:127
  15.6 4.5 %all-to-all-done.refs_3_ = bf16[4,48,256]{2,1,0:T(8,128)(2,1)S(1)} async-done(((bf16[4,48,256]{2,1,0:T(8,128)(2,1)}), bf16[4,48,256]{2,1,0:T(8,128)(2,1)S(1)}, u32[]{:S(2)}, u32[]{:S(2)}) %all-to-all-start) | async-done | bytes 98336 | tf_op jit(solution)/shard_map/all_to_all | solution.py:199
  20.1 0.7 %shard_map.65 = (f32[2,256,256]{2,1,0:T(8,128)S(1)}, f32[96,256]{1,0:T(8,128)S(1)}) custom-call(bf16[3,1024,256]{2,1,0:T(8,128)(2,1)S(1)} %bitcast.17, bf16[2,24,1024]{2,1,0:T(8,128)(2,1)S(1)} %pad_maximum_fusion.bases_ref.refs_1_, bf16[2,24,1024]{2,1,0:T(8,128)(2,1)S(1)} %collective-permute-done.across_ref.refs_2_, s32[1,1]{1,0:T(1,128)S(6)} %copy.8.columns_ref.refs_3_, ...), custom_call_target="tpu_custom_call" | custom-call | flops 402653184 | bytes 1572864 | tf_op jit(solution)/shard_map/pallas_call | solution.py:73
  20.8 0.7 %shard_map.66 = (f32[2,256,256]{2,1,0:T(8,128)S(1)}, f32[48,256]{1,0:T(8,128)S(1)}, f32[48,256]{1,0:T(8,128)S(1)}) custom-call(bf16[3,1024,256]{2,1,0:T(8,128)(2,1)S(1)} %bitcast.18, bf16[2,24,1024]{2,1,0:T(8,128)(2,1)S(1)} %pad_maximum_fusion.bases_ref.refs_1_, bf16[2,24,1024]{2,1,0:T(8,128)(2,1)S(1)} %collective-permute-done.across_ref.refs_2_, ...), custom_call_target="tpu_custom_call" | custom-call | flops 402653184 | bytes 1572864 | tf_op jit(solution)/shard_map/pallas_call | solution.py:73
  21.5 0.6 %collective-permute-start.5 = (f32[48,256]{1,0:T(8,128)S(1)}, f32[48,256]{1,0:T(8,128)S(1)}, u32[]{:S(2)}, u32[]{:S(2)}) collective-permute-start(f32[48,256]{1,0:T(8,128)S(1)} %get-tuple-element.22), channel_id=1, source_target_pairs={{0,1},{1,0},{2,3},{3,2},{4,5},{5,4},{6,7},{7,6},{8,9},{9,8},{10,11... | collective-permute-start | bytes 147464 | tf_op jit(solution)/shard_map/ppermute | solution.py:127
  22.1 0.9 %collective-permute-done.5 = f32[48,256]{1,0:T(8,128)S(1)} collective-permute-done((f32[48,256]{1,0:T(8,128)S(1)}, f32[48,256]{1,0:T(8,128)S(1)}, u32[]{:S(2)}, u32[]{:S(2)}) %collective-permute-start.5) | collective-permute-done | bytes 49184 | tf_op jit(solution)/shard_map/ppermute | solution.py:127
  23.1 1.6 %collective-permute-start.7 = (bf16[256,256]{1,0:T(8,128)(2,1)S(1)}, bf16[256,256]{1,0:T(8,128)(2,1)S(1)}, u32[]{:S(2)}, u32[]{:S(2)}) collective-permute-start(bf16[256,256]{1,0:T(8,128)(2,1)S(1)} %fusion.2), channel_id=1, source_target_pairs={{0,2},{1,3},{2,0},{3,1},{4,6},{5,7},{6,4},{7,5},{8,10},{9,11},{10,... | collective-permute-start | bytes 393224 | tf_op jit(solution)/shard_map/ppermute | solution.py:127
  24.7 0.6 %broadcast_in_dim.7 = bf16[4,48,256]{2,1,0:T(8,128)(2,1)} broadcast(bf16[48,256]{1,0:T(8,128)(2,1)S(1)} %add_convert_fusion), dimensions={1,2} | broadcast | bytes 122880 | tf_op jit(solution)/shard_map/broadcast_in_dim | solution.py:198
  25.3 3.3 %all-to-all-start.1 = ((bf16[4,48,256]{2,1,0:T(8,128)(2,1)}), bf16[4,48,256]{2,1,0:T(8,128)(2,1)S(1)}, u32[]{:S(2)}, u32[]{:S(2)}) async-start(bf16[4,48,256]{2,1,0:T(8,128)(2,1)} %broadcast_in_dim.7), calls=%async_computation.1 | async-start | bytes 196608 | tf_op jit(solution)/shard_map/all_to_all | solution.py:199
  28.9 5.6 %all-to-all-done.1.refs_7_ = bf16[4,48,256]{2,1,0:T(8,128)(2,1)S(1)} async-done(((bf16[4,48,256]{2,1,0:T(8,128)(2,1)}), bf16[4,48,256]{2,1,0:T(8,128)(2,1)S(1)}, u32[]{:S(2)}, u32[]{:S(2)}) %all-to-all-start.1) | async-done | bytes 98336 | tf_op jit(solution)/shard_map/all_to_all | solution.py:199
  34.6 1.2 %collective-permute-start.8 = (bf16[256,256]{1,0:T(8,128)(2,1)S(1)}, bf16[256,256]{1,0:T(8,128)(2,1)S(1)}, u32[]{:S(2)}, u32[]{:S(2)}) collective-permute-start(bf16[256,256]{1,0:T(8,128)(2,1)S(1)} %fusion.1.refs_4_), channel_id=1, source_target_pairs={{0,4},{4,0},{8,12},{12,8},{1,5},{5,1},{9,13},{13,9},{2,6},{6,2},{1... | collective-permute-start | bytes 393224 | tf_op jit(solution)/shard_map/ppermute | solution.py:111
  35.9 4.6 %collective-permute-done.8.refs_5_ = bf16[256,256]{1,0:T(8,128)(2,1)S(1)} collective-permute-done((bf16[256,256]{1,0:T(8,128)(2,1)S(1)}, bf16[256,256]{1,0:T(8,128)(2,1)S(1)}, u32[]{:S(2)}, u32[]{:S(2)}) %collective-permute-start.8) | collective-permute-done | bytes 131104 | tf_op jit(solution)/shard_map/ppermute | solution.py:111
  41.0 0.4 shard_map.67
  41.4 1.5 %collective-permute-done.10 = f32[2,256,256]{2,1,0:T(8,128)S(1)} collective-permute-done((f32[2,256,256]{2,1,0:T(8,128)S(1)}, f32[2,256,256]{2,1,0:T(8,128)S(1)}, u32[]{:S(2)}, u32[]{:S(2)}) %collective-permute-start.10) | collective-permute-done | bytes 524320 | tf_op jit(solution)/shard_map/ppermute | solution.py:127
  43.0 0.6 %collective-permute-start.11 = (bf16[256,256]{1,0:T(8,128)(2,1)S(1)}, bf16[256,256]{1,0:T(8,128)(2,1)S(1)}, u32[]{:S(2)}, u32[]{:S(2)}) collective-permute-start(bf16[256,256]{1,0:T(8,128)(2,1)S(1)} %fusion.3), channel_id=1, source_target_pairs={{0,2},{1,3},{2,0},{3,1},{4,6},{5,7},{6,4},{7,5},{8,10},{9,11},{10,... | collective-permute-start | bytes 393224 | tf_op jit(solution)/shard_map/ppermute | solution.py:127
  43.6 5.0 %collective-permute-done.11 = bf16[256,256]{1,0:T(8,128)(2,1)S(1)} collective-permute-done((bf16[256,256]{1,0:T(8,128)(2,1)S(1)}, bf16[256,256]{1,0:T(8,128)(2,1)S(1)}, u32[]{:S(2)}, u32[]{:S(2)}) %collective-permute-start.11) | collective-permute-done | bytes 131104 | tf_op jit(solution)/shard_map/ppermute | solution.py:127
  48.6 0.7 %fusion = f32[256,256]{1,0:T(8,128)} fusion(f32[2,256,256]{2,1,0:T(8,128)S(1)} %add.18, bf16[256,256]{1,0:T(8,128)(2,1)S(1)} %collective-permute-done.11), kind=kLoop, calls=%fused_computation.2 | loop fusion | flops 131072 | bytes 655360 | tf_op jit(solution)/shard_map/add | solution.py:252
  (25 shorter events, 1.6 us)
Async XLA Ops:
  1.8 6.9 %collective-permute-start.3 = (bf16[256,256]{1,0:T(8,128)(2,1)S(1)}, bf16[256,256]{1,0:T(8,128)(2,1)S(1)}, u32[]{:S(2)}, u32[]{:S(2)}) collective-permute-start(bf16[256,256]{1,0:T(8,128)(2,1)S(1)} %convert_element_type.23.block_ref.refs_0_), channel_id=1, source_target_pairs={{0,1},{1,0},{2,3},{3,2},{4,5},{5,4},{6,7},{7,6},{8,9},{9,8},{10,11... | collective-permute-start | bytes 393224 | tf_op jit(solution)/shard_map/ppermute | solution.py:127
  2.3 6.4 %collective-permute-start = (bf16[2,24,1024]{2,1,0:T(8,128)(2,1)S(1)}, bf16[2,24,1024]{2,1,0:T(8,128)(2,1)S(1)}, u32[]{:S(2)}, u32[]{:S(2)}) collective-permute-start(bf16[2,24,1024]{2,1,0:T(8,128)(2,1)S(1)} %pad_maximum_fusion.bases_ref.refs_1_), channel_id=1, source_target_pairs={{0,2},{1,3},{2,0},{3,1},{4,6},{5,7},{6,4},{7,5},{8,10},{9,11},{10,... | collective-permute-start | bytes 294920 | tf_op jit(solution)/shard_map/ppermute | solution.py:127
  4.9 10.1 %collective-permute-start.2 = (bf16[256,256]{1,0:T(8,128)(2,1)S(1)}, bf16[256,256]{1,0:T(8,128)(2,1)S(1)}, u32[]{:S(2)}, u32[]{:S(2)}) collective-permute-start(bf16[256,256]{1,0:T(8,128)(2,1)S(1)} %convert_element_type.23.block_ref.refs_0_), channel_id=1, source_target_pairs={{0,1},{1,0},{2,3},{3,2},{4,8},{5,9},{6,10},{7,11},{8,4},{9,5},{10,... | collective-permute-start | bytes 393224 | tf_op jit(solution)/shard_map/ppermute | solution.py:123
  5.1 9.9 %collective-permute-start.1 = (bf16[256,256]{1,0:T(8,128)(2,1)S(1)}, bf16[256,256]{1,0:T(8,128)(2,1)S(1)}, u32[]{:S(2)}, u32[]{:S(2)}) collective-permute-start(bf16[256,256]{1,0:T(8,128)(2,1)S(1)} %convert_element_type.23.block_ref.refs_0_), channel_id=1, source_target_pairs={{0,4},{4,0},{8,12},{12,8},{1,5},{5,1},{9,13},{13,9},{2,6},{6,2},{1... | collective-permute-start | bytes 393224 | tf_op jit(solution)/shard_map/ppermute | solution.py:111
  8.7 11.4 %copy-start = (bf16[1,1024,3,256]{3,1,2,0:T(8,128)(2,1)S(1)}, bf16[1,1024,3,256]{3,1,2,0:T(8,128)(2,1)}, u32[]{:S(2)}) copy-start(bf16[1,1024,3,256]{3,1,2,0:T(8,128)(2,1)} %param.10) | copy-start | bytes 4718596
  9.6 10.5 %all-to-all-start = ((bf16[4,48,256]{2,1,0:T(8,128)(2,1)}), bf16[4,48,256]{2,1,0:T(8,128)(2,1)S(1)}, u32[]{:S(2)}, u32[]{:S(2)}) async-start(bf16[4,48,256]{2,1,0:T(8,128)(2,1)} %broadcast_in_dim.6), calls=%async_computation | async-start | bytes 196608 | tf_op jit(solution)/shard_map/all_to_all | solution.py:199
  14.3 1.4 %collective-permute-start.4 = (bf16[2,24,1024]{2,1,0:T(8,128)(2,1)S(1)}, bf16[2,24,1024]{2,1,0:T(8,128)(2,1)S(1)}, u32[]{:S(2)}, u32[]{:S(2)}) collective-permute-start(bf16[2,24,1024]{2,1,0:T(8,128)(2,1)S(1)} %pad_maximum_fusion.1), channel_id=1, source_target_pairs={{0,1},{1,0},{2,3},{3,2},{4,5},{5,4},{6,7},{7,6},{8,9},{9,8},{10,11... | collective-permute-start | bytes 294920 | tf_op jit(solution)/shard_map/ppermute | solution.py:127
  20.8 2.2 %collective-permute-start.6 = (f32[2,256,256]{2,1,0:T(8,128)S(1)}, f32[2,256,256]{2,1,0:T(8,128)S(1)}, u32[]{:S(2)}, u32[]{:S(2)}) collective-permute-start(f32[2,256,256]{2,1,0:T(8,128)S(1)} %get-tuple-element.24), channel_id=1, source_target_pairs={{0,1},{1,0},{2,3},{3,2},{4,5},{5,4},{6,7},{7,6},{8,9},{9,8},{10,11... | collective-permute-start | bytes 1572872 | tf_op jit(solution)/shard_map/ppermute | solution.py:127
  21.5 1.4 %collective-permute-start.5 = (f32[48,256]{1,0:T(8,128)S(1)}, f32[48,256]{1,0:T(8,128)S(1)}, u32[]{:S(2)}, u32[]{:S(2)}) collective-permute-start(f32[48,256]{1,0:T(8,128)S(1)} %get-tuple-element.22), channel_id=1, source_target_pairs={{0,1},{1,0},{2,3},{3,2},{4,5},{5,4},{6,7},{7,6},{8,9},{9,8},{10,11... | collective-permute-start | bytes 147464 | tf_op jit(solution)/shard_map/ppermute | solution.py:127
  23.1 5.8 %collective-permute-start.7 = (bf16[256,256]{1,0:T(8,128)(2,1)S(1)}, bf16[256,256]{1,0:T(8,128)(2,1)S(1)}, u32[]{:S(2)}, u32[]{:S(2)}) collective-permute-start(bf16[256,256]{1,0:T(8,128)(2,1)S(1)} %fusion.2), channel_id=1, source_target_pairs={{0,2},{1,3},{2,0},{3,1},{4,6},{5,7},{6,4},{7,5},{8,10},{9,11},{10,... | collective-permute-start | bytes 393224 | tf_op jit(solution)/shard_map/ppermute | solution.py:127
  25.3 9.3 %all-to-all-start.1 = ((bf16[4,48,256]{2,1,0:T(8,128)(2,1)}), bf16[4,48,256]{2,1,0:T(8,128)(2,1)S(1)}, u32[]{:S(2)}, u32[]{:S(2)}) async-start(bf16[4,48,256]{2,1,0:T(8,128)(2,1)} %broadcast_in_dim.7), calls=%async_computation.1 | async-start | bytes 196608 | tf_op jit(solution)/shard_map/all_to_all | solution.py:199
  34.6 1.3 %collective-permute-start.9 = (bf16[256,256]{1,0:T(8,128)(2,1)S(1)}, bf16[256,256]{1,0:T(8,128)(2,1)S(1)}, u32[]{:S(2)}, u32[]{:S(2)}) collective-permute-start(bf16[256,256]{1,0:T(8,128)(2,1)S(1)} %fusion.1.refs_4_), channel_id=1, source_target_pairs={{0,1},{1,0},{2,3},{3,2},{4,8},{5,9},{6,10},{7,11},{8,4},{9,5},{10,... | collective-permute-start | bytes 393224 | tf_op jit(solution)/shard_map/ppermute | solution.py:123
  34.6 5.9 %collective-permute-start.8 = (bf16[256,256]{1,0:T(8,128)(2,1)S(1)}, bf16[256,256]{1,0:T(8,128)(2,1)S(1)}, u32[]{:S(2)}, u32[]{:S(2)}) collective-permute-start(bf16[256,256]{1,0:T(8,128)(2,1)S(1)} %fusion.1.refs_4_), channel_id=1, source_target_pairs={{0,4},{4,0},{8,12},{12,8},{1,5},{5,1},{9,13},{13,9},{2,6},{6,2},{1... | collective-permute-start | bytes 393224 | tf_op jit(solution)/shard_map/ppermute | solution.py:111
  40.9 2.0 %collective-permute-start.10 = (f32[2,256,256]{2,1,0:T(8,128)S(1)}, f32[2,256,256]{2,1,0:T(8,128)S(1)}, u32[]{:S(2)}, u32[]{:S(2)}) collective-permute-start(f32[2,256,256]{2,1,0:T(8,128)S(1)} %shard_map.68), channel_id=1, source_target_pairs={{0,1},{1,0},{2,3},{3,2},{4,5},{5,4},{6,7},{7,6},{8,9},{9,8},{10,11... | collective-permute-start | bytes 1572872 | tf_op jit(solution)/shard_map/ppermute | solution.py:127
  43.0 5.6 %collective-permute-start.11 = (bf16[256,256]{1,0:T(8,128)(2,1)S(1)}, bf16[256,256]{1,0:T(8,128)(2,1)S(1)}, u32[]{:S(2)}, u32[]{:S(2)}) collective-permute-start(bf16[256,256]{1,0:T(8,128)(2,1)S(1)} %fusion.3), channel_id=1, source_target_pairs={{0,2},{1,3},{2,0},{3,1},{4,6},{5,7},{6,4},{7,5},{8,10},{9,11},{10,... | collective-permute-start | bytes 393224 | tf_op jit(solution)/shard_map/ppermute | solution.py:127

commit v10 on v8

--- a/solution.py
+++ b/solution.py
@@ -86,25 +86,31 @@
     return jnp.concatenate([piece.astype(F32) for piece in pieces]).astype(BF)
 
 
-def under_rank(values, group, rank_part, ranks_ref):
-    level = group * rank_part + lax.broadcasted_iota(jnp.int32, values.shape, 0)
-    return jnp.where(level < ranks_ref[...], values, 0.0)
-
-
-def coefficient_kernel(bases_ref, across_ref, block_ref, other_ref, ranks_ref, out_ref):
+def under_rank(sums, turns, rank_part, ranks_ref):
     me = lax.axis_index("list")
-    ranks = bases_ref.shape[1]
+    groups = []
+    for index, turn in enumerate(turns):
+        values = sums[index * rank_part : (index + 1) * rank_part]
+        level = (me ^ turn) * rank_part + lax.broadcasted_iota(jnp.int32, values.shape, 0)
+        groups.append(jnp.where(level < ranks_ref[...], values, 0.0))
+    return groups
+
+
+def basis_groups(side, cut, refs):
+    pieces = [ref[side, :, cut] for ref in refs[:2]]
+    return stacked(pieces + [ref[index, :, cut] for ref in refs[2:] for index in range(2)])
+
+
+def coefficient_kernel(bases_ref, across_ref, block_ref, beside_ref, ranks_ref, out_ref):
+    me = lax.axis_index("list")
     rows = block_ref.shape[0]
     total = 0.0
-    for part, operand_ref in ((me, block_ref), (me ^ 1, other_ref)):
+    for part, operand_ref in ((me, block_ref), (me ^ 1, beside_ref)):
         cut = pl.ds(pl.multiple_of(part * rows, rows), rows)
-        bases = stacked([bases_ref[0, :, cut], across_ref[0, :, cut]])
+        bases = basis_groups(0, cut, (bases_ref, across_ref))
         total += jnp.dot(bases, operand_ref[...], preferred_element_type=F32)
-    halves = [
-        under_rank(total[index * ranks : (index + 1) * ranks], group, ranks, ranks_ref)
-        for index, group in enumerate((me, me ^ 2))
-    ]
-    out_ref[...] = jnp.concatenate(halves).astype(out_ref.dtype)
+    groups = under_rank(total, (0, 2), bases_ref.shape[1], ranks_ref)
+    out_ref[...] = jnp.concatenate(groups).astype(out_ref.dtype)
 
 
 def tile_swap(block, turn):
@@ -123,22 +129,45 @@
     return lax.ppermute(block, ("tile", "list"), route)
 
 
+def far_swap(block):
+    tiles, parts = lax.axis_size("tile"), lax.axis_size("list")
+    route = [
+        (tile * parts + part, (tile ^ (2 + part % 2)) * parts + part)
+        for tile in range(tiles)
+        for part in range(parts)
+    ]
+    return lax.ppermute(block, ("tile", "list"), route)
+
+
 def list_swap(block, bit):
     return lax.ppermute(block, "list", [(i, i ^ bit) for i in range(lax.axis_size("list"))])
 
 
-def image_kernel(turns, near_ref, bases_ref, across_ref, columns_ref, *refs):
-    block_refs, coefficient_refs, out_ref = refs[:3], refs[3:7], refs[7]
+def near_choice(columns, tile, me, refs):
+    chosen = refs[0][...]
+    for turn in (1, 2, 3):
+        chosen = jnp.where(columns == tile ^ turn, refs[turn][...], chosen)
+    return chosen
+
+
+def far_choice(columns, tile, me, refs):
+    own_ref, message_ref, far_ref = refs
+    half = own_ref.shape[0] // 2
+    first = jnp.where(columns == tile, own_ref[:half, :], 0)
+    first = jnp.where(columns == tile ^ 1, message_ref[message_ref.shape[0] - half :, :], first)
+    far = columns == tile ^ (2 + lax.rem(me, 2))
+    return jnp.concatenate(
+        [jnp.where(far, far_ref[:half, :], first), jnp.where(far, far_ref[half:, :], 0)]
+    )
+
+
+def image_kernel(choice, turns, near_ref, columns_ref, bases_refs, *refs):
+    block_refs, coefficient_refs, out_ref = refs[:3], refs[3:-1], refs[-1]
     count = lax.axis_size("tile")
     tile = lax.axis_index("tile")
     me = lax.axis_index("list")
     rows = near_ref.shape[2]
-    chosen = coefficient_refs[0][...]
-    slots = chosen.shape[0]
-    for turn in (1, 2, 3):
-        other_ref = coefficient_refs[turn]
-        other = other_ref[other_ref.shape[0] - slots :, :]
-        chosen = jnp.where(columns_ref[...] == tile ^ turn, other, chosen)
+    chosen = choice(columns_ref[...], tile, me, coefficient_refs)
     odd = lax.rem(tile, 2)
     inside = (tile > 0) & (tile < count - 1)
     blocks = [
@@ -150,7 +179,7 @@
     for index, turn in enumerate(turns):
         part = me ^ turn
         cut = pl.ds(pl.multiple_of(part * rows, rows), rows)
-        left = stacked([bases_ref[1, :, cut], across_ref[1, :, cut]])
+        left = basis_groups(1, cut, bases_refs)
         total = lax.dot_general(
             left, chosen, (((0,), (0,)), ((), ())), preferred_element_type=F32
         )
@@ -161,40 +190,34 @@
     return totals
 
 
-def right_products(totals, bases_ref, across_ref, pair_ref):
-    sums = 0.0
-    for cut, total in totals:
-        groups = [bases_ref[0, :, cut], across_ref[0, :, cut], pair_ref[0, :, cut], pair_ref[1, :, cut]]
-        sums += jnp.dot(stacked(groups), total, preferred_element_type=F32)
-    return sums
-
-
-def sent_kernel(near_ref, bases_ref, across_ref, columns_ref, *refs):
-    operands, pair_ref, out_ref, sums_ref = refs[:7], *refs[7:]
+def right_products(totals, bases_refs):
+    return sum(
+        jnp.dot(basis_groups(0, cut, bases_refs), total, preferred_element_type=F32)
+        for cut, total in totals
+    )
+
+
+def sent_kernel(near_ref, columns_ref, bases_ref, across_ref, other_ref, *refs):
+    bases_refs = (bases_ref, across_ref)
+    totals = image_kernel(near_choice, (1, 3), near_ref, columns_ref, bases_refs, *refs[:-1])
+    refs[-1][...] = right_products(totals, (*bases_refs, other_ref))
+
+
+def kept_kernel(near_ref, columns_ref, bases_ref, across_ref, other_ref, *refs):
+    operands, (ranks_ref, sums_ref, out_ref, own_ref, send_ref) = refs[:-5], refs[-5:]
+    bases_refs = (bases_ref, across_ref)
     totals = image_kernel(
-        (1, 3), near_ref, bases_ref, across_ref, columns_ref, *operands, out_ref
-    )
-    sums_ref[...] = right_products(totals, bases_ref, across_ref, pair_ref)
-
-
-def kept_kernel(near_ref, bases_ref, across_ref, columns_ref, *refs):
-    operands, (pair_ref, ranks_ref, sums_ref), outs = refs[:7], refs[7:10], refs[10:]
-    totals = image_kernel(
-        (0, 2), near_ref, bases_ref, across_ref, columns_ref, *operands, outs[0]
-    )
-    sums = sums_ref[...] + right_products(totals, bases_ref, across_ref, pair_ref)
-    me = lax.axis_index("list")
-    ranks = bases_ref.shape[1]
-    for index, turn in enumerate((0, 2, 1, 3)):
-        values = sums[index * ranks : (index + 1) * ranks]
-        start = index % 2 * ranks
-        outs[1 + index // 2][start : start + ranks, :] = under_rank(
-            values, me ^ turn, ranks, ranks_ref
-        )
-
-
-def second_kernel(turns, *refs):
-    image_kernel(turns, *refs)
+        near_choice, (0, 2), near_ref, columns_ref, bases_refs, *operands, out_ref
+    )
+    sums = sums_ref[...] + right_products(totals, (*bases_refs, other_ref))
+    groups = under_rank(sums, (0, 2, 1, 3), bases_ref.shape[1], ranks_ref)
+    own_ref[...] = jnp.concatenate(groups)
+    send_ref[...] = jnp.concatenate(groups[2:] + groups[:2])
+
+
+def second_kernel(turns, near_ref, columns_ref, bases_ref, across_ref, other_ref, *refs):
+    bases_refs = (bases_ref, across_ref, other_ref)
+    image_kernel(far_choice, turns, near_ref, columns_ref, bases_refs, *refs)
 
 
 def one_slot(probes, right_bases, left_bases, near_tiles, tile_ranks, column_rows, row_columns):
@@ -203,44 +226,42 @@
     near = near_tiles[0].transpose(1, 0, 2)
     flops = 2 * near.size * probe_count
     halves = ((2, rows, probe_count), F32)
-    small = ((2 * rank_part, probe_count), F32)
+    ranks = 4 * rank_part
 
     bases = jnp.stack([right_bases[0, 0], left_bases[0, 0]])
     bases, probes = lax.optimization_barrier((bases, probes))
-    bases_across = list_swap(bases, 2)
+    across = list_swap(bases, 2)
     block = probes.astype(BF)
     beside = [block, tile_swap(block, 1), middle_swap(block)]
     (own,) = kernel_call(
         coefficient_kernel,
-        [((2 * rank_part, probe_count), BF)],
-        (bases, bases_across, block, list_swap(block, 1), tile_ranks),
+        [((ranks // 2, probe_count), BF)],
+        (bases, across, block, list_swap(block, 1), tile_ranks),
         8 * flops,
     )
     coefficients = [own] + [tile_swap(own, turn) for turn in (1, 2, 3)]
-    right = jnp.stack([bases[0], bases_across[0]])
-    right, _ = lax.optimization_barrier((right, own))
-    right_pair = list_swap(right, 1)
-
-    fixed = (near, bases, bases_across, row_columns)
-    operands = (*fixed, *beside, *coefficients, right_pair)
-    send, sums = kernel_call(
-        sent_kernel, [halves, ((4 * rank_part, probe_count), F32)], operands, flops
-    )
+    right, _ = lax.optimization_barrier((jnp.stack([bases[0], across[0]]), own))
+    fixed = (near, row_columns, bases, across)
+    operands = (*fixed, list_swap(right, 1), *beside, *coefficients)
+    send, sums = kernel_call(sent_kernel, [halves, ((ranks, probe_count), F32)], operands, flops)
     arrived = list_swap(send, 1)
-    keep, small_keep, small_send = kernel_call(
-        kept_kernel, [halves, small, small], (*operands, tile_ranks, sums), flops
-    )
-    own = (small_keep + list_swap(small_send, 1)).astype(BF)
+    keep, own, send = kernel_call(
+        kept_kernel,
+        [halves] + [((ranks, probe_count), F32)] * 2,
+        (*operands, tile_ranks, sums),
+        flops,
+    )
+    own = (own + list_swap(send, 1)).astype(BF)
     pair = keep + arrived
-    second, third = tile_swap(own, 2), tile_swap(own, 3)
+    held, held_across, pair = lax.optimization_barrier((bases, across, pair))
+    left = list_swap(jnp.stack([held[1], held_across[1]]), 1)
+    far = far_swap(own)
     block = (pair[0] + list_swap(pair[1].astype(BF), 2)).astype(BF)
-    message = jnp.concatenate([block, own])
-    message, second, third = lax.optimization_barrier((message, second, third))
+    message, far = lax.optimization_barrier((jnp.concatenate([block, own[: ranks // 2]]), far))
     message = tile_swap(message, 1)
     beside = [block, message, middle_swap(block)]
-    coefficients = [own, message, second, third]
-
-    operands = (*fixed, *beside, *coefficients)
+
+    operands = (*fixed, left, *beside, own, message, far)
     (send,) = kernel_call(
         functools.partial(second_kernel, (1, 3)), [halves], operands, flops
     )

time: 40.9 us -> 40.2 us (0.983)
  waiting for transfers between devices: 16.8 us -> 16 us
    ppermute x7 -> x5, waiting for transfers between devices: 7.04 us -> 4.41 us  [tile_swap(): lax.ppermute(block, 'tile', [(i, i ^ turn) for i in range(lax.axis_size('...]
    ppermute x7 -> x5, starting transfers between devices: 10.3 us -> 8.07 us  [tile_swap(): lax.ppermute(block, 'tile', [(i, i ^ turn) for i in range(lax.axis_size('...]
    ppermute x0 -> x1, starting transfers between devices: none -> 2.09 us  [far_swap(): return lax.ppermute(block, ('tile', 'list'), route)]
    ppermute x0 -> x1, waiting for transfers between devices: none -> 1.75 us  [far_swap(): return lax.ppermute(block, ('tile', 'list'), route)]
    ppermute x8 -> x9, waiting for transfers between devices: 8.38 us -> 9.84 us  [list_swap(): lax.ppermute(block, 'list', [(i, i ^ bit) for i in range(lax.axis_size('l...]
    ppermute x2, waiting for transfers between devices: 1.35 us -> 0.01 us  [middle_swap(): return lax.ppermute(block, ('tile', 'list'), route)]
    ppermute x8 -> x9, starting transfers between devices: 6.48 us -> 6.55 us  [list_swap(): lax.ppermute(block, 'list', [(i, i ^ bit) for i in range(lax.axis_size('l...]
  transfers between devices with their start and end apart: 17 -> 17, of which waited for: 10 -> 9; matrix products, arithmetic and copies ran while one was open for 3% -> 3% of each run, Pallas kernels for 3% -> 3%
where the time goes in v10:
time: 40.2 us; the launch traced here: 40 us
  starting transfers between devices  17.3 us (43%)
  waiting for transfers between devices  16 us (40%)
  other arithmetic  2.77 us (7%)
  Pallas kernels  2.41 us (6%)
  between operations  1.51 us (4%)
    ppermute x9, waiting for transfers between devices, list_swap(): lax.ppermute(block, 'list', [(i, i ^ bit) for i in range(lax.axis_size('l...  9.84 us
    ppermute x5, starting transfers between devices, tile_swap(): lax.ppermute(block, 'tile', [(i, i ^ turn) for i in range(lax.axis_size('...  8.07 us
    ppermute x9, starting transfers between devices, list_swap(): lax.ppermute(block, 'list', [(i, i ^ bit) for i in range(lax.axis_size('l...  6.55 us
    ppermute x5, waiting for transfers between devices, tile_swap(): lax.ppermute(block, 'tile', [(i, i ^ turn) for i in range(lax.axis_size('...  4.41 us
    pallas_call x5, Pallas kernels, kernel_call(): pl.pallas_call(kernel, out_shape=tuple((jax.ShapeDtypeStruct(shape, kind)...  2.41 us
    ppermute x1, starting transfers between devices, far_swap(): return lax.ppermute(block, ('tile', 'list'), route)  2.09 us
    ppermute x1, waiting for transfers between devices, far_swap(): return lax.ppermute(block, ('tile', 'list'), route)  1.75 us
    convert_element_type x1, other arithmetic, one_slot(): block = probes.astype(BF)  0.96 us
  transfers between devices with their start and end apart: 17, of which 9 were waited for; matrix products, arithmetic and copies ran while one was open for 3% of the time, Pallas kernels for 3%

profile of v10, /device:TPU:0, one launch (start us, length us, event | category | flops | bytes accessed | tf_op | source)
XLA Modules:
  0.0 40.0 jit_solution(1314803226702083894)
XLA Ops:
  0.0 0.8 %pad_maximum_fusion.1.bases_ref = bf16[2,24,1024]{2,1,0:T(8,128)(2,1)S(1)} fusion(bf16[1,24,1024]{2,1,0:T(8,128)(2,1)} %bitcast.21, bf16[1,24,1024]{2,1,0:T(8,128)(2,1)} %bitcast.22), kind=kLoop, calls=%fused_computation.9 | loop fusion | flops 49152 | bytes 196608 | tf_op jit(solution)/shard_map/stack | solution.py:231
  0.8 3.0 %collective-permute-start = (bf16[2,24,1024]{2,1,0:T(8,128)(2,1)S(1)}, bf16[2,24,1024]{2,1,0:T(8,128)(2,1)S(1)}, u32[]{:S(2)}, u32[]{:S(2)}) collective-permute-start(bf16[2,24,1024]{2,1,0:T(8,128)(2,1)S(1)} %pad_maximum_fusion.1.bases_ref), channel_id=1, source_target_pairs={{0,2},{1,3},{2,0},{3,1},{4,6},{5,7},{6,4},{7,5},{8,10},{9,11},{10,... | collective-permute-start | bytes 294920 | tf_op jit(solution)/shard_map/ppermute | solution.py:143
  3.8 1.0 %convert_element_type.23.block_ref.refs_0_ = bf16[256,256]{1,0:T(8,128)(2,1)S(1)} convert(f32[256,256]{1,0:T(8,128)} %param.7) | non-fusion elementwise | flops 65536 | bytes 393216 | tf_op jit(solution)/shard_map/convert_element_type | solution.py:234
  4.9 0.5 %collective-permute-start.4 = (bf16[256,256]{1,0:T(8,128)(2,1)S(1)}, bf16[256,256]{1,0:T(8,128)(2,1)S(1)}, u32[]{:S(2)}, u32[]{:S(2)}) collective-permute-start(bf16[256,256]{1,0:T(8,128)(2,1)S(1)} %convert_element_type.23.block_ref.refs_0_), channel_id=1, source_target_pairs={{0,1},{1,0},{2,3},{3,2},{4,8},{5,9},{6,10},{7,11},{8,4},{9,5},{10,... | collective-permute-start | bytes 393224 | tf_op jit(solution)/shard_map/ppermute | solution.py:129
  5.4 2.7 %collective-permute-start.3 = (bf16[256,256]{1,0:T(8,128)(2,1)S(1)}, bf16[256,256]{1,0:T(8,128)(2,1)S(1)}, u32[]{:S(2)}, u32[]{:S(2)}) collective-permute-start(bf16[256,256]{1,0:T(8,128)(2,1)S(1)} %convert_element_type.23.block_ref.refs_0_), channel_id=1, source_target_pairs={{0,4},{4,0},{8,12},{12,8},{1,5},{5,1},{9,13},{13,9},{2,6},{6,2},{1... | collective-permute-start | bytes 393224 | tf_op jit(solution)/shard_map/ppermute | solution.py:117
  9.1 1.8 %collective-permute-start.7 = (bf16[48,256]{1,0:T(8,128)(2,1)S(1)}, bf16[48,256]{1,0:T(8,128)(2,1)S(1)}, u32[]{:S(2)}, u32[]{:S(2)}) collective-permute-start(bf16[48,256]{1,0:T(8,128)(2,1)S(1)} %shard_map.64.refs_3_), channel_id=1, source_target_pairs={{0,12},{4,8},{8,4},{12,0},{1,13},{5,9},{9,5},{13,1},{2,14},{6,10},... | collective-permute-start | bytes 73736 | tf_op jit(solution)/shard_map/ppermute | solution.py:117
  10.9 2.6 %collective-permute-start.5 = (bf16[48,256]{1,0:T(8,128)(2,1)S(1)}, bf16[48,256]{1,0:T(8,128)(2,1)S(1)}, u32[]{:S(2)}, u32[]{:S(2)}) collective-permute-start(bf16[48,256]{1,0:T(8,128)(2,1)S(1)} %shard_map.64.refs_3_), channel_id=1, source_target_pairs={{0,4},{4,0},{8,12},{12,8},{1,5},{5,1},{9,13},{13,9},{2,6},{6,2},{1... | collective-permute-start | bytes 73736 | tf_op jit(solution)/shard_map/ppermute | solution.py:117
  14.2 0.6 %collective-permute-done.7.refs_6_ = bf16[48,256]{1,0:T(8,128)(2,1)S(1)} collective-permute-done((bf16[48,256]{1,0:T(8,128)(2,1)S(1)}, bf16[48,256]{1,0:T(8,128)(2,1)S(1)}, u32[]{:S(2)}, u32[]{:S(2)}) %collective-permute-start.7) | collective-permute-done | bytes 24608 | tf_op jit(solution)/shard_map/ppermute | solution.py:117
  14.8 0.8 %collective-permute-done.6.refs_5_ = bf16[48,256]{1,0:T(8,128)(2,1)S(1)} collective-permute-done((bf16[48,256]{1,0:T(8,128)(2,1)S(1)}, bf16[48,256]{1,0:T(8,128)(2,1)S(1)}, u32[]{:S(2)}, u32[]{:S(2)}) %collective-permute-start.6) | collective-permute-done | bytes 24608 | tf_op jit(solution)/shard_map/ppermute | solution.py:117
  15.7 0.7 %shard_map.65 = (f32[2,256,256]{2,1,0:T(8,128)S(1)}, f32[96,256]{1,0:T(8,128)S(1)}) custom-call(bf16[3,1024,256]{2,1,0:T(8,128)(2,1)S(1)} %bitcast.17, s32[1,1]{1,0:T(1,128)S(6)} %copy.8.columns_ref, bf16[2,24,1024]{2,1,0:T(8,128)(2,1)S(1)} %pad_maximum_fusion.1.bases_ref, bf16[2,24,1024]{2,1,0:T(8,128)(2,1)S(1)} %collective-permute-done.across_ref, ...), custom_call_target="tpu_custom_call" | custom-call | flops 402653184 | bytes 1572864 | tf_op jit(solution)/shard_map/pallas_call | solution.py:73
  16.4 0.7 %shard_map.66 = (f32[2,256,256]{2,1,0:T(8,128)S(1)}, f32[96,256]{1,0:T(8,128)S(1)}, f32[96,256]{1,0:T(8,128)S(1)}) custom-call(bf16[3,1024,256]{2,1,0:T(8,128)(2,1)S(1)} %bitcast.18, s32[1,1]{1,0:T(1,128)S(6)} %copy.8.columns_ref, bf16[2,24,1024]{2,1,0:T(8,128)(2,1)S(1)} %pad_maximum_fusion.1.bases_ref, ...), custom_call_target="tpu_custom_call" | custom-call | flops 402653184 | bytes 1572864 | tf_op jit(solution)/shard_map/pallas_call | solution.py:73
  17.1 0.6 %collective-permute-start.11 = (f32[96,256]{1,0:T(8,128)S(1)}, f32[96,256]{1,0:T(8,128)S(1)}, u32[]{:S(2)}, u32[]{:S(2)}) collective-permute-start(f32[96,256]{1,0:T(8,128)S(1)} %get-tuple-element.28), channel_id=1, source_target_pairs={{0,1},{1,0},{2,3},{3,2},{4,5},{5,4},{6,7},{7,6},{8,9},{9,8},{10,11... | collective-permute-start | bytes 294920 | tf_op jit(solution)/shard_map/ppermute | solution.py:143
  17.7 0.6 %collective-permute-done.8 = f32[2,256,256]{2,1,0:T(8,128)S(1)} collective-permute-done((f32[2,256,256]{2,1,0:T(8,128)S(1)}, f32[2,256,256]{2,1,0:T(8,128)S(1)}, u32[]{:S(2)}, u32[]{:S(2)}) %collective-permute-start.8) | collective-permute-done | bytes 524320 | tf_op jit(solution)/shard_map/ppermute | solution.py:143
  18.4 1.6 %collective-permute-start.10 = (bf16[256,256]{1,0:T(8,128)(2,1)S(1)}, bf16[256,256]{1,0:T(8,128)(2,1)S(1)}, u32[]{:S(2)}, u32[]{:S(2)}) collective-permute-start(bf16[256,256]{1,0:T(8,128)(2,1)S(1)} %fusion.2), channel_id=1, source_target_pairs={{0,2},{1,3},{2,0},{3,1},{4,6},{5,7},{6,4},{7,5},{8,10},{9,11},{10,... | collective-permute-start | bytes 393224 | tf_op jit(solution)/shard_map/ppermute | solution.py:143
  20.0 2.1 %collective-permute-start.12 = (bf16[96,256]{1,0:T(8,128)(2,1)S(1)}, bf16[96,256]{1,0:T(8,128)(2,1)S(1)}, u32[]{:S(2)}, u32[]{:S(2)}) collective-permute-start(bf16[96,256]{1,0:T(8,128)(2,1)S(1)} %add_convert_fusion.refs_3_), channel_id=1, source_target_pairs={{0,8},{1,13},{2,10},{3,15},{4,12},{5,9},{6,14},{7,11},{8,0},{9,5},... | collective-permute-start | bytes 147464 | tf_op jit(solution)/shard_map/ppermute | solution.py:139
  22.1 1.9 %collective-permute-done.10 = bf16[256,256]{1,0:T(8,128)(2,1)S(1)} collective-permute-done((bf16[256,256]{1,0:T(8,128)(2,1)S(1)}, bf16[256,256]{1,0:T(8,128)(2,1)S(1)}, u32[]{:S(2)}, u32[]{:S(2)}) %collective-permute-start.10) | collective-permute-done | bytes 131104 | tf_op jit(solution)/shard_map/ppermute | solution.py:143
  24.2 1.7 %collective-permute-done.12.refs_5_ = bf16[96,256]{1,0:T(8,128)(2,1)S(1)} collective-permute-done((bf16[96,256]{1,0:T(8,128)(2,1)S(1)}, bf16[96,256]{1,0:T(8,128)(2,1)S(1)}, u32[]{:S(2)}, u32[]{:S(2)}) %collective-permute-start.12) | collective-permute-done | bytes 49184 | tf_op jit(solution)/shard_map/ppermute | solution.py:139
  25.9 0.9 %collective-permute-start.13 = (bf16[304,256]{1,0:T(8,128)(2,1)S(1)}, bf16[304,256]{1,0:T(8,128)(2,1)S(1)}, u32[]{:S(2)}, u32[]{:S(2)}) collective-permute-start(bf16[304,256]{1,0:T(8,128)(2,1)S(1)} %pad_maximum_fusion), channel_id=1, source_target_pairs={{0,4},{4,0},{8,12},{12,8},{1,5},{5,1},{9,13},{13,9},{2,6},{6,2},{1... | collective-permute-start | bytes 466952 | tf_op jit(solution)/shard_map/ppermute | solution.py:117
  26.9 1.3 %collective-permute-done.9.other_ref = bf16[2,24,1024]{2,1,0:T(8,128)(2,1)S(1)} collective-permute-done((bf16[2,24,1024]{2,1,0:T(8,128)(2,1)S(1)}, bf16[2,24,1024]{2,1,0:T(8,128)(2,1)S(1)}, u32[]{:S(2)}, u32[]{:S(2)}) %collective-permute-start.9) | collective-permute-done | bytes 98336 | tf_op jit(solution)/shard_map/ppermute | solution.py:143
  28.2 3.0 %collective-permute-done.13.refs_1_.refs_4_ = bf16[304,256]{1,0:T(8,128)(2,1)S(1)} collective-permute-done((bf16[304,256]{1,0:T(8,128)(2,1)S(1)}, bf16[304,256]{1,0:T(8,128)(2,1)S(1)}, u32[]{:S(2)}, u32[]{:S(2)}) %collective-permute-start.13) | collective-permute-done | bytes 155680 | tf_op jit(solution)/shard_map/ppermute | solution.py:117
  32.1 1.5 %collective-permute-done.15 = f32[2,256,256]{2,1,0:T(8,128)S(1)} collective-permute-done((f32[2,256,256]{2,1,0:T(8,128)S(1)}, f32[2,256,256]{2,1,0:T(8,128)S(1)}, u32[]{:S(2)}, u32[]{:S(2)}) %collective-permute-start.15) | collective-permute-done | bytes 524320 | tf_op jit(solution)/shard_map/ppermute | solution.py:143
  33.7 1.1 %collective-permute-start.16 = (bf16[256,256]{1,0:T(8,128)(2,1)S(1)}, bf16[256,256]{1,0:T(8,128)(2,1)S(1)}, u32[]{:S(2)}, u32[]{:S(2)}) collective-permute-start(bf16[256,256]{1,0:T(8,128)(2,1)S(1)} %fusion.3), channel_id=1, source_target_pairs={{0,2},{1,3},{2,0},{3,1},{4,6},{5,7},{6,4},{7,5},{8,10},{9,11},{10,... | collective-permute-start | bytes 393224 | tf_op jit(solution)/shard_map/ppermute | solution.py:143
  34.8 4.5 %collective-permute-done.16 = bf16[256,256]{1,0:T(8,128)(2,1)S(1)} collective-permute-done((bf16[256,256]{1,0:T(8,128)(2,1)S(1)}, bf16[256,256]{1,0:T(8,128)(2,1)S(1)}, u32[]{:S(2)}, u32[]{:S(2)}) %collective-permute-start.16) | collective-permute-done | bytes 131104 | tf_op jit(solution)/shard_map/ppermute | solution.py:143
  39.3 0.7 %fusion = f32[256,256]{1,0:T(8,128)} fusion(f32[2,256,256]{2,1,0:T(8,128)S(1)} %add.18, bf16[256,256]{1,0:T(8,128)(2,1)S(1)} %collective-permute-done.16), kind=kLoop, calls=%fused_computation.2 | loop fusion | flops 131072 | bytes 655360 | tf_op jit(solution)/shard_map/add | solution.py:273
  (34 shorter events, 1.8 us)
Async XLA Ops:
  0.8 7.9 %collective-permute-start = (bf16[2,24,1024]{2,1,0:T(8,128)(2,1)S(1)}, bf16[2,24,1024]{2,1,0:T(8,128)(2,1)S(1)}, u32[]{:S(2)}, u32[]{:S(2)}) collective-permute-start(bf16[2,24,1024]{2,1,0:T(8,128)(2,1)S(1)} %pad_maximum_fusion.1.bases_ref), channel_id=1, source_target_pairs={{0,2},{1,3},{2,0},{3,1},{4,6},{5,7},{6,4},{7,5},{8,10},{9,11},{10,... | collective-permute-start | bytes 294920 | tf_op jit(solution)/shard_map/ppermute | solution.py:143
  4.8 4.0 %collective-permute-start.1 = (bf16[256,256]{1,0:T(8,128)(2,1)S(1)}, bf16[256,256]{1,0:T(8,128)(2,1)S(1)}, u32[]{:S(2)}, u32[]{:S(2)}) collective-permute-start(bf16[256,256]{1,0:T(8,128)(2,1)S(1)} %convert_element_type.23.block_ref.refs_0_), channel_id=1, source_target_pairs={{0,1},{1,0},{2,3},{3,2},{4,5},{5,4},{6,7},{7,6},{8,9},{9,8},{10,11... | collective-permute-start | bytes 393224 | tf_op jit(solution)/shard_map/ppermute | solution.py:143
  4.9 6.0 %collective-permute-start.4 = (bf16[256,256]{1,0:T(8,128)(2,1)S(1)}, bf16[256,256]{1,0:T(8,128)(2,1)S(1)}, u32[]{:S(2)}, u32[]{:S(2)}) collective-permute-start(bf16[256,256]{1,0:T(8,128)(2,1)S(1)} %convert_element_type.23.block_ref.refs_0_), channel_id=1, source_target_pairs={{0,1},{1,0},{2,3},{3,2},{4,8},{5,9},{6,10},{7,11},{8,4},{9,5},{10,... | collective-permute-start | bytes 393224 | tf_op jit(solution)/shard_map/ppermute | solution.py:129
  5.4 8.8 %collective-permute-start.3 = (bf16[256,256]{1,0:T(8,128)(2,1)S(1)}, bf16[256,256]{1,0:T(8,128)(2,1)S(1)}, u32[]{:S(2)}, u32[]{:S(2)}) collective-permute-start(bf16[256,256]{1,0:T(8,128)(2,1)S(1)} %convert_element_type.23.block_ref.refs_0_), channel_id=1, source_target_pairs={{0,4},{4,0},{8,12},{12,8},{1,5},{5,1},{9,13},{13,9},{2,6},{6,2},{1... | collective-permute-start | bytes 393224 | tf_op jit(solution)/shard_map/ppermute | solution.py:117
  8.8 6.9 %copy-start = (bf16[1,1024,3,256]{3,1,2,0:T(8,128)(2,1)S(1)}, bf16[1,1024,3,256]{3,1,2,0:T(8,128)(2,1)}, u32[]{:S(2)}) copy-start(bf16[1,1024,3,256]{3,1,2,0:T(8,128)(2,1)} %param.10) | copy-start | bytes 4718596
  9.0 6.7 %collective-permute-start.2 = (bf16[2,24,1024]{2,1,0:T(8,128)(2,1)S(1)}, bf16[2,24,1024]{2,1,0:T(8,128)(2,1)S(1)}, u32[]{:S(2)}, u32[]{:S(2)}) collective-permute-start(bf16[2,24,1024]{2,1,0:T(8,128)(2,1)S(1)} %pad_maximum_fusion.2), channel_id=1, source_target_pairs={{0,1},{1,0},{2,3},{3,2},{4,5},{5,4},{6,7},{7,6},{8,9},{9,8},{10,11... | collective-permute-start | bytes 294920 | tf_op jit(solution)/shard_map/ppermute | solution.py:143
  9.1 5.7 %collective-permute-start.7 = (bf16[48,256]{1,0:T(8,128)(2,1)S(1)}, bf16[48,256]{1,0:T(8,128)(2,1)S(1)}, u32[]{:S(2)}, u32[]{:S(2)}) collective-permute-start(bf16[48,256]{1,0:T(8,128)(2,1)S(1)} %shard_map.64.refs_3_), channel_id=1, source_target_pairs={{0,12},{4,8},{8,4},{12,0},{1,13},{5,9},{9,5},{13,1},{2,14},{6,10},... | collective-permute-start | bytes 73736 | tf_op jit(solution)/shard_map/ppermute | solution.py:117
  10.9 4.7 %collective-permute-start.6 = (bf16[48,256]{1,0:T(8,128)(2,1)S(1)}, bf16[48,256]{1,0:T(8,128)(2,1)S(1)}, u32[]{:S(2)}, u32[]{:S(2)}) collective-permute-start(bf16[48,256]{1,0:T(8,128)(2,1)S(1)} %shard_map.64.refs_3_), channel_id=1, source_target_pairs={{0,8},{4,12},{8,0},{12,4},{1,9},{5,13},{9,1},{13,5},{2,10},{6,14},... | collective-permute-start | bytes 73736 | tf_op jit(solution)/shard_map/ppermute | solution.py:117
  10.9 4.7 %collective-permute-start.5 = (bf16[48,256]{1,0:T(8,128)(2,1)S(1)}, bf16[48,256]{1,0:T(8,128)(2,1)S(1)}, u32[]{:S(2)}, u32[]{:S(2)}) collective-permute-start(bf16[48,256]{1,0:T(8,128)(2,1)S(1)} %shard_map.64.refs_3_), channel_id=1, source_target_pairs={{0,4},{4,0},{8,12},{12,8},{1,5},{5,1},{9,13},{13,9},{2,6},{6,2},{1... | collective-permute-start | bytes 73736 | tf_op jit(solution)/shard_map/ppermute | solution.py:117
  16.4 2.0 %collective-permute-start.8 = (f32[2,256,256]{2,1,0:T(8,128)S(1)}, f32[2,256,256]{2,1,0:T(8,128)S(1)}, u32[]{:S(2)}, u32[]{:S(2)}) collective-permute-start(f32[2,256,256]{2,1,0:T(8,128)S(1)} %get-tuple-element.23), channel_id=1, source_target_pairs={{0,1},{1,0},{2,3},{3,2},{4,5},{5,4},{6,7},{7,6},{8,9},{9,8},{10,11... | collective-permute-start | bytes 1572872 | tf_op jit(solution)/shard_map/ppermute | solution.py:143
  17.1 2.9 %collective-permute-start.11 = (f32[96,256]{1,0:T(8,128)S(1)}, f32[96,256]{1,0:T(8,128)S(1)}, u32[]{:S(2)}, u32[]{:S(2)}) collective-permute-start(f32[96,256]{1,0:T(8,128)S(1)} %get-tuple-element.28), channel_id=1, source_target_pairs={{0,1},{1,0},{2,3},{3,2},{4,5},{5,4},{6,7},{7,6},{8,9},{9,8},{10,11... | collective-permute-start | bytes 294920 | tf_op jit(solution)/shard_map/ppermute | solution.py:143
  18.4 5.6 %collective-permute-start.10 = (bf16[256,256]{1,0:T(8,128)(2,1)S(1)}, bf16[256,256]{1,0:T(8,128)(2,1)S(1)}, u32[]{:S(2)}, u32[]{:S(2)}) collective-permute-start(bf16[256,256]{1,0:T(8,128)(2,1)S(1)} %fusion.2), channel_id=1, source_target_pairs={{0,2},{1,3},{2,0},{3,1},{4,6},{5,7},{6,4},{7,5},{8,10},{9,11},{10,... | collective-permute-start | bytes 393224 | tf_op jit(solution)/shard_map/ppermute | solution.py:143
  20.0 5.9 %collective-permute-start.12 = (bf16[96,256]{1,0:T(8,128)(2,1)S(1)}, bf16[96,256]{1,0:T(8,128)(2,1)S(1)}, u32[]{:S(2)}, u32[]{:S(2)}) collective-permute-start(bf16[96,256]{1,0:T(8,128)(2,1)S(1)} %add_convert_fusion.refs_3_), channel_id=1, source_target_pairs={{0,8},{1,13},{2,10},{3,15},{4,12},{5,9},{6,14},{7,11},{8,0},{9,5},... | collective-permute-start | bytes 147464 | tf_op jit(solution)/shard_map/ppermute | solution.py:139
  24.1 4.1 %collective-permute-start.14 = (bf16[256,256]{1,0:T(8,128)(2,1)S(1)}, bf16[256,256]{1,0:T(8,128)(2,1)S(1)}, u32[]{:S(2)}, u32[]{:S(2)}) collective-permute-start(bf16[256,256]{1,0:T(8,128)(2,1)S(1)} %fusion.1.refs_0_), channel_id=1, source_target_pairs={{0,1},{1,0},{2,3},{3,2},{4,8},{5,9},{6,10},{7,11},{8,4},{9,5},{10,... | collective-permute-start | bytes 393224 | tf_op jit(solution)/shard_map/ppermute | solution.py:129
  25.9 5.2 %collective-permute-start.13 = (bf16[304,256]{1,0:T(8,128)(2,1)S(1)}, bf16[304,256]{1,0:T(8,128)(2,1)S(1)}, u32[]{:S(2)}, u32[]{:S(2)}) collective-permute-start(bf16[304,256]{1,0:T(8,128)(2,1)S(1)} %pad_maximum_fusion), channel_id=1, source_target_pairs={{0,4},{4,0},{8,12},{12,8},{1,5},{5,1},{9,13},{13,9},{2,6},{6,2},{1... | collective-permute-start | bytes 466952 | tf_op jit(solution)/shard_map/ppermute | solution.py:117
  26.8 1.4 %collective-permute-start.9 = (bf16[2,24,1024]{2,1,0:T(8,128)(2,1)S(1)}, bf16[2,24,1024]{2,1,0:T(8,128)(2,1)S(1)}, u32[]{:S(2)}, u32[]{:S(2)}) collective-permute-start(bf16[2,24,1024]{2,1,0:T(8,128)(2,1)S(1)} %pad_maximum_fusion.3), channel_id=1, source_target_pairs={{0,1},{1,0},{2,3},{3,2},{4,5},{5,4},{6,7},{7,6},{8,9},{9,8},{10,11... | collective-permute-start | bytes 294920 | tf_op jit(solution)/shard_map/ppermute | solution.py:143
  31.6 2.0 %collective-permute-start.15 = (f32[2,256,256]{2,1,0:T(8,128)S(1)}, f32[2,256,256]{2,1,0:T(8,128)S(1)}, u32[]{:S(2)}, u32[]{:S(2)}) collective-permute-start(f32[2,256,256]{2,1,0:T(8,128)S(1)} %shard_map.68), channel_id=1, source_target_pairs={{0,1},{1,0},{2,3},{3,2},{4,5},{5,4},{6,7},{7,6},{8,9},{9,8},{10,11... | collective-permute-start | bytes 1572872 | tf_op jit(solution)/shard_map/ppermute | solution.py:143
  33.7 5.6 %collective-permute-start.16 = (bf16[256,256]{1,0:T(8,128)(2,1)S(1)}, bf16[256,256]{1,0:T(8,128)(2,1)S(1)}, u32[]{:S(2)}, u32[]{:S(2)}) collective-permute-start(bf16[256,256]{1,0:T(8,128)(2,1)S(1)} %fusion.3), channel_id=1, source_target_pairs={{0,2},{1,3},{2,0},{3,1},{4,6},{5,7},{6,4},{7,5},{8,10},{9,11},{10,... | collective-permute-start | bytes 393224 | tf_op jit(solution)/shard_map/ppermute | solution.py:143

commit v11 on v10

--- a/solution.py
+++ b/solution.py
@@ -69,6 +69,10 @@
 VMEM = pl.BlockSpec(memory_space=pltpu.VMEM)
 
 
+def list_swap_in_pieces(block, bit, pieces):
+    return jnp.concatenate([list_swap(piece, bit) for piece in jnp.split(block, pieces)])
+
+
 def kernel_call(kernel, outs, operands, flops=0):
     return pl.pallas_call(
         kernel,
@@ -161,8 +165,8 @@
     )
 
 
-def image_kernel(choice, turns, near_ref, columns_ref, bases_refs, *refs):
-    block_refs, coefficient_refs, out_ref = refs[:3], refs[3:-1], refs[-1]
+def image_kernel(choice, turns, near_ref, columns_ref, bases_refs, operand_refs, out_refs):
+    block_refs, coefficient_refs = operand_refs[:3], operand_refs[3:]
     count = lax.axis_size("tile")
     tile = lax.axis_index("tile")
     me = lax.axis_index("list")
@@ -176,7 +180,7 @@
         (2 * odd, jnp.where(inside, block_refs[2][...], 0)),
     ]
     totals = []
-    for index, turn in enumerate(turns):
+    for turn, out_ref in zip(turns, out_refs):
         part = me ^ turn
         cut = pl.ds(pl.multiple_of(part * rows, rows), rows)
         left = basis_groups(1, cut, bases_refs)
@@ -185,7 +189,7 @@
         )
         for side, block in blocks:
             total += jnp.dot(near_ref[side, cut, :], block, preferred_element_type=F32)
-        out_ref[index] = total
+        out_ref[...] = total
         totals.append((cut, total.astype(BF)))
     return totals
 
@@ -197,27 +201,29 @@
     )
 
 
-def sent_kernel(near_ref, columns_ref, bases_ref, across_ref, other_ref, *refs):
-    bases_refs = (bases_ref, across_ref)
-    totals = image_kernel(near_choice, (1, 3), near_ref, columns_ref, bases_refs, *refs[:-1])
-    refs[-1][...] = right_products(totals, (*bases_refs, other_ref))
-
-
-def kept_kernel(near_ref, columns_ref, bases_ref, across_ref, other_ref, *refs):
-    operands, (ranks_ref, sums_ref, out_ref, own_ref, send_ref) = refs[:-5], refs[-5:]
+def first_kernel(turns, near_ref, columns_ref, bases_ref, across_ref, other_ref, *refs):
+    operand_refs, refs = refs[:7], refs[7:]
+    last = 0 in turns
+    sums_before, refs = (refs[:1], refs[1:]) if 3 not in turns else ((), refs)
+    ranks_ref, refs = (refs[0], refs[1:]) if last else (None, refs)
     bases_refs = (bases_ref, across_ref)
     totals = image_kernel(
-        near_choice, (0, 2), near_ref, columns_ref, bases_refs, *operands, out_ref
-    )
-    sums = sums_ref[...] + right_products(totals, (*bases_refs, other_ref))
+        near_choice, turns, near_ref, columns_ref, bases_refs, operand_refs, refs
+    )
+    sums = right_products(totals, (*bases_refs, other_ref))
+    for ref in sums_before:
+        sums += ref[...]
+    if not last:
+        refs[-1][...] = sums
+        return
     groups = under_rank(sums, (0, 2, 1, 3), bases_ref.shape[1], ranks_ref)
-    own_ref[...] = jnp.concatenate(groups)
-    send_ref[...] = jnp.concatenate(groups[2:] + groups[:2])
+    refs[-2][...] = jnp.concatenate(groups)
+    refs[-1][...] = jnp.concatenate(groups[2:] + groups[:2])
 
 
 def second_kernel(turns, near_ref, columns_ref, bases_ref, across_ref, other_ref, *refs):
     bases_refs = (bases_ref, across_ref, other_ref)
-    image_kernel(far_choice, turns, near_ref, columns_ref, bases_refs, *refs)
+    image_kernel(far_choice, turns, near_ref, columns_ref, bases_refs, refs[:6], refs[6:])
 
 
 def one_slot(probes, right_bases, left_bases, near_tiles, tile_ranks, column_rows, row_columns):
@@ -225,7 +231,7 @@
     rank_part = right_bases.shape[2]
     near = near_tiles[0].transpose(1, 0, 2)
     flops = 2 * near.size * probe_count
-    halves = ((2, rows, probe_count), F32)
+    part = ((rows, probe_count), F32)
     ranks = 4 * rank_part
 
     bases = jnp.stack([right_bases[0, 0], left_bases[0, 0]])
@@ -243,34 +249,40 @@
     right, _ = lax.optimization_barrier((jnp.stack([bases[0], across[0]]), own))
     fixed = (near, row_columns, bases, across)
     operands = (*fixed, list_swap(right, 1), *beside, *coefficients)
-    send, sums = kernel_call(sent_kernel, [halves, ((ranks, probe_count), F32)], operands, flops)
+    small = ((ranks, probe_count), F32)
+
+    def first(turns, outs, more=()):
+        kernel = functools.partial(first_kernel, turns)
+        return kernel_call(kernel, outs, (*operands, *more), len(turns) * flops // 4)
+
+    send, sums = first((3,), [part, small])
     arrived = list_swap(send, 1)
-    keep, own, send = kernel_call(
-        kept_kernel,
-        [halves] + [((ranks, probe_count), F32)] * 2,
-        (*operands, tile_ranks, sums),
-        flops,
-    )
-    own = (own + list_swap(send, 1)).astype(BF)
-    pair = keep + arrived
-    held, held_across, pair = lax.optimization_barrier((bases, across, pair))
+    crossing, send, keep, own, other = first(
+        (2, 1, 0), [part] * 3 + [small] * 2, (sums, tile_ranks)
+    )
+    crossed = list_swap((crossing + arrived).astype(BF), 2)
+    own = (own + list_swap(other, 1)).astype(BF)
+    far = far_swap(own)
+    block = (keep + list_swap(send, 1) + crossed).astype(BF)
+    message = tile_swap(jnp.concatenate([block, own[: ranks // 2]]), 1)
+    beside = [block, message, middle_swap(block)]
+    held, held_across, far, block = lax.optimization_barrier((bases, across, far, block))
     left = list_swap(jnp.stack([held[1], held_across[1]]), 1)
-    far = far_swap(own)
-    block = (pair[0] + list_swap(pair[1].astype(BF), 2)).astype(BF)
-    message, far = lax.optimization_barrier((jnp.concatenate([block, own[: ranks // 2]]), far))
-    message = tile_swap(message, 1)
-    beside = [block, message, middle_swap(block)]
 
     operands = (*fixed, left, *beside, own, message, far)
-    (send,) = kernel_call(
-        functools.partial(second_kernel, (1, 3)), [halves], operands, flops
-    )
+
+    def second(turns, operands):
+        kernel = functools.partial(second_kernel, turns)
+        return kernel_call(kernel, [part] * len(turns), operands, len(turns) * flops // 4)
+
+    (send,) = second((3,), operands)
     arrived = list_swap(send, 1)
-    (keep,) = kernel_call(
-        functools.partial(second_kernel, (0, 2)), [halves], operands, flops
-    )
-    pair = keep + arrived
-    return pair[0] + list_swap(pair[1].astype(BF), 2)
+    (keep,) = second((2,), operands)
+    crossing = (keep + arrived).astype(BF)
+    near, crossing = lax.optimization_barrier((near, crossing))
+    crossed = list_swap(crossing, 2)
+    send, keep = second((1, 0), (near, *operands[1:]))
+    return keep + list_swap_in_pieces(send, 1, 2) + crossed
 
 
 def local(probes, right_bases, left_bases, near_tiles, tile_ranks, column_rows, row_columns):

time: 40.2 us -> 39.5 us (0.983)
  waiting for transfers between devices: 16 us -> 14.3 us
  starting transfers between devices: 17.3 us -> 18 us
    ppermute x9 -> x12, waiting for transfers between devices: 9.84 us -> 8.19 us  [list_swap(): lax.ppermute(block, 'list', [(i, i ^ bit) for i in range(lax.axis_size('l...]
    ppermute x9 -> x12, starting transfers between devices: 6.55 us -> 7.2 us  [list_swap(): lax.ppermute(block, 'list', [(i, i ^ bit) for i in range(lax.axis_size('l...]
    pallas_call x5 -> x6, Pallas kernels: 2.41 us -> 2.71 us  [kernel_call(): pl.pallas_call(kernel, out_shape=tuple((jax.ShapeDtypeStruct(shape, kind)...]
    add x3 -> x1, other arithmetic: 0.89 us -> 0.75 us  [one_slot(): return keep + list_swap_in_pieces(send, 1, 2) + crossed]
  transfers between devices with their start and end apart: 17 -> 20, of which waited for: 9 -> 8; matrix products, arithmetic and copies ran while one was open for 3% -> 3% of each run, Pallas kernels for 3% -> 5%
where the time goes in v11:
time: 39.5 us; the launch traced here: 39.2 us
  starting transfers between devices  18 us (46%)
  waiting for transfers between devices  14.3 us (36%)
  other arithmetic  2.71 us (7%)
  Pallas kernels  2.71 us (7%)
  between operations  1.51 us (4%)
    ppermute x12, waiting for transfers between devices, list_swap(): lax.ppermute(block, 'list', [(i, i ^ bit) for i in range(lax.axis_size('l...  8.19 us
    ppermute x5, starting transfers between devices, tile_swap(): lax.ppermute(block, 'tile', [(i, i ^ turn) for i in range(lax.axis_size('...  8.14 us
    ppermute x12, starting transfers between devices, list_swap(): lax.ppermute(block, 'list', [(i, i ^ bit) for i in range(lax.axis_size('l...  7.2 us
    ppermute x5, waiting for transfers between devices, tile_swap(): lax.ppermute(block, 'tile', [(i, i ^ turn) for i in range(lax.axis_size('...  4.4 us
    pallas_call x6, Pallas kernels, kernel_call(): pl.pallas_call(kernel, out_shape=tuple((jax.ShapeDtypeStruct(shape, kind)...  2.71 us
    ppermute x1, starting transfers between devices, far_swap(): return lax.ppermute(block, ('tile', 'list'), route)  2.08 us
    ppermute x1, waiting for transfers between devices, far_swap(): return lax.ppermute(block, ('tile', 'list'), route)  1.68 us
    convert_element_type x1, other arithmetic, one_slot(): block = probes.astype(BF)  0.96 us
  transfers between devices with their start and end apart: 20, of which 8 were waited for; matrix products, arithmetic and copies ran while one was open for 3% of the time, Pallas kernels for 5%

profile of v11, /device:TPU:0, one launch (start us, length us, event | category | flops | bytes accessed | tf_op | source)
XLA Modules:
  0.0 39.2 jit_solution(7616295806328688794)
XLA Ops:
  0.0 0.8 %pad_maximum_fusion.1.bases_ref = bf16[2,24,1024]{2,1,0:T(8,128)(2,1)S(1)} fusion(bf16[1,24,1024]{2,1,0:T(8,128)(2,1)} %bitcast.10, bf16[1,24,1024]{2,1,0:T(8,128)(2,1)} %bitcast.11), kind=kLoop, calls=%fused_computation.6 | loop fusion | flops 49152 | bytes 196608 | tf_op jit(solution)/shard_map/stack | solution.py:237
  0.8 3.0 %collective-permute-start = (bf16[2,24,1024]{2,1,0:T(8,128)(2,1)S(1)}, bf16[2,24,1024]{2,1,0:T(8,128)(2,1)S(1)}, u32[]{:S(2)}, u32[]{:S(2)}) collective-permute-start(bf16[2,24,1024]{2,1,0:T(8,128)(2,1)S(1)} %pad_maximum_fusion.1.bases_ref), channel_id=1, source_target_pairs={{0,2},{1,3},{2,0},{3,1},{4,6},{5,7},{6,4},{7,5},{8,10},{9,11},{10,... | collective-permute-start | bytes 294920 | tf_op jit(solution)/shard_map/ppermute | solution.py:147
  3.8 1.0 %convert_element_type.21.block_ref.refs_0_ = bf16[256,256]{1,0:T(8,128)(2,1)S(1)} convert(f32[256,256]{1,0:T(8,128)} %param.7) | non-fusion elementwise | flops 65536 | bytes 393216 | tf_op jit(solution)/shard_map/convert_element_type | solution.py:240
  4.9 0.5 %collective-permute-start.4 = (bf16[256,256]{1,0:T(8,128)(2,1)S(1)}, bf16[256,256]{1,0:T(8,128)(2,1)S(1)}, u32[]{:S(2)}, u32[]{:S(2)}) collective-permute-start(bf16[256,256]{1,0:T(8,128)(2,1)S(1)} %convert_element_type.21.block_ref.refs_0_), channel_id=1, source_target_pairs={{0,1},{1,0},{2,3},{3,2},{4,8},{5,9},{6,10},{7,11},{8,4},{9,5},{10,... | collective-permute-start | bytes 393224 | tf_op jit(solution)/shard_map/ppermute | solution.py:133
  5.4 2.7 %collective-permute-start.3 = (bf16[256,256]{1,0:T(8,128)(2,1)S(1)}, bf16[256,256]{1,0:T(8,128)(2,1)S(1)}, u32[]{:S(2)}, u32[]{:S(2)}) collective-permute-start(bf16[256,256]{1,0:T(8,128)(2,1)S(1)} %convert_element_type.21.block_ref.refs_0_), channel_id=1, source_target_pairs={{0,4},{4,0},{8,12},{12,8},{1,5},{5,1},{9,13},{13,9},{2,6},{6,2},{1... | collective-permute-start | bytes 393224 | tf_op jit(solution)/shard_map/ppermute | solution.py:121
  9.1 1.8 %collective-permute-start.7 = (bf16[48,256]{1,0:T(8,128)(2,1)S(1)}, bf16[48,256]{1,0:T(8,128)(2,1)S(1)}, u32[]{:S(2)}, u32[]{:S(2)}) collective-permute-start(bf16[48,256]{1,0:T(8,128)(2,1)S(1)} %shard_map.64.refs_3_), channel_id=1, source_target_pairs={{0,12},{4,8},{8,4},{12,0},{1,13},{5,9},{9,5},{13,1},{2,14},{6,10},... | collective-permute-start | bytes 73736 | tf_op jit(solution)/shard_map/ppermute | solution.py:121
  10.9 2.6 %collective-permute-start.5 = (bf16[48,256]{1,0:T(8,128)(2,1)S(1)}, bf16[48,256]{1,0:T(8,128)(2,1)S(1)}, u32[]{:S(2)}, u32[]{:S(2)}) collective-permute-start(bf16[48,256]{1,0:T(8,128)(2,1)S(1)} %shard_map.64.refs_3_), channel_id=1, source_target_pairs={{0,4},{4,0},{8,12},{12,8},{1,5},{5,1},{9,13},{13,9},{2,6},{6,2},{1... | collective-permute-start | bytes 73736 | tf_op jit(solution)/shard_map/ppermute | solution.py:121
  14.2 0.6 %collective-permute-done.7.refs_6_ = bf16[48,256]{1,0:T(8,128)(2,1)S(1)} collective-permute-done((bf16[48,256]{1,0:T(8,128)(2,1)S(1)}, bf16[48,256]{1,0:T(8,128)(2,1)S(1)}, u32[]{:S(2)}, u32[]{:S(2)}) %collective-permute-start.7) | collective-permute-done | bytes 24608 | tf_op jit(solution)/shard_map/ppermute | solution.py:121
  14.8 0.8 %collective-permute-done.6.refs_5_ = bf16[48,256]{1,0:T(8,128)(2,1)S(1)} collective-permute-done((bf16[48,256]{1,0:T(8,128)(2,1)S(1)}, bf16[48,256]{1,0:T(8,128)(2,1)S(1)}, u32[]{:S(2)}, u32[]{:S(2)}) %collective-permute-start.6) | collective-permute-done | bytes 24608 | tf_op jit(solution)/shard_map/ppermute | solution.py:121
  15.7 0.5 %shard_map.65 = (f32[256,256]{1,0:T(8,128)S(1)}, f32[96,256]{1,0:T(8,128)S(1)}) custom-call(bf16[3,1024,256]{2,1,0:T(8,128)(2,1)S(1)} %bitcast.5, s32[1,1]{1,0:T(1,128)S(6)} %copy.8.columns_ref, bf16[2,24,1024]{2,1,0:T(8,128)(2,1)S(1)} %pad_maximum_fusion.1.bases_ref, bf16[2,24,1024]{2,1,0:T(8,128)(2,1)S(1)} %collective-permute-done.across_ref, ...), custom_call_target="tpu_custom_call" | custom-call | flops 100663296 | bytes 1572864 | tf_op jit(solution)/shard_map/pallas_call | solution.py:77
  16.3 0.9 %shard_map.66 = (f32[256,256]{1,0:T(8,128)S(1)}, f32[256,256]{1,0:T(8,128)S(1)}, f32[256,256]{1,0:T(8,128)S(1)}, f32[96,256]{1,0:T(8,128)S(1)}, f32[96,256]{1,0:T(8,128)S(1)}) custom-call(bf16[3,1024,256]{2,1,0:T(8,128)(2,1)S(1)} %bitcast.6, s32[1,1]{1,0:T(1,128)S(6)} %copy.8.columns_ref, bf16[2,24,1024]{2,1,0:T(8,128)(2,1)S(1)} %pad_maximum_fusion.1.bases_ref, ...), custom_call_target="tpu_custom_call" | custom-call | flops 301989888 | bytes 1572864 | tf_op jit(solution)/shard_map/pallas_call | solution.py:77
  17.1 0.6 %collective-permute-start.8 = (f32[96,256]{1,0:T(8,128)S(1)}, f32[96,256]{1,0:T(8,128)S(1)}, u32[]{:S(2)}, u32[]{:S(2)}) collective-permute-start(f32[96,256]{1,0:T(8,128)S(1)} %get-tuple-element.27), channel_id=1, source_target_pairs={{0,1},{1,0},{2,3},{3,2},{4,5},{5,4},{6,7},{7,6},{8,9},{9,8},{10,11... | collective-permute-start | bytes 294920 | tf_op jit(solution)/shard_map/ppermute | solution.py:147
  17.9 1.6 %collective-permute-start.12 = (bf16[256,256]{1,0:T(8,128)(2,1)S(1)}, bf16[256,256]{1,0:T(8,128)(2,1)S(1)}, u32[]{:S(2)}, u32[]{:S(2)}) collective-permute-start(bf16[256,256]{1,0:T(8,128)(2,1)S(1)} %add_convert_fusion.2), channel_id=1, source_target_pairs={{0,2},{1,3},{2,0},{3,1},{4,6},{5,7},{6,4},{7,5},{8,10},{9,11},{10,... | collective-permute-start | bytes 393224 | tf_op jit(solution)/shard_map/ppermute | solution.py:147
  19.4 2.1 %collective-permute-start.9 = (bf16[96,256]{1,0:T(8,128)(2,1)S(1)}, bf16[96,256]{1,0:T(8,128)(2,1)S(1)}, u32[]{:S(2)}, u32[]{:S(2)}) collective-permute-start(bf16[96,256]{1,0:T(8,128)(2,1)S(1)} %add_convert_fusion.3.refs_3_), channel_id=1, source_target_pairs={{0,8},{1,13},{2,10},{3,15},{4,12},{5,9},{6,14},{7,11},{8,0},{9,5},... | collective-permute-start | bytes 147464 | tf_op jit(solution)/shard_map/ppermute | solution.py:143
  21.5 2.2 %collective-permute-done.12 = bf16[256,256]{1,0:T(8,128)(2,1)S(1)} collective-permute-done((bf16[256,256]{1,0:T(8,128)(2,1)S(1)}, bf16[256,256]{1,0:T(8,128)(2,1)S(1)}, u32[]{:S(2)}, u32[]{:S(2)}) %collective-permute-start.12) | collective-permute-done | bytes 131104 | tf_op jit(solution)/shard_map/ppermute | solution.py:147
  23.9 1.7 %collective-permute-done.9.refs_5_ = bf16[96,256]{1,0:T(8,128)(2,1)S(1)} collective-permute-done((bf16[96,256]{1,0:T(8,128)(2,1)S(1)}, bf16[96,256]{1,0:T(8,128)(2,1)S(1)}, u32[]{:S(2)}, u32[]{:S(2)}) %collective-permute-start.9) | collective-permute-done | bytes 49184 | tf_op jit(solution)/shard_map/ppermute | solution.py:143
  25.6 1.0 %collective-permute-start.14 = (bf16[304,256]{1,0:T(8,128)(2,1)S(1)}, bf16[304,256]{1,0:T(8,128)(2,1)S(1)}, u32[]{:S(2)}, u32[]{:S(2)}) collective-permute-start(bf16[304,256]{1,0:T(8,128)(2,1)S(1)} %pad_maximum_fusion), channel_id=1, source_target_pairs={{0,4},{4,0},{8,12},{12,8},{1,5},{5,1},{9,13},{13,9},{2,6},{6,2},{1... | collective-permute-start | bytes 466952 | tf_op jit(solution)/shard_map/ppermute | solution.py:121
  26.6 1.3 %collective-permute-done.13.other_ref = bf16[2,24,1024]{2,1,0:T(8,128)(2,1)S(1)} collective-permute-done((bf16[2,24,1024]{2,1,0:T(8,128)(2,1)S(1)}, bf16[2,24,1024]{2,1,0:T(8,128)(2,1)S(1)}, u32[]{:S(2)}, u32[]{:S(2)}) %collective-permute-start.13) | collective-permute-done | bytes 98336 | tf_op jit(solution)/shard_map/ppermute | solution.py:147
  27.9 2.9 %collective-permute-done.14.refs_1_.refs_4_ = bf16[304,256]{1,0:T(8,128)(2,1)S(1)} collective-permute-done((bf16[304,256]{1,0:T(8,128)(2,1)S(1)}, bf16[304,256]{1,0:T(8,128)(2,1)S(1)}, u32[]{:S(2)}, u32[]{:S(2)}) %collective-permute-start.14) | collective-permute-done | bytes 155680 | tf_op jit(solution)/shard_map/ppermute | solution.py:121
  31.7 1.1 %collective-permute-done.16 = f32[256,256]{1,0:T(8,128)S(1)} collective-permute-done((f32[256,256]{1,0:T(8,128)S(1)}, f32[256,256]{1,0:T(8,128)S(1)}, u32[]{:S(2)}, u32[]{:S(2)}) %collective-permute-start.16) | collective-permute-done | bytes 262176 | tf_op jit(solution)/shard_map/ppermute | solution.py:147
  32.9 1.1 %collective-permute-start.19 = (bf16[256,256]{1,0:T(8,128)(2,1)S(1)}, bf16[256,256]{1,0:T(8,128)(2,1)S(1)}, u32[]{:S(2)}, u32[]{:S(2)}) collective-permute-start(bf16[256,256]{1,0:T(8,128)(2,1)S(1)} %add_convert_fusion), channel_id=1, source_target_pairs={{0,2},{1,3},{2,0},{3,1},{4,6},{5,7},{6,4},{7,5},{8,10},{9,11},{10,... | collective-permute-start | bytes 393224 | tf_op jit(solution)/shard_map/ppermute | solution.py:147
  34.5 0.5 %collective-permute-start.18 = (f32[128,256]{1,0:T(8,128)S(1)}, f32[128,256]{1,0:T(8,128)S(1)}, u32[]{:S(2)}, u32[]{:S(2)}) collective-permute-start(f32[128,256]{1,0:T(8,128)S(1)} %get-tuple-element.40), channel_id=1, source_target_pairs={{0,1},{1,0},{2,3},{3,2},{4,5},{5,4},{6,7},{7,6},{8,9},{9,8},{10,11... | collective-permute-start | bytes 393224 | tf_op jit(solution)/shard_map/ppermute | solution.py:147
  35.0 3.5 %collective-permute-done.19 = bf16[256,256]{1,0:T(8,128)(2,1)S(1)} collective-permute-done((bf16[256,256]{1,0:T(8,128)(2,1)S(1)}, bf16[256,256]{1,0:T(8,128)(2,1)S(1)}, u32[]{:S(2)}, u32[]{:S(2)}) %collective-permute-start.19) | collective-permute-done | bytes 131104 | tf_op jit(solution)/shard_map/ppermute | solution.py:147
  38.5 0.7 %fusion = f32[256,256]{1,0:T(8,128)} fusion(f32[256,256]{1,0:T(8,128)S(1)} %get-tuple-element.36, f32[128,256]{1,0:T(8,128)S(1)} %collective-permute-done.18, f32[128,256]{1,0:T(8,128)S(1)} %collective-permute-done.17, bf16[256,256]{1,0:T(8,128)(2,1)S(1)} %collective-permute-done.19), kind=kLoop, calls=%fused_computation.1 | loop fusion | flops 262144 | bytes 917504 | tf_op jit(solution)/shard_map/add | solution.py:285
  (40 shorter events, 2.2 us)
Async XLA Ops:
  0.8 7.9 %collective-permute-start = (bf16[2,24,1024]{2,1,0:T(8,128)(2,1)S(1)}, bf16[2,24,1024]{2,1,0:T(8,128)(2,1)S(1)}, u32[]{:S(2)}, u32[]{:S(2)}) collective-permute-start(bf16[2,24,1024]{2,1,0:T(8,128)(2,1)S(1)} %pad_maximum_fusion.1.bases_ref), channel_id=1, source_target_pairs={{0,2},{1,3},{2,0},{3,1},{4,6},{5,7},{6,4},{7,5},{8,10},{9,11},{10,... | collective-permute-start | bytes 294920 | tf_op jit(solution)/shard_map/ppermute | solution.py:147
  4.8 4.0 %collective-permute-start.1 = (bf16[256,256]{1,0:T(8,128)(2,1)S(1)}, bf16[256,256]{1,0:T(8,128)(2,1)S(1)}, u32[]{:S(2)}, u32[]{:S(2)}) collective-permute-start(bf16[256,256]{1,0:T(8,128)(2,1)S(1)} %convert_element_type.21.block_ref.refs_0_), channel_id=1, source_target_pairs={{0,1},{1,0},{2,3},{3,2},{4,5},{5,4},{6,7},{7,6},{8,9},{9,8},{10,11... | collective-permute-start | bytes 393224 | tf_op jit(solution)/shard_map/ppermute | solution.py:147
  4.9 6.0 %collective-permute-start.4 = (bf16[256,256]{1,0:T(8,128)(2,1)S(1)}, bf16[256,256]{1,0:T(8,128)(2,1)S(1)}, u32[]{:S(2)}, u32[]{:S(2)}) collective-permute-start(bf16[256,256]{1,0:T(8,128)(2,1)S(1)} %convert_element_type.21.block_ref.refs_0_), channel_id=1, source_target_pairs={{0,1},{1,0},{2,3},{3,2},{4,8},{5,9},{6,10},{7,11},{8,4},{9,5},{10,... | collective-permute-start | bytes 393224 | tf_op jit(solution)/shard_map/ppermute | solution.py:133
  5.4 8.8 %collective-permute-start.3 = (bf16[256,256]{1,0:T(8,128)(2,1)S(1)}, bf16[256,256]{1,0:T(8,128)(2,1)S(1)}, u32[]{:S(2)}, u32[]{:S(2)}) collective-permute-start(bf16[256,256]{1,0:T(8,128)(2,1)S(1)} %convert_element_type.21.block_ref.refs_0_), channel_id=1, source_target_pairs={{0,4},{4,0},{8,12},{12,8},{1,5},{5,1},{9,13},{13,9},{2,6},{6,2},{1... | collective-permute-start | bytes 393224 | tf_op jit(solution)/shard_map/ppermute | solution.py:121
  8.8 6.9 %copy-start = (bf16[1,1024,3,256]{3,1,2,0:T(8,128)(2,1)S(1)}, bf16[1,1024,3,256]{3,1,2,0:T(8,128)(2,1)}, u32[]{:S(2)}) copy-start(bf16[1,1024,3,256]{3,1,2,0:T(8,128)(2,1)} %param.10) | copy-start | bytes 4718596
  9.0 6.7 %collective-permute-start.2 = (bf16[2,24,1024]{2,1,0:T(8,128)(2,1)S(1)}, bf16[2,24,1024]{2,1,0:T(8,128)(2,1)S(1)}, u32[]{:S(2)}, u32[]{:S(2)}) collective-permute-start(bf16[2,24,1024]{2,1,0:T(8,128)(2,1)S(1)} %pad_maximum_fusion.2), channel_id=1, source_target_pairs={{0,1},{1,0},{2,3},{3,2},{4,5},{5,4},{6,7},{7,6},{8,9},{9,8},{10,11... | collective-permute-start | bytes 294920 | tf_op jit(solution)/shard_map/ppermute | solution.py:147
  9.1 5.7 %collective-permute-start.7 = (bf16[48,256]{1,0:T(8,128)(2,1)S(1)}, bf16[48,256]{1,0:T(8,128)(2,1)S(1)}, u32[]{:S(2)}, u32[]{:S(2)}) collective-permute-start(bf16[48,256]{1,0:T(8,128)(2,1)S(1)} %shard_map.64.refs_3_), channel_id=1, source_target_pairs={{0,12},{4,8},{8,4},{12,0},{1,13},{5,9},{9,5},{13,1},{2,14},{6,10},... | collective-permute-start | bytes 73736 | tf_op jit(solution)/shard_map/ppermute | solution.py:121
  10.9 4.7 %collective-permute-start.6 = (bf16[48,256]{1,0:T(8,128)(2,1)S(1)}, bf16[48,256]{1,0:T(8,128)(2,1)S(1)}, u32[]{:S(2)}, u32[]{:S(2)}) collective-permute-start(bf16[48,256]{1,0:T(8,128)(2,1)S(1)} %shard_map.64.refs_3_), channel_id=1, source_target_pairs={{0,8},{4,12},{8,0},{12,4},{1,9},{5,13},{9,1},{13,5},{2,10},{6,14},... | collective-permute-start | bytes 73736 | tf_op jit(solution)/shard_map/ppermute | solution.py:121
  10.9 4.7 %collective-permute-start.5 = (bf16[48,256]{1,0:T(8,128)(2,1)S(1)}, bf16[48,256]{1,0:T(8,128)(2,1)S(1)}, u32[]{:S(2)}, u32[]{:S(2)}) collective-permute-start(bf16[48,256]{1,0:T(8,128)(2,1)S(1)} %shard_map.64.refs_3_), channel_id=1, source_target_pairs={{0,4},{4,0},{8,12},{12,8},{1,5},{5,1},{9,13},{13,9},{2,6},{6,2},{1... | collective-permute-start | bytes 73736 | tf_op jit(solution)/shard_map/ppermute | solution.py:121
  16.2 1.6 %collective-permute-start.11 = (f32[256,256]{1,0:T(8,128)S(1)}, f32[256,256]{1,0:T(8,128)S(1)}, u32[]{:S(2)}, u32[]{:S(2)}) collective-permute-start(f32[256,256]{1,0:T(8,128)S(1)} %get-tuple-element.31), channel_id=1, source_target_pairs={{0,1},{1,0},{2,3},{3,2},{4,5},{5,4},{6,7},{7,6},{8,9},{9,8},{10,11... | collective-permute-start | bytes 786440 | tf_op jit(solution)/shard_map/ppermute | solution.py:147
  17.1 2.3 %collective-permute-start.8 = (f32[96,256]{1,0:T(8,128)S(1)}, f32[96,256]{1,0:T(8,128)S(1)}, u32[]{:S(2)}, u32[]{:S(2)}) collective-permute-start(f32[96,256]{1,0:T(8,128)S(1)} %get-tuple-element.27), channel_id=1, source_target_pairs={{0,1},{1,0},{2,3},{3,2},{4,5},{5,4},{6,7},{7,6},{8,9},{9,8},{10,11... | collective-permute-start | bytes 294920 | tf_op jit(solution)/shard_map/ppermute | solution.py:147
  17.7 3.8 %collective-permute-start.10 = (f32[256,256]{1,0:T(8,128)S(1)}, f32[256,256]{1,0:T(8,128)S(1)}, u32[]{:S(2)}, u32[]{:S(2)}) collective-permute-start(f32[256,256]{1,0:T(8,128)S(1)} %get-tuple-element.29), channel_id=1, source_target_pairs={{0,1},{1,0},{2,3},{3,2},{4,5},{5,4},{6,7},{7,6},{8,9},{9,8},{10,11... | collective-permute-start | bytes 786440 | tf_op jit(solution)/shard_map/ppermute | solution.py:147
  17.9 5.9 %collective-permute-start.12 = (bf16[256,256]{1,0:T(8,128)(2,1)S(1)}, bf16[256,256]{1,0:T(8,128)(2,1)S(1)}, u32[]{:S(2)}, u32[]{:S(2)}) collective-permute-start(bf16[256,256]{1,0:T(8,128)(2,1)S(1)} %add_convert_fusion.2), channel_id=1, source_target_pairs={{0,2},{1,3},{2,0},{3,1},{4,6},{5,7},{6,4},{7,5},{8,10},{9,11},{10,... | collective-permute-start | bytes 393224 | tf_op jit(solution)/shard_map/ppermute | solution.py:147
  19.4 6.1 %collective-permute-start.9 = (bf16[96,256]{1,0:T(8,128)(2,1)S(1)}, bf16[96,256]{1,0:T(8,128)(2,1)S(1)}, u32[]{:S(2)}, u32[]{:S(2)}) collective-permute-start(bf16[96,256]{1,0:T(8,128)(2,1)S(1)} %add_convert_fusion.3.refs_3_), channel_id=1, source_target_pairs={{0,8},{1,13},{2,10},{3,15},{4,12},{5,9},{6,14},{7,11},{8,0},{9,5},... | collective-permute-start | bytes 147464 | tf_op jit(solution)/shard_map/ppermute | solution.py:143
  23.8 4.1 %collective-permute-start.15 = (bf16[256,256]{1,0:T(8,128)(2,1)S(1)}, bf16[256,256]{1,0:T(8,128)(2,1)S(1)}, u32[]{:S(2)}, u32[]{:S(2)}) collective-permute-start(bf16[256,256]{1,0:T(8,128)(2,1)S(1)} %add_convert_fusion.1.refs_0_), channel_id=1, source_target_pairs={{0,1},{1,0},{2,3},{3,2},{4,8},{5,9},{6,10},{7,11},{8,4},{9,5},{10,... | collective-permute-start | bytes 393224 | tf_op jit(solution)/shard_map/ppermute | solution.py:133
  25.6 5.3 %collective-permute-start.14 = (bf16[304,256]{1,0:T(8,128)(2,1)S(1)}, bf16[304,256]{1,0:T(8,128)(2,1)S(1)}, u32[]{:S(2)}, u32[]{:S(2)}) collective-permute-start(bf16[304,256]{1,0:T(8,128)(2,1)S(1)} %pad_maximum_fusion), channel_id=1, source_target_pairs={{0,4},{4,0},{8,12},{12,8},{1,5},{5,1},{9,13},{13,9},{2,6},{6,2},{1... | collective-permute-start | bytes 466952 | tf_op jit(solution)/shard_map/ppermute | solution.py:121
  26.6 1.4 %collective-permute-start.13 = (bf16[2,24,1024]{2,1,0:T(8,128)(2,1)S(1)}, bf16[2,24,1024]{2,1,0:T(8,128)(2,1)S(1)}, u32[]{:S(2)}, u32[]{:S(2)}) collective-permute-start(bf16[2,24,1024]{2,1,0:T(8,128)(2,1)S(1)} %pad_maximum_fusion.3), channel_id=1, source_target_pairs={{0,1},{1,0},{2,3},{3,2},{4,5},{5,4},{6,7},{7,6},{8,9},{9,8},{10,11... | collective-permute-start | bytes 294920 | tf_op jit(solution)/shard_map/ppermute | solution.py:147
  31.2 1.6 %collective-permute-start.16 = (f32[256,256]{1,0:T(8,128)S(1)}, f32[256,256]{1,0:T(8,128)S(1)}, u32[]{:S(2)}, u32[]{:S(2)}) collective-permute-start(f32[256,256]{1,0:T(8,128)S(1)} %shard_map.68), channel_id=1, source_target_pairs={{0,1},{1,0},{2,3},{3,2},{4,5},{5,4},{6,7},{7,6},{8,9},{9,8},{10,11... | collective-permute-start | bytes 786440 | tf_op jit(solution)/shard_map/ppermute | solution.py:147
  32.9 5.6 %collective-permute-start.19 = (bf16[256,256]{1,0:T(8,128)(2,1)S(1)}, bf16[256,256]{1,0:T(8,128)(2,1)S(1)}, u32[]{:S(2)}, u32[]{:S(2)}) collective-permute-start(bf16[256,256]{1,0:T(8,128)(2,1)S(1)} %add_convert_fusion), channel_id=1, source_target_pairs={{0,2},{1,3},{2,0},{3,1},{4,6},{5,7},{6,4},{7,5},{8,10},{9,11},{10,... | collective-permute-start | bytes 393224 | tf_op jit(solution)/shard_map/ppermute | solution.py:147
  34.4 4.1 %collective-permute-start.17 = (f32[128,256]{1,0:T(8,128)S(1)}, f32[128,256]{1,0:T(8,128)S(1)}, u32[]{:S(2)}, u32[]{:S(2)}) collective-permute-start(f32[128,256]{1,0:T(8,128)S(1)} %get-tuple-element.39), channel_id=1, source_target_pairs={{0,1},{1,0},{2,3},{3,2},{4,5},{5,4},{6,7},{7,6},{8,9},{9,8},{10,11... | collective-permute-start | bytes 393224 | tf_op jit(solution)/shard_map/ppermute | solution.py:147
  34.5 4.0 %collective-permute-start.18 = (f32[128,256]{1,0:T(8,128)S(1)}, f32[128,256]{1,0:T(8,128)S(1)}, u32[]{:S(2)}, u32[]{:S(2)}) collective-permute-start(f32[128,256]{1,0:T(8,128)S(1)} %get-tuple-element.40), channel_id=1, source_target_pairs={{0,1},{1,0},{2,3},{3,2},{4,5},{5,4},{6,7},{7,6},{8,9},{9,8},{10,11... | collective-permute-start | bytes 393224 | tf_op jit(solution)/shard_map/ppermute | solution.py:147

commit v12 on v11

--- a/solution.py
+++ b/solution.py
@@ -166,7 +166,8 @@
 
 
 def image_kernel(choice, turns, near_ref, columns_ref, bases_refs, operand_refs, out_refs):
-    block_refs, coefficient_refs = operand_refs[:3], operand_refs[3:]
+    count_refs = len(operand_refs) - (4 if choice is near_choice else 3)
+    block_refs, coefficient_refs = operand_refs[:count_refs], operand_refs[count_refs:]
     count = lax.axis_size("tile")
     tile = lax.axis_index("tile")
     me = lax.axis_index("list")
@@ -174,11 +175,16 @@
     chosen = choice(columns_ref[...], tile, me, coefficient_refs)
     odd = lax.rem(tile, 2)
     inside = (tile > 0) & (tile < count - 1)
-    blocks = [
-        (1, block_refs[0][...]),
-        (2 - 2 * odd, block_refs[1][:rows, :]),
-        (2 * odd, jnp.where(inside, block_refs[2][...], 0)),
-    ]
+    blocks = []
+    start = 0
+    for index in range(0, count_refs, 3):
+        own_ref, first_ref, second_ref = block_refs[index : index + 3]
+        step = own_ref.shape[0]
+        place = slice(start, start + step)
+        blocks.append((1, place, own_ref[...]))
+        blocks.append((2 - 2 * odd, place, first_ref[:step, :]))
+        blocks.append((2 * odd, place, jnp.where(inside, second_ref[...], 0)))
+        start += step
     totals = []
     for turn, out_ref in zip(turns, out_refs):
         part = me ^ turn
@@ -187,8 +193,8 @@
         total = lax.dot_general(
             left, chosen, (((0,), (0,)), ((), ())), preferred_element_type=F32
         )
-        for side, block in blocks:
-            total += jnp.dot(near_ref[side, cut, :], block, preferred_element_type=F32)
+        for side, place, block in blocks:
+            total += jnp.dot(near_ref[side, cut, place], block, preferred_element_type=F32)
         out_ref[...] = total
         totals.append((cut, total.astype(BF)))
     return totals
@@ -223,7 +229,7 @@
 
 def second_kernel(turns, near_ref, columns_ref, bases_ref, across_ref, other_ref, *refs):
     bases_refs = (bases_ref, across_ref, other_ref)
-    image_kernel(far_choice, turns, near_ref, columns_ref, bases_refs, refs[:6], refs[6:])
+    image_kernel(far_choice, turns, near_ref, columns_ref, bases_refs, refs[:9], refs[9:])
 
 
 def one_slot(probes, right_bases, left_bases, near_tiles, tile_ranks, column_rows, row_columns):
@@ -260,13 +266,22 @@
     crossing, send, keep, own, other = first(
         (2, 1, 0), [part] * 3 + [small] * 2, (sums, tile_ranks)
     )
-    crossed = list_swap((crossing + arrived).astype(BF), 2)
+    crossing = (crossing + arrived).astype(BF)
     own = (own + list_swap(other, 1)).astype(BF)
     far = far_swap(own)
-    block = (keep + list_swap(send, 1) + crossed).astype(BF)
-    message = tile_swap(jnp.concatenate([block, own[: ranks // 2]]), 1)
-    beside = [block, message, middle_swap(block)]
-    held, held_across, far, block = lax.optimization_barrier((bases, across, far, block))
+    keep += list_swap(send, 1)
+    beside = []
+    split = 5 * rows // 8
+    for piece in (slice(0, split), slice(split, rows)):
+        block = (keep[piece] + list_swap(crossing[piece], 2)).astype(BF)
+        if piece.start:
+            block, far = lax.optimization_barrier((block, far))
+        keep, block = lax.optimization_barrier((keep, block))
+        message = block if piece.start else jnp.concatenate([block, own[: ranks // 2]])
+        message = tile_swap(message, 1)
+        beside += [block, message, middle_swap(block)]
+    message = beside[1]
+    held, held_across, _ = lax.optimization_barrier((bases, across, beside[0]))
     left = list_swap(jnp.stack([held[1], held_across[1]]), 1)
 
     operands = (*fixed, left, *beside, own, message, far)

time: 39.5 us -> 39.1 us (0.990)
  waiting for transfers between devices: 14.3 us -> 8.65 us
  starting transfers between devices: 18 us -> 22.8 us
  Pallas kernels: 2.71 us -> 3.17 us
    ppermute x12 -> x13, waiting for transfers between devices: 8.19 us -> 4.04 us  [list_swap(): lax.ppermute(block, 'list', [(i, i ^ bit) for i in range(lax.axis_size('l...]
    ppermute x5 -> x6, starting transfers between devices: 8.14 us -> 10.7 us  [tile_swap(): lax.ppermute(block, 'tile', [(i, i ^ turn) for i in range(lax.axis_size('...]
    ppermute x12 -> x13, starting transfers between devices: 7.2 us -> 9.18 us  [list_swap(): lax.ppermute(block, 'list', [(i, i ^ bit) for i in range(lax.axis_size('l...]
    ppermute x1, waiting for transfers between devices: 1.68 us -> 0.01 us  [far_swap(): return lax.ppermute(block, ('tile', 'list'), route)]
    pallas_call x6, Pallas kernels: 2.71 us -> 3.17 us  [kernel_call(): pl.pallas_call(kernel, out_shape=tuple((jax.ShapeDtypeStruct(shape, kind)...]
    ppermute x2 -> x3, starting transfers between devices: 0.57 us -> 0.8 us  [middle_swap(): return lax.ppermute(block, ('tile', 'list'), route)]
    ppermute x5 -> x6, waiting for transfers between devices: 4.4 us -> 4.61 us  [tile_swap(): lax.ppermute(block, 'tile', [(i, i ^ turn) for i in range(lax.axis_size('...]
  transfers between devices with their start and end apart: 20 -> 23, of which waited for: 8 -> 6; matrix products, arithmetic and copies ran while one was open for 3% -> 3% of each run, Pallas kernels for 5% -> 6%
where the time goes in v12:
time: 39.1 us; the launch traced here: 38.9 us
  starting transfers between devices  22.8 us (58%)
  waiting for transfers between devices  8.65 us (22%)
  Pallas kernels  3.17 us (8%)
  other arithmetic  2.73 us (7%)
  between operations  1.55 us (4%)
    ppermute x6, starting transfers between devices, tile_swap(): lax.ppermute(block, 'tile', [(i, i ^ turn) for i in range(lax.axis_size('...  10.7 us
    ppermute x13, starting transfers between devices, list_swap(): lax.ppermute(block, 'list', [(i, i ^ bit) for i in range(lax.axis_size('l...  9.18 us
    ppermute x6, waiting for transfers between devices, tile_swap(): lax.ppermute(block, 'tile', [(i, i ^ turn) for i in range(lax.axis_size('...  4.61 us
    ppermute x13, waiting for transfers between devices, list_swap(): lax.ppermute(block, 'list', [(i, i ^ bit) for i in range(lax.axis_size('l...  4.04 us
    pallas_call x6, Pallas kernels, kernel_call(): pl.pallas_call(kernel, out_shape=tuple((jax.ShapeDtypeStruct(shape, kind)...  3.17 us
    ppermute x1, starting transfers between devices, far_swap(): return lax.ppermute(block, ('tile', 'list'), route)  2.08 us
    convert_element_type x1, other arithmetic, one_slot(): block = probes.astype(BF)  0.96 us
    another operation x1, other arithmetic, one_slot(): bases = jnp.stack([right_bases[0, 0], left_bases[0, 0]])  0.83 us
  transfers between devices with their start and end apart: 23, of which 6 were waited for; matrix products, arithmetic and copies ran while one was open for 3% of the time, Pallas kernels for 6%

profile of v12, /device:TPU:0, one launch (start us, length us, event | category | flops | bytes accessed | tf_op | source)
XLA Modules:
  0.0 38.9 jit_solution(3512715500045316723)
XLA Ops:
  0.0 0.8 %pad_maximum_fusion.1.bases_ref = bf16[2,24,1024]{2,1,0:T(8,128)(2,1)S(1)} fusion(bf16[1,24,1024]{2,1,0:T(8,128)(2,1)} %bitcast.10, bf16[1,24,1024]{2,1,0:T(8,128)(2,1)} %bitcast.11), kind=kLoop, calls=%fused_computation.7 | loop fusion | flops 49152 | bytes 196608 | tf_op jit(solution)/shard_map/stack | solution.py:243
  0.8 3.0 %collective-permute-start = (bf16[2,24,1024]{2,1,0:T(8,128)(2,1)S(1)}, bf16[2,24,1024]{2,1,0:T(8,128)(2,1)S(1)}, u32[]{:S(2)}, u32[]{:S(2)}) collective-permute-start(bf16[2,24,1024]{2,1,0:T(8,128)(2,1)S(1)} %pad_maximum_fusion.1.bases_ref), channel_id=1, source_target_pairs={{0,2},{1,3},{2,0},{3,1},{4,6},{5,7},{6,4},{7,5},{8,10},{9,11},{10,... | collective-permute-start | bytes 294920 | tf_op jit(solution)/shard_map/ppermute | solution.py:147
  3.8 1.0 %convert_element_type.27.block_ref.refs_0_ = bf16[256,256]{1,0:T(8,128)(2,1)S(1)} convert(f32[256,256]{1,0:T(8,128)} %param.7) | non-fusion elementwise | flops 65536 | bytes 393216 | tf_op jit(solution)/shard_map/convert_element_type | solution.py:246
  4.9 0.5 %collective-permute-start.4 = (bf16[256,256]{1,0:T(8,128)(2,1)S(1)}, bf16[256,256]{1,0:T(8,128)(2,1)S(1)}, u32[]{:S(2)}, u32[]{:S(2)}) collective-permute-start(bf16[256,256]{1,0:T(8,128)(2,1)S(1)} %convert_element_type.27.block_ref.refs_0_), channel_id=1, source_target_pairs={{0,1},{1,0},{2,3},{3,2},{4,8},{5,9},{6,10},{7,11},{8,4},{9,5},{10,... | collective-permute-start | bytes 393224 | tf_op jit(solution)/shard_map/ppermute | solution.py:133
  5.4 2.7 %collective-permute-start.3 = (bf16[256,256]{1,0:T(8,128)(2,1)S(1)}, bf16[256,256]{1,0:T(8,128)(2,1)S(1)}, u32[]{:S(2)}, u32[]{:S(2)}) collective-permute-start(bf16[256,256]{1,0:T(8,128)(2,1)S(1)} %convert_element_type.27.block_ref.refs_0_), channel_id=1, source_target_pairs={{0,4},{4,0},{8,12},{12,8},{1,5},{5,1},{9,13},{13,9},{2,6},{6,2},{1... | collective-permute-start | bytes 393224 | tf_op jit(solution)/shard_map/ppermute | solution.py:121
  9.1 1.8 %collective-permute-start.7 = (bf16[48,256]{1,0:T(8,128)(2,1)S(1)}, bf16[48,256]{1,0:T(8,128)(2,1)S(1)}, u32[]{:S(2)}, u32[]{:S(2)}) collective-permute-start(bf16[48,256]{1,0:T(8,128)(2,1)S(1)} %shard_map.64.refs_3_), channel_id=1, source_target_pairs={{0,12},{4,8},{8,4},{12,0},{1,13},{5,9},{9,5},{13,1},{2,14},{6,10},... | collective-permute-start | bytes 73736 | tf_op jit(solution)/shard_map/ppermute | solution.py:121
  10.9 2.6 %collective-permute-start.5 = (bf16[48,256]{1,0:T(8,128)(2,1)S(1)}, bf16[48,256]{1,0:T(8,128)(2,1)S(1)}, u32[]{:S(2)}, u32[]{:S(2)}) collective-permute-start(bf16[48,256]{1,0:T(8,128)(2,1)S(1)} %shard_map.64.refs_3_), channel_id=1, source_target_pairs={{0,4},{4,0},{8,12},{12,8},{1,5},{5,1},{9,13},{13,9},{2,6},{6,2},{1... | collective-permute-start | bytes 73736 | tf_op jit(solution)/shard_map/ppermute | solution.py:121
  14.2 0.6 %collective-permute-done.7.refs_6_ = bf16[48,256]{1,0:T(8,128)(2,1)S(1)} collective-permute-done((bf16[48,256]{1,0:T(8,128)(2,1)S(1)}, bf16[48,256]{1,0:T(8,128)(2,1)S(1)}, u32[]{:S(2)}, u32[]{:S(2)}) %collective-permute-start.7) | collective-permute-done | bytes 24608 | tf_op jit(solution)/shard_map/ppermute | solution.py:121
  14.8 0.8 %collective-permute-done.6.refs_5_ = bf16[48,256]{1,0:T(8,128)(2,1)S(1)} collective-permute-done((bf16[48,256]{1,0:T(8,128)(2,1)S(1)}, bf16[48,256]{1,0:T(8,128)(2,1)S(1)}, u32[]{:S(2)}, u32[]{:S(2)}) %collective-permute-start.6) | collective-permute-done | bytes 24608 | tf_op jit(solution)/shard_map/ppermute | solution.py:121
  15.7 0.5 %shard_map.65 = (f32[256,256]{1,0:T(8,128)S(1)}, f32[96,256]{1,0:T(8,128)S(1)}) custom-call(bf16[3,1024,256]{2,1,0:T(8,128)(2,1)S(1)} %bitcast.5, s32[1,1]{1,0:T(1,128)S(6)} %copy.8.columns_ref, bf16[2,24,1024]{2,1,0:T(8,128)(2,1)S(1)} %pad_maximum_fusion.1.bases_ref, bf16[2,24,1024]{2,1,0:T(8,128)(2,1)S(1)} %collective-permute-done.across_ref, ...), custom_call_target="tpu_custom_call" | custom-call | flops 100663296 | bytes 1572864 | tf_op jit(solution)/shard_map/pallas_call | solution.py:77
  16.3 0.9 %shard_map.66 = (f32[256,256]{1,0:T(8,128)S(1)}, f32[256,256]{1,0:T(8,128)S(1)}, f32[256,256]{1,0:T(8,128)S(1)}, f32[96,256]{1,0:T(8,128)S(1)}, f32[96,256]{1,0:T(8,128)S(1)}) custom-call(bf16[3,1024,256]{2,1,0:T(8,128)(2,1)S(1)} %bitcast.6, s32[1,1]{1,0:T(1,128)S(6)} %copy.8.columns_ref, bf16[2,24,1024]{2,1,0:T(8,128)(2,1)S(1)} %pad_maximum_fusion.1.bases_ref, ...), custom_call_target="tpu_custom_call" | custom-call | flops 301989888 | bytes 1572864 | tf_op jit(solution)/shard_map/pallas_call | solution.py:77
  17.1 0.6 %collective-permute-start.12 = (f32[96,256]{1,0:T(8,128)S(1)}, f32[96,256]{1,0:T(8,128)S(1)}, u32[]{:S(2)}, u32[]{:S(2)}) collective-permute-start(f32[96,256]{1,0:T(8,128)S(1)} %get-tuple-element.38), channel_id=1, source_target_pairs={{0,1},{1,0},{2,3},{3,2},{4,5},{5,4},{6,7},{7,6},{8,9},{9,8},{10,11... | collective-permute-start | bytes 294920 | tf_op jit(solution)/shard_map/ppermute | solution.py:147
  17.9 1.6 %collective-permute-start.10 = (bf16[160,256]{1,0:T(8,128)(2,1)S(1)}, bf16[160,256]{1,0:T(8,128)(2,1)S(1)}, u32[]{:S(2)}, u32[]{:S(2)}) collective-permute-start(bf16[160,256]{1,0:T(8,128)(2,1)S(1)} %slice.38), channel_id=1, source_target_pairs={{0,2},{1,3},{2,0},{3,1},{4,6},{5,7},{6,4},{7,5},{8,10},{9,11},{10,... | collective-permute-start | bytes 245768 | tf_op jit(solution)/shard_map/ppermute | solution.py:147
  19.5 2.1 %collective-permute-start.16 = (bf16[96,256]{1,0:T(8,128)(2,1)S(1)}, bf16[96,256]{1,0:T(8,128)(2,1)S(1)}, u32[]{:S(2)}, u32[]{:S(2)}) collective-permute-start(bf16[96,256]{1,0:T(8,128)(2,1)S(1)} %add_convert_fusion.3.refs_6_), channel_id=1, source_target_pairs={{0,8},{1,13},{2,10},{3,15},{4,12},{5,9},{6,14},{7,11},{8,0},{9,5},... | collective-permute-start | bytes 147464 | tf_op jit(solution)/shard_map/ppermute | solution.py:143
  21.5 0.7 %collective-permute-start.15 = (bf16[96,256]{1,0:T(8,128)(2,1)S(1)}, bf16[96,256]{1,0:T(8,128)(2,1)S(1)}, u32[]{:S(2)}, u32[]{:S(2)}) collective-permute-start(bf16[96,256]{1,0:T(8,128)(2,1)S(1)} %slice.40), channel_id=1, source_target_pairs={{0,2},{1,3},{2,0},{3,1},{4,6},{5,7},{6,4},{7,5},{8,10},{9,11},{10,... | collective-permute-start | bytes 147464 | tf_op jit(solution)/shard_map/ppermute | solution.py:147
  22.9 0.5 %collective-permute-start.11 = (bf16[2,24,1024]{2,1,0:T(8,128)(2,1)S(1)}, bf16[2,24,1024]{2,1,0:T(8,128)(2,1)S(1)}, u32[]{:S(2)}, u32[]{:S(2)}) collective-permute-start(bf16[2,24,1024]{2,1,0:T(8,128)(2,1)S(1)} %pad_maximum_fusion.3), channel_id=1, source_target_pairs={{0,1},{1,0},{2,3},{3,2},{4,5},{5,4},{6,7},{7,6},{8,9},{9,8},{10,11... | collective-permute-start | bytes 294920 | tf_op jit(solution)/shard_map/ppermute | solution.py:147
  23.4 2.3 %collective-permute-start.13 = (bf16[208,256]{1,0:T(8,128)(2,1)S(1)}, bf16[208,256]{1,0:T(8,128)(2,1)S(1)}, u32[]{:S(2)}, u32[]{:S(2)}) collective-permute-start(bf16[208,256]{1,0:T(8,128)(2,1)S(1)} %pad_maximum_fusion), channel_id=1, source_target_pairs={{0,4},{4,0},{8,12},{12,8},{1,5},{5,1},{9,13},{13,9},{2,6},{6,2},{1... | collective-permute-start | bytes 319496 | tf_op jit(solution)/shard_map/ppermute | solution.py:121
  26.0 1.2 %collective-permute-start.17 = (bf16[96,256]{1,0:T(8,128)(2,1)S(1)}, bf16[96,256]{1,0:T(8,128)(2,1)S(1)}, u32[]{:S(2)}, u32[]{:S(2)}) collective-permute-start(bf16[96,256]{1,0:T(8,128)(2,1)S(1)} %add_convert_fusion.2.refs_3_), channel_id=1, source_target_pairs={{0,4},{4,0},{8,12},{12,8},{1,5},{5,1},{9,13},{13,9},{2,6},{6,2},{1... | collective-permute-start | bytes 147464 | tf_op jit(solution)/shard_map/ppermute | solution.py:121
  27.2 3.1 %collective-permute-done.17.refs_4_ = bf16[96,256]{1,0:T(8,128)(2,1)S(1)} collective-permute-done((bf16[96,256]{1,0:T(8,128)(2,1)S(1)}, bf16[96,256]{1,0:T(8,128)(2,1)S(1)}, u32[]{:S(2)}, u32[]{:S(2)}) %collective-permute-start.17) | collective-permute-done | bytes 49184 | tf_op jit(solution)/shard_map/ppermute | solution.py:121
  31.4 1.0 %collective-permute-done.19 = f32[256,256]{1,0:T(8,128)S(1)} collective-permute-done((f32[256,256]{1,0:T(8,128)S(1)}, f32[256,256]{1,0:T(8,128)S(1)}, u32[]{:S(2)}, u32[]{:S(2)}) %collective-permute-start.19) | collective-permute-done | bytes 262176 | tf_op jit(solution)/shard_map/ppermute | solution.py:147
  32.5 1.9 %collective-permute-start.22 = (bf16[256,256]{1,0:T(8,128)(2,1)S(1)}, bf16[256,256]{1,0:T(8,128)(2,1)S(1)}, u32[]{:S(2)}, u32[]{:S(2)}) collective-permute-start(bf16[256,256]{1,0:T(8,128)(2,1)S(1)} %add_convert_fusion), channel_id=1, source_target_pairs={{0,2},{1,3},{2,0},{3,1},{4,6},{5,7},{6,4},{7,5},{8,10},{9,11},{10,... | collective-permute-start | bytes 393224 | tf_op jit(solution)/shard_map/ppermute | solution.py:147
  34.4 0.6 %shard_map.69 = (f32[256,256]{1,0:T(8,128)S(1)}, f32[256,256]{1,0:T(8,128)S(1)}) custom-call(bf16[3,1024,256]{2,1,0:T(8,128)(2,1)S(1)} %bitcast.9, s32[1,1]{1,0:T(1,128)S(6)} %copy.8.columns_ref, bf16[2,24,1024]{2,1,0:T(8,128)(2,1)S(1)} %pad_maximum_fusion.1.bases_ref, bf16[2,24,1024]{2,1,0:T(8,128)(2,1)S(1)} %collective-permute-done.across_ref, ...), custom_call_target="tpu_custom_call" | custom-call | flops 201326592 | bytes 1572864 | tf_op jit(solution)/shard_map/pallas_call | solution.py:77
  35.6 2.5 %collective-permute-done.22 = bf16[256,256]{1,0:T(8,128)(2,1)S(1)} collective-permute-done((bf16[256,256]{1,0:T(8,128)(2,1)S(1)}, bf16[256,256]{1,0:T(8,128)(2,1)S(1)}, u32[]{:S(2)}, u32[]{:S(2)}) %collective-permute-start.22) | collective-permute-done | bytes 131104 | tf_op jit(solution)/shard_map/ppermute | solution.py:147
  38.2 0.7 %fusion = f32[256,256]{1,0:T(8,128)} fusion(f32[256,256]{1,0:T(8,128)S(1)} %get-tuple-element.44, f32[128,256]{1,0:T(8,128)S(1)} %collective-permute-done.21, f32[128,256]{1,0:T(8,128)S(1)} %collective-permute-done.20, bf16[256,256]{1,0:T(8,128)(2,1)S(1)} %collective-permute-done.22), kind=kLoop, calls=%fused_computation.1 | loop fusion | flops 262144 | bytes 917504 | tf_op jit(solution)/shard_map/add | solution.py:300
  (50 shorter events, 3.1 us)
Async XLA Ops:
  0.8 7.9 %collective-permute-start = (bf16[2,24,1024]{2,1,0:T(8,128)(2,1)S(1)}, bf16[2,24,1024]{2,1,0:T(8,128)(2,1)S(1)}, u32[]{:S(2)}, u32[]{:S(2)}) collective-permute-start(bf16[2,24,1024]{2,1,0:T(8,128)(2,1)S(1)} %pad_maximum_fusion.1.bases_ref), channel_id=1, source_target_pairs={{0,2},{1,3},{2,0},{3,1},{4,6},{5,7},{6,4},{7,5},{8,10},{9,11},{10,... | collective-permute-start | bytes 294920 | tf_op jit(solution)/shard_map/ppermute | solution.py:147
  4.8 4.0 %collective-permute-start.1 = (bf16[256,256]{1,0:T(8,128)(2,1)S(1)}, bf16[256,256]{1,0:T(8,128)(2,1)S(1)}, u32[]{:S(2)}, u32[]{:S(2)}) collective-permute-start(bf16[256,256]{1,0:T(8,128)(2,1)S(1)} %convert_element_type.27.block_ref.refs_0_), channel_id=1, source_target_pairs={{0,1},{1,0},{2,3},{3,2},{4,5},{5,4},{6,7},{7,6},{8,9},{9,8},{10,11... | collective-permute-start | bytes 393224 | tf_op jit(solution)/shard_map/ppermute | solution.py:147
  4.9 6.0 %collective-permute-start.4 = (bf16[256,256]{1,0:T(8,128)(2,1)S(1)}, bf16[256,256]{1,0:T(8,128)(2,1)S(1)}, u32[]{:S(2)}, u32[]{:S(2)}) collective-permute-start(bf16[256,256]{1,0:T(8,128)(2,1)S(1)} %convert_element_type.27.block_ref.refs_0_), channel_id=1, source_target_pairs={{0,1},{1,0},{2,3},{3,2},{4,8},{5,9},{6,10},{7,11},{8,4},{9,5},{10,... | collective-permute-start | bytes 393224 | tf_op jit(solution)/shard_map/ppermute | solution.py:133
  5.4 8.8 %collective-permute-start.3 = (bf16[256,256]{1,0:T(8,128)(2,1)S(1)}, bf16[256,256]{1,0:T(8,128)(2,1)S(1)}, u32[]{:S(2)}, u32[]{:S(2)}) collective-permute-start(bf16[256,256]{1,0:T(8,128)(2,1)S(1)} %convert_element_type.27.block_ref.refs_0_), channel_id=1, source_target_pairs={{0,4},{4,0},{8,12},{12,8},{1,5},{5,1},{9,13},{13,9},{2,6},{6,2},{1... | collective-permute-start | bytes 393224 | tf_op jit(solution)/shard_map/ppermute | solution.py:121
  8.8 6.9 %copy-start = (bf16[1,1024,3,256]{3,1,2,0:T(8,128)(2,1)S(1)}, bf16[1,1024,3,256]{3,1,2,0:T(8,128)(2,1)}, u32[]{:S(2)}) copy-start(bf16[1,1024,3,256]{3,1,2,0:T(8,128)(2,1)} %param.10) | copy-start | bytes 4718596
  9.0 6.7 %collective-permute-start.2 = (bf16[2,24,1024]{2,1,0:T(8,128)(2,1)S(1)}, bf16[2,24,1024]{2,1,0:T(8,128)(2,1)S(1)}, u32[]{:S(2)}, u32[]{:S(2)}) collective-permute-start(bf16[2,24,1024]{2,1,0:T(8,128)(2,1)S(1)} %pad_maximum_fusion.2), channel_id=1, source_target_pairs={{0,1},{1,0},{2,3},{3,2},{4,5},{5,4},{6,7},{7,6},{8,9},{9,8},{10,11... | collective-permute-start | bytes 294920 | tf_op jit(solution)/shard_map/ppermute | solution.py:147
  9.1 5.7 %collective-permute-start.7 = (bf16[48,256]{1,0:T(8,128)(2,1)S(1)}, bf16[48,256]{1,0:T(8,128)(2,1)S(1)}, u32[]{:S(2)}, u32[]{:S(2)}) collective-permute-start(bf16[48,256]{1,0:T(8,128)(2,1)S(1)} %shard_map.64.refs_3_), channel_id=1, source_target_pairs={{0,12},{4,8},{8,4},{12,0},{1,13},{5,9},{9,5},{13,1},{2,14},{6,10},... | collective-permute-start | bytes 73736 | tf_op jit(solution)/shard_map/ppermute | solution.py:121
  10.9 4.7 %collective-permute-start.6 = (bf16[48,256]{1,0:T(8,128)(2,1)S(1)}, bf16[48,256]{1,0:T(8,128)(2,1)S(1)}, u32[]{:S(2)}, u32[]{:S(2)}) collective-permute-start(bf16[48,256]{1,0:T(8,128)(2,1)S(1)} %shard_map.64.refs_3_), channel_id=1, source_target_pairs={{0,8},{4,12},{8,0},{12,4},{1,9},{5,13},{9,1},{13,5},{2,10},{6,14},... | collective-permute-start | bytes 73736 | tf_op jit(solution)/shard_map/ppermute | solution.py:121
  10.9 4.7 %collective-permute-start.5 = (bf16[48,256]{1,0:T(8,128)(2,1)S(1)}, bf16[48,256]{1,0:T(8,128)(2,1)S(1)}, u32[]{:S(2)}, u32[]{:S(2)}) collective-permute-start(bf16[48,256]{1,0:T(8,128)(2,1)S(1)} %shard_map.64.refs_3_), channel_id=1, source_target_pairs={{0,4},{4,0},{8,12},{12,8},{1,5},{5,1},{9,13},{13,9},{2,6},{6,2},{1... | collective-permute-start | bytes 73736 | tf_op jit(solution)/shard_map/ppermute | solution.py:121
  16.2 1.6 %collective-permute-start.9 = (f32[256,256]{1,0:T(8,128)S(1)}, f32[256,256]{1,0:T(8,128)S(1)}, u32[]{:S(2)}, u32[]{:S(2)}) collective-permute-start(f32[256,256]{1,0:T(8,128)S(1)} %get-tuple-element.33), channel_id=1, source_target_pairs={{0,1},{1,0},{2,3},{3,2},{4,5},{5,4},{6,7},{7,6},{8,9},{9,8},{10,11... | collective-permute-start | bytes 786440 | tf_op jit(solution)/shard_map/ppermute | solution.py:147
  17.1 2.3 %collective-permute-start.12 = (f32[96,256]{1,0:T(8,128)S(1)}, f32[96,256]{1,0:T(8,128)S(1)}, u32[]{:S(2)}, u32[]{:S(2)}) collective-permute-start(f32[96,256]{1,0:T(8,128)S(1)} %get-tuple-element.38), channel_id=1, source_target_pairs={{0,1},{1,0},{2,3},{3,2},{4,5},{5,4},{6,7},{7,6},{8,9},{9,8},{10,11... | collective-permute-start | bytes 294920 | tf_op jit(solution)/shard_map/ppermute | solution.py:147
  17.7 4.6 %collective-permute-start.8 = (f32[256,256]{1,0:T(8,128)S(1)}, f32[256,256]{1,0:T(8,128)S(1)}, u32[]{:S(2)}, u32[]{:S(2)}) collective-permute-start(f32[256,256]{1,0:T(8,128)S(1)} %get-tuple-element.31), channel_id=1, source_target_pairs={{0,1},{1,0},{2,3},{3,2},{4,5},{5,4},{6,7},{7,6},{8,9},{9,8},{10,11... | collective-permute-start | bytes 786440 | tf_op jit(solution)/shard_map/ppermute | solution.py:147
  17.9 4.8 %collective-permute-start.10 = (bf16[160,256]{1,0:T(8,128)(2,1)S(1)}, bf16[160,256]{1,0:T(8,128)(2,1)S(1)}, u32[]{:S(2)}, u32[]{:S(2)}) collective-permute-start(bf16[160,256]{1,0:T(8,128)(2,1)S(1)} %slice.38), channel_id=1, source_target_pairs={{0,2},{1,3},{2,0},{3,1},{4,6},{5,7},{6,4},{7,5},{8,10},{9,11},{10,... | collective-permute-start | bytes 245768 | tf_op jit(solution)/shard_map/ppermute | solution.py:147
  19.5 6.3 %collective-permute-start.16 = (bf16[96,256]{1,0:T(8,128)(2,1)S(1)}, bf16[96,256]{1,0:T(8,128)(2,1)S(1)}, u32[]{:S(2)}, u32[]{:S(2)}) collective-permute-start(bf16[96,256]{1,0:T(8,128)(2,1)S(1)} %add_convert_fusion.3.refs_6_), channel_id=1, source_target_pairs={{0,8},{1,13},{2,10},{3,15},{4,12},{5,9},{6,14},{7,11},{8,0},{9,5},... | collective-permute-start | bytes 147464 | tf_op jit(solution)/shard_map/ppermute | solution.py:143
  21.5 4.2 %collective-permute-start.15 = (bf16[96,256]{1,0:T(8,128)(2,1)S(1)}, bf16[96,256]{1,0:T(8,128)(2,1)S(1)}, u32[]{:S(2)}, u32[]{:S(2)}) collective-permute-start(bf16[96,256]{1,0:T(8,128)(2,1)S(1)} %slice.40), channel_id=1, source_target_pairs={{0,2},{1,3},{2,0},{3,1},{4,6},{5,7},{6,4},{7,5},{8,10},{9,11},{10,... | collective-permute-start | bytes 147464 | tf_op jit(solution)/shard_map/ppermute | solution.py:147
  22.7 7.6 %collective-permute-start.14 = (bf16[160,256]{1,0:T(8,128)(2,1)S(1)}, bf16[160,256]{1,0:T(8,128)(2,1)S(1)}, u32[]{:S(2)}, u32[]{:S(2)}) collective-permute-start(bf16[160,256]{1,0:T(8,128)(2,1)S(1)} %fusion.1.refs_0_), channel_id=1, source_target_pairs={{0,1},{1,0},{2,3},{3,2},{4,8},{5,9},{6,10},{7,11},{8,4},{9,5},{10,... | collective-permute-start | bytes 245768 | tf_op jit(solution)/shard_map/ppermute | solution.py:133
  22.9 7.5 %collective-permute-start.11 = (bf16[2,24,1024]{2,1,0:T(8,128)(2,1)S(1)}, bf16[2,24,1024]{2,1,0:T(8,128)(2,1)S(1)}, u32[]{:S(2)}, u32[]{:S(2)}) collective-permute-start(bf16[2,24,1024]{2,1,0:T(8,128)(2,1)S(1)} %pad_maximum_fusion.3), channel_id=1, source_target_pairs={{0,1},{1,0},{2,3},{3,2},{4,5},{5,4},{6,7},{7,6},{8,9},{9,8},{10,11... | collective-permute-start | bytes 294920 | tf_op jit(solution)/shard_map/ppermute | solution.py:147
  23.4 6.9 %collective-permute-start.13 = (bf16[208,256]{1,0:T(8,128)(2,1)S(1)}, bf16[208,256]{1,0:T(8,128)(2,1)S(1)}, u32[]{:S(2)}, u32[]{:S(2)}) collective-permute-start(bf16[208,256]{1,0:T(8,128)(2,1)S(1)} %pad_maximum_fusion), channel_id=1, source_target_pairs={{0,4},{4,0},{8,12},{12,8},{1,5},{5,1},{9,13},{13,9},{2,6},{6,2},{1... | collective-permute-start | bytes 319496 | tf_op jit(solution)/shard_map/ppermute | solution.py:121
  25.8 1.4 %collective-permute-start.18 = (bf16[96,256]{1,0:T(8,128)(2,1)S(1)}, bf16[96,256]{1,0:T(8,128)(2,1)S(1)}, u32[]{:S(2)}, u32[]{:S(2)}) collective-permute-start(bf16[96,256]{1,0:T(8,128)(2,1)S(1)} %add_convert_fusion.2.refs_3_), channel_id=1, source_target_pairs={{0,1},{1,0},{2,3},{3,2},{4,8},{5,9},{6,10},{7,11},{8,4},{9,5},{10,... | collective-permute-start | bytes 147464 | tf_op jit(solution)/shard_map/ppermute | solution.py:133
  26.0 4.4 %collective-permute-start.17 = (bf16[96,256]{1,0:T(8,128)(2,1)S(1)}, bf16[96,256]{1,0:T(8,128)(2,1)S(1)}, u32[]{:S(2)}, u32[]{:S(2)}) collective-permute-start(bf16[96,256]{1,0:T(8,128)(2,1)S(1)} %add_convert_fusion.2.refs_3_), channel_id=1, source_target_pairs={{0,4},{4,0},{8,12},{12,8},{1,5},{5,1},{9,13},{13,9},{2,6},{6,2},{1... | collective-permute-start | bytes 147464 | tf_op jit(solution)/shard_map/ppermute | solution.py:121
  30.9 1.6 %collective-permute-start.19 = (f32[256,256]{1,0:T(8,128)S(1)}, f32[256,256]{1,0:T(8,128)S(1)}, u32[]{:S(2)}, u32[]{:S(2)}) collective-permute-start(f32[256,256]{1,0:T(8,128)S(1)} %shard_map.68), channel_id=1, source_target_pairs={{0,1},{1,0},{2,3},{3,2},{4,5},{5,4},{6,7},{7,6},{8,9},{9,8},{10,11... | collective-permute-start | bytes 786440 | tf_op jit(solution)/shard_map/ppermute | solution.py:147
  32.5 5.7 %collective-permute-start.22 = (bf16[256,256]{1,0:T(8,128)(2,1)S(1)}, bf16[256,256]{1,0:T(8,128)(2,1)S(1)}, u32[]{:S(2)}, u32[]{:S(2)}) collective-permute-start(bf16[256,256]{1,0:T(8,128)(2,1)S(1)} %add_convert_fusion), channel_id=1, source_target_pairs={{0,2},{1,3},{2,0},{3,1},{4,6},{5,7},{6,4},{7,5},{8,10},{9,11},{10,... | collective-permute-start | bytes 393224 | tf_op jit(solution)/shard_map/ppermute | solution.py:147
  35.1 3.1 %collective-permute-start.20 = (f32[128,256]{1,0:T(8,128)S(1)}, f32[128,256]{1,0:T(8,128)S(1)}, u32[]{:S(2)}, u32[]{:S(2)}) collective-permute-start(f32[128,256]{1,0:T(8,128)S(1)} %get-tuple-element.47), channel_id=1, source_target_pairs={{0,1},{1,0},{2,3},{3,2},{4,5},{5,4},{6,7},{7,6},{8,9},{9,8},{10,11... | collective-permute-start | bytes 393224 | tf_op jit(solution)/shard_map/ppermute | solution.py:147
  35.1 3.0 %collective-permute-start.21 = (f32[128,256]{1,0:T(8,128)S(1)}, f32[128,256]{1,0:T(8,128)S(1)}, u32[]{:S(2)}, u32[]{:S(2)}) collective-permute-start(f32[128,256]{1,0:T(8,128)S(1)} %get-tuple-element.48), channel_id=1, source_target_pairs={{0,1},{1,0},{2,3},{3,2},{4,5},{5,4},{6,7},{7,6},{8,9},{9,8},{10,11... | collective-permute-start | bytes 393224 | tf_op jit(solution)/shard_map/ppermute | solution.py:147

commit v13 on v11

--- a/solution.py
+++ b/solution.py
@@ -155,10 +155,10 @@
 
 
 def far_choice(columns, tile, me, refs):
-    own_ref, message_ref, far_ref = refs
+    own_ref, near_by_ref, far_ref = refs
     half = own_ref.shape[0] // 2
     first = jnp.where(columns == tile, own_ref[:half, :], 0)
-    first = jnp.where(columns == tile ^ 1, message_ref[message_ref.shape[0] - half :, :], first)
+    first = jnp.where(columns == tile ^ 1, near_by_ref[...], first)
     far = columns == tile ^ (2 + lax.rem(me, 2))
     return jnp.concatenate(
         [jnp.where(far, far_ref[:half, :], first), jnp.where(far, far_ref[half:, :], 0)]
@@ -176,7 +176,7 @@
     inside = (tile > 0) & (tile < count - 1)
     blocks = [
         (1, block_refs[0][...]),
-        (2 - 2 * odd, block_refs[1][:rows, :]),
+        (2 - 2 * odd, block_refs[1][...]),
         (2 * odd, jnp.where(inside, block_refs[2][...], 0)),
     ]
     totals = []
@@ -262,14 +262,15 @@
     )
     crossed = list_swap((crossing + arrived).astype(BF), 2)
     own = (own + list_swap(other, 1)).astype(BF)
-    far = far_swap(own)
+    near_by, far = tile_swap(own[: ranks // 2], 1), far_swap(own)
     block = (keep + list_swap(send, 1) + crossed).astype(BF)
-    message = tile_swap(jnp.concatenate([block, own[: ranks // 2]]), 1)
-    beside = [block, message, middle_swap(block)]
-    held, held_across, far, block = lax.optimization_barrier((bases, across, far, block))
+    held, held_across, near_by, far, ready = lax.optimization_barrier(
+        (bases, across, near_by, far, block)
+    )
+    beside = [block, tile_swap(ready, 1), middle_swap(block)]
     left = list_swap(jnp.stack([held[1], held_across[1]]), 1)
 
-    operands = (*fixed, left, *beside, own, message, far)
+    operands = (*fixed, left, *beside, own, near_by, far)
 
     def second(turns, operands):
         kernel = functools.partial(second_kernel, turns)

time: 39.5 us -> 39.3 us (level)
  waiting for transfers between devices: 14.3 us -> 13.8 us
    ppermute x1, waiting for transfers between devices: 1.68 us -> 0.01 us  [far_swap(): return lax.ppermute(block, ('tile', 'list'), route)]
    ppermute x5 -> x6, waiting for transfers between devices: 4.4 us -> 6.03 us  [tile_swap(): lax.ppermute(block, 'tile', [(i, i ^ turn) for i in range(lax.axis_size('...]
    ppermute x5 -> x6, starting transfers between devices: 8.14 us -> 8.37 us  [tile_swap(): lax.ppermute(block, 'tile', [(i, i ^ turn) for i in range(lax.axis_size('...]
  transfers between devices with their start and end apart: 20 -> 21, of which waited for: 8 -> 8; matrix products, arithmetic and copies ran while one was open for 3% -> 3% of each run, Pallas kernels for 5% -> 5%
where the time goes in v13:
time: 39.3 us; the launch traced here: 39.1 us
  starting transfers between devices  18.2 us (46%)
  waiting for transfers between devices  13.8 us (35%)
  other arithmetic  2.73 us (7%)
  Pallas kernels  2.71 us (7%)
  between operations  1.51 us (4%)
    ppermute x6, starting transfers between devices, tile_swap(): lax.ppermute(block, 'tile', [(i, i ^ turn) for i in range(lax.axis_size('...  8.37 us
    ppermute x12, waiting for transfers between devices, list_swap(): lax.ppermute(block, 'list', [(i, i ^ bit) for i in range(lax.axis_size('l...  7.82 us
    ppermute x12, starting transfers between devices, list_swap(): lax.ppermute(block, 'list', [(i, i ^ bit) for i in range(lax.axis_size('l...  7.22 us
    ppermute x6, waiting for transfers between devices, tile_swap(): lax.ppermute(block, 'tile', [(i, i ^ turn) for i in range(lax.axis_size('...  6.03 us
    pallas_call x6, Pallas kernels, kernel_call(): pl.pallas_call(kernel, out_shape=tuple((jax.ShapeDtypeStruct(shape, kind)...  2.71 us
    ppermute x1, starting transfers between devices, far_swap(): return lax.ppermute(block, ('tile', 'list'), route)  2.08 us
    convert_element_type x1, other arithmetic, one_slot(): block = probes.astype(BF)  0.96 us
    another operation x1, other arithmetic, one_slot(): bases = jnp.stack([right_bases[0, 0], left_bases[0, 0]])  0.83 us
  transfers between devices with their start and end apart: 21, of which 8 were waited for; matrix products, arithmetic and copies ran while one was open for 3% of the time, Pallas kernels for 5%

profile of v13, /device:TPU:0, one launch (start us, length us, event | category | flops | bytes accessed | tf_op | source)
XLA Modules:
  0.0 39.1 jit_solution(11665990600687286262)
XLA Ops:
  0.0 0.8 %pad_maximum_fusion.bases_ref = bf16[2,24,1024]{2,1,0:T(8,128)(2,1)S(1)} fusion(bf16[1,24,1024]{2,1,0:T(8,128)(2,1)} %bitcast.10, bf16[1,24,1024]{2,1,0:T(8,128)(2,1)} %bitcast.11), kind=kLoop, calls=%fused_computation.5 | loop fusion | flops 49152 | bytes 196608 | tf_op jit(solution)/shard_map/stack | solution.py:237
  0.8 3.0 %collective-permute-start = (bf16[2,24,1024]{2,1,0:T(8,128)(2,1)S(1)}, bf16[2,24,1024]{2,1,0:T(8,128)(2,1)S(1)}, u32[]{:S(2)}, u32[]{:S(2)}) collective-permute-start(bf16[2,24,1024]{2,1,0:T(8,128)(2,1)S(1)} %pad_maximum_fusion.bases_ref), channel_id=1, source_target_pairs={{0,2},{1,3},{2,0},{3,1},{4,6},{5,7},{6,4},{7,5},{8,10},{9,11},{10,... | collective-permute-start | bytes 294920 | tf_op jit(solution)/shard_map/ppermute | solution.py:147
  3.8 1.0 %convert_element_type.21.block_ref.refs_0_ = bf16[256,256]{1,0:T(8,128)(2,1)S(1)} convert(f32[256,256]{1,0:T(8,128)} %param.7) | non-fusion elementwise | flops 65536 | bytes 393216 | tf_op jit(solution)/shard_map/convert_element_type | solution.py:240
  4.9 0.5 %collective-permute-start.4 = (bf16[256,256]{1,0:T(8,128)(2,1)S(1)}, bf16[256,256]{1,0:T(8,128)(2,1)S(1)}, u32[]{:S(2)}, u32[]{:S(2)}) collective-permute-start(bf16[256,256]{1,0:T(8,128)(2,1)S(1)} %convert_element_type.21.block_ref.refs_0_), channel_id=1, source_target_pairs={{0,1},{1,0},{2,3},{3,2},{4,8},{5,9},{6,10},{7,11},{8,4},{9,5},{10,... | collective-permute-start | bytes 393224 | tf_op jit(solution)/shard_map/ppermute | solution.py:133
  5.4 2.7 %collective-permute-start.3 = (bf16[256,256]{1,0:T(8,128)(2,1)S(1)}, bf16[256,256]{1,0:T(8,128)(2,1)S(1)}, u32[]{:S(2)}, u32[]{:S(2)}) collective-permute-start(bf16[256,256]{1,0:T(8,128)(2,1)S(1)} %convert_element_type.21.block_ref.refs_0_), channel_id=1, source_target_pairs={{0,4},{4,0},{8,12},{12,8},{1,5},{5,1},{9,13},{13,9},{2,6},{6,2},{1... | collective-permute-start | bytes 393224 | tf_op jit(solution)/shard_map/ppermute | solution.py:121
  9.1 1.8 %collective-permute-start.7 = (bf16[48,256]{1,0:T(8,128)(2,1)S(1)}, bf16[48,256]{1,0:T(8,128)(2,1)S(1)}, u32[]{:S(2)}, u32[]{:S(2)}) collective-permute-start(bf16[48,256]{1,0:T(8,128)(2,1)S(1)} %shard_map.64.refs_3_), channel_id=1, source_target_pairs={{0,12},{4,8},{8,4},{12,0},{1,13},{5,9},{9,5},{13,1},{2,14},{6,10},... | collective-permute-start | bytes 73736 | tf_op jit(solution)/shard_map/ppermute | solution.py:121
  10.9 2.6 %collective-permute-start.5 = (bf16[48,256]{1,0:T(8,128)(2,1)S(1)}, bf16[48,256]{1,0:T(8,128)(2,1)S(1)}, u32[]{:S(2)}, u32[]{:S(2)}) collective-permute-start(bf16[48,256]{1,0:T(8,128)(2,1)S(1)} %shard_map.64.refs_3_), channel_id=1, source_target_pairs={{0,4},{4,0},{8,12},{12,8},{1,5},{5,1},{9,13},{13,9},{2,6},{6,2},{1... | collective-permute-start | bytes 73736 | tf_op jit(solution)/shard_map/ppermute | solution.py:121
  14.2 0.6 %collective-permute-done.7.refs_6_ = bf16[48,256]{1,0:T(8,128)(2,1)S(1)} collective-permute-done((bf16[48,256]{1,0:T(8,128)(2,1)S(1)}, bf16[48,256]{1,0:T(8,128)(2,1)S(1)}, u32[]{:S(2)}, u32[]{:S(2)}) %collective-permute-start.7) | collective-permute-done | bytes 24608 | tf_op jit(solution)/shard_map/ppermute | solution.py:121
  14.8 0.8 %collective-permute-done.6.refs_5_ = bf16[48,256]{1,0:T(8,128)(2,1)S(1)} collective-permute-done((bf16[48,256]{1,0:T(8,128)(2,1)S(1)}, bf16[48,256]{1,0:T(8,128)(2,1)S(1)}, u32[]{:S(2)}, u32[]{:S(2)}) %collective-permute-start.6) | collective-permute-done | bytes 24608 | tf_op jit(solution)/shard_map/ppermute | solution.py:121
  15.7 0.5 %shard_map.65 = (f32[256,256]{1,0:T(8,128)S(1)}, f32[96,256]{1,0:T(8,128)S(1)}) custom-call(bf16[3,1024,256]{2,1,0:T(8,128)(2,1)S(1)} %bitcast.5, s32[1,1]{1,0:T(1,128)S(6)} %copy.8.columns_ref, bf16[2,24,1024]{2,1,0:T(8,128)(2,1)S(1)} %pad_maximum_fusion.bases_ref, bf16[2,24,1024]{2,1,0:T(8,128)(2,1)S(1)} %collective-permute-done.across_ref, ...), custom_call_target="tpu_custom_call" | custom-call | flops 100663296 | bytes 1572864 | tf_op jit(solution)/shard_map/pallas_call | solution.py:77
  16.3 0.9 %shard_map.66 = (f32[256,256]{1,0:T(8,128)S(1)}, f32[256,256]{1,0:T(8,128)S(1)}, f32[256,256]{1,0:T(8,128)S(1)}, f32[96,256]{1,0:T(8,128)S(1)}, f32[96,256]{1,0:T(8,128)S(1)}) custom-call(bf16[3,1024,256]{2,1,0:T(8,128)(2,1)S(1)} %bitcast.6, s32[1,1]{1,0:T(1,128)S(6)} %copy.8.columns_ref, bf16[2,24,1024]{2,1,0:T(8,128)(2,1)S(1)} %pad_maximum_fusion.bases_ref, ...), custom_call_target="tpu_custom_call" | custom-call | flops 301989888 | bytes 1572864 | tf_op jit(solution)/shard_map/pallas_call | solution.py:77
  17.1 0.6 %collective-permute-start.8 = (f32[96,256]{1,0:T(8,128)S(1)}, f32[96,256]{1,0:T(8,128)S(1)}, u32[]{:S(2)}, u32[]{:S(2)}) collective-permute-start(f32[96,256]{1,0:T(8,128)S(1)} %get-tuple-element.29), channel_id=1, source_target_pairs={{0,1},{1,0},{2,3},{3,2},{4,5},{5,4},{6,7},{7,6},{8,9},{9,8},{10,11... | collective-permute-start | bytes 294920 | tf_op jit(solution)/shard_map/ppermute | solution.py:147
  17.9 1.6 %collective-permute-start.13 = (bf16[256,256]{1,0:T(8,128)(2,1)S(1)}, bf16[256,256]{1,0:T(8,128)(2,1)S(1)}, u32[]{:S(2)}, u32[]{:S(2)}) collective-permute-start(bf16[256,256]{1,0:T(8,128)(2,1)S(1)} %add_convert_fusion.2), channel_id=1, source_target_pairs={{0,2},{1,3},{2,0},{3,1},{4,6},{5,7},{6,4},{7,5},{8,10},{9,11},{10,... | collective-permute-start | bytes 393224 | tf_op jit(solution)/shard_map/ppermute | solution.py:147
  19.4 2.1 %collective-permute-start.10 = (bf16[96,256]{1,0:T(8,128)(2,1)S(1)}, bf16[96,256]{1,0:T(8,128)(2,1)S(1)}, u32[]{:S(2)}, u32[]{:S(2)}) collective-permute-start(bf16[96,256]{1,0:T(8,128)(2,1)S(1)} %add_convert_fusion.3.refs_3_), channel_id=1, source_target_pairs={{0,8},{1,13},{2,10},{3,15},{4,12},{5,9},{6,14},{7,11},{8,0},{9,5},... | collective-permute-start | bytes 147464 | tf_op jit(solution)/shard_map/ppermute | solution.py:143
  21.9 1.9 %collective-permute-done.13 = bf16[256,256]{1,0:T(8,128)(2,1)S(1)} collective-permute-done((bf16[256,256]{1,0:T(8,128)(2,1)S(1)}, bf16[256,256]{1,0:T(8,128)(2,1)S(1)}, u32[]{:S(2)}, u32[]{:S(2)}) %collective-permute-start.13) | collective-permute-done | bytes 131104 | tf_op jit(solution)/shard_map/ppermute | solution.py:147
  23.9 1.8 %collective-permute-done.9.refs_4_ = bf16[48,256]{1,0:T(8,128)(2,1)S(1)} collective-permute-done((bf16[48,256]{1,0:T(8,128)(2,1)S(1)}, bf16[48,256]{1,0:T(8,128)(2,1)S(1)}, u32[]{:S(2)}, u32[]{:S(2)}) %collective-permute-start.9) | collective-permute-done | bytes 24608 | tf_op jit(solution)/shard_map/ppermute | solution.py:121
  25.7 0.9 %collective-permute-start.15 = (bf16[256,256]{1,0:T(8,128)(2,1)S(1)}, bf16[256,256]{1,0:T(8,128)(2,1)S(1)}, u32[]{:S(2)}, u32[]{:S(2)}) collective-permute-start(bf16[256,256]{1,0:T(8,128)(2,1)S(1)} %add_convert_fusion.1.refs_0_), channel_id=1, source_target_pairs={{0,4},{4,0},{8,12},{12,8},{1,5},{5,1},{9,13},{13,9},{2,6},{6,2},{1... | collective-permute-start | bytes 393224 | tf_op jit(solution)/shard_map/ppermute | solution.py:121
  26.6 1.3 %collective-permute-done.14.other_ref = bf16[2,24,1024]{2,1,0:T(8,128)(2,1)S(1)} collective-permute-done((bf16[2,24,1024]{2,1,0:T(8,128)(2,1)S(1)}, bf16[2,24,1024]{2,1,0:T(8,128)(2,1)S(1)}, u32[]{:S(2)}, u32[]{:S(2)}) %collective-permute-start.14) | collective-permute-done | bytes 98336 | tf_op jit(solution)/shard_map/ppermute | solution.py:147
  27.9 2.8 %collective-permute-done.15.refs_1_ = bf16[256,256]{1,0:T(8,128)(2,1)S(1)} collective-permute-done((bf16[256,256]{1,0:T(8,128)(2,1)S(1)}, bf16[256,256]{1,0:T(8,128)(2,1)S(1)}, u32[]{:S(2)}, u32[]{:S(2)}) %collective-permute-start.15) | collective-permute-done | bytes 131104 | tf_op jit(solution)/shard_map/ppermute | solution.py:121
  31.5 1.2 %collective-permute-done.17 = f32[256,256]{1,0:T(8,128)S(1)} collective-permute-done((f32[256,256]{1,0:T(8,128)S(1)}, f32[256,256]{1,0:T(8,128)S(1)}, u32[]{:S(2)}, u32[]{:S(2)}) %collective-permute-start.17) | collective-permute-done | bytes 262176 | tf_op jit(solution)/shard_map/ppermute | solution.py:147
  32.7 1.1 %collective-permute-start.20 = (bf16[256,256]{1,0:T(8,128)(2,1)S(1)}, bf16[256,256]{1,0:T(8,128)(2,1)S(1)}, u32[]{:S(2)}, u32[]{:S(2)}) collective-permute-start(bf16[256,256]{1,0:T(8,128)(2,1)S(1)} %add_convert_fusion), channel_id=1, source_target_pairs={{0,2},{1,3},{2,0},{3,1},{4,6},{5,7},{6,4},{7,5},{8,10},{9,11},{10,... | collective-permute-start | bytes 393224 | tf_op jit(solution)/shard_map/ppermute | solution.py:147
  34.4 0.5 %collective-permute-start.19 = (f32[128,256]{1,0:T(8,128)S(1)}, f32[128,256]{1,0:T(8,128)S(1)}, u32[]{:S(2)}, u32[]{:S(2)}) collective-permute-start(f32[128,256]{1,0:T(8,128)S(1)} %get-tuple-element.44), channel_id=1, source_target_pairs={{0,1},{1,0},{2,3},{3,2},{4,5},{5,4},{6,7},{7,6},{8,9},{9,8},{10,11... | collective-permute-start | bytes 393224 | tf_op jit(solution)/shard_map/ppermute | solution.py:147
  34.9 3.4 %collective-permute-done.20 = bf16[256,256]{1,0:T(8,128)(2,1)S(1)} collective-permute-done((bf16[256,256]{1,0:T(8,128)(2,1)S(1)}, bf16[256,256]{1,0:T(8,128)(2,1)S(1)}, u32[]{:S(2)}, u32[]{:S(2)}) %collective-permute-start.20) | collective-permute-done | bytes 131104 | tf_op jit(solution)/shard_map/ppermute | solution.py:147
  38.4 0.7 %fusion = f32[256,256]{1,0:T(8,128)} fusion(f32[256,256]{1,0:T(8,128)S(1)} %get-tuple-element.40, f32[128,256]{1,0:T(8,128)S(1)} %collective-permute-done.19, f32[128,256]{1,0:T(8,128)S(1)} %collective-permute-done.18, bf16[256,256]{1,0:T(8,128)(2,1)S(1)} %collective-permute-done.20), kind=kLoop, calls=%fused_computation.1 | loop fusion | flops 262144 | bytes 917504 | tf_op jit(solution)/shard_map/add | solution.py:286
  (41 shorter events, 2.5 us)
Async XLA Ops:
  0.8 7.9 %collective-permute-start = (bf16[2,24,1024]{2,1,0:T(8,128)(2,1)S(1)}, bf16[2,24,1024]{2,1,0:T(8,128)(2,1)S(1)}, u32[]{:S(2)}, u32[]{:S(2)}) collective-permute-start(bf16[2,24,1024]{2,1,0:T(8,128)(2,1)S(1)} %pad_maximum_fusion.bases_ref), channel_id=1, source_target_pairs={{0,2},{1,3},{2,0},{3,1},{4,6},{5,7},{6,4},{7,5},{8,10},{9,11},{10,... | collective-permute-start | bytes 294920 | tf_op jit(solution)/shard_map/ppermute | solution.py:147
  4.8 4.0 %collective-permute-start.1 = (bf16[256,256]{1,0:T(8,128)(2,1)S(1)}, bf16[256,256]{1,0:T(8,128)(2,1)S(1)}, u32[]{:S(2)}, u32[]{:S(2)}) collective-permute-start(bf16[256,256]{1,0:T(8,128)(2,1)S(1)} %convert_element_type.21.block_ref.refs_0_), channel_id=1, source_target_pairs={{0,1},{1,0},{2,3},{3,2},{4,5},{5,4},{6,7},{7,6},{8,9},{9,8},{10,11... | collective-permute-start | bytes 393224 | tf_op jit(solution)/shard_map/ppermute | solution.py:147
  4.9 6.0 %collective-permute-start.4 = (bf16[256,256]{1,0:T(8,128)(2,1)S(1)}, bf16[256,256]{1,0:T(8,128)(2,1)S(1)}, u32[]{:S(2)}, u32[]{:S(2)}) collective-permute-start(bf16[256,256]{1,0:T(8,128)(2,1)S(1)} %convert_element_type.21.block_ref.refs_0_), channel_id=1, source_target_pairs={{0,1},{1,0},{2,3},{3,2},{4,8},{5,9},{6,10},{7,11},{8,4},{9,5},{10,... | collective-permute-start | bytes 393224 | tf_op jit(solution)/shard_map/ppermute | solution.py:133
  5.4 8.8 %collective-permute-start.3 = (bf16[256,256]{1,0:T(8,128)(2,1)S(1)}, bf16[256,256]{1,0:T(8,128)(2,1)S(1)}, u32[]{:S(2)}, u32[]{:S(2)}) collective-permute-start(bf16[256,256]{1,0:T(8,128)(2,1)S(1)} %convert_element_type.21.block_ref.refs_0_), channel_id=1, source_target_pairs={{0,4},{4,0},{8,12},{12,8},{1,5},{5,1},{9,13},{13,9},{2,6},{6,2},{1... | collective-permute-start | bytes 393224 | tf_op jit(solution)/shard_map/ppermute | solution.py:121
  8.8 6.9 %copy-start = (bf16[1,1024,3,256]{3,1,2,0:T(8,128)(2,1)S(1)}, bf16[1,1024,3,256]{3,1,2,0:T(8,128)(2,1)}, u32[]{:S(2)}) copy-start(bf16[1,1024,3,256]{3,1,2,0:T(8,128)(2,1)} %param.10) | copy-start | bytes 4718596
  9.0 6.7 %collective-permute-start.2 = (bf16[2,24,1024]{2,1,0:T(8,128)(2,1)S(1)}, bf16[2,24,1024]{2,1,0:T(8,128)(2,1)S(1)}, u32[]{:S(2)}, u32[]{:S(2)}) collective-permute-start(bf16[2,24,1024]{2,1,0:T(8,128)(2,1)S(1)} %pad_maximum_fusion.1), channel_id=1, source_target_pairs={{0,1},{1,0},{2,3},{3,2},{4,5},{5,4},{6,7},{7,6},{8,9},{9,8},{10,11... | collective-permute-start | bytes 294920 | tf_op jit(solution)/shard_map/ppermute | solution.py:147
  9.1 5.7 %collective-permute-start.7 = (bf16[48,256]{1,0:T(8,128)(2,1)S(1)}, bf16[48,256]{1,0:T(8,128)(2,1)S(1)}, u32[]{:S(2)}, u32[]{:S(2)}) collective-permute-start(bf16[48,256]{1,0:T(8,128)(2,1)S(1)} %shard_map.64.refs_3_), channel_id=1, source_target_pairs={{0,12},{4,8},{8,4},{12,0},{1,13},{5,9},{9,5},{13,1},{2,14},{6,10},... | collective-permute-start | bytes 73736 | tf_op jit(solution)/shard_map/ppermute | solution.py:121
  10.9 4.7 %collective-permute-start.6 = (bf16[48,256]{1,0:T(8,128)(2,1)S(1)}, bf16[48,256]{1,0:T(8,128)(2,1)S(1)}, u32[]{:S(2)}, u32[]{:S(2)}) collective-permute-start(bf16[48,256]{1,0:T(8,128)(2,1)S(1)} %shard_map.64.refs_3_), channel_id=1, source_target_pairs={{0,8},{4,12},{8,0},{12,4},{1,9},{5,13},{9,1},{13,5},{2,10},{6,14},... | collective-permute-start | bytes 73736 | tf_op jit(solution)/shard_map/ppermute | solution.py:121
  10.9 4.7 %collective-permute-start.5 = (bf16[48,256]{1,0:T(8,128)(2,1)S(1)}, bf16[48,256]{1,0:T(8,128)(2,1)S(1)}, u32[]{:S(2)}, u32[]{:S(2)}) collective-permute-start(bf16[48,256]{1,0:T(8,128)(2,1)S(1)} %shard_map.64.refs_3_), channel_id=1, source_target_pairs={{0,4},{4,0},{8,12},{12,8},{1,5},{5,1},{9,13},{13,9},{2,6},{6,2},{1... | collective-permute-start | bytes 73736 | tf_op jit(solution)/shard_map/ppermute | solution.py:121
  16.2 1.6 %collective-permute-start.12 = (f32[256,256]{1,0:T(8,128)S(1)}, f32[256,256]{1,0:T(8,128)S(1)}, u32[]{:S(2)}, u32[]{:S(2)}) collective-permute-start(f32[256,256]{1,0:T(8,128)S(1)} %get-tuple-element.33), channel_id=1, source_target_pairs={{0,1},{1,0},{2,3},{3,2},{4,5},{5,4},{6,7},{7,6},{8,9},{9,8},{10,11... | collective-permute-start | bytes 786440 | tf_op jit(solution)/shard_map/ppermute | solution.py:147
  17.1 2.3 %collective-permute-start.8 = (f32[96,256]{1,0:T(8,128)S(1)}, f32[96,256]{1,0:T(8,128)S(1)}, u32[]{:S(2)}, u32[]{:S(2)}) collective-permute-start(f32[96,256]{1,0:T(8,128)S(1)} %get-tuple-element.29), channel_id=1, source_target_pairs={{0,1},{1,0},{2,3},{3,2},{4,5},{5,4},{6,7},{7,6},{8,9},{9,8},{10,11... | collective-permute-start | bytes 294920 | tf_op jit(solution)/shard_map/ppermute | solution.py:147
  17.7 4.2 %collective-permute-start.11 = (f32[256,256]{1,0:T(8,128)S(1)}, f32[256,256]{1,0:T(8,128)S(1)}, u32[]{:S(2)}, u32[]{:S(2)}) collective-permute-start(f32[256,256]{1,0:T(8,128)S(1)} %get-tuple-element.31), channel_id=1, source_target_pairs={{0,1},{1,0},{2,3},{3,2},{4,5},{5,4},{6,7},{7,6},{8,9},{9,8},{10,11... | collective-permute-start | bytes 786440 | tf_op jit(solution)/shard_map/ppermute | solution.py:147
  17.9 5.9 %collective-permute-start.13 = (bf16[256,256]{1,0:T(8,128)(2,1)S(1)}, bf16[256,256]{1,0:T(8,128)(2,1)S(1)}, u32[]{:S(2)}, u32[]{:S(2)}) collective-permute-start(bf16[256,256]{1,0:T(8,128)(2,1)S(1)} %add_convert_fusion.2), channel_id=1, source_target_pairs={{0,2},{1,3},{2,0},{3,1},{4,6},{5,7},{6,4},{7,5},{8,10},{9,11},{10,... | collective-permute-start | bytes 393224 | tf_op jit(solution)/shard_map/ppermute | solution.py:147
  19.4 6.2 %collective-permute-start.10 = (bf16[96,256]{1,0:T(8,128)(2,1)S(1)}, bf16[96,256]{1,0:T(8,128)(2,1)S(1)}, u32[]{:S(2)}, u32[]{:S(2)}) collective-permute-start(bf16[96,256]{1,0:T(8,128)(2,1)S(1)} %add_convert_fusion.3.refs_3_), channel_id=1, source_target_pairs={{0,8},{1,13},{2,10},{3,15},{4,12},{5,9},{6,14},{7,11},{8,0},{9,5},... | collective-permute-start | bytes 147464 | tf_op jit(solution)/shard_map/ppermute | solution.py:143
  21.5 4.1 %collective-permute-start.9 = (bf16[48,256]{1,0:T(8,128)(2,1)S(1)}, bf16[48,256]{1,0:T(8,128)(2,1)S(1)}, u32[]{:S(2)}, u32[]{:S(2)}) collective-permute-start(bf16[48,256]{1,0:T(8,128)(2,1)S(1)} %slice.21), channel_id=1, source_target_pairs={{0,4},{4,0},{8,12},{12,8},{1,5},{5,1},{9,13},{13,9},{2,6},{6,2},{1... | collective-permute-start | bytes 73736 | tf_op jit(solution)/shard_map/ppermute | solution.py:121
  23.8 6.9 %collective-permute-start.16 = (bf16[256,256]{1,0:T(8,128)(2,1)S(1)}, bf16[256,256]{1,0:T(8,128)(2,1)S(1)}, u32[]{:S(2)}, u32[]{:S(2)}) collective-permute-start(bf16[256,256]{1,0:T(8,128)(2,1)S(1)} %add_convert_fusion.1.refs_0_), channel_id=1, source_target_pairs={{0,1},{1,0},{2,3},{3,2},{4,8},{5,9},{6,10},{7,11},{8,4},{9,5},{10,... | collective-permute-start | bytes 393224 | tf_op jit(solution)/shard_map/ppermute | solution.py:133
  25.7 5.0 %collective-permute-start.15 = (bf16[256,256]{1,0:T(8,128)(2,1)S(1)}, bf16[256,256]{1,0:T(8,128)(2,1)S(1)}, u32[]{:S(2)}, u32[]{:S(2)}) collective-permute-start(bf16[256,256]{1,0:T(8,128)(2,1)S(1)} %add_convert_fusion.1.refs_0_), channel_id=1, source_target_pairs={{0,4},{4,0},{8,12},{12,8},{1,5},{5,1},{9,13},{13,9},{2,6},{6,2},{1... | collective-permute-start | bytes 393224 | tf_op jit(solution)/shard_map/ppermute | solution.py:121
  26.6 1.4 %collective-permute-start.14 = (bf16[2,24,1024]{2,1,0:T(8,128)(2,1)S(1)}, bf16[2,24,1024]{2,1,0:T(8,128)(2,1)S(1)}, u32[]{:S(2)}, u32[]{:S(2)}) collective-permute-start(bf16[2,24,1024]{2,1,0:T(8,128)(2,1)S(1)} %pad_maximum_fusion.2), channel_id=1, source_target_pairs={{0,1},{1,0},{2,3},{3,2},{4,5},{5,4},{6,7},{7,6},{8,9},{9,8},{10,11... | collective-permute-start | bytes 294920 | tf_op jit(solution)/shard_map/ppermute | solution.py:147
  31.1 1.6 %collective-permute-start.17 = (f32[256,256]{1,0:T(8,128)S(1)}, f32[256,256]{1,0:T(8,128)S(1)}, u32[]{:S(2)}, u32[]{:S(2)}) collective-permute-start(f32[256,256]{1,0:T(8,128)S(1)} %shard_map.68), channel_id=1, source_target_pairs={{0,1},{1,0},{2,3},{3,2},{4,5},{5,4},{6,7},{7,6},{8,9},{9,8},{10,11... | collective-permute-start | bytes 786440 | tf_op jit(solution)/shard_map/ppermute | solution.py:147
  32.7 5.6 %collective-permute-start.20 = (bf16[256,256]{1,0:T(8,128)(2,1)S(1)}, bf16[256,256]{1,0:T(8,128)(2,1)S(1)}, u32[]{:S(2)}, u32[]{:S(2)}) collective-permute-start(bf16[256,256]{1,0:T(8,128)(2,1)S(1)} %add_convert_fusion), channel_id=1, source_target_pairs={{0,2},{1,3},{2,0},{3,1},{4,6},{5,7},{6,4},{7,5},{8,10},{9,11},{10,... | collective-permute-start | bytes 393224 | tf_op jit(solution)/shard_map/ppermute | solution.py:147
  34.3 4.0 %collective-permute-start.18 = (f32[128,256]{1,0:T(8,128)S(1)}, f32[128,256]{1,0:T(8,128)S(1)}, u32[]{:S(2)}, u32[]{:S(2)}) collective-permute-start(f32[128,256]{1,0:T(8,128)S(1)} %get-tuple-element.43), channel_id=1, source_target_pairs={{0,1},{1,0},{2,3},{3,2},{4,5},{5,4},{6,7},{7,6},{8,9},{9,8},{10,11... | collective-permute-start | bytes 393224 | tf_op jit(solution)/shard_map/ppermute | solution.py:147
  34.4 3.9 %collective-permute-start.19 = (f32[128,256]{1,0:T(8,128)S(1)}, f32[128,256]{1,0:T(8,128)S(1)}, u32[]{:S(2)}, u32[]{:S(2)}) collective-permute-start(f32[128,256]{1,0:T(8,128)S(1)} %get-tuple-element.44), channel_id=1, source_target_pairs={{0,1},{1,0},{2,3},{3,2},{4,5},{5,4},{6,7},{7,6},{8,9},{9,8},{10,11... | collective-permute-start | bytes 393224 | tf_op jit(solution)/shard_map/ppermute | solution.py:147

commit v14 on v13

--- a/solution.py
+++ b/solution.py
@@ -81,7 +81,7 @@
         out_specs=tuple(VMEM for _ in outs),
         compiler_params=pltpu.CompilerParams(vmem_limit_bytes=16 * 2**20),
         cost_estimate=pl.CostEstimate(
-            flops=flops, bytes_accessed=2 * operands[0].size, transcendentals=0
+            flops=flops, bytes_accessed=flops // 1024, transcendentals=0
         ),
     )(*operands)
 
@@ -165,33 +165,37 @@
     )
 
 
-def image_kernel(choice, turns, near_ref, columns_ref, bases_refs, operand_refs, out_refs):
-    block_refs, coefficient_refs = operand_refs[:3], operand_refs[3:]
+def near_kernel(turns, near_ref, own_ref, first_ref, second_ref, *refs):
+    base_refs, out_refs = refs[: -len(turns)], refs[-len(turns) :]
     count = lax.axis_size("tile")
     tile = lax.axis_index("tile")
     me = lax.axis_index("list")
     rows = near_ref.shape[2]
-    chosen = choice(columns_ref[...], tile, me, coefficient_refs)
     odd = lax.rem(tile, 2)
     inside = (tile > 0) & (tile < count - 1)
     blocks = [
-        (1, block_refs[0][...]),
-        (2 - 2 * odd, block_refs[1][...]),
-        (2 * odd, jnp.where(inside, block_refs[2][...], 0)),
+        (1, own_ref[...]),
+        (2 - 2 * odd, first_ref[...]),
+        (2 * odd, jnp.where(inside, second_ref[...], 0)),
     ]
-    totals = []
-    for turn, out_ref in zip(turns, out_refs):
-        part = me ^ turn
-        cut = pl.ds(pl.multiple_of(part * rows, rows), rows)
+    for index, turn in enumerate(turns):
+        cut = pl.ds(pl.multiple_of((me ^ turn) * rows, rows), rows)
+        total = base_refs[index][...] if base_refs else 0.0
+        for side, block in blocks:
+            total += jnp.dot(near_ref[side, cut, :], block, preferred_element_type=F32)
+        out_refs[index][...] = total
+
+
+def far_parts(choice, turns, columns_ref, bases_refs, coefficient_refs):
+    me = lax.axis_index("list")
+    chosen = choice(columns_ref[...], lax.axis_index("tile"), me, coefficient_refs)
+    rows = bases_refs[0].shape[2] // 4
+    for turn in turns:
+        cut = pl.ds(pl.multiple_of((me ^ turn) * rows, rows), rows)
         left = basis_groups(1, cut, bases_refs)
-        total = lax.dot_general(
+        yield cut, lax.dot_general(
             left, chosen, (((0,), (0,)), ((), ())), preferred_element_type=F32
         )
-        for side, block in blocks:
-            total += jnp.dot(near_ref[side, cut, :], block, preferred_element_type=F32)
-        out_ref[...] = total
-        totals.append((cut, total.astype(BF)))
-    return totals
 
 
 def right_products(totals, bases_refs):
@@ -201,15 +205,19 @@
     )
 
 
-def first_kernel(turns, near_ref, columns_ref, bases_ref, across_ref, other_ref, *refs):
-    operand_refs, refs = refs[:7], refs[7:]
+def first_kernel(turns, columns_ref, bases_ref, across_ref, other_ref, *refs):
+    coefficient_refs, refs = refs[:4], refs[4:]
+    base_refs, refs = refs[: len(turns)], refs[len(turns) :]
     last = 0 in turns
     sums_before, refs = (refs[:1], refs[1:]) if 3 not in turns else ((), refs)
     ranks_ref, refs = (refs[0], refs[1:]) if last else (None, refs)
     bases_refs = (bases_ref, across_ref)
-    totals = image_kernel(
-        near_choice, turns, near_ref, columns_ref, bases_refs, operand_refs, refs
-    )
+    totals = []
+    parts = far_parts(near_choice, turns, columns_ref, bases_refs, coefficient_refs)
+    for (cut, total), base_ref, out_ref in zip(parts, base_refs, refs):
+        total += base_ref[...]
+        out_ref[...] = total
+        totals.append((cut, total.astype(BF)))
     sums = right_products(totals, (*bases_refs, other_ref))
     for ref in sums_before:
         sums += ref[...]
@@ -221,9 +229,13 @@
     refs[-1][...] = jnp.concatenate(groups[2:] + groups[:2])
 
 
-def second_kernel(turns, near_ref, columns_ref, bases_ref, across_ref, other_ref, *refs):
+def second_kernel(turns, columns_ref, bases_ref, across_ref, other_ref, *refs):
+    operand_refs, out_refs = refs[3:-len(turns)], refs[-len(turns) :]
     bases_refs = (bases_ref, across_ref, other_ref)
-    image_kernel(far_choice, turns, near_ref, columns_ref, bases_refs, refs[:6], refs[6:])
+    parts = far_parts(far_choice, turns, columns_ref, bases_refs, refs[:3])
+    for (_, total), out_ref in zip(parts, out_refs):
+        out_ref[...] = total
+    near_kernel(turns, *operand_refs, *out_refs, *out_refs)
 
 
 def one_slot(probes, right_bases, left_bases, near_tiles, tile_ranks, column_rows, row_columns):
@@ -247,18 +259,20 @@
     )
     coefficients = [own] + [tile_swap(own, turn) for turn in (1, 2, 3)]
     right, _ = lax.optimization_barrier((jnp.stack([bases[0], across[0]]), own))
-    fixed = (near, row_columns, bases, across)
-    operands = (*fixed, list_swap(right, 1), *beside, *coefficients)
+    fixed = (row_columns, bases, across)
+    operands = (*fixed, list_swap(right, 1), *coefficients)
     small = ((ranks, probe_count), F32)
 
-    def first(turns, outs, more=()):
-        kernel = functools.partial(first_kernel, turns)
-        return kernel_call(kernel, outs, (*operands, *more), len(turns) * flops // 4)
-
-    send, sums = first((3,), [part, small])
+    def call(kernel, turns, operands, more=(), cost=1):
+        outs = [part] * len(turns) + list(more)
+        kernel = functools.partial(kernel, turns)
+        return kernel_call(kernel, outs, operands, cost * len(turns) * flops // 4)
+
+    base = call(near_kernel, (3, 2, 1, 0), (near, *beside), cost=0)
+    send, sums = call(first_kernel, (3,), (*operands, base[0]), [small])
     arrived = list_swap(send, 1)
-    crossing, send, keep, own, other = first(
-        (2, 1, 0), [part] * 3 + [small] * 2, (sums, tile_ranks)
+    crossing, send, keep, own, other = call(
+        first_kernel, (2, 1, 0), (*operands, *base[1:], sums, tile_ranks), [small] * 2
     )
     crossed = list_swap((crossing + arrived).astype(BF), 2)
     own = (own + list_swap(other, 1)).astype(BF)
@@ -267,22 +281,18 @@
     held, held_across, near_by, far, ready = lax.optimization_barrier(
         (bases, across, near_by, far, block)
     )
-    beside = [block, tile_swap(ready, 1), middle_swap(block)]
+    beside = [block, tile_swap(block, 1), middle_swap(ready)]
     left = list_swap(jnp.stack([held[1], held_across[1]]), 1)
 
-    operands = (*fixed, left, *beside, own, near_by, far)
-
-    def second(turns, operands):
-        kernel = functools.partial(second_kernel, turns)
-        return kernel_call(kernel, [part] * len(turns), operands, len(turns) * flops // 4)
-
-    (send,) = second((3,), operands)
+    operands = (*fixed, left, own, near_by, far, near, *beside)
+    (send,) = call(second_kernel, (3,), operands)
     arrived = list_swap(send, 1)
-    (keep,) = second((2,), operands)
+    (keep,) = call(second_kernel, (2,), operands)
     crossing = (keep + arrived).astype(BF)
-    near, crossing = lax.optimization_barrier((near, crossing))
+    left, crossing = lax.optimization_barrier((left, crossing))
     crossed = list_swap(crossing, 2)
-    send, keep = second((1, 0), (near, *operands[1:]))
+    operands = (*fixed, left, own, near_by, far, near, *beside)
+    send, keep = call(second_kernel, (1, 0), operands)
     return keep + list_swap_in_pieces(send, 1, 2) + crossed
 
 

time: 39.3 us -> 37 us (0.941)
  waiting for transfers between devices: 13.8 us -> 9.5 us
  starting transfers between devices: 18.2 us -> 20.1 us
    ppermute x6, waiting for transfers between devices: 6.03 us -> 2.51 us  [tile_swap(): lax.ppermute(block, 'tile', [(i, i ^ turn) for i in range(lax.axis_size('...]
    ppermute x12, starting transfers between devices: 7.22 us -> 8.15 us  [list_swap(): lax.ppermute(block, 'list', [(i, i ^ bit) for i in range(lax.axis_size('l...]
    ppermute x6, starting transfers between devices: 8.37 us -> 9.28 us  [tile_swap(): lax.ppermute(block, 'tile', [(i, i ^ turn) for i in range(lax.axis_size('...]
    ppermute x12, waiting for transfers between devices: 7.82 us -> 6.98 us  [list_swap(): lax.ppermute(block, 'list', [(i, i ^ bit) for i in range(lax.axis_size('l...]
    pallas_call x6 -> x7, Pallas kernels: 2.71 us -> 2.9 us  [kernel_call(): pl.pallas_call(kernel, out_shape=tuple((jax.ShapeDtypeStruct(shape, kind)...]
  transfers between devices with their start and end apart: 21 -> 21, of which waited for: 8 -> 8; matrix products, arithmetic and copies ran while one was open for 3% -> 3% of each run, Pallas kernels for 5% -> 6%
where the time goes in v14:
time: 37 us; the launch traced here: 36.8 us
  starting transfers between devices  20.1 us (54%)
  waiting for transfers between devices  9.5 us (26%)
  Pallas kernels  2.9 us (8%)
  other arithmetic  2.7 us (7%)
  between operations  1.52 us (4%)
    ppermute x6, starting transfers between devices, tile_swap(): lax.ppermute(block, 'tile', [(i, i ^ turn) for i in range(lax.axis_size('...  9.28 us
    ppermute x12, starting transfers between devices, list_swap(): lax.ppermute(block, 'list', [(i, i ^ bit) for i in range(lax.axis_size('l...  8.15 us
    ppermute x12, waiting for transfers between devices, list_swap(): lax.ppermute(block, 'list', [(i, i ^ bit) for i in range(lax.axis_size('l...  6.98 us
    pallas_call x7, Pallas kernels, kernel_call(): pl.pallas_call(kernel, out_shape=tuple((jax.ShapeDtypeStruct(shape, kind)...  2.9 us
    ppermute x6, waiting for transfers between devices, tile_swap(): lax.ppermute(block, 'tile', [(i, i ^ turn) for i in range(lax.axis_size('...  2.51 us
    ppermute x1, starting transfers between devices, far_swap(): return lax.ppermute(block, ('tile', 'list'), route)  2.09 us
    convert_element_type x1, other arithmetic, one_slot(): block = probes.astype(BF)  0.96 us
    another operation x1, other arithmetic, one_slot(): bases = jnp.stack([right_bases[0, 0], left_bases[0, 0]])  0.83 us
  transfers between devices with their start and end apart: 21, of which 8 were waited for; matrix products, arithmetic and copies ran while one was open for 3% of the time, Pallas kernels for 6%

profile of v14, /device:TPU:0, one launch (start us, length us, event | category | flops | bytes accessed | tf_op | source)
XLA Modules:
  0.0 36.8 jit_solution(3684133504492232493)
XLA Ops:
  0.0 0.8 %pad_maximum_fusion.bases_ref = bf16[2,24,1024]{2,1,0:T(8,128)(2,1)S(1)} fusion(bf16[1,24,1024]{2,1,0:T(8,128)(2,1)} %bitcast.9, bf16[1,24,1024]{2,1,0:T(8,128)(2,1)} %bitcast.10), kind=kLoop, calls=%fused_computation.5 | loop fusion | flops 49152 | bytes 196608 | tf_op jit(solution)/shard_map/stack | solution.py:249
  0.8 3.0 %collective-permute-start = (bf16[2,24,1024]{2,1,0:T(8,128)(2,1)S(1)}, bf16[2,24,1024]{2,1,0:T(8,128)(2,1)S(1)}, u32[]{:S(2)}, u32[]{:S(2)}) collective-permute-start(bf16[2,24,1024]{2,1,0:T(8,128)(2,1)S(1)} %pad_maximum_fusion.bases_ref), channel_id=1, source_target_pairs={{0,2},{1,3},{2,0},{3,1},{4,6},{5,7},{6,4},{7,5},{8,10},{9,11},{10,... | collective-permute-start | bytes 294920 | tf_op jit(solution)/shard_map/ppermute | solution.py:147
  3.8 1.0 %convert_element_type.21.block_ref.own_ref = bf16[256,256]{1,0:T(8,128)(2,1)S(1)} convert(f32[256,256]{1,0:T(8,128)} %param.7) | non-fusion elementwise | flops 65536 | bytes 393216 | tf_op jit(solution)/shard_map/convert_element_type | solution.py:252
  4.9 0.5 %collective-permute-start.7 = (bf16[256,256]{1,0:T(8,128)(2,1)S(1)}, bf16[256,256]{1,0:T(8,128)(2,1)S(1)}, u32[]{:S(2)}, u32[]{:S(2)}) collective-permute-start(bf16[256,256]{1,0:T(8,128)(2,1)S(1)} %convert_element_type.21.block_ref.own_ref), channel_id=1, source_target_pairs={{0,1},{1,0},{2,3},{3,2},{4,8},{5,9},{6,10},{7,11},{8,4},{9,5},{10,... | collective-permute-start | bytes 393224 | tf_op jit(solution)/shard_map/ppermute | solution.py:133
  5.4 2.7 %collective-permute-start.6 = (bf16[256,256]{1,0:T(8,128)(2,1)S(1)}, bf16[256,256]{1,0:T(8,128)(2,1)S(1)}, u32[]{:S(2)}, u32[]{:S(2)}) collective-permute-start(bf16[256,256]{1,0:T(8,128)(2,1)S(1)} %convert_element_type.21.block_ref.own_ref), channel_id=1, source_target_pairs={{0,4},{4,0},{8,12},{12,8},{1,5},{5,1},{9,13},{13,9},{2,6},{6,2},{1... | collective-permute-start | bytes 393224 | tf_op jit(solution)/shard_map/ppermute | solution.py:121
  9.1 1.8 %collective-permute-start.5 = (bf16[48,256]{1,0:T(8,128)(2,1)S(1)}, bf16[48,256]{1,0:T(8,128)(2,1)S(1)}, u32[]{:S(2)}, u32[]{:S(2)}) collective-permute-start(bf16[48,256]{1,0:T(8,128)(2,1)S(1)} %shard_map.64.refs_0_), channel_id=1, source_target_pairs={{0,12},{4,8},{8,4},{12,0},{1,13},{5,9},{9,5},{13,1},{2,14},{6,10},... | collective-permute-start | bytes 73736 | tf_op jit(solution)/shard_map/ppermute | solution.py:121
  10.9 2.6 %collective-permute-start.3 = (bf16[48,256]{1,0:T(8,128)(2,1)S(1)}, bf16[48,256]{1,0:T(8,128)(2,1)S(1)}, u32[]{:S(2)}, u32[]{:S(2)}) collective-permute-start(bf16[48,256]{1,0:T(8,128)(2,1)S(1)} %shard_map.64.refs_0_), channel_id=1, source_target_pairs={{0,4},{4,0},{8,12},{12,8},{1,5},{5,1},{9,13},{13,9},{2,6},{6,2},{1... | collective-permute-start | bytes 73736 | tf_op jit(solution)/shard_map/ppermute | solution.py:121
  14.2 0.6 %shard_map.65 = (f32[256,256]{1,0:T(8,128)S(1)}, f32[256,256]{1,0:T(8,128)S(1)}, f32[256,256]{1,0:T(8,128)S(1)}, f32[256,256]{1,0:T(8,128)S(1)}) custom-call(bf16[3,1024,256]{2,1,0:T(8,128)(2,1)S(1)} %bitcast.5, bf16[256,256]{1,0:T(8,128)(2,1)S(1)} %convert_element_type.21.block_ref.own_ref, bf16[256,256]{1,0:T(8,128)(2,1)S(1)} %collective-permute-done.6.first_ref, ...), custom_call_target="tpu_custom_call" | custom-call | tf_op jit(solution)/shard_map/pallas_call | solution.py:77
  14.8 0.8 %collective-permute-done.4.refs_2_ = bf16[48,256]{1,0:T(8,128)(2,1)S(1)} collective-permute-done((bf16[48,256]{1,0:T(8,128)(2,1)S(1)}, bf16[48,256]{1,0:T(8,128)(2,1)S(1)}, u32[]{:S(2)}, u32[]{:S(2)}) %collective-permute-start.4) | collective-permute-done | bytes 24608 | tf_op jit(solution)/shard_map/ppermute | solution.py:121
  16.1 0.5 %shard_map.67 = (f32[256,256]{1,0:T(8,128)S(1)}, f32[256,256]{1,0:T(8,128)S(1)}, f32[256,256]{1,0:T(8,128)S(1)}, f32[96,256]{1,0:T(8,128)S(1)}, f32[96,256]{1,0:T(8,128)S(1)}) custom-call(s32[1,1]{1,0:T(1,128)S(6)} %copy.8.columns_ref, bf16[2,24,1024]{2,1,0:T(8,128)(2,1)S(1)} %pad_maximum_fusion.bases_ref, ...), custom_call_target="tpu_custom_call" | custom-call | flops 301989888 | bytes 294912 | tf_op jit(solution)/shard_map/pallas_call | solution.py:77
  16.7 0.6 %collective-permute-start.8 = (f32[96,256]{1,0:T(8,128)S(1)}, f32[96,256]{1,0:T(8,128)S(1)}, u32[]{:S(2)}, u32[]{:S(2)}) collective-permute-start(f32[96,256]{1,0:T(8,128)S(1)} %get-tuple-element.37), channel_id=1, source_target_pairs={{0,1},{1,0},{2,3},{3,2},{4,5},{5,4},{6,7},{7,6},{8,9},{9,8},{10,11... | collective-permute-start | bytes 294920 | tf_op jit(solution)/shard_map/ppermute | solution.py:147
  17.7 1.6 %collective-permute-start.13 = (bf16[256,256]{1,0:T(8,128)(2,1)S(1)}, bf16[256,256]{1,0:T(8,128)(2,1)S(1)}, u32[]{:S(2)}, u32[]{:S(2)}) collective-permute-start(bf16[256,256]{1,0:T(8,128)(2,1)S(1)} %add_convert_fusion.2), channel_id=1, source_target_pairs={{0,2},{1,3},{2,0},{3,1},{4,6},{5,7},{6,4},{7,5},{8,10},{9,11},{10,... | collective-permute-start | bytes 393224 | tf_op jit(solution)/shard_map/ppermute | solution.py:147
  19.3 2.1 %collective-permute-start.10 = (bf16[96,256]{1,0:T(8,128)(2,1)S(1)}, bf16[96,256]{1,0:T(8,128)(2,1)S(1)}, u32[]{:S(2)}, u32[]{:S(2)}) collective-permute-start(bf16[96,256]{1,0:T(8,128)(2,1)S(1)} %add_convert_fusion.3.refs_0_), channel_id=1, source_target_pairs={{0,8},{1,13},{2,10},{3,15},{4,12},{5,9},{6,14},{7,11},{8,0},{9,5},... | collective-permute-start | bytes 147464 | tf_op jit(solution)/shard_map/ppermute | solution.py:143
  21.7 1.6 %collective-permute-done.13 = bf16[256,256]{1,0:T(8,128)(2,1)S(1)} collective-permute-done((bf16[256,256]{1,0:T(8,128)(2,1)S(1)}, bf16[256,256]{1,0:T(8,128)(2,1)S(1)}, u32[]{:S(2)}, u32[]{:S(2)}) %collective-permute-start.13) | collective-permute-done | bytes 131104 | tf_op jit(solution)/shard_map/ppermute | solution.py:147
  23.4 1.8 %collective-permute-start.15 = (bf16[256,256]{1,0:T(8,128)(2,1)S(1)}, bf16[256,256]{1,0:T(8,128)(2,1)S(1)}, u32[]{:S(2)}, u32[]{:S(2)}) collective-permute-start(bf16[256,256]{1,0:T(8,128)(2,1)S(1)} %add_convert_fusion.1.refs_4_), channel_id=1, source_target_pairs={{0,4},{4,0},{8,12},{12,8},{1,5},{5,1},{9,13},{13,9},{2,6},{6,2},{1... | collective-permute-start | bytes 393224 | tf_op jit(solution)/shard_map/ppermute | solution.py:121
  25.7 0.6 %collective-permute-start.14 = (bf16[2,24,1024]{2,1,0:T(8,128)(2,1)S(1)}, bf16[2,24,1024]{2,1,0:T(8,128)(2,1)S(1)}, u32[]{:S(2)}, u32[]{:S(2)}) collective-permute-start(bf16[2,24,1024]{2,1,0:T(8,128)(2,1)S(1)} %pad_maximum_fusion.2), channel_id=1, source_target_pairs={{0,1},{1,0},{2,3},{3,2},{4,5},{5,4},{6,7},{7,6},{8,9},{9,8},{10,11... | collective-permute-start | bytes 294920 | tf_op jit(solution)/shard_map/ppermute | solution.py:147
  26.3 0.9 %collective-permute-done.14.other_ref = bf16[2,24,1024]{2,1,0:T(8,128)(2,1)S(1)} collective-permute-done((bf16[2,24,1024]{2,1,0:T(8,128)(2,1)S(1)}, bf16[2,24,1024]{2,1,0:T(8,128)(2,1)S(1)}, u32[]{:S(2)}, u32[]{:S(2)}) %collective-permute-start.14) | collective-permute-done | bytes 98336 | tf_op jit(solution)/shard_map/ppermute | solution.py:147
  27.2 1.2 %collective-permute-done.15.refs_5_ = bf16[256,256]{1,0:T(8,128)(2,1)S(1)} collective-permute-done((bf16[256,256]{1,0:T(8,128)(2,1)S(1)}, bf16[256,256]{1,0:T(8,128)(2,1)S(1)}, u32[]{:S(2)}, u32[]{:S(2)}) %collective-permute-start.15) | collective-permute-done | bytes 131104 | tf_op jit(solution)/shard_map/ppermute | solution.py:121
  29.2 1.1 %collective-permute-done.17 = f32[256,256]{1,0:T(8,128)S(1)} collective-permute-done((f32[256,256]{1,0:T(8,128)S(1)}, f32[256,256]{1,0:T(8,128)S(1)}, u32[]{:S(2)}, u32[]{:S(2)}) %collective-permute-start.17) | collective-permute-done | bytes 262176 | tf_op jit(solution)/shard_map/ppermute | solution.py:147
  30.4 1.6 %collective-permute-start.20 = (bf16[256,256]{1,0:T(8,128)(2,1)S(1)}, bf16[256,256]{1,0:T(8,128)(2,1)S(1)}, u32[]{:S(2)}, u32[]{:S(2)}) collective-permute-start(bf16[256,256]{1,0:T(8,128)(2,1)S(1)} %add_convert_fusion), channel_id=1, source_target_pairs={{0,2},{1,3},{2,0},{3,1},{4,6},{5,7},{6,4},{7,5},{8,10},{9,11},{10,... | collective-permute-start | bytes 393224 | tf_op jit(solution)/shard_map/ppermute | solution.py:147
  32.0 0.5 %shard_map.70 = (f32[256,256]{1,0:T(8,128)S(1)}, f32[256,256]{1,0:T(8,128)S(1)}) custom-call(s32[1,1]{1,0:T(1,128)S(6)} %copy.8.columns_ref, bf16[2,24,1024]{2,1,0:T(8,128)(2,1)S(1)} %pad_maximum_fusion.bases_ref, bf16[2,24,1024]{2,1,0:T(8,128)(2,1)S(1)} %collective-permute-done.across_ref, bf16[2,24,1024]{2,1,0:T(8,128)(2,1)S(1)} %collective-permute-done.14.other_ref, ...), custom_call_target="tpu_custom_call" | custom-call | flops 201326592 | bytes 196608 | tf_op jit(solution)/shard_map/pallas_call | solution.py:77
  32.6 0.5 %collective-permute-start.19 = (f32[128,256]{1,0:T(8,128)S(1)}, f32[128,256]{1,0:T(8,128)S(1)}, u32[]{:S(2)}, u32[]{:S(2)}) collective-permute-start(f32[128,256]{1,0:T(8,128)S(1)} %get-tuple-element.52), channel_id=1, source_target_pairs={{0,1},{1,0},{2,3},{3,2},{4,5},{5,4},{6,7},{7,6},{8,9},{9,8},{10,11... | collective-permute-start | bytes 393224 | tf_op jit(solution)/shard_map/ppermute | solution.py:147
  33.1 3.0 %collective-permute-done.20 = bf16[256,256]{1,0:T(8,128)(2,1)S(1)} collective-permute-done((bf16[256,256]{1,0:T(8,128)(2,1)S(1)}, bf16[256,256]{1,0:T(8,128)(2,1)S(1)}, u32[]{:S(2)}, u32[]{:S(2)}) %collective-permute-start.20) | collective-permute-done | bytes 131104 | tf_op jit(solution)/shard_map/ppermute | solution.py:147
  36.0 0.7 %fusion = f32[256,256]{1,0:T(8,128)} fusion(f32[256,256]{1,0:T(8,128)S(1)} %get-tuple-element.48, f32[128,256]{1,0:T(8,128)S(1)} %collective-permute-done.19, f32[128,256]{1,0:T(8,128)S(1)} %collective-permute-done.18, bf16[256,256]{1,0:T(8,128)(2,1)S(1)} %collective-permute-done.20), kind=kLoop, calls=%fused_computation.1 | loop fusion | flops 262144 | bytes 917504 | tf_op jit(solution)/shard_map/add | solution.py:296
  (42 shorter events, 3.2 us)
Async XLA Ops:
  0.8 7.9 %collective-permute-start = (bf16[2,24,1024]{2,1,0:T(8,128)(2,1)S(1)}, bf16[2,24,1024]{2,1,0:T(8,128)(2,1)S(1)}, u32[]{:S(2)}, u32[]{:S(2)}) collective-permute-start(bf16[2,24,1024]{2,1,0:T(8,128)(2,1)S(1)} %pad_maximum_fusion.bases_ref), channel_id=1, source_target_pairs={{0,2},{1,3},{2,0},{3,1},{4,6},{5,7},{6,4},{7,5},{8,10},{9,11},{10,... | collective-permute-start | bytes 294920 | tf_op jit(solution)/shard_map/ppermute | solution.py:147
  4.8 4.0 %collective-permute-start.1 = (bf16[256,256]{1,0:T(8,128)(2,1)S(1)}, bf16[256,256]{1,0:T(8,128)(2,1)S(1)}, u32[]{:S(2)}, u32[]{:S(2)}) collective-permute-start(bf16[256,256]{1,0:T(8,128)(2,1)S(1)} %convert_element_type.21.block_ref.own_ref), channel_id=1, source_target_pairs={{0,1},{1,0},{2,3},{3,2},{4,5},{5,4},{6,7},{7,6},{8,9},{9,8},{10,11... | collective-permute-start | bytes 393224 | tf_op jit(solution)/shard_map/ppermute | solution.py:147
  4.9 6.0 %collective-permute-start.7 = (bf16[256,256]{1,0:T(8,128)(2,1)S(1)}, bf16[256,256]{1,0:T(8,128)(2,1)S(1)}, u32[]{:S(2)}, u32[]{:S(2)}) collective-permute-start(bf16[256,256]{1,0:T(8,128)(2,1)S(1)} %convert_element_type.21.block_ref.own_ref), channel_id=1, source_target_pairs={{0,1},{1,0},{2,3},{3,2},{4,8},{5,9},{6,10},{7,11},{8,4},{9,5},{10,... | collective-permute-start | bytes 393224 | tf_op jit(solution)/shard_map/ppermute | solution.py:133
  5.4 8.8 %collective-permute-start.6 = (bf16[256,256]{1,0:T(8,128)(2,1)S(1)}, bf16[256,256]{1,0:T(8,128)(2,1)S(1)}, u32[]{:S(2)}, u32[]{:S(2)}) collective-permute-start(bf16[256,256]{1,0:T(8,128)(2,1)S(1)} %convert_element_type.21.block_ref.own_ref), channel_id=1, source_target_pairs={{0,4},{4,0},{8,12},{12,8},{1,5},{5,1},{9,13},{13,9},{2,6},{6,2},{1... | collective-permute-start | bytes 393224 | tf_op jit(solution)/shard_map/ppermute | solution.py:121
  8.8 5.4 %copy-start = (bf16[1,1024,3,256]{3,1,2,0:T(8,128)(2,1)S(1)}, bf16[1,1024,3,256]{3,1,2,0:T(8,128)(2,1)}, u32[]{:S(2)}) copy-start(bf16[1,1024,3,256]{3,1,2,0:T(8,128)(2,1)} %param.10) | copy-start | bytes 4718596
  9.0 6.7 %collective-permute-start.2 = (bf16[2,24,1024]{2,1,0:T(8,128)(2,1)S(1)}, bf16[2,24,1024]{2,1,0:T(8,128)(2,1)S(1)}, u32[]{:S(2)}, u32[]{:S(2)}) collective-permute-start(bf16[2,24,1024]{2,1,0:T(8,128)(2,1)S(1)} %pad_maximum_fusion.1), channel_id=1, source_target_pairs={{0,1},{1,0},{2,3},{3,2},{4,5},{5,4},{6,7},{7,6},{8,9},{9,8},{10,11... | collective-permute-start | bytes 294920 | tf_op jit(solution)/shard_map/ppermute | solution.py:147
  9.1 5.7 %collective-permute-start.5 = (bf16[48,256]{1,0:T(8,128)(2,1)S(1)}, bf16[48,256]{1,0:T(8,128)(2,1)S(1)}, u32[]{:S(2)}, u32[]{:S(2)}) collective-permute-start(bf16[48,256]{1,0:T(8,128)(2,1)S(1)} %shard_map.64.refs_0_), channel_id=1, source_target_pairs={{0,12},{4,8},{8,4},{12,0},{1,13},{5,9},{9,5},{13,1},{2,14},{6,10},... | collective-permute-start | bytes 73736 | tf_op jit(solution)/shard_map/ppermute | solution.py:121
  10.9 4.7 %collective-permute-start.4 = (bf16[48,256]{1,0:T(8,128)(2,1)S(1)}, bf16[48,256]{1,0:T(8,128)(2,1)S(1)}, u32[]{:S(2)}, u32[]{:S(2)}) collective-permute-start(bf16[48,256]{1,0:T(8,128)(2,1)S(1)} %shard_map.64.refs_0_), channel_id=1, source_target_pairs={{0,8},{4,12},{8,0},{12,4},{1,9},{5,13},{9,1},{13,5},{2,10},{6,14},... | collective-permute-start | bytes 73736 | tf_op jit(solution)/shard_map/ppermute | solution.py:121
  10.9 4.7 %collective-permute-start.3 = (bf16[48,256]{1,0:T(8,128)(2,1)S(1)}, bf16[48,256]{1,0:T(8,128)(2,1)S(1)}, u32[]{:S(2)}, u32[]{:S(2)}) collective-permute-start(bf16[48,256]{1,0:T(8,128)(2,1)S(1)} %shard_map.64.refs_0_), channel_id=1, source_target_pairs={{0,4},{4,0},{8,12},{12,8},{1,5},{5,1},{9,13},{13,9},{2,6},{6,2},{1... | collective-permute-start | bytes 73736 | tf_op jit(solution)/shard_map/ppermute | solution.py:121
  16.1 1.6 %collective-permute-start.12 = (f32[256,256]{1,0:T(8,128)S(1)}, f32[256,256]{1,0:T(8,128)S(1)}, u32[]{:S(2)}, u32[]{:S(2)}) collective-permute-start(f32[256,256]{1,0:T(8,128)S(1)} %get-tuple-element.41), channel_id=1, source_target_pairs={{0,1},{1,0},{2,3},{3,2},{4,5},{5,4},{6,7},{7,6},{8,9},{9,8},{10,11... | collective-permute-start | bytes 786440 | tf_op jit(solution)/shard_map/ppermute | solution.py:147
  16.7 2.6 %collective-permute-start.8 = (f32[96,256]{1,0:T(8,128)S(1)}, f32[96,256]{1,0:T(8,128)S(1)}, u32[]{:S(2)}, u32[]{:S(2)}) collective-permute-start(f32[96,256]{1,0:T(8,128)S(1)} %get-tuple-element.37), channel_id=1, source_target_pairs={{0,1},{1,0},{2,3},{3,2},{4,5},{5,4},{6,7},{7,6},{8,9},{9,8},{10,11... | collective-permute-start | bytes 294920 | tf_op jit(solution)/shard_map/ppermute | solution.py:147
  17.3 4.5 %collective-permute-start.11 = (f32[256,256]{1,0:T(8,128)S(1)}, f32[256,256]{1,0:T(8,128)S(1)}, u32[]{:S(2)}, u32[]{:S(2)}) collective-permute-start(f32[256,256]{1,0:T(8,128)S(1)} %get-tuple-element.39), channel_id=1, source_target_pairs={{0,1},{1,0},{2,3},{3,2},{4,5},{5,4},{6,7},{7,6},{8,9},{9,8},{10,11... | collective-permute-start | bytes 786440 | tf_op jit(solution)/shard_map/ppermute | solution.py:147
  17.7 5.6 %collective-permute-start.13 = (bf16[256,256]{1,0:T(8,128)(2,1)S(1)}, bf16[256,256]{1,0:T(8,128)(2,1)S(1)}, u32[]{:S(2)}, u32[]{:S(2)}) collective-permute-start(bf16[256,256]{1,0:T(8,128)(2,1)S(1)} %add_convert_fusion.2), channel_id=1, source_target_pairs={{0,2},{1,3},{2,0},{3,1},{4,6},{5,7},{6,4},{7,5},{8,10},{9,11},{10,... | collective-permute-start | bytes 393224 | tf_op jit(solution)/shard_map/ppermute | solution.py:147
  19.3 6.3 %collective-permute-start.10 = (bf16[96,256]{1,0:T(8,128)(2,1)S(1)}, bf16[96,256]{1,0:T(8,128)(2,1)S(1)}, u32[]{:S(2)}, u32[]{:S(2)}) collective-permute-start(bf16[96,256]{1,0:T(8,128)(2,1)S(1)} %add_convert_fusion.3.refs_0_), channel_id=1, source_target_pairs={{0,8},{1,13},{2,10},{3,15},{4,12},{5,9},{6,14},{7,11},{8,0},{9,5},... | collective-permute-start | bytes 147464 | tf_op jit(solution)/shard_map/ppermute | solution.py:143
  21.4 4.2 %collective-permute-start.9 = (bf16[48,256]{1,0:T(8,128)(2,1)S(1)}, bf16[48,256]{1,0:T(8,128)(2,1)S(1)}, u32[]{:S(2)}, u32[]{:S(2)}) collective-permute-start(bf16[48,256]{1,0:T(8,128)(2,1)S(1)} %slice.21), channel_id=1, source_target_pairs={{0,4},{4,0},{8,12},{12,8},{1,5},{5,1},{9,13},{13,9},{2,6},{6,2},{1... | collective-permute-start | bytes 73736 | tf_op jit(solution)/shard_map/ppermute | solution.py:121
  23.4 5.0 %collective-permute-start.15 = (bf16[256,256]{1,0:T(8,128)(2,1)S(1)}, bf16[256,256]{1,0:T(8,128)(2,1)S(1)}, u32[]{:S(2)}, u32[]{:S(2)}) collective-permute-start(bf16[256,256]{1,0:T(8,128)(2,1)S(1)} %add_convert_fusion.1.refs_4_), channel_id=1, source_target_pairs={{0,4},{4,0},{8,12},{12,8},{1,5},{5,1},{9,13},{13,9},{2,6},{6,2},{1... | collective-permute-start | bytes 393224 | tf_op jit(solution)/shard_map/ppermute | solution.py:121
  25.6 1.6 %collective-permute-start.16 = (bf16[256,256]{1,0:T(8,128)(2,1)S(1)}, bf16[256,256]{1,0:T(8,128)(2,1)S(1)}, u32[]{:S(2)}, u32[]{:S(2)}) collective-permute-start(bf16[256,256]{1,0:T(8,128)(2,1)S(1)} %add_convert_fusion.1.refs_4_), channel_id=1, source_target_pairs={{0,1},{1,0},{2,3},{3,2},{4,8},{5,9},{6,10},{7,11},{8,4},{9,5},{10,... | collective-permute-start | bytes 393224 | tf_op jit(solution)/shard_map/ppermute | solution.py:133
  25.7 1.5 %collective-permute-start.14 = (bf16[2,24,1024]{2,1,0:T(8,128)(2,1)S(1)}, bf16[2,24,1024]{2,1,0:T(8,128)(2,1)S(1)}, u32[]{:S(2)}, u32[]{:S(2)}) collective-permute-start(bf16[2,24,1024]{2,1,0:T(8,128)(2,1)S(1)} %pad_maximum_fusion.2), channel_id=1, source_target_pairs={{0,1},{1,0},{2,3},{3,2},{4,5},{5,4},{6,7},{7,6},{8,9},{9,8},{10,11... | collective-permute-start | bytes 294920 | tf_op jit(solution)/shard_map/ppermute | solution.py:147
  28.8 1.6 %collective-permute-start.17 = (f32[256,256]{1,0:T(8,128)S(1)}, f32[256,256]{1,0:T(8,128)S(1)}, u32[]{:S(2)}, u32[]{:S(2)}) collective-permute-start(f32[256,256]{1,0:T(8,128)S(1)} %shard_map.69), channel_id=1, source_target_pairs={{0,1},{1,0},{2,3},{3,2},{4,5},{5,4},{6,7},{7,6},{8,9},{9,8},{10,11... | collective-permute-start | bytes 786440 | tf_op jit(solution)/shard_map/ppermute | solution.py:147
  30.4 5.6 %collective-permute-start.20 = (bf16[256,256]{1,0:T(8,128)(2,1)S(1)}, bf16[256,256]{1,0:T(8,128)(2,1)S(1)}, u32[]{:S(2)}, u32[]{:S(2)}) collective-permute-start(bf16[256,256]{1,0:T(8,128)(2,1)S(1)} %add_convert_fusion), channel_id=1, source_target_pairs={{0,2},{1,3},{2,0},{3,1},{4,6},{5,7},{6,4},{7,5},{8,10},{9,11},{10,... | collective-permute-start | bytes 393224 | tf_op jit(solution)/shard_map/ppermute | solution.py:147
  32.5 3.5 %collective-permute-start.18 = (f32[128,256]{1,0:T(8,128)S(1)}, f32[128,256]{1,0:T(8,128)S(1)}, u32[]{:S(2)}, u32[]{:S(2)}) collective-permute-start(f32[128,256]{1,0:T(8,128)S(1)} %get-tuple-element.51), channel_id=1, source_target_pairs={{0,1},{1,0},{2,3},{3,2},{4,5},{5,4},{6,7},{7,6},{8,9},{9,8},{10,11... | collective-permute-start | bytes 393224 | tf_op jit(solution)/shard_map/ppermute | solution.py:147
  32.6 3.5 %collective-permute-start.19 = (f32[128,256]{1,0:T(8,128)S(1)}, f32[128,256]{1,0:T(8,128)S(1)}, u32[]{:S(2)}, u32[]{:S(2)}) collective-permute-start(f32[128,256]{1,0:T(8,128)S(1)} %get-tuple-element.52), channel_id=1, source_target_pairs={{0,1},{1,0},{2,3},{3,2},{4,5},{5,4},{6,7},{7,6},{8,9},{9,8},{10,11... | collective-permute-start | bytes 393224 | tf_op jit(solution)/shard_map/ppermute | solution.py:147

commit v15 on v14

--- a/solution.py
+++ b/solution.py
@@ -165,7 +165,7 @@
     )
 
 
-def near_kernel(turns, near_ref, own_ref, first_ref, second_ref, *refs):
+def near_kernel(turns, near_ref, own_ref, second_ref, first_ref, *refs):
     base_refs, out_refs = refs[: -len(turns)], refs[-len(turns) :]
     count = lax.axis_size("tile")
     tile = lax.axis_index("tile")
@@ -229,13 +229,11 @@
     refs[-1][...] = jnp.concatenate(groups[2:] + groups[:2])
 
 
-def second_kernel(turns, columns_ref, bases_ref, across_ref, other_ref, *refs):
-    operand_refs, out_refs = refs[3:-len(turns)], refs[-len(turns) :]
+def far_kernel(turns, columns_ref, bases_ref, across_ref, other_ref, *refs):
     bases_refs = (bases_ref, across_ref, other_ref)
     parts = far_parts(far_choice, turns, columns_ref, bases_refs, refs[:3])
-    for (_, total), out_ref in zip(parts, out_refs):
+    for (_, total), out_ref in zip(parts, refs[3:]):
         out_ref[...] = total
-    near_kernel(turns, *operand_refs, *out_refs, *out_refs)
 
 
 def one_slot(probes, right_bases, left_bases, near_tiles, tile_ranks, column_rows, row_columns):
@@ -250,7 +248,7 @@
     bases, probes = lax.optimization_barrier((bases, probes))
     across = list_swap(bases, 2)
     block = probes.astype(BF)
-    beside = [block, tile_swap(block, 1), middle_swap(block)]
+    beside = [block, middle_swap(block), tile_swap(block, 1)]
     (own,) = kernel_call(
         coefficient_kernel,
         [((ranks // 2, probe_count), BF)],
@@ -281,18 +279,17 @@
     held, held_across, near_by, far, ready = lax.optimization_barrier(
         (bases, across, near_by, far, block)
     )
-    beside = [block, tile_swap(block, 1), middle_swap(ready)]
+    beside = [block, middle_swap(ready), tile_swap(block, 1)]
     left = list_swap(jnp.stack([held[1], held_across[1]]), 1)
 
-    operands = (*fixed, left, own, near_by, far, near, *beside)
-    (send,) = call(second_kernel, (3,), operands)
+    base = call(far_kernel, (3, 2, 1, 0), (*fixed, left, own, near_by, far), cost=0)
+    (send,) = call(near_kernel, (3,), (near, *beside, base[0]))
     arrived = list_swap(send, 1)
-    (keep,) = call(second_kernel, (2,), operands)
+    (keep,) = call(near_kernel, (2,), (near, *beside, base[1]))
     crossing = (keep + arrived).astype(BF)
-    left, crossing = lax.optimization_barrier((left, crossing))
+    near, crossing = lax.optimization_barrier((near, crossing))
     crossed = list_swap(crossing, 2)
-    operands = (*fixed, left, own, near_by, far, near, *beside)
-    send, keep = call(second_kernel, (1, 0), operands)
+    send, keep = call(near_kernel, (1, 0), (near, *beside, *base[2:]))
     return keep + list_swap_in_pieces(send, 1, 2) + crossed
 
 

time: 37 us -> 37.2 us (level)
  waiting for transfers between devices: 9.5 us -> 13.2 us
  starting transfers between devices: 20.1 us -> 16.6 us
    ppermute x6, starting transfers between devices: 9.28 us -> 6.51 us  [tile_swap(): lax.ppermute(block, 'tile', [(i, i ^ turn) for i in range(lax.axis_size('...]
    ppermute x6, waiting for transfers between devices: 2.51 us -> 5.09 us  [tile_swap(): lax.ppermute(block, 'tile', [(i, i ^ turn) for i in range(lax.axis_size('...]
    ppermute x12, waiting for transfers between devices: 6.98 us -> 8.09 us  [list_swap(): lax.ppermute(block, 'list', [(i, i ^ bit) for i in range(lax.axis_size('l...]
    pallas_call x7 -> x8, Pallas kernels: 2.9 us -> 2.95 us  [kernel_call(): pl.pallas_call(kernel, out_shape=tuple((jax.ShapeDtypeStruct(shape, kind)...]
  transfers between devices with their start and end apart: 21 -> 21, of which waited for: 8 -> 9; matrix products, arithmetic and copies ran while one was open for 3% -> 3% of each run, Pallas kernels for 6% -> 6%
where the time goes in v15:
time: 37.2 us; the launch traced here: 37 us
  starting transfers between devices  16.6 us (45%)
  waiting for transfers between devices  13.2 us (35%)
  Pallas kernels  2.95 us (8%)
  other arithmetic  2.69 us (7%)
  between operations  1.53 us (4%)
    ppermute x12, waiting for transfers between devices, list_swap(): lax.ppermute(block, 'list', [(i, i ^ bit) for i in range(lax.axis_size('l...  8.09 us
    ppermute x12, starting transfers between devices, list_swap(): lax.ppermute(block, 'list', [(i, i ^ bit) for i in range(lax.axis_size('l...  7.79 us
    ppermute x6, starting transfers between devices, tile_swap(): lax.ppermute(block, 'tile', [(i, i ^ turn) for i in range(lax.axis_size('...  6.51 us
    ppermute x6, waiting for transfers between devices, tile_swap(): lax.ppermute(block, 'tile', [(i, i ^ turn) for i in range(lax.axis_size('...  5.09 us
    pallas_call x8, Pallas kernels, kernel_call(): pl.pallas_call(kernel, out_shape=tuple((jax.ShapeDtypeStruct(shape, kind)...  2.95 us
    ppermute x1, starting transfers between devices, far_swap(): return lax.ppermute(block, ('tile', 'list'), route)  2.09 us
    convert_element_type x1, other arithmetic, one_slot(): block = probes.astype(BF)  0.96 us
    another operation x1, other arithmetic, one_slot(): bases = jnp.stack([right_bases[0, 0], left_bases[0, 0]])  0.83 us
  transfers between devices with their start and end apart: 21, of which 9 were waited for; matrix products, arithmetic and copies ran while one was open for 3% of the time, Pallas kernels for 6%

profile of v15, /device:TPU:0, one launch (start us, length us, event | category | flops | bytes accessed | tf_op | source)
XLA Modules:
  0.0 37.0 jit_solution(2468809871399070040)
XLA Ops:
  0.0 0.8 %pad_maximum_fusion.bases_ref = bf16[2,24,1024]{2,1,0:T(8,128)(2,1)S(1)} fusion(bf16[1,24,1024]{2,1,0:T(8,128)(2,1)} %bitcast.9, bf16[1,24,1024]{2,1,0:T(8,128)(2,1)} %bitcast.10), kind=kLoop, calls=%fused_computation.5 | loop fusion | flops 49152 | bytes 196608 | tf_op jit(solution)/shard_map/stack | solution.py:247
  0.8 3.0 %collective-permute-start = (bf16[2,24,1024]{2,1,0:T(8,128)(2,1)S(1)}, bf16[2,24,1024]{2,1,0:T(8,128)(2,1)S(1)}, u32[]{:S(2)}, u32[]{:S(2)}) collective-permute-start(bf16[2,24,1024]{2,1,0:T(8,128)(2,1)S(1)} %pad_maximum_fusion.bases_ref), channel_id=1, source_target_pairs={{0,2},{1,3},{2,0},{3,1},{4,6},{5,7},{6,4},{7,5},{8,10},{9,11},{10,... | collective-permute-start | bytes 294920 | tf_op jit(solution)/shard_map/ppermute | solution.py:147
  3.8 1.0 %convert_element_type.21.block_ref.own_ref = bf16[256,256]{1,0:T(8,128)(2,1)S(1)} convert(f32[256,256]{1,0:T(8,128)} %param.7) | non-fusion elementwise | flops 65536 | bytes 393216 | tf_op jit(solution)/shard_map/convert_element_type | solution.py:250
  4.9 1.6 %collective-permute-start.7 = (bf16[256,256]{1,0:T(8,128)(2,1)S(1)}, bf16[256,256]{1,0:T(8,128)(2,1)S(1)}, u32[]{:S(2)}, u32[]{:S(2)}) collective-permute-start(bf16[256,256]{1,0:T(8,128)(2,1)S(1)} %convert_element_type.21.block_ref.own_ref), channel_id=1, source_target_pairs={{0,4},{4,0},{8,12},{12,8},{1,5},{5,1},{9,13},{13,9},{2,6},{6,2},{1... | collective-permute-start | bytes 393224 | tf_op jit(solution)/shard_map/ppermute | solution.py:121
  7.6 0.4 %collective-permute-start.2 = (bf16[2,24,1024]{2,1,0:T(8,128)(2,1)S(1)}, bf16[2,24,1024]{2,1,0:T(8,128)(2,1)S(1)}, u32[]{:S(2)}, u32[]{:S(2)}) collective-permute-start(bf16[2,24,1024]{2,1,0:T(8,128)(2,1)S(1)} %pad_maximum_fusion.1), channel_id=1, source_target_pairs={{0,1},{1,0},{2,3},{3,2},{4,5},{5,4},{6,7},{7,6},{8,9},{9,8},{10,11... | collective-permute-start | bytes 294920 | tf_op jit(solution)/shard_map/ppermute | solution.py:147
  8.0 2.9 %collective-permute-start.5 = (bf16[48,256]{1,0:T(8,128)(2,1)S(1)}, bf16[48,256]{1,0:T(8,128)(2,1)S(1)}, u32[]{:S(2)}, u32[]{:S(2)}) collective-permute-start(bf16[48,256]{1,0:T(8,128)(2,1)S(1)} %shard_map.64.refs_0_), channel_id=1, source_target_pairs={{0,12},{4,8},{8,4},{12,0},{1,13},{5,9},{9,5},{13,1},{2,14},{6,10},... | collective-permute-start | bytes 73736 | tf_op jit(solution)/shard_map/ppermute | solution.py:121
  10.9 1.3 %collective-permute-start.4 = (bf16[48,256]{1,0:T(8,128)(2,1)S(1)}, bf16[48,256]{1,0:T(8,128)(2,1)S(1)}, u32[]{:S(2)}, u32[]{:S(2)}) collective-permute-start(bf16[48,256]{1,0:T(8,128)(2,1)S(1)} %shard_map.64.refs_0_), channel_id=1, source_target_pairs={{0,8},{4,12},{8,0},{12,4},{1,9},{5,13},{9,1},{13,5},{2,10},{6,14},... | collective-permute-start | bytes 73736 | tf_op jit(solution)/shard_map/ppermute | solution.py:121
  13.1 0.6 %shard_map.65 = (f32[256,256]{1,0:T(8,128)S(1)}, f32[256,256]{1,0:T(8,128)S(1)}, f32[256,256]{1,0:T(8,128)S(1)}, f32[256,256]{1,0:T(8,128)S(1)}) custom-call(bf16[3,1024,256]{2,1,0:T(8,128)(2,1)S(1)} %bitcast.5, bf16[256,256]{1,0:T(8,128)(2,1)S(1)} %convert_element_type.21.block_ref.own_ref, bf16[256,256]{1,0:T(8,128)(2,1)S(1)} %collective-permute-done.6.second_ref, ...), custom_call_target="tpu_custom_call" | custom-call | tf_op jit(solution)/shard_map/pallas_call | solution.py:77
  13.7 2.0 %collective-permute-done.4.refs_2_ = bf16[48,256]{1,0:T(8,128)(2,1)S(1)} collective-permute-done((bf16[48,256]{1,0:T(8,128)(2,1)S(1)}, bf16[48,256]{1,0:T(8,128)(2,1)S(1)}, u32[]{:S(2)}, u32[]{:S(2)}) %collective-permute-start.4) | collective-permute-done | bytes 24608 | tf_op jit(solution)/shard_map/ppermute | solution.py:121
  16.0 0.4 %shard_map.66 = (f32[256,256]{1,0:T(8,128)S(1)}, f32[96,256]{1,0:T(8,128)S(1)}) custom-call(s32[1,1]{1,0:T(1,128)S(6)} %copy.8.columns_ref, bf16[2,24,1024]{2,1,0:T(8,128)(2,1)S(1)} %pad_maximum_fusion.bases_ref, bf16[2,24,1024]{2,1,0:T(8,128)(2,1)S(1)} %collective-permute-done.across_ref, bf16[2,24,1024]{2,1,0:T(8,128)(2,1)S(1)} %collective-permute-done.2.other_ref, ...), custom_call_target="tpu_custom_call" | custom-call | flops 100663296 | bytes 98304 | tf_op jit(solution)/shard_map/pallas_call | solution.py:77
  16.5 0.5 %shard_map.67 = (f32[256,256]{1,0:T(8,128)S(1)}, f32[256,256]{1,0:T(8,128)S(1)}, f32[256,256]{1,0:T(8,128)S(1)}, f32[96,256]{1,0:T(8,128)S(1)}, f32[96,256]{1,0:T(8,128)S(1)}) custom-call(s32[1,1]{1,0:T(1,128)S(6)} %copy.8.columns_ref, bf16[2,24,1024]{2,1,0:T(8,128)(2,1)S(1)} %pad_maximum_fusion.bases_ref, ...), custom_call_target="tpu_custom_call" | custom-call | flops 301989888 | bytes 294912 | tf_op jit(solution)/shard_map/pallas_call | solution.py:77
  17.1 0.6 %collective-permute-start.11 = (f32[96,256]{1,0:T(8,128)S(1)}, f32[96,256]{1,0:T(8,128)S(1)}, u32[]{:S(2)}, u32[]{:S(2)}) collective-permute-start(f32[96,256]{1,0:T(8,128)S(1)} %get-tuple-element.45), channel_id=1, source_target_pairs={{0,1},{1,0},{2,3},{3,2},{4,5},{5,4},{6,7},{7,6},{8,9},{9,8},{10,11... | collective-permute-start | bytes 294920 | tf_op jit(solution)/shard_map/ppermute | solution.py:147
  18.1 1.2 %collective-permute-start.10 = (bf16[256,256]{1,0:T(8,128)(2,1)S(1)}, bf16[256,256]{1,0:T(8,128)(2,1)S(1)}, u32[]{:S(2)}, u32[]{:S(2)}) collective-permute-start(bf16[256,256]{1,0:T(8,128)(2,1)S(1)} %add_convert_fusion.2), channel_id=1, source_target_pairs={{0,2},{1,3},{2,0},{3,1},{4,6},{5,7},{6,4},{7,5},{8,10},{9,11},{10,... | collective-permute-start | bytes 393224 | tf_op jit(solution)/shard_map/ppermute | solution.py:147
  19.3 2.1 %collective-permute-start.13 = (bf16[96,256]{1,0:T(8,128)(2,1)S(1)}, bf16[96,256]{1,0:T(8,128)(2,1)S(1)}, u32[]{:S(2)}, u32[]{:S(2)}) collective-permute-start(bf16[96,256]{1,0:T(8,128)(2,1)S(1)} %add_convert_fusion.3.refs_0_), channel_id=1, source_target_pairs={{0,8},{1,13},{2,10},{3,15},{4,12},{5,9},{6,14},{7,11},{8,0},{9,5},... | collective-permute-start | bytes 147464 | tf_op jit(solution)/shard_map/ppermute | solution.py:143
  21.5 2.1 %collective-permute-done.10 = bf16[256,256]{1,0:T(8,128)(2,1)S(1)} collective-permute-done((bf16[256,256]{1,0:T(8,128)(2,1)S(1)}, bf16[256,256]{1,0:T(8,128)(2,1)S(1)}, u32[]{:S(2)}, u32[]{:S(2)}) %collective-permute-start.10) | collective-permute-done | bytes 131104 | tf_op jit(solution)/shard_map/ppermute | solution.py:147
  24.0 1.2 %collective-permute-done.12.refs_1_ = bf16[48,256]{1,0:T(8,128)(2,1)S(1)} collective-permute-done((bf16[48,256]{1,0:T(8,128)(2,1)S(1)}, bf16[48,256]{1,0:T(8,128)(2,1)S(1)}, u32[]{:S(2)}, u32[]{:S(2)}) %collective-permute-start.12) | collective-permute-done | bytes 24608 | tf_op jit(solution)/shard_map/ppermute | solution.py:121
  25.3 0.6 %collective-permute-start.16 = (bf16[2,24,1024]{2,1,0:T(8,128)(2,1)S(1)}, bf16[2,24,1024]{2,1,0:T(8,128)(2,1)S(1)}, u32[]{:S(2)}, u32[]{:S(2)}) collective-permute-start(bf16[2,24,1024]{2,1,0:T(8,128)(2,1)S(1)} %pad_maximum_fusion.2), channel_id=1, source_target_pairs={{0,1},{1,0},{2,3},{3,2},{4,5},{5,4},{6,7},{7,6},{8,9},{9,8},{10,11... | collective-permute-start | bytes 294920 | tf_op jit(solution)/shard_map/ppermute | solution.py:147
  25.9 0.9 %collective-permute-done.16.other_ref = bf16[2,24,1024]{2,1,0:T(8,128)(2,1)S(1)} collective-permute-done((bf16[2,24,1024]{2,1,0:T(8,128)(2,1)S(1)}, bf16[2,24,1024]{2,1,0:T(8,128)(2,1)S(1)}, u32[]{:S(2)}, u32[]{:S(2)}) %collective-permute-start.16) | collective-permute-done | bytes 98336 | tf_op jit(solution)/shard_map/ppermute | solution.py:147
  27.2 1.5 %collective-permute-done.15.first_ref = bf16[256,256]{1,0:T(8,128)(2,1)S(1)} collective-permute-done((bf16[256,256]{1,0:T(8,128)(2,1)S(1)}, bf16[256,256]{1,0:T(8,128)(2,1)S(1)}, u32[]{:S(2)}, u32[]{:S(2)}) %collective-permute-start.15) | collective-permute-done | bytes 131104 | tf_op jit(solution)/shard_map/ppermute | solution.py:121
  29.4 1.2 %collective-permute-done.17 = f32[256,256]{1,0:T(8,128)S(1)} collective-permute-done((f32[256,256]{1,0:T(8,128)S(1)}, f32[256,256]{1,0:T(8,128)S(1)}, u32[]{:S(2)}, u32[]{:S(2)}) %collective-permute-start.17) | collective-permute-done | bytes 262176 | tf_op jit(solution)/shard_map/ppermute | solution.py:147
  30.7 1.2 %collective-permute-start.20 = (bf16[256,256]{1,0:T(8,128)(2,1)S(1)}, bf16[256,256]{1,0:T(8,128)(2,1)S(1)}, u32[]{:S(2)}, u32[]{:S(2)}) collective-permute-start(bf16[256,256]{1,0:T(8,128)(2,1)S(1)} %add_convert_fusion), channel_id=1, source_target_pairs={{0,2},{1,3},{2,0},{3,1},{4,6},{5,7},{6,4},{7,5},{8,10},{9,11},{10,... | collective-permute-start | bytes 393224 | tf_op jit(solution)/shard_map/ppermute | solution.py:147
  32.3 0.5 %collective-permute-start.19 = (f32[128,256]{1,0:T(8,128)S(1)}, f32[128,256]{1,0:T(8,128)S(1)}, u32[]{:S(2)}, u32[]{:S(2)}) collective-permute-start(f32[128,256]{1,0:T(8,128)S(1)} %get-tuple-element.60), channel_id=1, source_target_pairs={{0,1},{1,0},{2,3},{3,2},{4,5},{5,4},{6,7},{7,6},{8,9},{9,8},{10,11... | collective-permute-start | bytes 393224 | tf_op jit(solution)/shard_map/ppermute | solution.py:147
  32.8 3.4 %collective-permute-done.20 = bf16[256,256]{1,0:T(8,128)(2,1)S(1)} collective-permute-done((bf16[256,256]{1,0:T(8,128)(2,1)S(1)}, bf16[256,256]{1,0:T(8,128)(2,1)S(1)}, u32[]{:S(2)}, u32[]{:S(2)}) %collective-permute-start.20) | collective-permute-done | bytes 131104 | tf_op jit(solution)/shard_map/ppermute | solution.py:147
  36.3 0.7 %fusion = f32[256,256]{1,0:T(8,128)} fusion(f32[256,256]{1,0:T(8,128)S(1)} %get-tuple-element.56, f32[128,256]{1,0:T(8,128)S(1)} %collective-permute-done.19, f32[128,256]{1,0:T(8,128)S(1)} %collective-permute-done.18, bf16[256,256]{1,0:T(8,128)(2,1)S(1)} %collective-permute-done.20), kind=kLoop, calls=%fused_computation.1 | loop fusion | flops 262144 | bytes 917504 | tf_op jit(solution)/shard_map/add | solution.py:293
  (43 shorter events, 3.7 us)
Async XLA Ops:
  0.8 6.5 %collective-permute-start = (bf16[2,24,1024]{2,1,0:T(8,128)(2,1)S(1)}, bf16[2,24,1024]{2,1,0:T(8,128)(2,1)S(1)}, u32[]{:S(2)}, u32[]{:S(2)}) collective-permute-start(bf16[2,24,1024]{2,1,0:T(8,128)(2,1)S(1)} %pad_maximum_fusion.bases_ref), channel_id=1, source_target_pairs={{0,2},{1,3},{2,0},{3,1},{4,6},{5,7},{6,4},{7,5},{8,10},{9,11},{10,... | collective-permute-start | bytes 294920 | tf_op jit(solution)/shard_map/ppermute | solution.py:147
  4.8 2.6 %collective-permute-start.1 = (bf16[256,256]{1,0:T(8,128)(2,1)S(1)}, bf16[256,256]{1,0:T(8,128)(2,1)S(1)}, u32[]{:S(2)}, u32[]{:S(2)}) collective-permute-start(bf16[256,256]{1,0:T(8,128)(2,1)S(1)} %convert_element_type.21.block_ref.own_ref), channel_id=1, source_target_pairs={{0,1},{1,0},{2,3},{3,2},{4,5},{5,4},{6,7},{7,6},{8,9},{9,8},{10,11... | collective-permute-start | bytes 393224 | tf_op jit(solution)/shard_map/ppermute | solution.py:147
  4.9 7.3 %collective-permute-start.7 = (bf16[256,256]{1,0:T(8,128)(2,1)S(1)}, bf16[256,256]{1,0:T(8,128)(2,1)S(1)}, u32[]{:S(2)}, u32[]{:S(2)}) collective-permute-start(bf16[256,256]{1,0:T(8,128)(2,1)S(1)} %convert_element_type.21.block_ref.own_ref), channel_id=1, source_target_pairs={{0,4},{4,0},{8,12},{12,8},{1,5},{5,1},{9,13},{13,9},{2,6},{6,2},{1... | collective-permute-start | bytes 393224 | tf_op jit(solution)/shard_map/ppermute | solution.py:121
  6.5 6.5 %collective-permute-start.6 = (bf16[256,256]{1,0:T(8,128)(2,1)S(1)}, bf16[256,256]{1,0:T(8,128)(2,1)S(1)}, u32[]{:S(2)}, u32[]{:S(2)}) collective-permute-start(bf16[256,256]{1,0:T(8,128)(2,1)S(1)} %convert_element_type.21.block_ref.own_ref), channel_id=1, source_target_pairs={{0,1},{1,0},{2,3},{3,2},{4,8},{5,9},{6,10},{7,11},{8,4},{9,5},{10,... | collective-permute-start | bytes 393224 | tf_op jit(solution)/shard_map/ppermute | solution.py:133
  7.4 5.7 %copy-start = (bf16[1,1024,3,256]{3,1,2,0:T(8,128)(2,1)S(1)}, bf16[1,1024,3,256]{3,1,2,0:T(8,128)(2,1)}, u32[]{:S(2)}) copy-start(bf16[1,1024,3,256]{3,1,2,0:T(8,128)(2,1)} %param.10) | copy-start | bytes 4718596
  7.6 8.4 %collective-permute-start.2 = (bf16[2,24,1024]{2,1,0:T(8,128)(2,1)S(1)}, bf16[2,24,1024]{2,1,0:T(8,128)(2,1)S(1)}, u32[]{:S(2)}, u32[]{:S(2)}) collective-permute-start(bf16[2,24,1024]{2,1,0:T(8,128)(2,1)S(1)} %pad_maximum_fusion.1), channel_id=1, source_target_pairs={{0,1},{1,0},{2,3},{3,2},{4,5},{5,4},{6,7},{7,6},{8,9},{9,8},{10,11... | collective-permute-start | bytes 294920 | tf_op jit(solution)/shard_map/ppermute | solution.py:147
  8.0 5.7 %collective-permute-start.5 = (bf16[48,256]{1,0:T(8,128)(2,1)S(1)}, bf16[48,256]{1,0:T(8,128)(2,1)S(1)}, u32[]{:S(2)}, u32[]{:S(2)}) collective-permute-start(bf16[48,256]{1,0:T(8,128)(2,1)S(1)} %shard_map.64.refs_0_), channel_id=1, source_target_pairs={{0,12},{4,8},{8,4},{12,0},{1,13},{5,9},{9,5},{13,1},{2,14},{6,10},... | collective-permute-start | bytes 73736 | tf_op jit(solution)/shard_map/ppermute | solution.py:121
  10.9 4.7 %collective-permute-start.4 = (bf16[48,256]{1,0:T(8,128)(2,1)S(1)}, bf16[48,256]{1,0:T(8,128)(2,1)S(1)}, u32[]{:S(2)}, u32[]{:S(2)}) collective-permute-start(bf16[48,256]{1,0:T(8,128)(2,1)S(1)} %shard_map.64.refs_0_), channel_id=1, source_target_pairs={{0,8},{4,12},{8,0},{12,4},{1,9},{5,13},{9,1},{13,5},{2,10},{6,14},... | collective-permute-start | bytes 73736 | tf_op jit(solution)/shard_map/ppermute | solution.py:121
  12.2 3.8 %collective-permute-start.3 = (bf16[48,256]{1,0:T(8,128)(2,1)S(1)}, bf16[48,256]{1,0:T(8,128)(2,1)S(1)}, u32[]{:S(2)}, u32[]{:S(2)}) collective-permute-start(bf16[48,256]{1,0:T(8,128)(2,1)S(1)} %shard_map.64.refs_0_), channel_id=1, source_target_pairs={{0,4},{4,0},{8,12},{12,8},{1,5},{5,1},{9,13},{13,9},{2,6},{6,2},{1... | collective-permute-start | bytes 73736 | tf_op jit(solution)/shard_map/ppermute | solution.py:121
  16.4 1.6 %collective-permute-start.9 = (f32[256,256]{1,0:T(8,128)S(1)}, f32[256,256]{1,0:T(8,128)S(1)}, u32[]{:S(2)}, u32[]{:S(2)}) collective-permute-start(f32[256,256]{1,0:T(8,128)S(1)} %get-tuple-element.43), channel_id=1, source_target_pairs={{0,1},{1,0},{2,3},{3,2},{4,5},{5,4},{6,7},{7,6},{8,9},{9,8},{10,11... | collective-permute-start | bytes 786440 | tf_op jit(solution)/shard_map/ppermute | solution.py:147
  17.1 2.2 %collective-permute-start.11 = (f32[96,256]{1,0:T(8,128)S(1)}, f32[96,256]{1,0:T(8,128)S(1)}, u32[]{:S(2)}, u32[]{:S(2)}) collective-permute-start(f32[96,256]{1,0:T(8,128)S(1)} %get-tuple-element.45), channel_id=1, source_target_pairs={{0,1},{1,0},{2,3},{3,2},{4,5},{5,4},{6,7},{7,6},{8,9},{9,8},{10,11... | collective-permute-start | bytes 294920 | tf_op jit(solution)/shard_map/ppermute | solution.py:147
  17.6 3.9 %collective-permute-start.8 = (f32[256,256]{1,0:T(8,128)S(1)}, f32[256,256]{1,0:T(8,128)S(1)}, u32[]{:S(2)}, u32[]{:S(2)}) collective-permute-start(f32[256,256]{1,0:T(8,128)S(1)} %get-tuple-element.41), channel_id=1, source_target_pairs={{0,1},{1,0},{2,3},{3,2},{4,5},{5,4},{6,7},{7,6},{8,9},{9,8},{10,11... | collective-permute-start | bytes 786440 | tf_op jit(solution)/shard_map/ppermute | solution.py:147
  18.1 5.6 %collective-permute-start.10 = (bf16[256,256]{1,0:T(8,128)(2,1)S(1)}, bf16[256,256]{1,0:T(8,128)(2,1)S(1)}, u32[]{:S(2)}, u32[]{:S(2)}) collective-permute-start(bf16[256,256]{1,0:T(8,128)(2,1)S(1)} %add_convert_fusion.2), channel_id=1, source_target_pairs={{0,2},{1,3},{2,0},{3,1},{4,6},{5,7},{6,4},{7,5},{8,10},{9,11},{10,... | collective-permute-start | bytes 393224 | tf_op jit(solution)/shard_map/ppermute | solution.py:147
  19.3 5.9 %collective-permute-start.13 = (bf16[96,256]{1,0:T(8,128)(2,1)S(1)}, bf16[96,256]{1,0:T(8,128)(2,1)S(1)}, u32[]{:S(2)}, u32[]{:S(2)}) collective-permute-start(bf16[96,256]{1,0:T(8,128)(2,1)S(1)} %add_convert_fusion.3.refs_0_), channel_id=1, source_target_pairs={{0,8},{1,13},{2,10},{3,15},{4,12},{5,9},{6,14},{7,11},{8,0},{9,5},... | collective-permute-start | bytes 147464 | tf_op jit(solution)/shard_map/ppermute | solution.py:143
  21.4 3.8 %collective-permute-start.12 = (bf16[48,256]{1,0:T(8,128)(2,1)S(1)}, bf16[48,256]{1,0:T(8,128)(2,1)S(1)}, u32[]{:S(2)}, u32[]{:S(2)}) collective-permute-start(bf16[48,256]{1,0:T(8,128)(2,1)S(1)} %slice.21), channel_id=1, source_target_pairs={{0,4},{4,0},{8,12},{12,8},{1,5},{5,1},{9,13},{13,9},{2,6},{6,2},{1... | collective-permute-start | bytes 73736 | tf_op jit(solution)/shard_map/ppermute | solution.py:121
  23.7 5.0 %collective-permute-start.15 = (bf16[256,256]{1,0:T(8,128)(2,1)S(1)}, bf16[256,256]{1,0:T(8,128)(2,1)S(1)}, u32[]{:S(2)}, u32[]{:S(2)}) collective-permute-start(bf16[256,256]{1,0:T(8,128)(2,1)S(1)} %add_convert_fusion.1.own_ref), channel_id=1, source_target_pairs={{0,4},{4,0},{8,12},{12,8},{1,5},{5,1},{9,13},{13,9},{2,6},{6,2},{1... | collective-permute-start | bytes 393224 | tf_op jit(solution)/shard_map/ppermute | solution.py:121
  25.2 2.0 %collective-permute-start.14 = (bf16[256,256]{1,0:T(8,128)(2,1)S(1)}, bf16[256,256]{1,0:T(8,128)(2,1)S(1)}, u32[]{:S(2)}, u32[]{:S(2)}) collective-permute-start(bf16[256,256]{1,0:T(8,128)(2,1)S(1)} %add_convert_fusion.1.own_ref), channel_id=1, source_target_pairs={{0,1},{1,0},{2,3},{3,2},{4,8},{5,9},{6,10},{7,11},{8,4},{9,5},{10,... | collective-permute-start | bytes 393224 | tf_op jit(solution)/shard_map/ppermute | solution.py:133
  25.3 1.5 %collective-permute-start.16 = (bf16[2,24,1024]{2,1,0:T(8,128)(2,1)S(1)}, bf16[2,24,1024]{2,1,0:T(8,128)(2,1)S(1)}, u32[]{:S(2)}, u32[]{:S(2)}) collective-permute-start(bf16[2,24,1024]{2,1,0:T(8,128)(2,1)S(1)} %pad_maximum_fusion.2), channel_id=1, source_target_pairs={{0,1},{1,0},{2,3},{3,2},{4,5},{5,4},{6,7},{7,6},{8,9},{9,8},{10,11... | collective-permute-start | bytes 294920 | tf_op jit(solution)/shard_map/ppermute | solution.py:147
  29.0 1.6 %collective-permute-start.17 = (f32[256,256]{1,0:T(8,128)S(1)}, f32[256,256]{1,0:T(8,128)S(1)}, u32[]{:S(2)}, u32[]{:S(2)}) collective-permute-start(f32[256,256]{1,0:T(8,128)S(1)} %shard_map.70), channel_id=1, source_target_pairs={{0,1},{1,0},{2,3},{3,2},{4,5},{5,4},{6,7},{7,6},{8,9},{9,8},{10,11... | collective-permute-start | bytes 786440 | tf_op jit(solution)/shard_map/ppermute | solution.py:147
  30.7 5.6 %collective-permute-start.20 = (bf16[256,256]{1,0:T(8,128)(2,1)S(1)}, bf16[256,256]{1,0:T(8,128)(2,1)S(1)}, u32[]{:S(2)}, u32[]{:S(2)}) collective-permute-start(bf16[256,256]{1,0:T(8,128)(2,1)S(1)} %add_convert_fusion), channel_id=1, source_target_pairs={{0,2},{1,3},{2,0},{3,1},{4,6},{5,7},{6,4},{7,5},{8,10},{9,11},{10,... | collective-permute-start | bytes 393224 | tf_op jit(solution)/shard_map/ppermute | solution.py:147
  32.3 4.0 %collective-permute-start.18 = (f32[128,256]{1,0:T(8,128)S(1)}, f32[128,256]{1,0:T(8,128)S(1)}, u32[]{:S(2)}, u32[]{:S(2)}) collective-permute-start(f32[128,256]{1,0:T(8,128)S(1)} %get-tuple-element.59), channel_id=1, source_target_pairs={{0,1},{1,0},{2,3},{3,2},{4,5},{5,4},{6,7},{7,6},{8,9},{9,8},{10,11... | collective-permute-start | bytes 393224 | tf_op jit(solution)/shard_map/ppermute | solution.py:147
  32.3 3.9 %collective-permute-start.19 = (f32[128,256]{1,0:T(8,128)S(1)}, f32[128,256]{1,0:T(8,128)S(1)}, u32[]{:S(2)}, u32[]{:S(2)}) collective-permute-start(f32[128,256]{1,0:T(8,128)S(1)} %get-tuple-element.60), channel_id=1, source_target_pairs={{0,1},{1,0},{2,3},{3,2},{4,5},{5,4},{6,7},{7,6},{8,9},{9,8},{10,11... | collective-permute-start | bytes 393224 | tf_op jit(solution)/shard_map/ppermute | solution.py:147

commit v16 on v15

--- a/solution.py
+++ b/solution.py
@@ -183,7 +183,7 @@
         total = base_refs[index][...] if base_refs else 0.0
         for side, block in blocks:
             total += jnp.dot(near_ref[side, cut, :], block, preferred_element_type=F32)
-        out_refs[index][...] = total
+        out_refs[index][...] = total.astype(out_refs[index].dtype)
 
 
 def far_parts(choice, turns, columns_ref, bases_refs, coefficient_refs):
@@ -216,7 +216,7 @@
     parts = far_parts(near_choice, turns, columns_ref, bases_refs, coefficient_refs)
     for (cut, total), base_ref, out_ref in zip(parts, base_refs, refs):
         total += base_ref[...]
-        out_ref[...] = total
+        out_ref[...] = total.astype(out_ref.dtype)
         totals.append((cut, total.astype(BF)))
     sums = right_products(totals, (*bases_refs, other_ref))
     for ref in sums_before:
@@ -241,7 +241,6 @@
     rank_part = right_bases.shape[2]
     near = near_tiles[0].transpose(1, 0, 2)
     flops = 2 * near.size * probe_count
-    part = ((rows, probe_count), F32)
     ranks = 4 * rank_part
 
     bases = jnp.stack([right_bases[0, 0], left_bases[0, 0]])
@@ -261,13 +260,13 @@
     operands = (*fixed, list_swap(right, 1), *coefficients)
     small = ((ranks, probe_count), F32)
 
-    def call(kernel, turns, operands, more=(), cost=1):
-        outs = [part] * len(turns) + list(more)
+    def call(kernel, turns, operands, more=(), cost=1, kind=F32):
+        outs = [((rows, probe_count), kind)] * len(turns) + list(more)
         kernel = functools.partial(kernel, turns)
         return kernel_call(kernel, outs, operands, cost * len(turns) * flops // 4)
 
     base = call(near_kernel, (3, 2, 1, 0), (near, *beside), cost=0)
-    send, sums = call(first_kernel, (3,), (*operands, base[0]), [small])
+    send, sums = call(first_kernel, (3,), (*operands, base[0]), [small], kind=BF)
     arrived = list_swap(send, 1)
     crossing, send, keep, own, other = call(
         first_kernel, (2, 1, 0), (*operands, *base[1:], sums, tile_ranks), [small] * 2
@@ -283,7 +282,7 @@
     left = list_swap(jnp.stack([held[1], held_across[1]]), 1)
 
     base = call(far_kernel, (3, 2, 1, 0), (*fixed, left, own, near_by, far), cost=0)
-    (send,) = call(near_kernel, (3,), (near, *beside, base[0]))
+    (send,) = call(near_kernel, (3,), (near, *beside, base[0]), kind=BF)
     arrived = list_swap(send, 1)
     (keep,) = call(near_kernel, (2,), (near, *beside, base[1]))
     crossing = (keep + arrived).astype(BF)

time: 37.2 us -> 37 us (level)
  no operation moved by 1% of the time
where the time goes in v16:
time: 37 us; the launch traced here: 36.8 us
  starting transfers between devices  16.7 us (45%)
  waiting for transfers between devices  12.9 us (35%)
  Pallas kernels  2.95 us (8%)
  other arithmetic  2.68 us (7%)
  between operations  1.53 us (4%)
    ppermute x12, waiting for transfers between devices, list_swap(): lax.ppermute(block, 'list', [(i, i ^ bit) for i in range(lax.axis_size('l...  7.79 us
    ppermute x12, starting transfers between devices, list_swap(): lax.ppermute(block, 'list', [(i, i ^ bit) for i in range(lax.axis_size('l...  7.79 us
    ppermute x6, starting transfers between devices, tile_swap(): lax.ppermute(block, 'tile', [(i, i ^ turn) for i in range(lax.axis_size('...  6.59 us
    ppermute x6, waiting for transfers between devices, tile_swap(): lax.ppermute(block, 'tile', [(i, i ^ turn) for i in range(lax.axis_size('...  5.09 us
    pallas_call x8, Pallas kernels, kernel_call(): pl.pallas_call(kernel, out_shape=tuple((jax.ShapeDtypeStruct(shape, kind)...  2.95 us
    ppermute x1, starting transfers between devices, far_swap(): return lax.ppermute(block, ('tile', 'list'), route)  2.09 us
    convert_element_type x1, other arithmetic, one_slot(): block = probes.astype(BF)  0.96 us
    another operation x1, other arithmetic, one_slot(): bases = jnp.stack([right_bases[0, 0], left_bases[0, 0]])  0.83 us
  transfers between devices with their start and end apart: 21, of which 9 were waited for; matrix products, arithmetic and copies ran while one was open for 3% of the time, Pallas kernels for 6%

profile of v16, /device:TPU:0, one launch (start us, length us, event | category | flops | bytes accessed | tf_op | source)
XLA Modules:
  0.0 36.8 jit_solution(10895824538172640755)
XLA Ops:
  0.0 0.8 %pad_maximum_fusion.bases_ref = bf16[2,24,1024]{2,1,0:T(8,128)(2,1)S(1)} fusion(bf16[1,24,1024]{2,1,0:T(8,128)(2,1)} %bitcast.9, bf16[1,24,1024]{2,1,0:T(8,128)(2,1)} %bitcast.10), kind=kLoop, calls=%fused_computation.5 | loop fusion | flops 49152 | bytes 196608 | tf_op jit(solution)/shard_map/stack | solution.py:246
  0.8 3.0 %collective-permute-start = (bf16[2,24,1024]{2,1,0:T(8,128)(2,1)S(1)}, bf16[2,24,1024]{2,1,0:T(8,128)(2,1)S(1)}, u32[]{:S(2)}, u32[]{:S(2)}) collective-permute-start(bf16[2,24,1024]{2,1,0:T(8,128)(2,1)S(1)} %pad_maximum_fusion.bases_ref), channel_id=1, source_target_pairs={{0,2},{1,3},{2,0},{3,1},{4,6},{5,7},{6,4},{7,5},{8,10},{9,11},{10,... | collective-permute-start | bytes 294920 | tf_op jit(solution)/shard_map/ppermute | solution.py:147
  3.8 1.0 %convert_element_type.27.block_ref.own_ref = bf16[256,256]{1,0:T(8,128)(2,1)S(1)} convert(f32[256,256]{1,0:T(8,128)} %param.7) | non-fusion elementwise | flops 65536 | bytes 393216 | tf_op jit(solution)/shard_map/convert_element_type | solution.py:249
  4.9 1.6 %collective-permute-start.7 = (bf16[256,256]{1,0:T(8,128)(2,1)S(1)}, bf16[256,256]{1,0:T(8,128)(2,1)S(1)}, u32[]{:S(2)}, u32[]{:S(2)}) collective-permute-start(bf16[256,256]{1,0:T(8,128)(2,1)S(1)} %convert_element_type.27.block_ref.own_ref), channel_id=1, source_target_pairs={{0,4},{4,0},{8,12},{12,8},{1,5},{5,1},{9,13},{13,9},{2,6},{6,2},{1... | collective-permute-start | bytes 393224 | tf_op jit(solution)/shard_map/ppermute | solution.py:121
  7.6 0.4 %collective-permute-start.2 = (bf16[2,24,1024]{2,1,0:T(8,128)(2,1)S(1)}, bf16[2,24,1024]{2,1,0:T(8,128)(2,1)S(1)}, u32[]{:S(2)}, u32[]{:S(2)}) collective-permute-start(bf16[2,24,1024]{2,1,0:T(8,128)(2,1)S(1)} %pad_maximum_fusion.1), channel_id=1, source_target_pairs={{0,1},{1,0},{2,3},{3,2},{4,5},{5,4},{6,7},{7,6},{8,9},{9,8},{10,11... | collective-permute-start | bytes 294920 | tf_op jit(solution)/shard_map/ppermute | solution.py:147
  8.0 2.9 %collective-permute-start.5 = (bf16[48,256]{1,0:T(8,128)(2,1)S(1)}, bf16[48,256]{1,0:T(8,128)(2,1)S(1)}, u32[]{:S(2)}, u32[]{:S(2)}) collective-permute-start(bf16[48,256]{1,0:T(8,128)(2,1)S(1)} %shard_map.64.refs_0_), channel_id=1, source_target_pairs={{0,12},{4,8},{8,4},{12,0},{1,13},{5,9},{9,5},{13,1},{2,14},{6,10},... | collective-permute-start | bytes 73736 | tf_op jit(solution)/shard_map/ppermute | solution.py:121
  10.9 1.3 %collective-permute-start.4 = (bf16[48,256]{1,0:T(8,128)(2,1)S(1)}, bf16[48,256]{1,0:T(8,128)(2,1)S(1)}, u32[]{:S(2)}, u32[]{:S(2)}) collective-permute-start(bf16[48,256]{1,0:T(8,128)(2,1)S(1)} %shard_map.64.refs_0_), channel_id=1, source_target_pairs={{0,8},{4,12},{8,0},{12,4},{1,9},{5,13},{9,1},{13,5},{2,10},{6,14},... | collective-permute-start | bytes 73736 | tf_op jit(solution)/shard_map/ppermute | solution.py:121
  13.1 0.6 %shard_map.65 = (f32[256,256]{1,0:T(8,128)S(1)}, f32[256,256]{1,0:T(8,128)S(1)}, f32[256,256]{1,0:T(8,128)S(1)}, f32[256,256]{1,0:T(8,128)S(1)}) custom-call(bf16[3,1024,256]{2,1,0:T(8,128)(2,1)S(1)} %bitcast.5, bf16[256,256]{1,0:T(8,128)(2,1)S(1)} %convert_element_type.27.block_ref.own_ref, bf16[256,256]{1,0:T(8,128)(2,1)S(1)} %collective-permute-done.6.second_ref, ...), custom_call_target="tpu_custom_call" | custom-call | tf_op jit(solution)/shard_map/pallas_call | solution.py:77
  13.7 2.0 %collective-permute-done.4.refs_2_ = bf16[48,256]{1,0:T(8,128)(2,1)S(1)} collective-permute-done((bf16[48,256]{1,0:T(8,128)(2,1)S(1)}, bf16[48,256]{1,0:T(8,128)(2,1)S(1)}, u32[]{:S(2)}, u32[]{:S(2)}) %collective-permute-start.4) | collective-permute-done | bytes 24608 | tf_op jit(solution)/shard_map/ppermute | solution.py:121
  16.0 0.4 %shard_map.66 = (bf16[256,256]{1,0:T(8,128)(2,1)S(1)}, f32[96,256]{1,0:T(8,128)S(1)}) custom-call(s32[1,1]{1,0:T(1,128)S(6)} %copy.8.columns_ref, bf16[2,24,1024]{2,1,0:T(8,128)(2,1)S(1)} %pad_maximum_fusion.bases_ref, bf16[2,24,1024]{2,1,0:T(8,128)(2,1)S(1)} %collective-permute-done.across_ref, bf16[2,24,1024]{2,1,0:T(8,128)(2,1)S(1)} %collective-permute-done.2.other_ref, ...), custom_call_target="tpu_custom_call" | custom-call | flops 100663296 | bytes 98304 | tf_op jit(solution)/shard_map/pallas_call | solution.py:77
  16.5 0.5 %shard_map.67 = (f32[256,256]{1,0:T(8,128)S(1)}, f32[256,256]{1,0:T(8,128)S(1)}, f32[256,256]{1,0:T(8,128)S(1)}, f32[96,256]{1,0:T(8,128)S(1)}, f32[96,256]{1,0:T(8,128)S(1)}) custom-call(s32[1,1]{1,0:T(1,128)S(6)} %copy.8.columns_ref, bf16[2,24,1024]{2,1,0:T(8,128)(2,1)S(1)} %pad_maximum_fusion.bases_ref, ...), custom_call_target="tpu_custom_call" | custom-call | flops 301989888 | bytes 294912 | tf_op jit(solution)/shard_map/pallas_call | solution.py:77
  17.1 0.6 %collective-permute-start.11 = (f32[96,256]{1,0:T(8,128)S(1)}, f32[96,256]{1,0:T(8,128)S(1)}, u32[]{:S(2)}, u32[]{:S(2)}) collective-permute-start(f32[96,256]{1,0:T(8,128)S(1)} %get-tuple-element.45), channel_id=1, source_target_pairs={{0,1},{1,0},{2,3},{3,2},{4,5},{5,4},{6,7},{7,6},{8,9},{9,8},{10,11... | collective-permute-start | bytes 294920 | tf_op jit(solution)/shard_map/ppermute | solution.py:147
  17.9 1.2 %collective-permute-start.10 = (bf16[256,256]{1,0:T(8,128)(2,1)S(1)}, bf16[256,256]{1,0:T(8,128)(2,1)S(1)}, u32[]{:S(2)}, u32[]{:S(2)}) collective-permute-start(bf16[256,256]{1,0:T(8,128)(2,1)S(1)} %add_convert_fusion.2), channel_id=1, source_target_pairs={{0,2},{1,3},{2,0},{3,1},{4,6},{5,7},{6,4},{7,5},{8,10},{9,11},{10,... | collective-permute-start | bytes 393224 | tf_op jit(solution)/shard_map/ppermute | solution.py:147
  19.1 2.1 %collective-permute-start.13 = (bf16[96,256]{1,0:T(8,128)(2,1)S(1)}, bf16[96,256]{1,0:T(8,128)(2,1)S(1)}, u32[]{:S(2)}, u32[]{:S(2)}) collective-permute-start(bf16[96,256]{1,0:T(8,128)(2,1)S(1)} %add_convert_fusion.3.refs_0_), channel_id=1, source_target_pairs={{0,8},{1,13},{2,10},{3,15},{4,12},{5,9},{6,14},{7,11},{8,0},{9,5},... | collective-permute-start | bytes 147464 | tf_op jit(solution)/shard_map/ppermute | solution.py:143
  21.4 2.2 %collective-permute-done.10 = bf16[256,256]{1,0:T(8,128)(2,1)S(1)} collective-permute-done((bf16[256,256]{1,0:T(8,128)(2,1)S(1)}, bf16[256,256]{1,0:T(8,128)(2,1)S(1)}, u32[]{:S(2)}, u32[]{:S(2)}) %collective-permute-start.10) | collective-permute-done | bytes 131104 | tf_op jit(solution)/shard_map/ppermute | solution.py:147
  24.0 1.1 %collective-permute-done.12.refs_1_ = bf16[48,256]{1,0:T(8,128)(2,1)S(1)} collective-permute-done((bf16[48,256]{1,0:T(8,128)(2,1)S(1)}, bf16[48,256]{1,0:T(8,128)(2,1)S(1)}, u32[]{:S(2)}, u32[]{:S(2)}) %collective-permute-start.12) | collective-permute-done | bytes 24608 | tf_op jit(solution)/shard_map/ppermute | solution.py:121
  25.2 0.6 %collective-permute-start.16 = (bf16[2,24,1024]{2,1,0:T(8,128)(2,1)S(1)}, bf16[2,24,1024]{2,1,0:T(8,128)(2,1)S(1)}, u32[]{:S(2)}, u32[]{:S(2)}) collective-permute-start(bf16[2,24,1024]{2,1,0:T(8,128)(2,1)S(1)} %pad_maximum_fusion.2), channel_id=1, source_target_pairs={{0,1},{1,0},{2,3},{3,2},{4,5},{5,4},{6,7},{7,6},{8,9},{9,8},{10,11... | collective-permute-start | bytes 294920 | tf_op jit(solution)/shard_map/ppermute | solution.py:147
  25.8 0.9 %collective-permute-done.16.other_ref = bf16[2,24,1024]{2,1,0:T(8,128)(2,1)S(1)} collective-permute-done((bf16[2,24,1024]{2,1,0:T(8,128)(2,1)S(1)}, bf16[2,24,1024]{2,1,0:T(8,128)(2,1)S(1)}, u32[]{:S(2)}, u32[]{:S(2)}) %collective-permute-start.16) | collective-permute-done | bytes 98336 | tf_op jit(solution)/shard_map/ppermute | solution.py:147
  27.1 1.6 %collective-permute-done.15.first_ref = bf16[256,256]{1,0:T(8,128)(2,1)S(1)} collective-permute-done((bf16[256,256]{1,0:T(8,128)(2,1)S(1)}, bf16[256,256]{1,0:T(8,128)(2,1)S(1)}, u32[]{:S(2)}, u32[]{:S(2)}) %collective-permute-start.15) | collective-permute-done | bytes 131104 | tf_op jit(solution)/shard_map/ppermute | solution.py:121
  29.3 1.1 %collective-permute-done.17 = bf16[256,256]{1,0:T(8,128)(2,1)S(1)} collective-permute-done((bf16[256,256]{1,0:T(8,128)(2,1)S(1)}, bf16[256,256]{1,0:T(8,128)(2,1)S(1)}, u32[]{:S(2)}, u32[]{:S(2)}) %collective-permute-start.17) | collective-permute-done | bytes 131104 | tf_op jit(solution)/shard_map/ppermute | solution.py:147
  30.4 1.2 %collective-permute-start.20 = (bf16[256,256]{1,0:T(8,128)(2,1)S(1)}, bf16[256,256]{1,0:T(8,128)(2,1)S(1)}, u32[]{:S(2)}, u32[]{:S(2)}) collective-permute-start(bf16[256,256]{1,0:T(8,128)(2,1)S(1)} %add_convert_fusion), channel_id=1, source_target_pairs={{0,2},{1,3},{2,0},{3,1},{4,6},{5,7},{6,4},{7,5},{8,10},{9,11},{10,... | collective-permute-start | bytes 393224 | tf_op jit(solution)/shard_map/ppermute | solution.py:147
  32.1 0.5 %collective-permute-start.19 = (f32[128,256]{1,0:T(8,128)S(1)}, f32[128,256]{1,0:T(8,128)S(1)}, u32[]{:S(2)}, u32[]{:S(2)}) collective-permute-start(f32[128,256]{1,0:T(8,128)S(1)} %get-tuple-element.60), channel_id=1, source_target_pairs={{0,1},{1,0},{2,3},{3,2},{4,5},{5,4},{6,7},{7,6},{8,9},{9,8},{10,11... | collective-permute-start | bytes 393224 | tf_op jit(solution)/shard_map/ppermute | solution.py:147
  32.6 3.4 %collective-permute-done.20 = bf16[256,256]{1,0:T(8,128)(2,1)S(1)} collective-permute-done((bf16[256,256]{1,0:T(8,128)(2,1)S(1)}, bf16[256,256]{1,0:T(8,128)(2,1)S(1)}, u32[]{:S(2)}, u32[]{:S(2)}) %collective-permute-start.20) | collective-permute-done | bytes 131104 | tf_op jit(solution)/shard_map/ppermute | solution.py:147
  36.1 0.7 %fusion = f32[256,256]{1,0:T(8,128)} fusion(f32[256,256]{1,0:T(8,128)S(1)} %get-tuple-element.56, f32[128,256]{1,0:T(8,128)S(1)} %collective-permute-done.19, f32[128,256]{1,0:T(8,128)S(1)} %collective-permute-done.18, bf16[256,256]{1,0:T(8,128)(2,1)S(1)} %collective-permute-done.20), kind=kLoop, calls=%fused_computation.1 | loop fusion | flops 262144 | bytes 917504 | tf_op jit(solution)/shard_map/add | solution.py:292
  (43 shorter events, 3.5 us)
Async XLA Ops:
  0.8 6.5 %collective-permute-start = (bf16[2,24,1024]{2,1,0:T(8,128)(2,1)S(1)}, bf16[2,24,1024]{2,1,0:T(8,128)(2,1)S(1)}, u32[]{:S(2)}, u32[]{:S(2)}) collective-permute-start(bf16[2,24,1024]{2,1,0:T(8,128)(2,1)S(1)} %pad_maximum_fusion.bases_ref), channel_id=1, source_target_pairs={{0,2},{1,3},{2,0},{3,1},{4,6},{5,7},{6,4},{7,5},{8,10},{9,11},{10,... | collective-permute-start | bytes 294920 | tf_op jit(solution)/shard_map/ppermute | solution.py:147
  4.8 2.6 %collective-permute-start.1 = (bf16[256,256]{1,0:T(8,128)(2,1)S(1)}, bf16[256,256]{1,0:T(8,128)(2,1)S(1)}, u32[]{:S(2)}, u32[]{:S(2)}) collective-permute-start(bf16[256,256]{1,0:T(8,128)(2,1)S(1)} %convert_element_type.27.block_ref.own_ref), channel_id=1, source_target_pairs={{0,1},{1,0},{2,3},{3,2},{4,5},{5,4},{6,7},{7,6},{8,9},{9,8},{10,11... | collective-permute-start | bytes 393224 | tf_op jit(solution)/shard_map/ppermute | solution.py:147
  4.9 7.3 %collective-permute-start.7 = (bf16[256,256]{1,0:T(8,128)(2,1)S(1)}, bf16[256,256]{1,0:T(8,128)(2,1)S(1)}, u32[]{:S(2)}, u32[]{:S(2)}) collective-permute-start(bf16[256,256]{1,0:T(8,128)(2,1)S(1)} %convert_element_type.27.block_ref.own_ref), channel_id=1, source_target_pairs={{0,4},{4,0},{8,12},{12,8},{1,5},{5,1},{9,13},{13,9},{2,6},{6,2},{1... | collective-permute-start | bytes 393224 | tf_op jit(solution)/shard_map/ppermute | solution.py:121
  6.5 6.5 %collective-permute-start.6 = (bf16[256,256]{1,0:T(8,128)(2,1)S(1)}, bf16[256,256]{1,0:T(8,128)(2,1)S(1)}, u32[]{:S(2)}, u32[]{:S(2)}) collective-permute-start(bf16[256,256]{1,0:T(8,128)(2,1)S(1)} %convert_element_type.27.block_ref.own_ref), channel_id=1, source_target_pairs={{0,1},{1,0},{2,3},{3,2},{4,8},{5,9},{6,10},{7,11},{8,4},{9,5},{10,... | collective-permute-start | bytes 393224 | tf_op jit(solution)/shard_map/ppermute | solution.py:133
  7.4 5.7 %copy-start = (bf16[1,1024,3,256]{3,1,2,0:T(8,128)(2,1)S(1)}, bf16[1,1024,3,256]{3,1,2,0:T(8,128)(2,1)}, u32[]{:S(2)}) copy-start(bf16[1,1024,3,256]{3,1,2,0:T(8,128)(2,1)} %param.10) | copy-start | bytes 4718596
  7.6 8.4 %collective-permute-start.2 = (bf16[2,24,1024]{2,1,0:T(8,128)(2,1)S(1)}, bf16[2,24,1024]{2,1,0:T(8,128)(2,1)S(1)}, u32[]{:S(2)}, u32[]{:S(2)}) collective-permute-start(bf16[2,24,1024]{2,1,0:T(8,128)(2,1)S(1)} %pad_maximum_fusion.1), channel_id=1, source_target_pairs={{0,1},{1,0},{2,3},{3,2},{4,5},{5,4},{6,7},{7,6},{8,9},{9,8},{10,11... | collective-permute-start | bytes 294920 | tf_op jit(solution)/shard_map/ppermute | solution.py:147
  8.0 5.7 %collective-permute-start.5 = (bf16[48,256]{1,0:T(8,128)(2,1)S(1)}, bf16[48,256]{1,0:T(8,128)(2,1)S(1)}, u32[]{:S(2)}, u32[]{:S(2)}) collective-permute-start(bf16[48,256]{1,0:T(8,128)(2,1)S(1)} %shard_map.64.refs_0_), channel_id=1, source_target_pairs={{0,12},{4,8},{8,4},{12,0},{1,13},{5,9},{9,5},{13,1},{2,14},{6,10},... | collective-permute-start | bytes 73736 | tf_op jit(solution)/shard_map/ppermute | solution.py:121
  10.9 4.7 %collective-permute-start.4 = (bf16[48,256]{1,0:T(8,128)(2,1)S(1)}, bf16[48,256]{1,0:T(8,128)(2,1)S(1)}, u32[]{:S(2)}, u32[]{:S(2)}) collective-permute-start(bf16[48,256]{1,0:T(8,128)(2,1)S(1)} %shard_map.64.refs_0_), channel_id=1, source_target_pairs={{0,8},{4,12},{8,0},{12,4},{1,9},{5,13},{9,1},{13,5},{2,10},{6,14},... | collective-permute-start | bytes 73736 | tf_op jit(solution)/shard_map/ppermute | solution.py:121
  12.2 3.8 %collective-permute-start.3 = (bf16[48,256]{1,0:T(8,128)(2,1)S(1)}, bf16[48,256]{1,0:T(8,128)(2,1)S(1)}, u32[]{:S(2)}, u32[]{:S(2)}) collective-permute-start(bf16[48,256]{1,0:T(8,128)(2,1)S(1)} %shard_map.64.refs_0_), channel_id=1, source_target_pairs={{0,4},{4,0},{8,12},{12,8},{1,5},{5,1},{9,13},{13,9},{2,6},{6,2},{1... | collective-permute-start | bytes 73736 | tf_op jit(solution)/shard_map/ppermute | solution.py:121
  16.4 1.4 %collective-permute-start.9 = (bf16[256,256]{1,0:T(8,128)(2,1)S(1)}, bf16[256,256]{1,0:T(8,128)(2,1)S(1)}, u32[]{:S(2)}, u32[]{:S(2)}) collective-permute-start(bf16[256,256]{1,0:T(8,128)(2,1)S(1)} %get-tuple-element.43), channel_id=1, source_target_pairs={{0,1},{1,0},{2,3},{3,2},{4,5},{5,4},{6,7},{7,6},{8,9},{9,8},{10,11... | collective-permute-start | bytes 393224 | tf_op jit(solution)/shard_map/ppermute | solution.py:147
  17.1 2.0 %collective-permute-start.11 = (f32[96,256]{1,0:T(8,128)S(1)}, f32[96,256]{1,0:T(8,128)S(1)}, u32[]{:S(2)}, u32[]{:S(2)}) collective-permute-start(f32[96,256]{1,0:T(8,128)S(1)} %get-tuple-element.45), channel_id=1, source_target_pairs={{0,1},{1,0},{2,3},{3,2},{4,5},{5,4},{6,7},{7,6},{8,9},{9,8},{10,11... | collective-permute-start | bytes 294920 | tf_op jit(solution)/shard_map/ppermute | solution.py:147
  17.6 6.0 %collective-permute-start.8 = (f32[256,256]{1,0:T(8,128)S(1)}, f32[256,256]{1,0:T(8,128)S(1)}, u32[]{:S(2)}, u32[]{:S(2)}) collective-permute-start(f32[256,256]{1,0:T(8,128)S(1)} %get-tuple-element.41), channel_id=1, source_target_pairs={{0,1},{1,0},{2,3},{3,2},{4,5},{5,4},{6,7},{7,6},{8,9},{9,8},{10,11... | collective-permute-start | bytes 786440 | tf_op jit(solution)/shard_map/ppermute | solution.py:147
  17.9 5.8 %collective-permute-start.10 = (bf16[256,256]{1,0:T(8,128)(2,1)S(1)}, bf16[256,256]{1,0:T(8,128)(2,1)S(1)}, u32[]{:S(2)}, u32[]{:S(2)}) collective-permute-start(bf16[256,256]{1,0:T(8,128)(2,1)S(1)} %add_convert_fusion.2), channel_id=1, source_target_pairs={{0,2},{1,3},{2,0},{3,1},{4,6},{5,7},{6,4},{7,5},{8,10},{9,11},{10,... | collective-permute-start | bytes 393224 | tf_op jit(solution)/shard_map/ppermute | solution.py:147
  19.1 6.0 %collective-permute-start.13 = (bf16[96,256]{1,0:T(8,128)(2,1)S(1)}, bf16[96,256]{1,0:T(8,128)(2,1)S(1)}, u32[]{:S(2)}, u32[]{:S(2)}) collective-permute-start(bf16[96,256]{1,0:T(8,128)(2,1)S(1)} %add_convert_fusion.3.refs_0_), channel_id=1, source_target_pairs={{0,8},{1,13},{2,10},{3,15},{4,12},{5,9},{6,14},{7,11},{8,0},{9,5},... | collective-permute-start | bytes 147464 | tf_op jit(solution)/shard_map/ppermute | solution.py:143
  21.2 3.9 %collective-permute-start.12 = (bf16[48,256]{1,0:T(8,128)(2,1)S(1)}, bf16[48,256]{1,0:T(8,128)(2,1)S(1)}, u32[]{:S(2)}, u32[]{:S(2)}) collective-permute-start(bf16[48,256]{1,0:T(8,128)(2,1)S(1)} %slice.21), channel_id=1, source_target_pairs={{0,4},{4,0},{8,12},{12,8},{1,5},{5,1},{9,13},{13,9},{2,6},{6,2},{1... | collective-permute-start | bytes 73736 | tf_op jit(solution)/shard_map/ppermute | solution.py:121
  23.7 5.0 %collective-permute-start.15 = (bf16[256,256]{1,0:T(8,128)(2,1)S(1)}, bf16[256,256]{1,0:T(8,128)(2,1)S(1)}, u32[]{:S(2)}, u32[]{:S(2)}) collective-permute-start(bf16[256,256]{1,0:T(8,128)(2,1)S(1)} %add_convert_fusion.1.own_ref), channel_id=1, source_target_pairs={{0,4},{4,0},{8,12},{12,8},{1,5},{5,1},{9,13},{13,9},{2,6},{6,2},{1... | collective-permute-start | bytes 393224 | tf_op jit(solution)/shard_map/ppermute | solution.py:121
  25.1 2.0 %collective-permute-start.14 = (bf16[256,256]{1,0:T(8,128)(2,1)S(1)}, bf16[256,256]{1,0:T(8,128)(2,1)S(1)}, u32[]{:S(2)}, u32[]{:S(2)}) collective-permute-start(bf16[256,256]{1,0:T(8,128)(2,1)S(1)} %add_convert_fusion.1.own_ref), channel_id=1, source_target_pairs={{0,1},{1,0},{2,3},{3,2},{4,8},{5,9},{6,10},{7,11},{8,4},{9,5},{10,... | collective-permute-start | bytes 393224 | tf_op jit(solution)/shard_map/ppermute | solution.py:133
  25.2 1.5 %collective-permute-start.16 = (bf16[2,24,1024]{2,1,0:T(8,128)(2,1)S(1)}, bf16[2,24,1024]{2,1,0:T(8,128)(2,1)S(1)}, u32[]{:S(2)}, u32[]{:S(2)}) collective-permute-start(bf16[2,24,1024]{2,1,0:T(8,128)(2,1)S(1)} %pad_maximum_fusion.2), channel_id=1, source_target_pairs={{0,1},{1,0},{2,3},{3,2},{4,5},{5,4},{6,7},{7,6},{8,9},{9,8},{10,11... | collective-permute-start | bytes 294920 | tf_op jit(solution)/shard_map/ppermute | solution.py:147
  29.0 1.4 %collective-permute-start.17 = (bf16[256,256]{1,0:T(8,128)(2,1)S(1)}, bf16[256,256]{1,0:T(8,128)(2,1)S(1)}, u32[]{:S(2)}, u32[]{:S(2)}) collective-permute-start(bf16[256,256]{1,0:T(8,128)(2,1)S(1)} %shard_map.70), channel_id=1, source_target_pairs={{0,1},{1,0},{2,3},{3,2},{4,5},{5,4},{6,7},{7,6},{8,9},{9,8},{10,11... | collective-permute-start | bytes 393224 | tf_op jit(solution)/shard_map/ppermute | solution.py:147
  30.4 5.6 %collective-permute-start.20 = (bf16[256,256]{1,0:T(8,128)(2,1)S(1)}, bf16[256,256]{1,0:T(8,128)(2,1)S(1)}, u32[]{:S(2)}, u32[]{:S(2)}) collective-permute-start(bf16[256,256]{1,0:T(8,128)(2,1)S(1)} %add_convert_fusion), channel_id=1, source_target_pairs={{0,2},{1,3},{2,0},{3,1},{4,6},{5,7},{6,4},{7,5},{8,10},{9,11},{10,... | collective-permute-start | bytes 393224 | tf_op jit(solution)/shard_map/ppermute | solution.py:147
  32.0 4.0 %collective-permute-start.18 = (f32[128,256]{1,0:T(8,128)S(1)}, f32[128,256]{1,0:T(8,128)S(1)}, u32[]{:S(2)}, u32[]{:S(2)}) collective-permute-start(f32[128,256]{1,0:T(8,128)S(1)} %get-tuple-element.59), channel_id=1, source_target_pairs={{0,1},{1,0},{2,3},{3,2},{4,5},{5,4},{6,7},{7,6},{8,9},{9,8},{10,11... | collective-permute-start | bytes 393224 | tf_op jit(solution)/shard_map/ppermute | solution.py:147
  32.1 3.9 %collective-permute-start.19 = (f32[128,256]{1,0:T(8,128)S(1)}, f32[128,256]{1,0:T(8,128)S(1)}, u32[]{:S(2)}, u32[]{:S(2)}) collective-permute-start(f32[128,256]{1,0:T(8,128)S(1)} %get-tuple-element.60), channel_id=1, source_target_pairs={{0,1},{1,0},{2,3},{3,2},{4,5},{5,4},{6,7},{7,6},{8,9},{9,8},{10,11... | collective-permute-start | bytes 393224 | tf_op jit(solution)/shard_map/ppermute | solution.py:147

commit v17 on v15

--- a/solution.py
+++ b/solution.py
@@ -84,6 +84,15 @@
             flops=flops, bytes_accessed=flops // 1024, transcendentals=0
         ),
     )(*operands)
+
+
+def round_kernel(probes_ref, out_ref):
+    out_ref[...] = probes_ref[...].astype(out_ref.dtype)
+
+
+def join_kernel(right_ref, left_ref, out_ref):
+    out_ref[0] = right_ref[0, 0]
+    out_ref[1] = left_ref[0, 0]
 
 
 def stacked(pieces):
@@ -244,10 +253,10 @@
     part = ((rows, probe_count), F32)
     ranks = 4 * rank_part
 
-    bases = jnp.stack([right_bases[0, 0], left_bases[0, 0]])
-    bases, probes = lax.optimization_barrier((bases, probes))
+    (block,) = kernel_call(round_kernel, [(probes.shape, BF)], (probes,), 8 * flops)
+    block, right, left = lax.optimization_barrier((block, right_bases, left_bases))
+    (bases,) = kernel_call(join_kernel, [((2, *right_bases.shape[2:]), BF)], (right, left))
     across = list_swap(bases, 2)
-    block = probes.astype(BF)
     beside = [block, middle_swap(block), tile_swap(block, 1)]
     (own,) = kernel_call(
         coefficient_kernel,

time: 37.2 us -> 37 us (level)
  other arithmetic: 2.69 us -> 0.89 us
  local copies, waits for them, and re-layouts: 0.05 us -> 1.01 us
  waiting for transfers between devices: 13.2 us -> 13.6 us
    convert_element_type x1 -> x0, other arithmetic: 0.96 us -> none  [one_slot(): block = probes.astype(BF)]
    unnamed x2 -> x8, local copies, waits for them, and re-layouts: 0.01 us -> 0.97 us
    another operation x1 -> x0, other arithmetic: 0.83 us -> none  [one_slot(): bases = jnp.stack([right_bases[0, 0], left_bases[0, 0]])]
    ppermute x6, waiting for transfers between devices: 5.09 us -> 5.69 us  [tile_swap(): lax.ppermute(block, 'tile', [(i, i ^ turn) for i in range(lax.axis_size('...]
    pallas_call x8 -> x10, Pallas kernels: 2.95 us -> 2.98 us  [kernel_call(): pl.pallas_call(kernel, out_shape=tuple((jax.ShapeDtypeStruct(shape, kind)...]
  transfers between devices with their start and end apart: 21 -> 21, of which waited for: 9 -> 9; matrix products, arithmetic and copies ran while one was open for 3% -> 0% of each run, Pallas kernels for 6% -> 6%
where the time goes in v17:
time: 37 us; the launch traced here: 36.8 us
  starting transfers between devices  16.9 us (46%)
  waiting for transfers between devices  13.6 us (37%)
  Pallas kernels  2.98 us (8%)
  between operations  1.54 us (4%)
  local copies, waits for them, and re-layouts  1.01 us (3%)
  other arithmetic  0.89 us (2%)
    ppermute x12, starting transfers between devices, list_swap(): lax.ppermute(block, 'list', [(i, i ^ bit) for i in range(lax.axis_size('l...  8.09 us
    ppermute x12, waiting for transfers between devices, list_swap(): lax.ppermute(block, 'list', [(i, i ^ bit) for i in range(lax.axis_size('l...  7.85 us
    ppermute x6, starting transfers between devices, tile_swap(): lax.ppermute(block, 'tile', [(i, i ^ turn) for i in range(lax.axis_size('...  6.4 us
    ppermute x6, waiting for transfers between devices, tile_swap(): lax.ppermute(block, 'tile', [(i, i ^ turn) for i in range(lax.axis_size('...  5.69 us
    pallas_call x10, Pallas kernels, kernel_call(): pl.pallas_call(kernel, out_shape=tuple((jax.ShapeDtypeStruct(shape, kind)...  2.98 us
    ppermute x1, starting transfers between devices, far_swap(): return lax.ppermute(block, ('tile', 'list'), route)  2.09 us
    unnamed x8, local copies, waits for them, and re-layouts  0.97 us
    add x1, other arithmetic, one_slot(): return keep + list_swap_in_pieces(send, 1, 2) + crossed  0.75 us
  transfers between devices with their start and end apart: 21, of which 9 were waited for; matrix products, arithmetic and copies ran while one was open for 0% of the time, Pallas kernels for 6%

profile of v17, /device:TPU:0, one launch (start us, length us, event | category | flops | bytes accessed | tf_op | source)
XLA Modules:
  0.0 36.8 jit_solution(9469860742824440337)
XLA Ops:
  0.0 1.0 %copy-done.3 = f32[256,256]{1,0:T(8,128)S(1)} copy-done((f32[256,256]{1,0:T(8,128)S(1)}, f32[256,256]{1,0:T(8,128)}, u32[]{:S(2)}) %copy-start.3) | copy-done | bytes 262168
  1.0 3.0 %collective-permute-start = (bf16[2,24,1024]{2,1,0:T(8,128)(2,1)S(1)}, bf16[2,24,1024]{2,1,0:T(8,128)(2,1)S(1)}, u32[]{:S(2)}, u32[]{:S(2)}) collective-permute-start(bf16[2,24,1024]{2,1,0:T(8,128)(2,1)S(1)} %shard_map.65.bases_ref), channel_id=1, source_target_pairs={{0,2},{1,3},{2,0},{3,1},{4,6},{5,7},{6,4},{7,5},{8,10},{9,11},{10,... | collective-permute-start | bytes 294920 | tf_op jit(solution)/shard_map/ppermute | solution.py:156
  4.0 1.6 %collective-permute-start.7 = (bf16[256,256]{1,0:T(8,128)(2,1)S(1)}, bf16[256,256]{1,0:T(8,128)(2,1)S(1)}, u32[]{:S(2)}, u32[]{:S(2)}) collective-permute-start(bf16[256,256]{1,0:T(8,128)(2,1)S(1)} %shard_map.64.block_ref.own_ref), channel_id=1, source_target_pairs={{0,4},{4,0},{8,12},{12,8},{1,5},{5,1},{9,13},{13,9},{2,6},{6,2},{1... | collective-permute-start | bytes 393224 | tf_op jit(solution)/shard_map/ppermute | solution.py:130
  7.1 4.0 %collective-permute-start.5 = (bf16[48,256]{1,0:T(8,128)(2,1)S(1)}, bf16[48,256]{1,0:T(8,128)(2,1)S(1)}, u32[]{:S(2)}, u32[]{:S(2)}) collective-permute-start(bf16[48,256]{1,0:T(8,128)(2,1)S(1)} %shard_map.66.refs_0_), channel_id=1, source_target_pairs={{0,12},{4,8},{8,4},{12,0},{1,13},{5,9},{9,5},{13,1},{2,14},{6,10},... | collective-permute-start | bytes 73736 | tf_op jit(solution)/shard_map/ppermute | solution.py:130
  11.3 0.5 %collective-permute-start.3 = (bf16[48,256]{1,0:T(8,128)(2,1)S(1)}, bf16[48,256]{1,0:T(8,128)(2,1)S(1)}, u32[]{:S(2)}, u32[]{:S(2)}) collective-permute-start(bf16[48,256]{1,0:T(8,128)(2,1)S(1)} %shard_map.66.refs_0_), channel_id=1, source_target_pairs={{0,4},{4,0},{8,12},{12,8},{1,5},{5,1},{9,13},{13,9},{2,6},{6,2},{1... | collective-permute-start | bytes 73736 | tf_op jit(solution)/shard_map/ppermute | solution.py:130
  12.4 0.6 %shard_map.67 = (f32[256,256]{1,0:T(8,128)S(1)}, f32[256,256]{1,0:T(8,128)S(1)}, f32[256,256]{1,0:T(8,128)S(1)}, f32[256,256]{1,0:T(8,128)S(1)}) custom-call(bf16[3,1024,256]{2,1,0:T(8,128)(2,1)S(1)} %bitcast.3, bf16[256,256]{1,0:T(8,128)(2,1)S(1)} %shard_map.64.block_ref.own_ref, bf16[256,256]{1,0:T(8,128)(2,1)S(1)} %collective-permute-done.6.second_ref, ...), custom_call_target="tpu_custom_call" | custom-call | tf_op jit(solution)/shard_map/pallas_call | solution.py:77
  13.0 2.8 %collective-permute-done.4.refs_2_ = bf16[48,256]{1,0:T(8,128)(2,1)S(1)} collective-permute-done((bf16[48,256]{1,0:T(8,128)(2,1)S(1)}, bf16[48,256]{1,0:T(8,128)(2,1)S(1)}, u32[]{:S(2)}, u32[]{:S(2)}) %collective-permute-start.4) | collective-permute-done | bytes 24608 | tf_op jit(solution)/shard_map/ppermute | solution.py:130
  15.8 0.4 %shard_map.68 = (f32[256,256]{1,0:T(8,128)S(1)}, f32[96,256]{1,0:T(8,128)S(1)}) custom-call(s32[1,1]{1,0:T(1,128)S(6)} %copy.8.columns_ref, bf16[2,24,1024]{2,1,0:T(8,128)(2,1)S(1)} %shard_map.65.bases_ref, bf16[2,24,1024]{2,1,0:T(8,128)(2,1)S(1)} %collective-permute-done.across_ref, bf16[2,24,1024]{2,1,0:T(8,128)(2,1)S(1)} %collective-permute-done.2.other_ref, ...), custom_call_target="tpu_custom_call" | custom-call | flops 100663296 | bytes 98304 | tf_op jit(solution)/shard_map/pallas_call | solution.py:77
  16.3 0.5 %shard_map.69 = (f32[256,256]{1,0:T(8,128)S(1)}, f32[256,256]{1,0:T(8,128)S(1)}, f32[256,256]{1,0:T(8,128)S(1)}, f32[96,256]{1,0:T(8,128)S(1)}, f32[96,256]{1,0:T(8,128)S(1)}) custom-call(s32[1,1]{1,0:T(1,128)S(6)} %copy.8.columns_ref, bf16[2,24,1024]{2,1,0:T(8,128)(2,1)S(1)} %shard_map.65.bases_ref, ...), custom_call_target="tpu_custom_call" | custom-call | flops 301989888 | bytes 294912 | tf_op jit(solution)/shard_map/pallas_call | solution.py:77
  16.9 0.6 %collective-permute-start.11 = (f32[96,256]{1,0:T(8,128)S(1)}, f32[96,256]{1,0:T(8,128)S(1)}, u32[]{:S(2)}, u32[]{:S(2)}) collective-permute-start(f32[96,256]{1,0:T(8,128)S(1)} %get-tuple-element.47), channel_id=1, source_target_pairs={{0,1},{1,0},{2,3},{3,2},{4,5},{5,4},{6,7},{7,6},{8,9},{9,8},{10,11... | collective-permute-start | bytes 294920 | tf_op jit(solution)/shard_map/ppermute | solution.py:156
  17.9 1.6 %collective-permute-start.10 = (bf16[256,256]{1,0:T(8,128)(2,1)S(1)}, bf16[256,256]{1,0:T(8,128)(2,1)S(1)}, u32[]{:S(2)}, u32[]{:S(2)}) collective-permute-start(bf16[256,256]{1,0:T(8,128)(2,1)S(1)} %add_convert_fusion.2), channel_id=1, source_target_pairs={{0,2},{1,3},{2,0},{3,1},{4,6},{5,7},{6,4},{7,5},{8,10},{9,11},{10,... | collective-permute-start | bytes 393224 | tf_op jit(solution)/shard_map/ppermute | solution.py:156
  19.5 2.1 %collective-permute-start.13 = (bf16[96,256]{1,0:T(8,128)(2,1)S(1)}, bf16[96,256]{1,0:T(8,128)(2,1)S(1)}, u32[]{:S(2)}, u32[]{:S(2)}) collective-permute-start(bf16[96,256]{1,0:T(8,128)(2,1)S(1)} %add_convert_fusion.3.refs_0_), channel_id=1, source_target_pairs={{0,8},{1,13},{2,10},{3,15},{4,12},{5,9},{6,14},{7,11},{8,0},{9,5},... | collective-permute-start | bytes 147464 | tf_op jit(solution)/shard_map/ppermute | solution.py:152
  21.6 1.9 %collective-permute-done.10 = bf16[256,256]{1,0:T(8,128)(2,1)S(1)} collective-permute-done((bf16[256,256]{1,0:T(8,128)(2,1)S(1)}, bf16[256,256]{1,0:T(8,128)(2,1)S(1)}, u32[]{:S(2)}, u32[]{:S(2)}) %collective-permute-start.10) | collective-permute-done | bytes 131104 | tf_op jit(solution)/shard_map/ppermute | solution.py:156
  23.7 1.7 %collective-permute-done.12.refs_1_ = bf16[48,256]{1,0:T(8,128)(2,1)S(1)} collective-permute-done((bf16[48,256]{1,0:T(8,128)(2,1)S(1)}, bf16[48,256]{1,0:T(8,128)(2,1)S(1)}, u32[]{:S(2)}, u32[]{:S(2)}) %collective-permute-start.12) | collective-permute-done | bytes 24608 | tf_op jit(solution)/shard_map/ppermute | solution.py:130
  25.5 0.6 %collective-permute-start.16 = (bf16[2,24,1024]{2,1,0:T(8,128)(2,1)S(1)}, bf16[2,24,1024]{2,1,0:T(8,128)(2,1)S(1)}, u32[]{:S(2)}, u32[]{:S(2)}) collective-permute-start(bf16[2,24,1024]{2,1,0:T(8,128)(2,1)S(1)} %pad_maximum_fusion.1), channel_id=1, source_target_pairs={{0,1},{1,0},{2,3},{3,2},{4,5},{5,4},{6,7},{7,6},{8,9},{9,8},{10,11... | collective-permute-start | bytes 294920 | tf_op jit(solution)/shard_map/ppermute | solution.py:156
  26.1 0.9 %collective-permute-done.16.other_ref = bf16[2,24,1024]{2,1,0:T(8,128)(2,1)S(1)} collective-permute-done((bf16[2,24,1024]{2,1,0:T(8,128)(2,1)S(1)}, bf16[2,24,1024]{2,1,0:T(8,128)(2,1)S(1)}, u32[]{:S(2)}, u32[]{:S(2)}) %collective-permute-start.16) | collective-permute-done | bytes 98336 | tf_op jit(solution)/shard_map/ppermute | solution.py:156
  27.0 0.4 shard_map.70
  27.4 1.2 %collective-permute-done.15.first_ref = bf16[256,256]{1,0:T(8,128)(2,1)S(1)} collective-permute-done((bf16[256,256]{1,0:T(8,128)(2,1)S(1)}, bf16[256,256]{1,0:T(8,128)(2,1)S(1)}, u32[]{:S(2)}, u32[]{:S(2)}) %collective-permute-start.15) | collective-permute-done | bytes 131104 | tf_op jit(solution)/shard_map/ppermute | solution.py:130
  29.2 1.2 %collective-permute-done.17 = f32[256,256]{1,0:T(8,128)S(1)} collective-permute-done((f32[256,256]{1,0:T(8,128)S(1)}, f32[256,256]{1,0:T(8,128)S(1)}, u32[]{:S(2)}, u32[]{:S(2)}) %collective-permute-start.17) | collective-permute-done | bytes 262176 | tf_op jit(solution)/shard_map/ppermute | solution.py:156
  30.5 1.6 %collective-permute-start.20 = (bf16[256,256]{1,0:T(8,128)(2,1)S(1)}, bf16[256,256]{1,0:T(8,128)(2,1)S(1)}, u32[]{:S(2)}, u32[]{:S(2)}) collective-permute-start(bf16[256,256]{1,0:T(8,128)(2,1)S(1)} %add_convert_fusion), channel_id=1, source_target_pairs={{0,2},{1,3},{2,0},{3,1},{4,6},{5,7},{6,4},{7,5},{8,10},{9,11},{10,... | collective-permute-start | bytes 393224 | tf_op jit(solution)/shard_map/ppermute | solution.py:156
  32.0 0.4 shard_map.73
  32.5 0.5 %collective-permute-start.19 = (f32[128,256]{1,0:T(8,128)S(1)}, f32[128,256]{1,0:T(8,128)S(1)}, u32[]{:S(2)}, u32[]{:S(2)}) collective-permute-start(f32[128,256]{1,0:T(8,128)S(1)} %get-tuple-element.62), channel_id=1, source_target_pairs={{0,1},{1,0},{2,3},{3,2},{4,5},{5,4},{6,7},{7,6},{8,9},{9,8},{10,11... | collective-permute-start | bytes 393224 | tf_op jit(solution)/shard_map/ppermute | solution.py:156
  33.0 3.1 %collective-permute-done.20 = bf16[256,256]{1,0:T(8,128)(2,1)S(1)} collective-permute-done((bf16[256,256]{1,0:T(8,128)(2,1)S(1)}, bf16[256,256]{1,0:T(8,128)(2,1)S(1)}, u32[]{:S(2)}, u32[]{:S(2)}) %collective-permute-start.20) | collective-permute-done | bytes 131104 | tf_op jit(solution)/shard_map/ppermute | solution.py:156
  36.1 0.7 %fusion = f32[256,256]{1,0:T(8,128)} fusion(f32[256,256]{1,0:T(8,128)S(1)} %get-tuple-element.58, f32[128,256]{1,0:T(8,128)S(1)} %collective-permute-done.19, f32[128,256]{1,0:T(8,128)S(1)} %collective-permute-done.18, bf16[256,256]{1,0:T(8,128)(2,1)S(1)} %collective-permute-done.20), kind=kLoop, calls=%fused_computation.1 | loop fusion | flops 262144 | bytes 917504 | tf_op jit(solution)/shard_map/add | solution.py:302
  (49 shorter events, 2.6 us)
Async XLA Ops:
  0.0 1.0 %copy-start.2 = (bf16[1,1,24,1024]{3,2,1,0:T(8,128)(2,1)S(1)}, bf16[1,1,24,1024]{3,2,1,0:T(8,128)(2,1)}, u32[]{:S(2)}) copy-start(bf16[1,1,24,1024]{3,2,1,0:T(8,128)(2,1)} %left_ref) | copy-start | bytes 147460
  0.0 1.0 %copy-start.1 = (bf16[1,1,24,1024]{3,2,1,0:T(8,128)(2,1)S(1)}, bf16[1,1,24,1024]{3,2,1,0:T(8,128)(2,1)}, u32[]{:S(2)}) copy-start(bf16[1,1,24,1024]{3,2,1,0:T(8,128)(2,1)} %right_ref) | copy-start | bytes 147460
  1.0 5.8 %collective-permute-start = (bf16[2,24,1024]{2,1,0:T(8,128)(2,1)S(1)}, bf16[2,24,1024]{2,1,0:T(8,128)(2,1)S(1)}, u32[]{:S(2)}, u32[]{:S(2)}) collective-permute-start(bf16[2,24,1024]{2,1,0:T(8,128)(2,1)S(1)} %shard_map.65.bases_ref), channel_id=1, source_target_pairs={{0,2},{1,3},{2,0},{3,1},{4,6},{5,7},{6,4},{7,5},{8,10},{9,11},{10,... | collective-permute-start | bytes 294920 | tf_op jit(solution)/shard_map/ppermute | solution.py:156
  4.0 2.8 %collective-permute-start.1 = (bf16[256,256]{1,0:T(8,128)(2,1)S(1)}, bf16[256,256]{1,0:T(8,128)(2,1)S(1)}, u32[]{:S(2)}, u32[]{:S(2)}) collective-permute-start(bf16[256,256]{1,0:T(8,128)(2,1)S(1)} %shard_map.64.block_ref.own_ref), channel_id=1, source_target_pairs={{0,1},{1,0},{2,3},{3,2},{4,5},{5,4},{6,7},{7,6},{8,9},{9,8},{10,11... | collective-permute-start | bytes 393224 | tf_op jit(solution)/shard_map/ppermute | solution.py:156
  4.0 7.2 %collective-permute-start.7 = (bf16[256,256]{1,0:T(8,128)(2,1)S(1)}, bf16[256,256]{1,0:T(8,128)(2,1)S(1)}, u32[]{:S(2)}, u32[]{:S(2)}) collective-permute-start(bf16[256,256]{1,0:T(8,128)(2,1)S(1)} %shard_map.64.block_ref.own_ref), channel_id=1, source_target_pairs={{0,4},{4,0},{8,12},{12,8},{1,5},{5,1},{9,13},{13,9},{2,6},{6,2},{1... | collective-permute-start | bytes 393224 | tf_op jit(solution)/shard_map/ppermute | solution.py:130
  5.6 6.8 %collective-permute-start.6 = (bf16[256,256]{1,0:T(8,128)(2,1)S(1)}, bf16[256,256]{1,0:T(8,128)(2,1)S(1)}, u32[]{:S(2)}, u32[]{:S(2)}) collective-permute-start(bf16[256,256]{1,0:T(8,128)(2,1)S(1)} %shard_map.64.block_ref.own_ref), channel_id=1, source_target_pairs={{0,1},{1,0},{2,3},{3,2},{4,8},{5,9},{6,10},{7,11},{8,4},{9,5},{10,... | collective-permute-start | bytes 393224 | tf_op jit(solution)/shard_map/ppermute | solution.py:142
  6.8 5.6 %copy-start = (bf16[1,1024,3,256]{3,1,2,0:T(8,128)(2,1)S(1)}, bf16[1,1024,3,256]{3,1,2,0:T(8,128)(2,1)}, u32[]{:S(2)}) copy-start(bf16[1,1024,3,256]{3,1,2,0:T(8,128)(2,1)} %param.10) | copy-start | bytes 4718596
  7.0 8.8 %collective-permute-start.2 = (bf16[2,24,1024]{2,1,0:T(8,128)(2,1)S(1)}, bf16[2,24,1024]{2,1,0:T(8,128)(2,1)S(1)}, u32[]{:S(2)}, u32[]{:S(2)}) collective-permute-start(bf16[2,24,1024]{2,1,0:T(8,128)(2,1)S(1)} %pad_maximum_fusion), channel_id=1, source_target_pairs={{0,1},{1,0},{2,3},{3,2},{4,5},{5,4},{6,7},{7,6},{8,9},{9,8},{10,11... | collective-permute-start | bytes 294920 | tf_op jit(solution)/shard_map/ppermute | solution.py:156
  7.1 5.9 %collective-permute-start.5 = (bf16[48,256]{1,0:T(8,128)(2,1)S(1)}, bf16[48,256]{1,0:T(8,128)(2,1)S(1)}, u32[]{:S(2)}, u32[]{:S(2)}) collective-permute-start(bf16[48,256]{1,0:T(8,128)(2,1)S(1)} %shard_map.66.refs_0_), channel_id=1, source_target_pairs={{0,12},{4,8},{8,4},{12,0},{1,13},{5,9},{9,5},{13,1},{2,14},{6,10},... | collective-permute-start | bytes 73736 | tf_op jit(solution)/shard_map/ppermute | solution.py:130
  11.1 4.7 %collective-permute-start.4 = (bf16[48,256]{1,0:T(8,128)(2,1)S(1)}, bf16[48,256]{1,0:T(8,128)(2,1)S(1)}, u32[]{:S(2)}, u32[]{:S(2)}) collective-permute-start(bf16[48,256]{1,0:T(8,128)(2,1)S(1)} %shard_map.66.refs_0_), channel_id=1, source_target_pairs={{0,8},{4,12},{8,0},{12,4},{1,9},{5,13},{9,1},{13,5},{2,10},{6,14},... | collective-permute-start | bytes 73736 | tf_op jit(solution)/shard_map/ppermute | solution.py:130
  11.3 4.6 %collective-permute-start.3 = (bf16[48,256]{1,0:T(8,128)(2,1)S(1)}, bf16[48,256]{1,0:T(8,128)(2,1)S(1)}, u32[]{:S(2)}, u32[]{:S(2)}) collective-permute-start(bf16[48,256]{1,0:T(8,128)(2,1)S(1)} %shard_map.66.refs_0_), channel_id=1, source_target_pairs={{0,4},{4,0},{8,12},{12,8},{1,5},{5,1},{9,13},{13,9},{2,6},{6,2},{1... | collective-permute-start | bytes 73736 | tf_op jit(solution)/shard_map/ppermute | solution.py:130
  16.2 1.6 %collective-permute-start.9 = (f32[256,256]{1,0:T(8,128)S(1)}, f32[256,256]{1,0:T(8,128)S(1)}, u32[]{:S(2)}, u32[]{:S(2)}) collective-permute-start(f32[256,256]{1,0:T(8,128)S(1)} %get-tuple-element.45), channel_id=1, source_target_pairs={{0,1},{1,0},{2,3},{3,2},{4,5},{5,4},{6,7},{7,6},{8,9},{9,8},{10,11... | collective-permute-start | bytes 786440 | tf_op jit(solution)/shard_map/ppermute | solution.py:156
  16.9 2.6 %collective-permute-start.11 = (f32[96,256]{1,0:T(8,128)S(1)}, f32[96,256]{1,0:T(8,128)S(1)}, u32[]{:S(2)}, u32[]{:S(2)}) collective-permute-start(f32[96,256]{1,0:T(8,128)S(1)} %get-tuple-element.47), channel_id=1, source_target_pairs={{0,1},{1,0},{2,3},{3,2},{4,5},{5,4},{6,7},{7,6},{8,9},{9,8},{10,11... | collective-permute-start | bytes 294920 | tf_op jit(solution)/shard_map/ppermute | solution.py:156
  17.4 4.1 %collective-permute-start.8 = (f32[256,256]{1,0:T(8,128)S(1)}, f32[256,256]{1,0:T(8,128)S(1)}, u32[]{:S(2)}, u32[]{:S(2)}) collective-permute-start(f32[256,256]{1,0:T(8,128)S(1)} %get-tuple-element.43), channel_id=1, source_target_pairs={{0,1},{1,0},{2,3},{3,2},{4,5},{5,4},{6,7},{7,6},{8,9},{9,8},{10,11... | collective-permute-start | bytes 786440 | tf_op jit(solution)/shard_map/ppermute | solution.py:156
  17.9 5.6 %collective-permute-start.10 = (bf16[256,256]{1,0:T(8,128)(2,1)S(1)}, bf16[256,256]{1,0:T(8,128)(2,1)S(1)}, u32[]{:S(2)}, u32[]{:S(2)}) collective-permute-start(bf16[256,256]{1,0:T(8,128)(2,1)S(1)} %add_convert_fusion.2), channel_id=1, source_target_pairs={{0,2},{1,3},{2,0},{3,1},{4,6},{5,7},{6,4},{7,5},{8,10},{9,11},{10,... | collective-permute-start | bytes 393224 | tf_op jit(solution)/shard_map/ppermute | solution.py:156
  19.5 5.9 %collective-permute-start.13 = (bf16[96,256]{1,0:T(8,128)(2,1)S(1)}, bf16[96,256]{1,0:T(8,128)(2,1)S(1)}, u32[]{:S(2)}, u32[]{:S(2)}) collective-permute-start(bf16[96,256]{1,0:T(8,128)(2,1)S(1)} %add_convert_fusion.3.refs_0_), channel_id=1, source_target_pairs={{0,8},{1,13},{2,10},{3,15},{4,12},{5,9},{6,14},{7,11},{8,0},{9,5},... | collective-permute-start | bytes 147464 | tf_op jit(solution)/shard_map/ppermute | solution.py:152
  21.6 3.8 %collective-permute-start.12 = (bf16[48,256]{1,0:T(8,128)(2,1)S(1)}, bf16[48,256]{1,0:T(8,128)(2,1)S(1)}, u32[]{:S(2)}, u32[]{:S(2)}) collective-permute-start(bf16[48,256]{1,0:T(8,128)(2,1)S(1)} %slice.22), channel_id=1, source_target_pairs={{0,4},{4,0},{8,12},{12,8},{1,5},{5,1},{9,13},{13,9},{2,6},{6,2},{1... | collective-permute-start | bytes 73736 | tf_op jit(solution)/shard_map/ppermute | solution.py:130
  23.5 5.0 %collective-permute-start.15 = (bf16[256,256]{1,0:T(8,128)(2,1)S(1)}, bf16[256,256]{1,0:T(8,128)(2,1)S(1)}, u32[]{:S(2)}, u32[]{:S(2)}) collective-permute-start(bf16[256,256]{1,0:T(8,128)(2,1)S(1)} %add_convert_fusion.1.own_ref), channel_id=1, source_target_pairs={{0,4},{4,0},{8,12},{12,8},{1,5},{5,1},{9,13},{13,9},{2,6},{6,2},{1... | collective-permute-start | bytes 393224 | tf_op jit(solution)/shard_map/ppermute | solution.py:130
  25.4 2.0 %collective-permute-start.14 = (bf16[256,256]{1,0:T(8,128)(2,1)S(1)}, bf16[256,256]{1,0:T(8,128)(2,1)S(1)}, u32[]{:S(2)}, u32[]{:S(2)}) collective-permute-start(bf16[256,256]{1,0:T(8,128)(2,1)S(1)} %add_convert_fusion.1.own_ref), channel_id=1, source_target_pairs={{0,1},{1,0},{2,3},{3,2},{4,8},{5,9},{6,10},{7,11},{8,4},{9,5},{10,... | collective-permute-start | bytes 393224 | tf_op jit(solution)/shard_map/ppermute | solution.py:142
  25.5 1.5 %collective-permute-start.16 = (bf16[2,24,1024]{2,1,0:T(8,128)(2,1)S(1)}, bf16[2,24,1024]{2,1,0:T(8,128)(2,1)S(1)}, u32[]{:S(2)}, u32[]{:S(2)}) collective-permute-start(bf16[2,24,1024]{2,1,0:T(8,128)(2,1)S(1)} %pad_maximum_fusion.1), channel_id=1, source_target_pairs={{0,1},{1,0},{2,3},{3,2},{4,5},{5,4},{6,7},{7,6},{8,9},{9,8},{10,11... | collective-permute-start | bytes 294920 | tf_op jit(solution)/shard_map/ppermute | solution.py:156
  28.8 1.6 %collective-permute-start.17 = (f32[256,256]{1,0:T(8,128)S(1)}, f32[256,256]{1,0:T(8,128)S(1)}, u32[]{:S(2)}, u32[]{:S(2)}) collective-permute-start(f32[256,256]{1,0:T(8,128)S(1)} %shard_map.72), channel_id=1, source_target_pairs={{0,1},{1,0},{2,3},{3,2},{4,5},{5,4},{6,7},{7,6},{8,9},{9,8},{10,11... | collective-permute-start | bytes 786440 | tf_op jit(solution)/shard_map/ppermute | solution.py:156
  30.5 5.6 %collective-permute-start.20 = (bf16[256,256]{1,0:T(8,128)(2,1)S(1)}, bf16[256,256]{1,0:T(8,128)(2,1)S(1)}, u32[]{:S(2)}, u32[]{:S(2)}) collective-permute-start(bf16[256,256]{1,0:T(8,128)(2,1)S(1)} %add_convert_fusion), channel_id=1, source_target_pairs={{0,2},{1,3},{2,0},{3,1},{4,6},{5,7},{6,4},{7,5},{8,10},{9,11},{10,... | collective-permute-start | bytes 393224 | tf_op jit(solution)/shard_map/ppermute | solution.py:156
  32.4 3.6 %collective-permute-start.18 = (f32[128,256]{1,0:T(8,128)S(1)}, f32[128,256]{1,0:T(8,128)S(1)}, u32[]{:S(2)}, u32[]{:S(2)}) collective-permute-start(f32[128,256]{1,0:T(8,128)S(1)} %get-tuple-element.61), channel_id=1, source_target_pairs={{0,1},{1,0},{2,3},{3,2},{4,5},{5,4},{6,7},{7,6},{8,9},{9,8},{10,11... | collective-permute-start | bytes 393224 | tf_op jit(solution)/shard_map/ppermute | solution.py:156
  32.5 3.6 %collective-permute-start.19 = (f32[128,256]{1,0:T(8,128)S(1)}, f32[128,256]{1,0:T(8,128)S(1)}, u32[]{:S(2)}, u32[]{:S(2)}) collective-permute-start(f32[128,256]{1,0:T(8,128)S(1)} %get-tuple-element.62), channel_id=1, source_target_pairs={{0,1},{1,0},{2,3},{3,2},{4,5},{5,4},{6,7},{7,6},{8,9},{9,8},{10,11... | collective-permute-start | bytes 393224 | tf_op jit(solution)/shard_map/ppermute | solution.py:156
  (1 other events, 1.0 us)

commit v18 on v17

--- a/solution.py
+++ b/solution.py
@@ -256,16 +256,17 @@
     (block,) = kernel_call(round_kernel, [(probes.shape, BF)], (probes,), 8 * flops)
     block, right, left = lax.optimization_barrier((block, right_bases, left_bases))
     (bases,) = kernel_call(join_kernel, [((2, *right_bases.shape[2:]), BF)], (right, left))
-    across = list_swap(bases, 2)
+    right_across = list_swap(right_bases[0], 2)
     beside = [block, middle_swap(block), tile_swap(block, 1)]
     (own,) = kernel_call(
         coefficient_kernel,
         [((ranks // 2, probe_count), BF)],
-        (bases, across, block, list_swap(block, 1), tile_ranks),
+        (bases, right_across, block, list_swap(block, 1), tile_ranks),
         8 * flops,
     )
     coefficients = [own] + [tile_swap(own, turn) for turn in (1, 2, 3)]
-    right, _ = lax.optimization_barrier((jnp.stack([bases[0], across[0]]), own))
+    right, _ = lax.optimization_barrier((jnp.stack([bases[0], right_across[0]]), own))
+    across = jnp.concatenate([right_across, list_swap(left_bases[0], 2)])
     fixed = (row_columns, bases, across)
     operands = (*fixed, list_swap(right, 1), *coefficients)
     small = ((ranks, probe_count), F32)

time: 37 us -> 37.4 us (1.011)
  starting transfers between devices: 16.9 us -> 17.6 us
  waiting for transfers between devices: 13.6 us -> 13.2 us
    ppermute x12 -> x13, starting transfers between devices: 8.09 us -> 9 us  [list_swap(): lax.ppermute(block, 'list', [(i, i ^ bit) for i in range(lax.axis_size('l...]
    ppermute x6, starting transfers between devices: 6.4 us -> 7.16 us  [tile_swap(): lax.ppermute(block, 'tile', [(i, i ^ turn) for i in range(lax.axis_size('...]
    ppermute x1, starting transfers between devices: 2.09 us -> 1.36 us  [far_swap(): return lax.ppermute(block, ('tile', 'list'), route)]
    ppermute x6, waiting for transfers between devices: 5.69 us -> 5.16 us  [tile_swap(): lax.ppermute(block, 'tile', [(i, i ^ turn) for i in range(lax.axis_size('...]
    ppermute x12 -> x13, waiting for transfers between devices: 7.85 us -> 8.01 us  [list_swap(): lax.ppermute(block, 'list', [(i, i ^ bit) for i in range(lax.axis_size('l...]
    unnamed x8 -> x9, local copies, waits for them, and re-layouts: 0.97 us -> 0.97 us
  transfers between devices with their start and end apart: 21 -> 22, of which waited for: 9 -> 10; matrix products, arithmetic and copies ran while one was open for 0% -> 0% of each run, Pallas kernels for 6% -> 6%
where the time goes in v18:
time: 37.4 us; the launch traced here: 37.2 us
  starting transfers between devices  17.6 us (47%)
  waiting for transfers between devices  13.2 us (35%)
  Pallas kernels  2.97 us (8%)
  between operations  1.55 us (4%)
  local copies, waits for them, and re-layouts  1.01 us (3%)
  other arithmetic  0.89 us (2%)
    ppermute x13, starting transfers between devices, list_swap(): lax.ppermute(block, 'list', [(i, i ^ bit) for i in range(lax.axis_size('l...  9 us
    ppermute x13, waiting for transfers between devices, list_swap(): lax.ppermute(block, 'list', [(i, i ^ bit) for i in range(lax.axis_size('l...  8.01 us
    ppermute x6, starting transfers between devices, tile_swap(): lax.ppermute(block, 'tile', [(i, i ^ turn) for i in range(lax.axis_size('...  7.16 us
    ppermute x6, waiting for transfers between devices, tile_swap(): lax.ppermute(block, 'tile', [(i, i ^ turn) for i in range(lax.axis_size('...  5.16 us
    pallas_call x10, Pallas kernels, kernel_call(): pl.pallas_call(kernel, out_shape=tuple((jax.ShapeDtypeStruct(shape, kind)...  2.97 us
    ppermute x1, starting transfers between devices, far_swap(): return lax.ppermute(block, ('tile', 'list'), route)  1.36 us
    unnamed x9, local copies, waits for them, and re-layouts  0.97 us
  transfers between devices with their start and end apart: 22, of which 10 were waited for; matrix products, arithmetic and copies ran while one was open for 0% of the time, Pallas kernels for 6%

profile of v18, /device:TPU:0, one launch (start us, length us, event | category | flops | bytes accessed | tf_op | source)
XLA Modules:
  0.0 37.2 jit_solution(8477450364725588294)
XLA Ops:
  0.0 2.9 %collective-permute-start = (bf16[1,24,1024]{2,1,0:T(8,128)(2,1)}, bf16[1,24,1024]{2,1,0:T(8,128)(2,1)S(1)}, u32[]{:S(2)}, u32[]{:S(2)}) collective-permute-start(bf16[1,24,1024]{2,1,0:T(8,128)(2,1)} %bitcast.9), channel_id=1, source_target_pairs={{0,2},{1,3},{2,0},{3,1},{4,6},{5,7},{6,4},{7,5},{8,10},{9,11},{10,... | collective-permute-start | bytes 147464 | tf_op jit(solution)/shard_map/ppermute | solution.py:156
  2.9 0.9 %copy-done.3 = f32[256,256]{1,0:T(8,128)S(1)} copy-done((f32[256,256]{1,0:T(8,128)S(1)}, f32[256,256]{1,0:T(8,128)}, u32[]{:S(2)}) %copy-start.3) | copy-done | bytes 262168
  3.9 1.6 %collective-permute-start.8 = (bf16[256,256]{1,0:T(8,128)(2,1)S(1)}, bf16[256,256]{1,0:T(8,128)(2,1)S(1)}, u32[]{:S(2)}, u32[]{:S(2)}) collective-permute-start(bf16[256,256]{1,0:T(8,128)(2,1)S(1)} %shard_map.64.block_ref.own_ref), channel_id=1, source_target_pairs={{0,4},{4,0},{8,12},{12,8},{1,5},{5,1},{9,13},{13,9},{2,6},{6,2},{1... | collective-permute-start | bytes 393224 | tf_op jit(solution)/shard_map/ppermute | solution.py:130
  6.1 0.5 %collective-permute-start.1 = (bf16[1,24,1024]{2,1,0:T(8,128)(2,1)S(1)}, bf16[1,24,1024]{2,1,0:T(8,128)(2,1)S(1)}, u32[]{:S(2)}, u32[]{:S(2)}) collective-permute-start(bf16[1,24,1024]{2,1,0:T(8,128)(2,1)S(1)} %bitcast.10), channel_id=1, source_target_pairs={{0,2},{1,3},{2,0},{3,1},{4,6},{5,7},{6,4},{7,5},{8,10},{9,11},{10,... | collective-permute-start | bytes 147464 | tf_op jit(solution)/shard_map/ppermute | solution.py:156
  8.2 2.5 %collective-permute-start.6 = (bf16[48,256]{1,0:T(8,128)(2,1)S(1)}, bf16[48,256]{1,0:T(8,128)(2,1)S(1)}, u32[]{:S(2)}, u32[]{:S(2)}) collective-permute-start(bf16[48,256]{1,0:T(8,128)(2,1)S(1)} %shard_map.66.refs_0_), channel_id=1, source_target_pairs={{0,12},{4,8},{8,4},{12,0},{1,13},{5,9},{9,5},{13,1},{2,14},{6,10},... | collective-permute-start | bytes 73736 | tf_op jit(solution)/shard_map/ppermute | solution.py:130
  10.7 1.6 %collective-permute-start.5 = (bf16[48,256]{1,0:T(8,128)(2,1)S(1)}, bf16[48,256]{1,0:T(8,128)(2,1)S(1)}, u32[]{:S(2)}, u32[]{:S(2)}) collective-permute-start(bf16[48,256]{1,0:T(8,128)(2,1)S(1)} %shard_map.66.refs_0_), channel_id=1, source_target_pairs={{0,8},{4,12},{8,0},{12,4},{1,9},{5,13},{9,1},{13,5},{2,10},{6,14},... | collective-permute-start | bytes 73736 | tf_op jit(solution)/shard_map/ppermute | solution.py:130
  12.4 0.5 %collective-permute-start.4 = (bf16[48,256]{1,0:T(8,128)(2,1)S(1)}, bf16[48,256]{1,0:T(8,128)(2,1)S(1)}, u32[]{:S(2)}, u32[]{:S(2)}) collective-permute-start(bf16[48,256]{1,0:T(8,128)(2,1)S(1)} %shard_map.66.refs_0_), channel_id=1, source_target_pairs={{0,4},{4,0},{8,12},{12,8},{1,5},{5,1},{9,13},{13,9},{2,6},{6,2},{1... | collective-permute-start | bytes 73736 | tf_op jit(solution)/shard_map/ppermute | solution.py:130
  12.9 0.6 %shard_map.67 = (f32[256,256]{1,0:T(8,128)S(1)}, f32[256,256]{1,0:T(8,128)S(1)}, f32[256,256]{1,0:T(8,128)S(1)}, f32[256,256]{1,0:T(8,128)S(1)}) custom-call(bf16[3,1024,256]{2,1,0:T(8,128)(2,1)S(1)} %bitcast.5, bf16[256,256]{1,0:T(8,128)(2,1)S(1)} %shard_map.64.block_ref.own_ref, bf16[256,256]{1,0:T(8,128)(2,1)S(1)} %collective-permute-done.7.second_ref, ...), custom_call_target="tpu_custom_call" | custom-call | tf_op jit(solution)/shard_map/pallas_call | solution.py:77
  13.9 1.7 %collective-permute-done.5.refs_2_ = bf16[48,256]{1,0:T(8,128)(2,1)S(1)} collective-permute-done((bf16[48,256]{1,0:T(8,128)(2,1)S(1)}, bf16[48,256]{1,0:T(8,128)(2,1)S(1)}, u32[]{:S(2)}, u32[]{:S(2)}) %collective-permute-start.5) | collective-permute-done | bytes 24608 | tf_op jit(solution)/shard_map/ppermute | solution.py:130
  15.5 0.6 %collective-permute-done.4.refs_1_ = bf16[48,256]{1,0:T(8,128)(2,1)S(1)} collective-permute-done((bf16[48,256]{1,0:T(8,128)(2,1)S(1)}, bf16[48,256]{1,0:T(8,128)(2,1)S(1)}, u32[]{:S(2)}, u32[]{:S(2)}) %collective-permute-start.4) | collective-permute-done | bytes 24608 | tf_op jit(solution)/shard_map/ppermute | solution.py:130
  16.7 0.5 %shard_map.69 = (f32[256,256]{1,0:T(8,128)S(1)}, f32[256,256]{1,0:T(8,128)S(1)}, f32[256,256]{1,0:T(8,128)S(1)}, f32[96,256]{1,0:T(8,128)S(1)}, f32[96,256]{1,0:T(8,128)S(1)}) custom-call(s32[1,1]{1,0:T(1,128)S(6)} %copy.9.columns_ref, bf16[2,24,1024]{2,1,0:T(8,128)(2,1)S(1)} %shard_map.65.bases_ref, ...), custom_call_target="tpu_custom_call" | custom-call | flops 301989888 | bytes 294912 | tf_op jit(solution)/shard_map/pallas_call | solution.py:77
  17.2 0.6 %collective-permute-start.12 = (f32[96,256]{1,0:T(8,128)S(1)}, f32[96,256]{1,0:T(8,128)S(1)}, u32[]{:S(2)}, u32[]{:S(2)}) collective-permute-start(f32[96,256]{1,0:T(8,128)S(1)} %get-tuple-element.47), channel_id=1, source_target_pairs={{0,1},{1,0},{2,3},{3,2},{4,5},{5,4},{6,7},{7,6},{8,9},{9,8},{10,11... | collective-permute-start | bytes 294920 | tf_op jit(solution)/shard_map/ppermute | solution.py:156
  18.2 1.6 %collective-permute-start.11 = (bf16[256,256]{1,0:T(8,128)(2,1)S(1)}, bf16[256,256]{1,0:T(8,128)(2,1)S(1)}, u32[]{:S(2)}, u32[]{:S(2)}) collective-permute-start(bf16[256,256]{1,0:T(8,128)(2,1)S(1)} %add_convert_fusion.2), channel_id=1, source_target_pairs={{0,2},{1,3},{2,0},{3,1},{4,6},{5,7},{6,4},{7,5},{8,10},{9,11},{10,... | collective-permute-start | bytes 393224 | tf_op jit(solution)/shard_map/ppermute | solution.py:156
  19.8 1.4 %collective-permute-start.14 = (bf16[96,256]{1,0:T(8,128)(2,1)S(1)}, bf16[96,256]{1,0:T(8,128)(2,1)S(1)}, u32[]{:S(2)}, u32[]{:S(2)}) collective-permute-start(bf16[96,256]{1,0:T(8,128)(2,1)S(1)} %add_convert_fusion.3.refs_0_), channel_id=1, source_target_pairs={{0,8},{1,13},{2,10},{3,15},{4,12},{5,9},{6,14},{7,11},{8,0},{9,5},... | collective-permute-start | bytes 147464 | tf_op jit(solution)/shard_map/ppermute | solution.py:152
  21.4 2.4 %collective-permute-done.11 = bf16[256,256]{1,0:T(8,128)(2,1)S(1)} collective-permute-done((bf16[256,256]{1,0:T(8,128)(2,1)S(1)}, bf16[256,256]{1,0:T(8,128)(2,1)S(1)}, u32[]{:S(2)}, u32[]{:S(2)}) %collective-permute-start.11) | collective-permute-done | bytes 131104 | tf_op jit(solution)/shard_map/ppermute | solution.py:156
  23.9 0.6 %collective-permute-start.16 = (bf16[256,256]{1,0:T(8,128)(2,1)S(1)}, bf16[256,256]{1,0:T(8,128)(2,1)S(1)}, u32[]{:S(2)}, u32[]{:S(2)}) collective-permute-start(bf16[256,256]{1,0:T(8,128)(2,1)S(1)} %add_convert_fusion.1.own_ref), channel_id=1, source_target_pairs={{0,4},{4,0},{8,12},{12,8},{1,5},{5,1},{9,13},{13,9},{2,6},{6,2},{1... | collective-permute-start | bytes 393224 | tf_op jit(solution)/shard_map/ppermute | solution.py:130
  24.5 1.3 %collective-permute-done.13.refs_1_ = bf16[48,256]{1,0:T(8,128)(2,1)S(1)} collective-permute-done((bf16[48,256]{1,0:T(8,128)(2,1)S(1)}, bf16[48,256]{1,0:T(8,128)(2,1)S(1)}, u32[]{:S(2)}, u32[]{:S(2)}) %collective-permute-start.13) | collective-permute-done | bytes 24608 | tf_op jit(solution)/shard_map/ppermute | solution.py:130
  25.9 0.6 %collective-permute-start.17 = (bf16[2,24,1024]{2,1,0:T(8,128)(2,1)S(1)}, bf16[2,24,1024]{2,1,0:T(8,128)(2,1)S(1)}, u32[]{:S(2)}, u32[]{:S(2)}) collective-permute-start(bf16[2,24,1024]{2,1,0:T(8,128)(2,1)S(1)} %pad_maximum_fusion.1), channel_id=1, source_target_pairs={{0,1},{1,0},{2,3},{3,2},{4,5},{5,4},{6,7},{7,6},{8,9},{9,8},{10,11... | collective-permute-start | bytes 294920 | tf_op jit(solution)/shard_map/ppermute | solution.py:156
  26.4 0.9 %collective-permute-done.17.other_ref = bf16[2,24,1024]{2,1,0:T(8,128)(2,1)S(1)} collective-permute-done((bf16[2,24,1024]{2,1,0:T(8,128)(2,1)S(1)}, bf16[2,24,1024]{2,1,0:T(8,128)(2,1)S(1)}, u32[]{:S(2)}, u32[]{:S(2)}) %collective-permute-start.17) | collective-permute-done | bytes 98336 | tf_op jit(solution)/shard_map/ppermute | solution.py:156
  27.7 1.2 %collective-permute-done.16.first_ref = bf16[256,256]{1,0:T(8,128)(2,1)S(1)} collective-permute-done((bf16[256,256]{1,0:T(8,128)(2,1)S(1)}, bf16[256,256]{1,0:T(8,128)(2,1)S(1)}, u32[]{:S(2)}, u32[]{:S(2)}) %collective-permute-start.16) | collective-permute-done | bytes 131104 | tf_op jit(solution)/shard_map/ppermute | solution.py:130
  29.6 1.2 %collective-permute-done.18 = f32[256,256]{1,0:T(8,128)S(1)} collective-permute-done((f32[256,256]{1,0:T(8,128)S(1)}, f32[256,256]{1,0:T(8,128)S(1)}, u32[]{:S(2)}, u32[]{:S(2)}) %collective-permute-start.18) | collective-permute-done | bytes 262176 | tf_op jit(solution)/shard_map/ppermute | solution.py:156
  30.8 1.6 %collective-permute-start.21 = (bf16[256,256]{1,0:T(8,128)(2,1)S(1)}, bf16[256,256]{1,0:T(8,128)(2,1)S(1)}, u32[]{:S(2)}, u32[]{:S(2)}) collective-permute-start(bf16[256,256]{1,0:T(8,128)(2,1)S(1)} %add_convert_fusion), channel_id=1, source_target_pairs={{0,2},{1,3},{2,0},{3,1},{4,6},{5,7},{6,4},{7,5},{8,10},{9,11},{10,... | collective-permute-start | bytes 393224 | tf_op jit(solution)/shard_map/ppermute | solution.py:156
  33.4 3.1 %collective-permute-done.21 = bf16[256,256]{1,0:T(8,128)(2,1)S(1)} collective-permute-done((bf16[256,256]{1,0:T(8,128)(2,1)S(1)}, bf16[256,256]{1,0:T(8,128)(2,1)S(1)}, u32[]{:S(2)}, u32[]{:S(2)}) %collective-permute-start.21) | collective-permute-done | bytes 131104 | tf_op jit(solution)/shard_map/ppermute | solution.py:156
  36.4 0.7 %fusion = f32[256,256]{1,0:T(8,128)} fusion(f32[256,256]{1,0:T(8,128)S(1)} %get-tuple-element.58, f32[128,256]{1,0:T(8,128)S(1)} %collective-permute-done.20, f32[128,256]{1,0:T(8,128)S(1)} %collective-permute-done.19, bf16[256,256]{1,0:T(8,128)(2,1)S(1)} %collective-permute-done.21), kind=kLoop, calls=%fused_computation.1 | loop fusion | flops 262144 | bytes 917504 | tf_op jit(solution)/shard_map/add | solution.py:303
  (52 shorter events, 4.5 us)
Async XLA Ops:
  0.0 6.1 %copy-start.2 = (bf16[1,1,24,1024]{3,2,1,0:T(8,128)(2,1)S(1)}, bf16[1,1,24,1024]{3,2,1,0:T(8,128)(2,1)}, u32[]{:S(2)}) copy-start(bf16[1,1,24,1024]{3,2,1,0:T(8,128)(2,1)} %left_ref) | copy-start | bytes 147460
  0.0 7.9 %copy-start.1 = (bf16[1,1,24,1024]{3,2,1,0:T(8,128)(2,1)S(1)}, bf16[1,1,24,1024]{3,2,1,0:T(8,128)(2,1)}, u32[]{:S(2)}) copy-start(bf16[1,1,24,1024]{3,2,1,0:T(8,128)(2,1)} %right_ref) | copy-start | bytes 147460
  0.0 7.9 %collective-permute-start = (bf16[1,24,1024]{2,1,0:T(8,128)(2,1)}, bf16[1,24,1024]{2,1,0:T(8,128)(2,1)S(1)}, u32[]{:S(2)}, u32[]{:S(2)}) collective-permute-start(bf16[1,24,1024]{2,1,0:T(8,128)(2,1)} %bitcast.9), channel_id=1, source_target_pairs={{0,2},{1,3},{2,0},{3,1},{4,6},{5,7},{6,4},{7,5},{8,10},{9,11},{10,... | collective-permute-start | bytes 147464 | tf_op jit(solution)/shard_map/ppermute | solution.py:156
  3.9 9.0 %collective-permute-start.8 = (bf16[256,256]{1,0:T(8,128)(2,1)S(1)}, bf16[256,256]{1,0:T(8,128)(2,1)S(1)}, u32[]{:S(2)}, u32[]{:S(2)}) collective-permute-start(bf16[256,256]{1,0:T(8,128)(2,1)S(1)} %shard_map.64.block_ref.own_ref), channel_id=1, source_target_pairs={{0,4},{4,0},{8,12},{12,8},{1,5},{5,1},{9,13},{13,9},{2,6},{6,2},{1... | collective-permute-start | bytes 393224 | tf_op jit(solution)/shard_map/ppermute | solution.py:130
  5.6 7.3 %collective-permute-start.7 = (bf16[256,256]{1,0:T(8,128)(2,1)S(1)}, bf16[256,256]{1,0:T(8,128)(2,1)S(1)}, u32[]{:S(2)}, u32[]{:S(2)}) collective-permute-start(bf16[256,256]{1,0:T(8,128)(2,1)S(1)} %shard_map.64.block_ref.own_ref), channel_id=1, source_target_pairs={{0,1},{1,0},{2,3},{3,2},{4,8},{5,9},{6,10},{7,11},{8,4},{9,5},{10,... | collective-permute-start | bytes 393224 | tf_op jit(solution)/shard_map/ppermute | solution.py:142
  5.6 2.4 %collective-permute-start.2 = (bf16[256,256]{1,0:T(8,128)(2,1)S(1)}, bf16[256,256]{1,0:T(8,128)(2,1)S(1)}, u32[]{:S(2)}, u32[]{:S(2)}) collective-permute-start(bf16[256,256]{1,0:T(8,128)(2,1)S(1)} %shard_map.64.block_ref.own_ref), channel_id=1, source_target_pairs={{0,1},{1,0},{2,3},{3,2},{4,5},{5,4},{6,7},{7,6},{8,9},{9,8},{10,11... | collective-permute-start | bytes 393224 | tf_op jit(solution)/shard_map/ppermute | solution.py:156
  6.1 6.3 %collective-permute-start.1 = (bf16[1,24,1024]{2,1,0:T(8,128)(2,1)S(1)}, bf16[1,24,1024]{2,1,0:T(8,128)(2,1)S(1)}, u32[]{:S(2)}, u32[]{:S(2)}) collective-permute-start(bf16[1,24,1024]{2,1,0:T(8,128)(2,1)S(1)} %bitcast.10), channel_id=1, source_target_pairs={{0,2},{1,3},{2,0},{3,1},{4,6},{5,7},{6,4},{7,5},{8,10},{9,11},{10,... | collective-permute-start | bytes 147464 | tf_op jit(solution)/shard_map/ppermute | solution.py:156
  8.2 5.7 %collective-permute-start.6 = (bf16[48,256]{1,0:T(8,128)(2,1)S(1)}, bf16[48,256]{1,0:T(8,128)(2,1)S(1)}, u32[]{:S(2)}, u32[]{:S(2)}) collective-permute-start(bf16[48,256]{1,0:T(8,128)(2,1)S(1)} %shard_map.66.refs_0_), channel_id=1, source_target_pairs={{0,12},{4,8},{8,4},{12,0},{1,13},{5,9},{9,5},{13,1},{2,14},{6,10},... | collective-permute-start | bytes 73736 | tf_op jit(solution)/shard_map/ppermute | solution.py:130
  10.7 4.8 %collective-permute-start.5 = (bf16[48,256]{1,0:T(8,128)(2,1)S(1)}, bf16[48,256]{1,0:T(8,128)(2,1)S(1)}, u32[]{:S(2)}, u32[]{:S(2)}) collective-permute-start(bf16[48,256]{1,0:T(8,128)(2,1)S(1)} %shard_map.66.refs_0_), channel_id=1, source_target_pairs={{0,8},{4,12},{8,0},{12,4},{1,9},{5,13},{9,1},{13,5},{2,10},{6,14},... | collective-permute-start | bytes 73736 | tf_op jit(solution)/shard_map/ppermute | solution.py:130
  12.4 3.8 %collective-permute-start.4 = (bf16[48,256]{1,0:T(8,128)(2,1)S(1)}, bf16[48,256]{1,0:T(8,128)(2,1)S(1)}, u32[]{:S(2)}, u32[]{:S(2)}) collective-permute-start(bf16[48,256]{1,0:T(8,128)(2,1)S(1)} %shard_map.66.refs_0_), channel_id=1, source_target_pairs={{0,4},{4,0},{8,12},{12,8},{1,5},{5,1},{9,13},{13,9},{2,6},{6,2},{1... | collective-permute-start | bytes 73736 | tf_op jit(solution)/shard_map/ppermute | solution.py:130
  12.9 3.3 %collective-permute-start.3 = (bf16[2,24,1024]{2,1,0:T(8,128)(2,1)S(1)}, bf16[2,24,1024]{2,1,0:T(8,128)(2,1)S(1)}, u32[]{:S(2)}, u32[]{:S(2)}) collective-permute-start(bf16[2,24,1024]{2,1,0:T(8,128)(2,1)S(1)} %pad_maximum_fusion), channel_id=1, source_target_pairs={{0,1},{1,0},{2,3},{3,2},{4,5},{5,4},{6,7},{7,6},{8,9},{9,8},{10,11... | collective-permute-start | bytes 294920 | tf_op jit(solution)/shard_map/ppermute | solution.py:156
  16.6 1.6 %collective-permute-start.10 = (f32[256,256]{1,0:T(8,128)S(1)}, f32[256,256]{1,0:T(8,128)S(1)}, u32[]{:S(2)}, u32[]{:S(2)}) collective-permute-start(f32[256,256]{1,0:T(8,128)S(1)} %get-tuple-element.45), channel_id=1, source_target_pairs={{0,1},{1,0},{2,3},{3,2},{4,5},{5,4},{6,7},{7,6},{8,9},{9,8},{10,11... | collective-permute-start | bytes 786440 | tf_op jit(solution)/shard_map/ppermute | solution.py:156
  17.2 2.6 %collective-permute-start.12 = (f32[96,256]{1,0:T(8,128)S(1)}, f32[96,256]{1,0:T(8,128)S(1)}, u32[]{:S(2)}, u32[]{:S(2)}) collective-permute-start(f32[96,256]{1,0:T(8,128)S(1)} %get-tuple-element.47), channel_id=1, source_target_pairs={{0,1},{1,0},{2,3},{3,2},{4,5},{5,4},{6,7},{7,6},{8,9},{9,8},{10,11... | collective-permute-start | bytes 294920 | tf_op jit(solution)/shard_map/ppermute | solution.py:156
  17.8 3.7 %collective-permute-start.9 = (f32[256,256]{1,0:T(8,128)S(1)}, f32[256,256]{1,0:T(8,128)S(1)}, u32[]{:S(2)}, u32[]{:S(2)}) collective-permute-start(f32[256,256]{1,0:T(8,128)S(1)} %get-tuple-element.43), channel_id=1, source_target_pairs={{0,1},{1,0},{2,3},{3,2},{4,5},{5,4},{6,7},{7,6},{8,9},{9,8},{10,11... | collective-permute-start | bytes 786440 | tf_op jit(solution)/shard_map/ppermute | solution.py:156
  18.2 5.6 %collective-permute-start.11 = (bf16[256,256]{1,0:T(8,128)(2,1)S(1)}, bf16[256,256]{1,0:T(8,128)(2,1)S(1)}, u32[]{:S(2)}, u32[]{:S(2)}) collective-permute-start(bf16[256,256]{1,0:T(8,128)(2,1)S(1)} %add_convert_fusion.2), channel_id=1, source_target_pairs={{0,2},{1,3},{2,0},{3,1},{4,6},{5,7},{6,4},{7,5},{8,10},{9,11},{10,... | collective-permute-start | bytes 393224 | tf_op jit(solution)/shard_map/ppermute | solution.py:156
  19.8 5.9 %collective-permute-start.14 = (bf16[96,256]{1,0:T(8,128)(2,1)S(1)}, bf16[96,256]{1,0:T(8,128)(2,1)S(1)}, u32[]{:S(2)}, u32[]{:S(2)}) collective-permute-start(bf16[96,256]{1,0:T(8,128)(2,1)S(1)} %add_convert_fusion.3.refs_0_), channel_id=1, source_target_pairs={{0,8},{1,13},{2,10},{3,15},{4,12},{5,9},{6,14},{7,11},{8,0},{9,5},... | collective-permute-start | bytes 147464 | tf_op jit(solution)/shard_map/ppermute | solution.py:152
  21.2 4.6 %collective-permute-start.13 = (bf16[48,256]{1,0:T(8,128)(2,1)S(1)}, bf16[48,256]{1,0:T(8,128)(2,1)S(1)}, u32[]{:S(2)}, u32[]{:S(2)}) collective-permute-start(bf16[48,256]{1,0:T(8,128)(2,1)S(1)} %slice.17), channel_id=1, source_target_pairs={{0,4},{4,0},{8,12},{12,8},{1,5},{5,1},{9,13},{13,9},{2,6},{6,2},{1... | collective-permute-start | bytes 73736 | tf_op jit(solution)/shard_map/ppermute | solution.py:130
  23.9 5.0 %collective-permute-start.16 = (bf16[256,256]{1,0:T(8,128)(2,1)S(1)}, bf16[256,256]{1,0:T(8,128)(2,1)S(1)}, u32[]{:S(2)}, u32[]{:S(2)}) collective-permute-start(bf16[256,256]{1,0:T(8,128)(2,1)S(1)} %add_convert_fusion.1.own_ref), channel_id=1, source_target_pairs={{0,4},{4,0},{8,12},{12,8},{1,5},{5,1},{9,13},{13,9},{2,6},{6,2},{1... | collective-permute-start | bytes 393224 | tf_op jit(solution)/shard_map/ppermute | solution.py:130
  25.8 2.0 %collective-permute-start.15 = (bf16[256,256]{1,0:T(8,128)(2,1)S(1)}, bf16[256,256]{1,0:T(8,128)(2,1)S(1)}, u32[]{:S(2)}, u32[]{:S(2)}) collective-permute-start(bf16[256,256]{1,0:T(8,128)(2,1)S(1)} %add_convert_fusion.1.own_ref), channel_id=1, source_target_pairs={{0,1},{1,0},{2,3},{3,2},{4,8},{5,9},{6,10},{7,11},{8,4},{9,5},{10,... | collective-permute-start | bytes 393224 | tf_op jit(solution)/shard_map/ppermute | solution.py:142
  25.9 1.5 %collective-permute-start.17 = (bf16[2,24,1024]{2,1,0:T(8,128)(2,1)S(1)}, bf16[2,24,1024]{2,1,0:T(8,128)(2,1)S(1)}, u32[]{:S(2)}, u32[]{:S(2)}) collective-permute-start(bf16[2,24,1024]{2,1,0:T(8,128)(2,1)S(1)} %pad_maximum_fusion.1), channel_id=1, source_target_pairs={{0,1},{1,0},{2,3},{3,2},{4,5},{5,4},{6,7},{7,6},{8,9},{9,8},{10,11... | collective-permute-start | bytes 294920 | tf_op jit(solution)/shard_map/ppermute | solution.py:156
  29.2 1.6 %collective-permute-start.18 = (f32[256,256]{1,0:T(8,128)S(1)}, f32[256,256]{1,0:T(8,128)S(1)}, u32[]{:S(2)}, u32[]{:S(2)}) collective-permute-start(f32[256,256]{1,0:T(8,128)S(1)} %shard_map.72), channel_id=1, source_target_pairs={{0,1},{1,0},{2,3},{3,2},{4,5},{5,4},{6,7},{7,6},{8,9},{9,8},{10,11... | collective-permute-start | bytes 786440 | tf_op jit(solution)/shard_map/ppermute | solution.py:156
  30.8 5.6 %collective-permute-start.21 = (bf16[256,256]{1,0:T(8,128)(2,1)S(1)}, bf16[256,256]{1,0:T(8,128)(2,1)S(1)}, u32[]{:S(2)}, u32[]{:S(2)}) collective-permute-start(bf16[256,256]{1,0:T(8,128)(2,1)S(1)} %add_convert_fusion), channel_id=1, source_target_pairs={{0,2},{1,3},{2,0},{3,1},{4,6},{5,7},{6,4},{7,5},{8,10},{9,11},{10,... | collective-permute-start | bytes 393224 | tf_op jit(solution)/shard_map/ppermute | solution.py:156
  32.8 3.6 %collective-permute-start.19 = (f32[128,256]{1,0:T(8,128)S(1)}, f32[128,256]{1,0:T(8,128)S(1)}, u32[]{:S(2)}, u32[]{:S(2)}) collective-permute-start(f32[128,256]{1,0:T(8,128)S(1)} %get-tuple-element.61), channel_id=1, source_target_pairs={{0,1},{1,0},{2,3},{3,2},{4,5},{5,4},{6,7},{7,6},{8,9},{9,8},{10,11... | collective-permute-start | bytes 393224 | tf_op jit(solution)/shard_map/ppermute | solution.py:156
  32.9 3.6 %collective-permute-start.20 = (f32[128,256]{1,0:T(8,128)S(1)}, f32[128,256]{1,0:T(8,128)S(1)}, u32[]{:S(2)}, u32[]{:S(2)}) collective-permute-start(f32[128,256]{1,0:T(8,128)S(1)} %get-tuple-element.62), channel_id=1, source_target_pairs={{0,1},{1,0},{2,3},{3,2},{4,5},{5,4},{6,7},{7,6},{8,9},{9,8},{10,11... | collective-permute-start | bytes 393224 | tf_op jit(solution)/shard_map/ppermute | solution.py:156
  (2 other events, 5.9 us)

commit v19 on v17

--- a/solution.py
+++ b/solution.py
@@ -174,7 +174,7 @@
     )
 
 
-def near_kernel(turns, near_ref, own_ref, second_ref, first_ref, *refs):
+def near_kernel(turns, near_ref, own_ref, first_ref, second_ref, *refs):
     base_refs, out_refs = refs[: -len(turns)], refs[-len(turns) :]
     count = lax.axis_size("tile")
     tile = lax.axis_index("tile")
@@ -257,7 +257,7 @@
     block, right, left = lax.optimization_barrier((block, right_bases, left_bases))
     (bases,) = kernel_call(join_kernel, [((2, *right_bases.shape[2:]), BF)], (right, left))
     across = list_swap(bases, 2)
-    beside = [block, middle_swap(block), tile_swap(block, 1)]
+    beside = [block, tile_swap(block, 1), middle_swap(block)]
     (own,) = kernel_call(
         coefficient_kernel,
         [((ranks // 2, probe_count), BF)],
@@ -288,7 +288,7 @@
     held, held_across, near_by, far, ready = lax.optimization_barrier(
         (bases, across, near_by, far, block)
     )
-    beside = [block, middle_swap(ready), tile_swap(block, 1)]
+    beside = [block, tile_swap(block, 1), middle_swap(ready)]
     left = list_swap(jnp.stack([held[1], held_across[1]]), 1)
 
     base = call(far_kernel, (3, 2, 1, 0), (*fixed, left, own, near_by, far), cost=0)

time: 37 us -> 37 us (level)
  waiting for transfers between devices: 13.6 us -> 11.9 us
  starting transfers between devices: 16.9 us -> 18.5 us
    ppermute x6, starting transfers between devices: 6.4 us -> 7.77 us  [tile_swap(): lax.ppermute(block, 'tile', [(i, i ^ turn) for i in range(lax.axis_size('...]
    ppermute x6, waiting for transfers between devices: 5.69 us -> 4.35 us  [tile_swap(): lax.ppermute(block, 'tile', [(i, i ^ turn) for i in range(lax.axis_size('...]
where the time goes in v19:
time: 37 us; the launch traced here: 36.8 us
  starting transfers between devices  18.5 us (50%)
  waiting for transfers between devices  11.9 us (32%)
  Pallas kernels  2.97 us (8%)
  between operations  1.56 us (4%)
  local copies, waits for them, and re-layouts  1.01 us (3%)
  other arithmetic  0.89 us (2%)
    ppermute x12, starting transfers between devices, list_swap(): lax.ppermute(block, 'list', [(i, i ^ bit) for i in range(lax.axis_size('l...  8.09 us
    ppermute x6, starting transfers between devices, tile_swap(): lax.ppermute(block, 'tile', [(i, i ^ turn) for i in range(lax.axis_size('...  7.77 us
    ppermute x12, waiting for transfers between devices, list_swap(): lax.ppermute(block, 'list', [(i, i ^ bit) for i in range(lax.axis_size('l...  7.52 us
    ppermute x6, waiting for transfers between devices, tile_swap(): lax.ppermute(block, 'tile', [(i, i ^ turn) for i in range(lax.axis_size('...  4.35 us
    pallas_call x10, Pallas kernels, kernel_call(): pl.pallas_call(kernel, out_shape=tuple((jax.ShapeDtypeStruct(shape, kind)...  2.97 us
    ppermute x1, starting transfers between devices, far_swap(): return lax.ppermute(block, ('tile', 'list'), route)  2.09 us
    unnamed x8, local copies, waits for them, and re-layouts  0.97 us
    add x1, other arithmetic, one_slot(): return keep + list_swap_in_pieces(send, 1, 2) + crossed  0.75 us
  transfers between devices with their start and end apart: 21, of which 9 were waited for; matrix products, arithmetic and copies ran while one was open for 0% of the time, Pallas kernels for 6%

profile of v19, /device:TPU:0, one launch (start us, length us, event | category | flops | bytes accessed | tf_op | source)
XLA Modules:
  0.0 36.8 jit_solution(1156301926848586599)
XLA Ops:
  0.0 1.0 %copy-done.3 = f32[256,256]{1,0:T(8,128)S(1)} copy-done((f32[256,256]{1,0:T(8,128)S(1)}, f32[256,256]{1,0:T(8,128)}, u32[]{:S(2)}) %copy-start.3) | copy-done | bytes 262168
  1.0 3.0 %collective-permute-start = (bf16[2,24,1024]{2,1,0:T(8,128)(2,1)S(1)}, bf16[2,24,1024]{2,1,0:T(8,128)(2,1)S(1)}, u32[]{:S(2)}, u32[]{:S(2)}) collective-permute-start(bf16[2,24,1024]{2,1,0:T(8,128)(2,1)S(1)} %shard_map.65.bases_ref), channel_id=1, source_target_pairs={{0,2},{1,3},{2,0},{3,1},{4,6},{5,7},{6,4},{7,5},{8,10},{9,11},{10,... | collective-permute-start | bytes 294920 | tf_op jit(solution)/shard_map/ppermute | solution.py:156
  4.0 0.5 %collective-permute-start.7 = (bf16[256,256]{1,0:T(8,128)(2,1)S(1)}, bf16[256,256]{1,0:T(8,128)(2,1)S(1)}, u32[]{:S(2)}, u32[]{:S(2)}) collective-permute-start(bf16[256,256]{1,0:T(8,128)(2,1)S(1)} %shard_map.64.block_ref.own_ref), channel_id=1, source_target_pairs={{0,1},{1,0},{2,3},{3,2},{4,8},{5,9},{6,10},{7,11},{8,4},{9,5},{10,... | collective-permute-start | bytes 393224 | tf_op jit(solution)/shard_map/ppermute | solution.py:142
  4.5 2.6 %collective-permute-start.6 = (bf16[256,256]{1,0:T(8,128)(2,1)S(1)}, bf16[256,256]{1,0:T(8,128)(2,1)S(1)}, u32[]{:S(2)}, u32[]{:S(2)}) collective-permute-start(bf16[256,256]{1,0:T(8,128)(2,1)S(1)} %shard_map.64.block_ref.own_ref), channel_id=1, source_target_pairs={{0,4},{4,0},{8,12},{12,8},{1,5},{5,1},{9,13},{13,9},{2,6},{6,2},{1... | collective-permute-start | bytes 393224 | tf_op jit(solution)/shard_map/ppermute | solution.py:130
  8.1 3.0 %collective-permute-start.5 = (bf16[48,256]{1,0:T(8,128)(2,1)S(1)}, bf16[48,256]{1,0:T(8,128)(2,1)S(1)}, u32[]{:S(2)}, u32[]{:S(2)}) collective-permute-start(bf16[48,256]{1,0:T(8,128)(2,1)S(1)} %shard_map.66.refs_0_), channel_id=1, source_target_pairs={{0,12},{4,8},{8,4},{12,0},{1,13},{5,9},{9,5},{13,1},{2,14},{6,10},... | collective-permute-start | bytes 73736 | tf_op jit(solution)/shard_map/ppermute | solution.py:130
  11.1 1.5 %collective-permute-start.3 = (bf16[48,256]{1,0:T(8,128)(2,1)S(1)}, bf16[48,256]{1,0:T(8,128)(2,1)S(1)}, u32[]{:S(2)}, u32[]{:S(2)}) collective-permute-start(bf16[48,256]{1,0:T(8,128)(2,1)S(1)} %shard_map.66.refs_0_), channel_id=1, source_target_pairs={{0,4},{4,0},{8,12},{12,8},{1,5},{5,1},{9,13},{13,9},{2,6},{6,2},{1... | collective-permute-start | bytes 73736 | tf_op jit(solution)/shard_map/ppermute | solution.py:130
  13.3 0.6 %shard_map.67 = (f32[256,256]{1,0:T(8,128)S(1)}, f32[256,256]{1,0:T(8,128)S(1)}, f32[256,256]{1,0:T(8,128)S(1)}, f32[256,256]{1,0:T(8,128)S(1)}) custom-call(bf16[3,1024,256]{2,1,0:T(8,128)(2,1)S(1)} %bitcast.3, bf16[256,256]{1,0:T(8,128)(2,1)S(1)} %shard_map.64.block_ref.own_ref, bf16[256,256]{1,0:T(8,128)(2,1)S(1)} %collective-permute-done.6.first_ref, ...), custom_call_target="tpu_custom_call" | custom-call | tf_op jit(solution)/shard_map/pallas_call | solution.py:77
  13.9 1.9 %collective-permute-done.4.refs_2_ = bf16[48,256]{1,0:T(8,128)(2,1)S(1)} collective-permute-done((bf16[48,256]{1,0:T(8,128)(2,1)S(1)}, bf16[48,256]{1,0:T(8,128)(2,1)S(1)}, u32[]{:S(2)}, u32[]{:S(2)}) %collective-permute-start.4) | collective-permute-done | bytes 24608 | tf_op jit(solution)/shard_map/ppermute | solution.py:130
  15.8 0.4 %shard_map.68 = (f32[256,256]{1,0:T(8,128)S(1)}, f32[96,256]{1,0:T(8,128)S(1)}) custom-call(s32[1,1]{1,0:T(1,128)S(6)} %copy.8.columns_ref, bf16[2,24,1024]{2,1,0:T(8,128)(2,1)S(1)} %shard_map.65.bases_ref, bf16[2,24,1024]{2,1,0:T(8,128)(2,1)S(1)} %collective-permute-done.across_ref, bf16[2,24,1024]{2,1,0:T(8,128)(2,1)S(1)} %collective-permute-done.2.other_ref, ...), custom_call_target="tpu_custom_call" | custom-call | flops 100663296 | bytes 98304 | tf_op jit(solution)/shard_map/pallas_call | solution.py:77
  16.3 0.5 %shard_map.69 = (f32[256,256]{1,0:T(8,128)S(1)}, f32[256,256]{1,0:T(8,128)S(1)}, f32[256,256]{1,0:T(8,128)S(1)}, f32[96,256]{1,0:T(8,128)S(1)}, f32[96,256]{1,0:T(8,128)S(1)}) custom-call(s32[1,1]{1,0:T(1,128)S(6)} %copy.8.columns_ref, bf16[2,24,1024]{2,1,0:T(8,128)(2,1)S(1)} %shard_map.65.bases_ref, ...), custom_call_target="tpu_custom_call" | custom-call | flops 301989888 | bytes 294912 | tf_op jit(solution)/shard_map/pallas_call | solution.py:77
  16.9 0.6 %collective-permute-start.12 = (f32[96,256]{1,0:T(8,128)S(1)}, f32[96,256]{1,0:T(8,128)S(1)}, u32[]{:S(2)}, u32[]{:S(2)}) collective-permute-start(f32[96,256]{1,0:T(8,128)S(1)} %get-tuple-element.47), channel_id=1, source_target_pairs={{0,1},{1,0},{2,3},{3,2},{4,5},{5,4},{6,7},{7,6},{8,9},{9,8},{10,11... | collective-permute-start | bytes 294920 | tf_op jit(solution)/shard_map/ppermute | solution.py:156
  17.9 1.6 %collective-permute-start.10 = (bf16[256,256]{1,0:T(8,128)(2,1)S(1)}, bf16[256,256]{1,0:T(8,128)(2,1)S(1)}, u32[]{:S(2)}, u32[]{:S(2)}) collective-permute-start(bf16[256,256]{1,0:T(8,128)(2,1)S(1)} %add_convert_fusion.2), channel_id=1, source_target_pairs={{0,2},{1,3},{2,0},{3,1},{4,6},{5,7},{6,4},{7,5},{8,10},{9,11},{10,... | collective-permute-start | bytes 393224 | tf_op jit(solution)/shard_map/ppermute | solution.py:156
  19.5 2.1 %collective-permute-start.14 = (bf16[96,256]{1,0:T(8,128)(2,1)S(1)}, bf16[96,256]{1,0:T(8,128)(2,1)S(1)}, u32[]{:S(2)}, u32[]{:S(2)}) collective-permute-start(bf16[96,256]{1,0:T(8,128)(2,1)S(1)} %add_convert_fusion.3.refs_0_), channel_id=1, source_target_pairs={{0,8},{1,13},{2,10},{3,15},{4,12},{5,9},{6,14},{7,11},{8,0},{9,5},... | collective-permute-start | bytes 147464 | tf_op jit(solution)/shard_map/ppermute | solution.py:152
  21.6 1.9 %collective-permute-done.10 = bf16[256,256]{1,0:T(8,128)(2,1)S(1)} collective-permute-done((bf16[256,256]{1,0:T(8,128)(2,1)S(1)}, bf16[256,256]{1,0:T(8,128)(2,1)S(1)}, u32[]{:S(2)}, u32[]{:S(2)}) %collective-permute-start.10) | collective-permute-done | bytes 131104 | tf_op jit(solution)/shard_map/ppermute | solution.py:156
  23.5 0.7 %collective-permute-start.11 = (bf16[256,256]{1,0:T(8,128)(2,1)S(1)}, bf16[256,256]{1,0:T(8,128)(2,1)S(1)}, u32[]{:S(2)}, u32[]{:S(2)}) collective-permute-start(bf16[256,256]{1,0:T(8,128)(2,1)S(1)} %add_convert_fusion.1.own_ref), channel_id=1, source_target_pairs={{0,4},{4,0},{8,12},{12,8},{1,5},{5,1},{9,13},{13,9},{2,6},{6,2},{1... | collective-permute-start | bytes 393224 | tf_op jit(solution)/shard_map/ppermute | solution.py:130
  24.2 1.2 %collective-permute-done.13.refs_1_ = bf16[48,256]{1,0:T(8,128)(2,1)S(1)} collective-permute-done((bf16[48,256]{1,0:T(8,128)(2,1)S(1)}, bf16[48,256]{1,0:T(8,128)(2,1)S(1)}, u32[]{:S(2)}, u32[]{:S(2)}) %collective-permute-start.13) | collective-permute-done | bytes 24608 | tf_op jit(solution)/shard_map/ppermute | solution.py:130
  25.5 0.6 %collective-permute-start.16 = (bf16[2,24,1024]{2,1,0:T(8,128)(2,1)S(1)}, bf16[2,24,1024]{2,1,0:T(8,128)(2,1)S(1)}, u32[]{:S(2)}, u32[]{:S(2)}) collective-permute-start(bf16[2,24,1024]{2,1,0:T(8,128)(2,1)S(1)} %pad_maximum_fusion.1), channel_id=1, source_target_pairs={{0,1},{1,0},{2,3},{3,2},{4,5},{5,4},{6,7},{7,6},{8,9},{9,8},{10,11... | collective-permute-start | bytes 294920 | tf_op jit(solution)/shard_map/ppermute | solution.py:156
  26.1 0.9 %collective-permute-done.16.other_ref = bf16[2,24,1024]{2,1,0:T(8,128)(2,1)S(1)} collective-permute-done((bf16[2,24,1024]{2,1,0:T(8,128)(2,1)S(1)}, bf16[2,24,1024]{2,1,0:T(8,128)(2,1)S(1)}, u32[]{:S(2)}, u32[]{:S(2)}) %collective-permute-start.16) | collective-permute-done | bytes 98336 | tf_op jit(solution)/shard_map/ppermute | solution.py:156
  27.4 1.2 %collective-permute-done.11.first_ref = bf16[256,256]{1,0:T(8,128)(2,1)S(1)} collective-permute-done((bf16[256,256]{1,0:T(8,128)(2,1)S(1)}, bf16[256,256]{1,0:T(8,128)(2,1)S(1)}, u32[]{:S(2)}, u32[]{:S(2)}) %collective-permute-start.11) | collective-permute-done | bytes 131104 | tf_op jit(solution)/shard_map/ppermute | solution.py:130
  29.2 1.2 %collective-permute-done.17 = f32[256,256]{1,0:T(8,128)S(1)} collective-permute-done((f32[256,256]{1,0:T(8,128)S(1)}, f32[256,256]{1,0:T(8,128)S(1)}, u32[]{:S(2)}, u32[]{:S(2)}) %collective-permute-start.17) | collective-permute-done | bytes 262176 | tf_op jit(solution)/shard_map/ppermute | solution.py:156
  30.5 1.6 %collective-permute-start.20 = (bf16[256,256]{1,0:T(8,128)(2,1)S(1)}, bf16[256,256]{1,0:T(8,128)(2,1)S(1)}, u32[]{:S(2)}, u32[]{:S(2)}) collective-permute-start(bf16[256,256]{1,0:T(8,128)(2,1)S(1)} %add_convert_fusion), channel_id=1, source_target_pairs={{0,2},{1,3},{2,0},{3,1},{4,6},{5,7},{6,4},{7,5},{8,10},{9,11},{10,... | collective-permute-start | bytes 393224 | tf_op jit(solution)/shard_map/ppermute | solution.py:156
  32.5 0.5 %collective-permute-start.19 = (f32[128,256]{1,0:T(8,128)S(1)}, f32[128,256]{1,0:T(8,128)S(1)}, u32[]{:S(2)}, u32[]{:S(2)}) collective-permute-start(f32[128,256]{1,0:T(8,128)S(1)} %get-tuple-element.62), channel_id=1, source_target_pairs={{0,1},{1,0},{2,3},{3,2},{4,5},{5,4},{6,7},{7,6},{8,9},{9,8},{10,11... | collective-permute-start | bytes 393224 | tf_op jit(solution)/shard_map/ppermute | solution.py:156
  33.0 3.1 %collective-permute-done.20 = bf16[256,256]{1,0:T(8,128)(2,1)S(1)} collective-permute-done((bf16[256,256]{1,0:T(8,128)(2,1)S(1)}, bf16[256,256]{1,0:T(8,128)(2,1)S(1)}, u32[]{:S(2)}, u32[]{:S(2)}) %collective-permute-start.20) | collective-permute-done | bytes 131104 | tf_op jit(solution)/shard_map/ppermute | solution.py:156
  36.1 0.7 %fusion = f32[256,256]{1,0:T(8,128)} fusion(f32[256,256]{1,0:T(8,128)S(1)} %get-tuple-element.58, f32[128,256]{1,0:T(8,128)S(1)} %collective-permute-done.19, f32[128,256]{1,0:T(8,128)S(1)} %collective-permute-done.18, bf16[256,256]{1,0:T(8,128)(2,1)S(1)} %collective-permute-done.20), kind=kLoop, calls=%fused_computation.1 | loop fusion | flops 262144 | bytes 917504 | tf_op jit(solution)/shard_map/add | solution.py:302
  (49 shorter events, 2.6 us)
Async XLA Ops:
  0.0 1.0 %copy-start.2 = (bf16[1,1,24,1024]{3,2,1,0:T(8,128)(2,1)S(1)}, bf16[1,1,24,1024]{3,2,1,0:T(8,128)(2,1)}, u32[]{:S(2)}) copy-start(bf16[1,1,24,1024]{3,2,1,0:T(8,128)(2,1)} %left_ref) | copy-start | bytes 147460
  0.0 1.0 %copy-start.1 = (bf16[1,1,24,1024]{3,2,1,0:T(8,128)(2,1)S(1)}, bf16[1,1,24,1024]{3,2,1,0:T(8,128)(2,1)}, u32[]{:S(2)}) copy-start(bf16[1,1,24,1024]{3,2,1,0:T(8,128)(2,1)} %right_ref) | copy-start | bytes 147460
  1.0 6.8 %collective-permute-start = (bf16[2,24,1024]{2,1,0:T(8,128)(2,1)S(1)}, bf16[2,24,1024]{2,1,0:T(8,128)(2,1)S(1)}, u32[]{:S(2)}, u32[]{:S(2)}) collective-permute-start(bf16[2,24,1024]{2,1,0:T(8,128)(2,1)S(1)} %shard_map.65.bases_ref), channel_id=1, source_target_pairs={{0,2},{1,3},{2,0},{3,1},{4,6},{5,7},{6,4},{7,5},{8,10},{9,11},{10,... | collective-permute-start | bytes 294920 | tf_op jit(solution)/shard_map/ppermute | solution.py:156
  4.0 3.9 %collective-permute-start.1 = (bf16[256,256]{1,0:T(8,128)(2,1)S(1)}, bf16[256,256]{1,0:T(8,128)(2,1)S(1)}, u32[]{:S(2)}, u32[]{:S(2)}) collective-permute-start(bf16[256,256]{1,0:T(8,128)(2,1)S(1)} %shard_map.64.block_ref.own_ref), channel_id=1, source_target_pairs={{0,1},{1,0},{2,3},{3,2},{4,5},{5,4},{6,7},{7,6},{8,9},{9,8},{10,11... | collective-permute-start | bytes 393224 | tf_op jit(solution)/shard_map/ppermute | solution.py:156
  4.0 7.1 %collective-permute-start.7 = (bf16[256,256]{1,0:T(8,128)(2,1)S(1)}, bf16[256,256]{1,0:T(8,128)(2,1)S(1)}, u32[]{:S(2)}, u32[]{:S(2)}) collective-permute-start(bf16[256,256]{1,0:T(8,128)(2,1)S(1)} %shard_map.64.block_ref.own_ref), channel_id=1, source_target_pairs={{0,1},{1,0},{2,3},{3,2},{4,8},{5,9},{6,10},{7,11},{8,4},{9,5},{10,... | collective-permute-start | bytes 393224 | tf_op jit(solution)/shard_map/ppermute | solution.py:142
  4.5 8.7 %collective-permute-start.6 = (bf16[256,256]{1,0:T(8,128)(2,1)S(1)}, bf16[256,256]{1,0:T(8,128)(2,1)S(1)}, u32[]{:S(2)}, u32[]{:S(2)}) collective-permute-start(bf16[256,256]{1,0:T(8,128)(2,1)S(1)} %shard_map.64.block_ref.own_ref), channel_id=1, source_target_pairs={{0,4},{4,0},{8,12},{12,8},{1,5},{5,1},{9,13},{13,9},{2,6},{6,2},{1... | collective-permute-start | bytes 393224 | tf_op jit(solution)/shard_map/ppermute | solution.py:130
  7.9 5.4 %copy-start = (bf16[1,1024,3,256]{3,1,2,0:T(8,128)(2,1)S(1)}, bf16[1,1024,3,256]{3,1,2,0:T(8,128)(2,1)}, u32[]{:S(2)}) copy-start(bf16[1,1024,3,256]{3,1,2,0:T(8,128)(2,1)} %param.10) | copy-start | bytes 4718596
  8.1 7.8 %collective-permute-start.2 = (bf16[2,24,1024]{2,1,0:T(8,128)(2,1)S(1)}, bf16[2,24,1024]{2,1,0:T(8,128)(2,1)S(1)}, u32[]{:S(2)}, u32[]{:S(2)}) collective-permute-start(bf16[2,24,1024]{2,1,0:T(8,128)(2,1)S(1)} %pad_maximum_fusion), channel_id=1, source_target_pairs={{0,1},{1,0},{2,3},{3,2},{4,5},{5,4},{6,7},{7,6},{8,9},{9,8},{10,11... | collective-permute-start | bytes 294920 | tf_op jit(solution)/shard_map/ppermute | solution.py:156
  8.1 5.8 %collective-permute-start.5 = (bf16[48,256]{1,0:T(8,128)(2,1)S(1)}, bf16[48,256]{1,0:T(8,128)(2,1)S(1)}, u32[]{:S(2)}, u32[]{:S(2)}) collective-permute-start(bf16[48,256]{1,0:T(8,128)(2,1)S(1)} %shard_map.66.refs_0_), channel_id=1, source_target_pairs={{0,12},{4,8},{8,4},{12,0},{1,13},{5,9},{9,5},{13,1},{2,14},{6,10},... | collective-permute-start | bytes 73736 | tf_op jit(solution)/shard_map/ppermute | solution.py:130
  11.1 4.7 %collective-permute-start.4 = (bf16[48,256]{1,0:T(8,128)(2,1)S(1)}, bf16[48,256]{1,0:T(8,128)(2,1)S(1)}, u32[]{:S(2)}, u32[]{:S(2)}) collective-permute-start(bf16[48,256]{1,0:T(8,128)(2,1)S(1)} %shard_map.66.refs_0_), channel_id=1, source_target_pairs={{0,8},{4,12},{8,0},{12,4},{1,9},{5,13},{9,1},{13,5},{2,10},{6,14},... | collective-permute-start | bytes 73736 | tf_op jit(solution)/shard_map/ppermute | solution.py:130
  11.1 4.7 %collective-permute-start.3 = (bf16[48,256]{1,0:T(8,128)(2,1)S(1)}, bf16[48,256]{1,0:T(8,128)(2,1)S(1)}, u32[]{:S(2)}, u32[]{:S(2)}) collective-permute-start(bf16[48,256]{1,0:T(8,128)(2,1)S(1)} %shard_map.66.refs_0_), channel_id=1, source_target_pairs={{0,4},{4,0},{8,12},{12,8},{1,5},{5,1},{9,13},{13,9},{2,6},{6,2},{1... | collective-permute-start | bytes 73736 | tf_op jit(solution)/shard_map/ppermute | solution.py:130
  16.2 1.6 %collective-permute-start.9 = (f32[256,256]{1,0:T(8,128)S(1)}, f32[256,256]{1,0:T(8,128)S(1)}, u32[]{:S(2)}, u32[]{:S(2)}) collective-permute-start(f32[256,256]{1,0:T(8,128)S(1)} %get-tuple-element.45), channel_id=1, source_target_pairs={{0,1},{1,0},{2,3},{3,2},{4,5},{5,4},{6,7},{7,6},{8,9},{9,8},{10,11... | collective-permute-start | bytes 786440 | tf_op jit(solution)/shard_map/ppermute | solution.py:156
  16.9 2.6 %collective-permute-start.12 = (f32[96,256]{1,0:T(8,128)S(1)}, f32[96,256]{1,0:T(8,128)S(1)}, u32[]{:S(2)}, u32[]{:S(2)}) collective-permute-start(f32[96,256]{1,0:T(8,128)S(1)} %get-tuple-element.47), channel_id=1, source_target_pairs={{0,1},{1,0},{2,3},{3,2},{4,5},{5,4},{6,7},{7,6},{8,9},{9,8},{10,11... | collective-permute-start | bytes 294920 | tf_op jit(solution)/shard_map/ppermute | solution.py:156
  17.4 4.1 %collective-permute-start.8 = (f32[256,256]{1,0:T(8,128)S(1)}, f32[256,256]{1,0:T(8,128)S(1)}, u32[]{:S(2)}, u32[]{:S(2)}) collective-permute-start(f32[256,256]{1,0:T(8,128)S(1)} %get-tuple-element.43), channel_id=1, source_target_pairs={{0,1},{1,0},{2,3},{3,2},{4,5},{5,4},{6,7},{7,6},{8,9},{9,8},{10,11... | collective-permute-start | bytes 786440 | tf_op jit(solution)/shard_map/ppermute | solution.py:156
  17.9 5.6 %collective-permute-start.10 = (bf16[256,256]{1,0:T(8,128)(2,1)S(1)}, bf16[256,256]{1,0:T(8,128)(2,1)S(1)}, u32[]{:S(2)}, u32[]{:S(2)}) collective-permute-start(bf16[256,256]{1,0:T(8,128)(2,1)S(1)} %add_convert_fusion.2), channel_id=1, source_target_pairs={{0,2},{1,3},{2,0},{3,1},{4,6},{5,7},{6,4},{7,5},{8,10},{9,11},{10,... | collective-permute-start | bytes 393224 | tf_op jit(solution)/shard_map/ppermute | solution.py:156
  19.5 5.9 %collective-permute-start.14 = (bf16[96,256]{1,0:T(8,128)(2,1)S(1)}, bf16[96,256]{1,0:T(8,128)(2,1)S(1)}, u32[]{:S(2)}, u32[]{:S(2)}) collective-permute-start(bf16[96,256]{1,0:T(8,128)(2,1)S(1)} %add_convert_fusion.3.refs_0_), channel_id=1, source_target_pairs={{0,8},{1,13},{2,10},{3,15},{4,12},{5,9},{6,14},{7,11},{8,0},{9,5},... | collective-permute-start | bytes 147464 | tf_op jit(solution)/shard_map/ppermute | solution.py:152
  21.6 3.8 %collective-permute-start.13 = (bf16[48,256]{1,0:T(8,128)(2,1)S(1)}, bf16[48,256]{1,0:T(8,128)(2,1)S(1)}, u32[]{:S(2)}, u32[]{:S(2)}) collective-permute-start(bf16[48,256]{1,0:T(8,128)(2,1)S(1)} %slice.22), channel_id=1, source_target_pairs={{0,4},{4,0},{8,12},{12,8},{1,5},{5,1},{9,13},{13,9},{2,6},{6,2},{1... | collective-permute-start | bytes 73736 | tf_op jit(solution)/shard_map/ppermute | solution.py:130
  23.5 5.0 %collective-permute-start.11 = (bf16[256,256]{1,0:T(8,128)(2,1)S(1)}, bf16[256,256]{1,0:T(8,128)(2,1)S(1)}, u32[]{:S(2)}, u32[]{:S(2)}) collective-permute-start(bf16[256,256]{1,0:T(8,128)(2,1)S(1)} %add_convert_fusion.1.own_ref), channel_id=1, source_target_pairs={{0,4},{4,0},{8,12},{12,8},{1,5},{5,1},{9,13},{13,9},{2,6},{6,2},{1... | collective-permute-start | bytes 393224 | tf_op jit(solution)/shard_map/ppermute | solution.py:130
  25.4 2.0 %collective-permute-start.15 = (bf16[256,256]{1,0:T(8,128)(2,1)S(1)}, bf16[256,256]{1,0:T(8,128)(2,1)S(1)}, u32[]{:S(2)}, u32[]{:S(2)}) collective-permute-start(bf16[256,256]{1,0:T(8,128)(2,1)S(1)} %add_convert_fusion.1.own_ref), channel_id=1, source_target_pairs={{0,1},{1,0},{2,3},{3,2},{4,8},{5,9},{6,10},{7,11},{8,4},{9,5},{10,... | collective-permute-start | bytes 393224 | tf_op jit(solution)/shard_map/ppermute | solution.py:142
  25.5 1.5 %collective-permute-start.16 = (bf16[2,24,1024]{2,1,0:T(8,128)(2,1)S(1)}, bf16[2,24,1024]{2,1,0:T(8,128)(2,1)S(1)}, u32[]{:S(2)}, u32[]{:S(2)}) collective-permute-start(bf16[2,24,1024]{2,1,0:T(8,128)(2,1)S(1)} %pad_maximum_fusion.1), channel_id=1, source_target_pairs={{0,1},{1,0},{2,3},{3,2},{4,5},{5,4},{6,7},{7,6},{8,9},{9,8},{10,11... | collective-permute-start | bytes 294920 | tf_op jit(solution)/shard_map/ppermute | solution.py:156
  28.8 1.6 %collective-permute-start.17 = (f32[256,256]{1,0:T(8,128)S(1)}, f32[256,256]{1,0:T(8,128)S(1)}, u32[]{:S(2)}, u32[]{:S(2)}) collective-permute-start(f32[256,256]{1,0:T(8,128)S(1)} %shard_map.72), channel_id=1, source_target_pairs={{0,1},{1,0},{2,3},{3,2},{4,5},{5,4},{6,7},{7,6},{8,9},{9,8},{10,11... | collective-permute-start | bytes 786440 | tf_op jit(solution)/shard_map/ppermute | solution.py:156
  30.5 5.6 %collective-permute-start.20 = (bf16[256,256]{1,0:T(8,128)(2,1)S(1)}, bf16[256,256]{1,0:T(8,128)(2,1)S(1)}, u32[]{:S(2)}, u32[]{:S(2)}) collective-permute-start(bf16[256,256]{1,0:T(8,128)(2,1)S(1)} %add_convert_fusion), channel_id=1, source_target_pairs={{0,2},{1,3},{2,0},{3,1},{4,6},{5,7},{6,4},{7,5},{8,10},{9,11},{10,... | collective-permute-start | bytes 393224 | tf_op jit(solution)/shard_map/ppermute | solution.py:156
  32.4 3.6 %collective-permute-start.18 = (f32[128,256]{1,0:T(8,128)S(1)}, f32[128,256]{1,0:T(8,128)S(1)}, u32[]{:S(2)}, u32[]{:S(2)}) collective-permute-start(f32[128,256]{1,0:T(8,128)S(1)} %get-tuple-element.61), channel_id=1, source_target_pairs={{0,1},{1,0},{2,3},{3,2},{4,5},{5,4},{6,7},{7,6},{8,9},{9,8},{10,11... | collective-permute-start | bytes 393224 | tf_op jit(solution)/shard_map/ppermute | solution.py:156
  32.5 3.6 %collective-permute-start.19 = (f32[128,256]{1,0:T(8,128)S(1)}, f32[128,256]{1,0:T(8,128)S(1)}, u32[]{:S(2)}, u32[]{:S(2)}) collective-permute-start(f32[128,256]{1,0:T(8,128)S(1)} %get-tuple-element.62), channel_id=1, source_target_pairs={{0,1},{1,0},{2,3},{3,2},{4,5},{5,4},{6,7},{7,6},{8,9},{9,8},{10,11... | collective-permute-start | bytes 393224 | tf_op jit(solution)/shard_map/ppermute | solution.py:156
  (1 other events, 1.0 us)

commit v20 on v19

--- a/solution.py
+++ b/solution.py
@@ -218,8 +218,7 @@
     coefficient_refs, refs = refs[:4], refs[4:]
     base_refs, refs = refs[: len(turns)], refs[len(turns) :]
     last = 0 in turns
-    sums_before, refs = (refs[:1], refs[1:]) if 3 not in turns else ((), refs)
-    ranks_ref, refs = (refs[0], refs[1:]) if last else (None, refs)
+    (before_ref, ranks_ref), refs = (refs[:2], refs[2:]) if last else ((None, None), refs)
     bases_refs = (bases_ref, across_ref)
     totals = []
     parts = far_parts(near_choice, turns, columns_ref, bases_refs, coefficient_refs)
@@ -227,12 +226,12 @@
         total += base_ref[...]
         out_ref[...] = total
         totals.append((cut, total.astype(BF)))
+    if not last:
+        return
+    rows = before_ref.shape[0]
+    cut = pl.ds(pl.multiple_of((lax.axis_index("list") ^ 3) * rows, rows), rows)
+    totals.append((cut, before_ref[...].astype(BF)))
     sums = right_products(totals, (*bases_refs, other_ref))
-    for ref in sums_before:
-        sums += ref[...]
-    if not last:
-        refs[-1][...] = sums
-        return
     groups = under_rank(sums, (0, 2, 1, 3), bases_ref.shape[1], ranks_ref)
     refs[-2][...] = jnp.concatenate(groups)
     refs[-1][...] = jnp.concatenate(groups[2:] + groups[:2])
@@ -276,10 +275,10 @@
         return kernel_call(kernel, outs, operands, cost * len(turns) * flops // 4)
 
     base = call(near_kernel, (3, 2, 1, 0), (near, *beside), cost=0)
-    send, sums = call(first_kernel, (3,), (*operands, base[0]), [small])
+    (send,) = call(first_kernel, (3,), (*operands, base[0]))
     arrived = list_swap(send, 1)
     crossing, send, keep, own, other = call(
-        first_kernel, (2, 1, 0), (*operands, *base[1:], sums, tile_ranks), [small] * 2
+        first_kernel, (2, 1, 0), (*operands, *base[1:], send, tile_ranks), [small] * 2
     )
     crossed = list_swap((crossing + arrived).astype(BF), 2)
     own = (own + list_swap(other, 1)).astype(BF)

time: 37 us -> 36.8 us (level)
  no operation moved by 1% of the time
where the time goes in v20:
time: 36.8 us; the launch traced here: 36.7 us
  starting transfers between devices  18.5 us (50%)
  waiting for transfers between devices  11.9 us (32%)
  Pallas kernels  2.81 us (8%)
  between operations  1.56 us (4%)
  local copies, waits for them, and re-layouts  1.01 us (3%)
  other arithmetic  0.89 us (2%)
    ppermute x12, starting transfers between devices, list_swap(): lax.ppermute(block, 'list', [(i, i ^ bit) for i in range(lax.axis_size('l...  8.1 us
    ppermute x6, starting transfers between devices, tile_swap(): lax.ppermute(block, 'tile', [(i, i ^ turn) for i in range(lax.axis_size('...  7.77 us
    ppermute x12, waiting for transfers between devices, list_swap(): lax.ppermute(block, 'list', [(i, i ^ bit) for i in range(lax.axis_size('l...  7.51 us
    ppermute x6, waiting for transfers between devices, tile_swap(): lax.ppermute(block, 'tile', [(i, i ^ turn) for i in range(lax.axis_size('...  4.35 us
    pallas_call x10, Pallas kernels, kernel_call(): pl.pallas_call(kernel, out_shape=tuple((jax.ShapeDtypeStruct(shape, kind)...  2.81 us
    ppermute x1, starting transfers between devices, far_swap(): return lax.ppermute(block, ('tile', 'list'), route)  2.09 us
    unnamed x8, local copies, waits for them, and re-layouts  0.97 us
    add x1, other arithmetic, one_slot(): return keep + list_swap_in_pieces(send, 1, 2) + crossed  0.75 us
  transfers between devices with their start and end apart: 21, of which 9 were waited for; matrix products, arithmetic and copies ran while one was open for 0% of the time, Pallas kernels for 6%

profile of v20, /device:TPU:0, one launch (start us, length us, event | category | flops | bytes accessed | tf_op | source)
XLA Modules:
  0.0 36.7 jit_solution(4897542544476925613)
XLA Ops:
  0.0 1.0 %copy-done.3 = f32[256,256]{1,0:T(8,128)S(1)} copy-done((f32[256,256]{1,0:T(8,128)S(1)}, f32[256,256]{1,0:T(8,128)}, u32[]{:S(2)}) %copy-start.3) | copy-done | bytes 262168
  1.0 3.0 %collective-permute-start = (bf16[2,24,1024]{2,1,0:T(8,128)(2,1)S(1)}, bf16[2,24,1024]{2,1,0:T(8,128)(2,1)S(1)}, u32[]{:S(2)}, u32[]{:S(2)}) collective-permute-start(bf16[2,24,1024]{2,1,0:T(8,128)(2,1)S(1)} %shard_map.65.bases_ref), channel_id=1, source_target_pairs={{0,2},{1,3},{2,0},{3,1},{4,6},{5,7},{6,4},{7,5},{8,10},{9,11},{10,... | collective-permute-start | bytes 294920 | tf_op jit(solution)/shard_map/ppermute | solution.py:156
  4.0 0.5 %collective-permute-start.7 = (bf16[256,256]{1,0:T(8,128)(2,1)S(1)}, bf16[256,256]{1,0:T(8,128)(2,1)S(1)}, u32[]{:S(2)}, u32[]{:S(2)}) collective-permute-start(bf16[256,256]{1,0:T(8,128)(2,1)S(1)} %shard_map.64.block_ref.own_ref), channel_id=1, source_target_pairs={{0,1},{1,0},{2,3},{3,2},{4,8},{5,9},{6,10},{7,11},{8,4},{9,5},{10,... | collective-permute-start | bytes 393224 | tf_op jit(solution)/shard_map/ppermute | solution.py:142
  4.5 2.6 %collective-permute-start.6 = (bf16[256,256]{1,0:T(8,128)(2,1)S(1)}, bf16[256,256]{1,0:T(8,128)(2,1)S(1)}, u32[]{:S(2)}, u32[]{:S(2)}) collective-permute-start(bf16[256,256]{1,0:T(8,128)(2,1)S(1)} %shard_map.64.block_ref.own_ref), channel_id=1, source_target_pairs={{0,4},{4,0},{8,12},{12,8},{1,5},{5,1},{9,13},{13,9},{2,6},{6,2},{1... | collective-permute-start | bytes 393224 | tf_op jit(solution)/shard_map/ppermute | solution.py:130
  8.1 3.0 %collective-permute-start.5 = (bf16[48,256]{1,0:T(8,128)(2,1)S(1)}, bf16[48,256]{1,0:T(8,128)(2,1)S(1)}, u32[]{:S(2)}, u32[]{:S(2)}) collective-permute-start(bf16[48,256]{1,0:T(8,128)(2,1)S(1)} %shard_map.66.refs_0_), channel_id=1, source_target_pairs={{0,12},{4,8},{8,4},{12,0},{1,13},{5,9},{9,5},{13,1},{2,14},{6,10},... | collective-permute-start | bytes 73736 | tf_op jit(solution)/shard_map/ppermute | solution.py:130
  11.1 1.5 %collective-permute-start.3 = (bf16[48,256]{1,0:T(8,128)(2,1)S(1)}, bf16[48,256]{1,0:T(8,128)(2,1)S(1)}, u32[]{:S(2)}, u32[]{:S(2)}) collective-permute-start(bf16[48,256]{1,0:T(8,128)(2,1)S(1)} %shard_map.66.refs_0_), channel_id=1, source_target_pairs={{0,4},{4,0},{8,12},{12,8},{1,5},{5,1},{9,13},{13,9},{2,6},{6,2},{1... | collective-permute-start | bytes 73736 | tf_op jit(solution)/shard_map/ppermute | solution.py:130
  13.3 0.6 %shard_map.67 = (f32[256,256]{1,0:T(8,128)S(1)}, f32[256,256]{1,0:T(8,128)S(1)}, f32[256,256]{1,0:T(8,128)S(1)}, f32[256,256]{1,0:T(8,128)S(1)}) custom-call(bf16[3,1024,256]{2,1,0:T(8,128)(2,1)S(1)} %bitcast.3, bf16[256,256]{1,0:T(8,128)(2,1)S(1)} %shard_map.64.block_ref.own_ref, bf16[256,256]{1,0:T(8,128)(2,1)S(1)} %collective-permute-done.6.first_ref, ...), custom_call_target="tpu_custom_call" | custom-call | tf_op jit(solution)/shard_map/pallas_call | solution.py:77
  13.9 1.9 %collective-permute-done.4.refs_2_ = bf16[48,256]{1,0:T(8,128)(2,1)S(1)} collective-permute-done((bf16[48,256]{1,0:T(8,128)(2,1)S(1)}, bf16[48,256]{1,0:T(8,128)(2,1)S(1)}, u32[]{:S(2)}, u32[]{:S(2)}) %collective-permute-start.4) | collective-permute-done | bytes 24608 | tf_op jit(solution)/shard_map/ppermute | solution.py:130
  16.2 0.5 %shard_map.69 = (f32[256,256]{1,0:T(8,128)S(1)}, f32[256,256]{1,0:T(8,128)S(1)}, f32[256,256]{1,0:T(8,128)S(1)}, f32[96,256]{1,0:T(8,128)S(1)}, f32[96,256]{1,0:T(8,128)S(1)}) custom-call(s32[1,1]{1,0:T(1,128)S(6)} %copy.8.columns_ref, bf16[2,24,1024]{2,1,0:T(8,128)(2,1)S(1)} %shard_map.65.bases_ref, ...), custom_call_target="tpu_custom_call" | custom-call | flops 301989888 | bytes 294912 | tf_op jit(solution)/shard_map/pallas_call | solution.py:77
  16.7 0.6 %collective-permute-start.12 = (f32[96,256]{1,0:T(8,128)S(1)}, f32[96,256]{1,0:T(8,128)S(1)}, u32[]{:S(2)}, u32[]{:S(2)}) collective-permute-start(f32[96,256]{1,0:T(8,128)S(1)} %get-tuple-element.43), channel_id=1, source_target_pairs={{0,1},{1,0},{2,3},{3,2},{4,5},{5,4},{6,7},{7,6},{8,9},{9,8},{10,11... | collective-permute-start | bytes 294920 | tf_op jit(solution)/shard_map/ppermute | solution.py:156
  17.7 1.6 %collective-permute-start.10 = (bf16[256,256]{1,0:T(8,128)(2,1)S(1)}, bf16[256,256]{1,0:T(8,128)(2,1)S(1)}, u32[]{:S(2)}, u32[]{:S(2)}) collective-permute-start(bf16[256,256]{1,0:T(8,128)(2,1)S(1)} %add_convert_fusion.2), channel_id=1, source_target_pairs={{0,2},{1,3},{2,0},{3,1},{4,6},{5,7},{6,4},{7,5},{8,10},{9,11},{10,... | collective-permute-start | bytes 393224 | tf_op jit(solution)/shard_map/ppermute | solution.py:156
  19.3 2.1 %collective-permute-start.14 = (bf16[96,256]{1,0:T(8,128)(2,1)S(1)}, bf16[96,256]{1,0:T(8,128)(2,1)S(1)}, u32[]{:S(2)}, u32[]{:S(2)}) collective-permute-start(bf16[96,256]{1,0:T(8,128)(2,1)S(1)} %add_convert_fusion.3.refs_0_), channel_id=1, source_target_pairs={{0,8},{1,13},{2,10},{3,15},{4,12},{5,9},{6,14},{7,11},{8,0},{9,5},... | collective-permute-start | bytes 147464 | tf_op jit(solution)/shard_map/ppermute | solution.py:152
  21.4 1.9 %collective-permute-done.10 = bf16[256,256]{1,0:T(8,128)(2,1)S(1)} collective-permute-done((bf16[256,256]{1,0:T(8,128)(2,1)S(1)}, bf16[256,256]{1,0:T(8,128)(2,1)S(1)}, u32[]{:S(2)}, u32[]{:S(2)}) %collective-permute-start.10) | collective-permute-done | bytes 131104 | tf_op jit(solution)/shard_map/ppermute | solution.py:156
  23.4 0.7 %collective-permute-start.11 = (bf16[256,256]{1,0:T(8,128)(2,1)S(1)}, bf16[256,256]{1,0:T(8,128)(2,1)S(1)}, u32[]{:S(2)}, u32[]{:S(2)}) collective-permute-start(bf16[256,256]{1,0:T(8,128)(2,1)S(1)} %add_convert_fusion.1.own_ref), channel_id=1, source_target_pairs={{0,4},{4,0},{8,12},{12,8},{1,5},{5,1},{9,13},{13,9},{2,6},{6,2},{1... | collective-permute-start | bytes 393224 | tf_op jit(solution)/shard_map/ppermute | solution.py:130
  24.0 1.2 %collective-permute-done.13.refs_1_ = bf16[48,256]{1,0:T(8,128)(2,1)S(1)} collective-permute-done((bf16[48,256]{1,0:T(8,128)(2,1)S(1)}, bf16[48,256]{1,0:T(8,128)(2,1)S(1)}, u32[]{:S(2)}, u32[]{:S(2)}) %collective-permute-start.13) | collective-permute-done | bytes 24608 | tf_op jit(solution)/shard_map/ppermute | solution.py:130
  25.4 0.6 %collective-permute-start.16 = (bf16[2,24,1024]{2,1,0:T(8,128)(2,1)S(1)}, bf16[2,24,1024]{2,1,0:T(8,128)(2,1)S(1)}, u32[]{:S(2)}, u32[]{:S(2)}) collective-permute-start(bf16[2,24,1024]{2,1,0:T(8,128)(2,1)S(1)} %pad_maximum_fusion.1), channel_id=1, source_target_pairs={{0,1},{1,0},{2,3},{3,2},{4,5},{5,4},{6,7},{7,6},{8,9},{9,8},{10,11... | collective-permute-start | bytes 294920 | tf_op jit(solution)/shard_map/ppermute | solution.py:156
  25.9 0.9 %collective-permute-done.16.other_ref = bf16[2,24,1024]{2,1,0:T(8,128)(2,1)S(1)} collective-permute-done((bf16[2,24,1024]{2,1,0:T(8,128)(2,1)S(1)}, bf16[2,24,1024]{2,1,0:T(8,128)(2,1)S(1)}, u32[]{:S(2)}, u32[]{:S(2)}) %collective-permute-start.16) | collective-permute-done | bytes 98336 | tf_op jit(solution)/shard_map/ppermute | solution.py:156
  27.2 1.2 %collective-permute-done.11.first_ref = bf16[256,256]{1,0:T(8,128)(2,1)S(1)} collective-permute-done((bf16[256,256]{1,0:T(8,128)(2,1)S(1)}, bf16[256,256]{1,0:T(8,128)(2,1)S(1)}, u32[]{:S(2)}, u32[]{:S(2)}) %collective-permute-start.11) | collective-permute-done | bytes 131104 | tf_op jit(solution)/shard_map/ppermute | solution.py:130
  29.1 1.2 %collective-permute-done.17 = f32[256,256]{1,0:T(8,128)S(1)} collective-permute-done((f32[256,256]{1,0:T(8,128)S(1)}, f32[256,256]{1,0:T(8,128)S(1)}, u32[]{:S(2)}, u32[]{:S(2)}) %collective-permute-start.17) | collective-permute-done | bytes 262176 | tf_op jit(solution)/shard_map/ppermute | solution.py:156
  30.3 1.6 %collective-permute-start.20 = (bf16[256,256]{1,0:T(8,128)(2,1)S(1)}, bf16[256,256]{1,0:T(8,128)(2,1)S(1)}, u32[]{:S(2)}, u32[]{:S(2)}) collective-permute-start(bf16[256,256]{1,0:T(8,128)(2,1)S(1)} %add_convert_fusion), channel_id=1, source_target_pairs={{0,2},{1,3},{2,0},{3,1},{4,6},{5,7},{6,4},{7,5},{8,10},{9,11},{10,... | collective-permute-start | bytes 393224 | tf_op jit(solution)/shard_map/ppermute | solution.py:156
  31.9 0.4 shard_map.73
  32.4 0.5 %collective-permute-start.19 = (f32[128,256]{1,0:T(8,128)S(1)}, f32[128,256]{1,0:T(8,128)S(1)}, u32[]{:S(2)}, u32[]{:S(2)}) collective-permute-start(f32[128,256]{1,0:T(8,128)S(1)} %get-tuple-element.58), channel_id=1, source_target_pairs={{0,1},{1,0},{2,3},{3,2},{4,5},{5,4},{6,7},{7,6},{8,9},{9,8},{10,11... | collective-permute-start | bytes 393224 | tf_op jit(solution)/shard_map/ppermute | solution.py:156
  32.9 3.1 %collective-permute-done.20 = bf16[256,256]{1,0:T(8,128)(2,1)S(1)} collective-permute-done((bf16[256,256]{1,0:T(8,128)(2,1)S(1)}, bf16[256,256]{1,0:T(8,128)(2,1)S(1)}, u32[]{:S(2)}, u32[]{:S(2)}) %collective-permute-start.20) | collective-permute-done | bytes 131104 | tf_op jit(solution)/shard_map/ppermute | solution.py:156
  35.9 0.7 %fusion = f32[256,256]{1,0:T(8,128)} fusion(f32[256,256]{1,0:T(8,128)S(1)} %get-tuple-element.54, f32[128,256]{1,0:T(8,128)S(1)} %collective-permute-done.19, f32[128,256]{1,0:T(8,128)S(1)} %collective-permute-done.18, bf16[256,256]{1,0:T(8,128)(2,1)S(1)} %collective-permute-done.20), kind=kLoop, calls=%fused_computation.1 | loop fusion | flops 262144 | bytes 917504 | tf_op jit(solution)/shard_map/add | solution.py:301
  (49 shorter events, 2.4 us)
Async XLA Ops:
  0.0 1.0 %copy-start.2 = (bf16[1,1,24,1024]{3,2,1,0:T(8,128)(2,1)S(1)}, bf16[1,1,24,1024]{3,2,1,0:T(8,128)(2,1)}, u32[]{:S(2)}) copy-start(bf16[1,1,24,1024]{3,2,1,0:T(8,128)(2,1)} %left_ref) | copy-start | bytes 147460
  0.0 1.0 %copy-start.1 = (bf16[1,1,24,1024]{3,2,1,0:T(8,128)(2,1)S(1)}, bf16[1,1,24,1024]{3,2,1,0:T(8,128)(2,1)}, u32[]{:S(2)}) copy-start(bf16[1,1,24,1024]{3,2,1,0:T(8,128)(2,1)} %right_ref) | copy-start | bytes 147460
  1.0 6.8 %collective-permute-start = (bf16[2,24,1024]{2,1,0:T(8,128)(2,1)S(1)}, bf16[2,24,1024]{2,1,0:T(8,128)(2,1)S(1)}, u32[]{:S(2)}, u32[]{:S(2)}) collective-permute-start(bf16[2,24,1024]{2,1,0:T(8,128)(2,1)S(1)} %shard_map.65.bases_ref), channel_id=1, source_target_pairs={{0,2},{1,3},{2,0},{3,1},{4,6},{5,7},{6,4},{7,5},{8,10},{9,11},{10,... | collective-permute-start | bytes 294920 | tf_op jit(solution)/shard_map/ppermute | solution.py:156
  4.0 3.9 %collective-permute-start.1 = (bf16[256,256]{1,0:T(8,128)(2,1)S(1)}, bf16[256,256]{1,0:T(8,128)(2,1)S(1)}, u32[]{:S(2)}, u32[]{:S(2)}) collective-permute-start(bf16[256,256]{1,0:T(8,128)(2,1)S(1)} %shard_map.64.block_ref.own_ref), channel_id=1, source_target_pairs={{0,1},{1,0},{2,3},{3,2},{4,5},{5,4},{6,7},{7,6},{8,9},{9,8},{10,11... | collective-permute-start | bytes 393224 | tf_op jit(solution)/shard_map/ppermute | solution.py:156
  4.0 7.1 %collective-permute-start.7 = (bf16[256,256]{1,0:T(8,128)(2,1)S(1)}, bf16[256,256]{1,0:T(8,128)(2,1)S(1)}, u32[]{:S(2)}, u32[]{:S(2)}) collective-permute-start(bf16[256,256]{1,0:T(8,128)(2,1)S(1)} %shard_map.64.block_ref.own_ref), channel_id=1, source_target_pairs={{0,1},{1,0},{2,3},{3,2},{4,8},{5,9},{6,10},{7,11},{8,4},{9,5},{10,... | collective-permute-start | bytes 393224 | tf_op jit(solution)/shard_map/ppermute | solution.py:142
  4.5 8.7 %collective-permute-start.6 = (bf16[256,256]{1,0:T(8,128)(2,1)S(1)}, bf16[256,256]{1,0:T(8,128)(2,1)S(1)}, u32[]{:S(2)}, u32[]{:S(2)}) collective-permute-start(bf16[256,256]{1,0:T(8,128)(2,1)S(1)} %shard_map.64.block_ref.own_ref), channel_id=1, source_target_pairs={{0,4},{4,0},{8,12},{12,8},{1,5},{5,1},{9,13},{13,9},{2,6},{6,2},{1... | collective-permute-start | bytes 393224 | tf_op jit(solution)/shard_map/ppermute | solution.py:130
  7.9 5.4 %copy-start = (bf16[1,1024,3,256]{3,1,2,0:T(8,128)(2,1)S(1)}, bf16[1,1024,3,256]{3,1,2,0:T(8,128)(2,1)}, u32[]{:S(2)}) copy-start(bf16[1,1024,3,256]{3,1,2,0:T(8,128)(2,1)} %param.10) | copy-start | bytes 4718596
  8.1 7.8 %collective-permute-start.2 = (bf16[2,24,1024]{2,1,0:T(8,128)(2,1)S(1)}, bf16[2,24,1024]{2,1,0:T(8,128)(2,1)S(1)}, u32[]{:S(2)}, u32[]{:S(2)}) collective-permute-start(bf16[2,24,1024]{2,1,0:T(8,128)(2,1)S(1)} %pad_maximum_fusion), channel_id=1, source_target_pairs={{0,1},{1,0},{2,3},{3,2},{4,5},{5,4},{6,7},{7,6},{8,9},{9,8},{10,11... | collective-permute-start | bytes 294920 | tf_op jit(solution)/shard_map/ppermute | solution.py:156
  8.1 5.8 %collective-permute-start.5 = (bf16[48,256]{1,0:T(8,128)(2,1)S(1)}, bf16[48,256]{1,0:T(8,128)(2,1)S(1)}, u32[]{:S(2)}, u32[]{:S(2)}) collective-permute-start(bf16[48,256]{1,0:T(8,128)(2,1)S(1)} %shard_map.66.refs_0_), channel_id=1, source_target_pairs={{0,12},{4,8},{8,4},{12,0},{1,13},{5,9},{9,5},{13,1},{2,14},{6,10},... | collective-permute-start | bytes 73736 | tf_op jit(solution)/shard_map/ppermute | solution.py:130
  11.1 4.7 %collective-permute-start.4 = (bf16[48,256]{1,0:T(8,128)(2,1)S(1)}, bf16[48,256]{1,0:T(8,128)(2,1)S(1)}, u32[]{:S(2)}, u32[]{:S(2)}) collective-permute-start(bf16[48,256]{1,0:T(8,128)(2,1)S(1)} %shard_map.66.refs_0_), channel_id=1, source_target_pairs={{0,8},{4,12},{8,0},{12,4},{1,9},{5,13},{9,1},{13,5},{2,10},{6,14},... | collective-permute-start | bytes 73736 | tf_op jit(solution)/shard_map/ppermute | solution.py:130
  11.1 4.7 %collective-permute-start.3 = (bf16[48,256]{1,0:T(8,128)(2,1)S(1)}, bf16[48,256]{1,0:T(8,128)(2,1)S(1)}, u32[]{:S(2)}, u32[]{:S(2)}) collective-permute-start(bf16[48,256]{1,0:T(8,128)(2,1)S(1)} %shard_map.66.refs_0_), channel_id=1, source_target_pairs={{0,4},{4,0},{8,12},{12,8},{1,5},{5,1},{9,13},{13,9},{2,6},{6,2},{1... | collective-permute-start | bytes 73736 | tf_op jit(solution)/shard_map/ppermute | solution.py:130
  16.1 1.6 %collective-permute-start.9 = (f32[256,256]{1,0:T(8,128)S(1)}, f32[256,256]{1,0:T(8,128)S(1)}, u32[]{:S(2)}, u32[]{:S(2)}) collective-permute-start(f32[256,256]{1,0:T(8,128)S(1)} %shard_map.68.refs_7_), channel_id=1, source_target_pairs={{0,1},{1,0},{2,3},{3,2},{4,5},{5,4},{6,7},{7,6},{8,9},{9,8},{10,11... | collective-permute-start | bytes 786440 | tf_op jit(solution)/shard_map/ppermute | solution.py:156
  16.7 2.6 %collective-permute-start.12 = (f32[96,256]{1,0:T(8,128)S(1)}, f32[96,256]{1,0:T(8,128)S(1)}, u32[]{:S(2)}, u32[]{:S(2)}) collective-permute-start(f32[96,256]{1,0:T(8,128)S(1)} %get-tuple-element.43), channel_id=1, source_target_pairs={{0,1},{1,0},{2,3},{3,2},{4,5},{5,4},{6,7},{7,6},{8,9},{9,8},{10,11... | collective-permute-start | bytes 294920 | tf_op jit(solution)/shard_map/ppermute | solution.py:156
  17.3 4.1 %collective-permute-start.8 = (f32[256,256]{1,0:T(8,128)S(1)}, f32[256,256]{1,0:T(8,128)S(1)}, u32[]{:S(2)}, u32[]{:S(2)}) collective-permute-start(f32[256,256]{1,0:T(8,128)S(1)} %get-tuple-element.40), channel_id=1, source_target_pairs={{0,1},{1,0},{2,3},{3,2},{4,5},{5,4},{6,7},{7,6},{8,9},{9,8},{10,11... | collective-permute-start | bytes 786440 | tf_op jit(solution)/shard_map/ppermute | solution.py:156
  17.7 5.6 %collective-permute-start.10 = (bf16[256,256]{1,0:T(8,128)(2,1)S(1)}, bf16[256,256]{1,0:T(8,128)(2,1)S(1)}, u32[]{:S(2)}, u32[]{:S(2)}) collective-permute-start(bf16[256,256]{1,0:T(8,128)(2,1)S(1)} %add_convert_fusion.2), channel_id=1, source_target_pairs={{0,2},{1,3},{2,0},{3,1},{4,6},{5,7},{6,4},{7,5},{8,10},{9,11},{10,... | collective-permute-start | bytes 393224 | tf_op jit(solution)/shard_map/ppermute | solution.py:156
  19.3 5.9 %collective-permute-start.14 = (bf16[96,256]{1,0:T(8,128)(2,1)S(1)}, bf16[96,256]{1,0:T(8,128)(2,1)S(1)}, u32[]{:S(2)}, u32[]{:S(2)}) collective-permute-start(bf16[96,256]{1,0:T(8,128)(2,1)S(1)} %add_convert_fusion.3.refs_0_), channel_id=1, source_target_pairs={{0,8},{1,13},{2,10},{3,15},{4,12},{5,9},{6,14},{7,11},{8,0},{9,5},... | collective-permute-start | bytes 147464 | tf_op jit(solution)/shard_map/ppermute | solution.py:152
  21.4 3.8 %collective-permute-start.13 = (bf16[48,256]{1,0:T(8,128)(2,1)S(1)}, bf16[48,256]{1,0:T(8,128)(2,1)S(1)}, u32[]{:S(2)}, u32[]{:S(2)}) collective-permute-start(bf16[48,256]{1,0:T(8,128)(2,1)S(1)} %slice.22), channel_id=1, source_target_pairs={{0,4},{4,0},{8,12},{12,8},{1,5},{5,1},{9,13},{13,9},{2,6},{6,2},{1... | collective-permute-start | bytes 73736 | tf_op jit(solution)/shard_map/ppermute | solution.py:130
  23.4 5.0 %collective-permute-start.11 = (bf16[256,256]{1,0:T(8,128)(2,1)S(1)}, bf16[256,256]{1,0:T(8,128)(2,1)S(1)}, u32[]{:S(2)}, u32[]{:S(2)}) collective-permute-start(bf16[256,256]{1,0:T(8,128)(2,1)S(1)} %add_convert_fusion.1.own_ref), channel_id=1, source_target_pairs={{0,4},{4,0},{8,12},{12,8},{1,5},{5,1},{9,13},{13,9},{2,6},{6,2},{1... | collective-permute-start | bytes 393224 | tf_op jit(solution)/shard_map/ppermute | solution.py:130
  25.3 2.0 %collective-permute-start.15 = (bf16[256,256]{1,0:T(8,128)(2,1)S(1)}, bf16[256,256]{1,0:T(8,128)(2,1)S(1)}, u32[]{:S(2)}, u32[]{:S(2)}) collective-permute-start(bf16[256,256]{1,0:T(8,128)(2,1)S(1)} %add_convert_fusion.1.own_ref), channel_id=1, source_target_pairs={{0,1},{1,0},{2,3},{3,2},{4,8},{5,9},{6,10},{7,11},{8,4},{9,5},{10,... | collective-permute-start | bytes 393224 | tf_op jit(solution)/shard_map/ppermute | solution.py:142
  25.4 1.5 %collective-permute-start.16 = (bf16[2,24,1024]{2,1,0:T(8,128)(2,1)S(1)}, bf16[2,24,1024]{2,1,0:T(8,128)(2,1)S(1)}, u32[]{:S(2)}, u32[]{:S(2)}) collective-permute-start(bf16[2,24,1024]{2,1,0:T(8,128)(2,1)S(1)} %pad_maximum_fusion.1), channel_id=1, source_target_pairs={{0,1},{1,0},{2,3},{3,2},{4,5},{5,4},{6,7},{7,6},{8,9},{9,8},{10,11... | collective-permute-start | bytes 294920 | tf_op jit(solution)/shard_map/ppermute | solution.py:156
  28.7 1.6 %collective-permute-start.17 = (f32[256,256]{1,0:T(8,128)S(1)}, f32[256,256]{1,0:T(8,128)S(1)}, u32[]{:S(2)}, u32[]{:S(2)}) collective-permute-start(f32[256,256]{1,0:T(8,128)S(1)} %shard_map.72), channel_id=1, source_target_pairs={{0,1},{1,0},{2,3},{3,2},{4,5},{5,4},{6,7},{7,6},{8,9},{9,8},{10,11... | collective-permute-start | bytes 786440 | tf_op jit(solution)/shard_map/ppermute | solution.py:156
  30.3 5.6 %collective-permute-start.20 = (bf16[256,256]{1,0:T(8,128)(2,1)S(1)}, bf16[256,256]{1,0:T(8,128)(2,1)S(1)}, u32[]{:S(2)}, u32[]{:S(2)}) collective-permute-start(bf16[256,256]{1,0:T(8,128)(2,1)S(1)} %add_convert_fusion), channel_id=1, source_target_pairs={{0,2},{1,3},{2,0},{3,1},{4,6},{5,7},{6,4},{7,5},{8,10},{9,11},{10,... | collective-permute-start | bytes 393224 | tf_op jit(solution)/shard_map/ppermute | solution.py:156
  32.3 3.6 %collective-permute-start.18 = (f32[128,256]{1,0:T(8,128)S(1)}, f32[128,256]{1,0:T(8,128)S(1)}, u32[]{:S(2)}, u32[]{:S(2)}) collective-permute-start(f32[128,256]{1,0:T(8,128)S(1)} %get-tuple-element.57), channel_id=1, source_target_pairs={{0,1},{1,0},{2,3},{3,2},{4,5},{5,4},{6,7},{7,6},{8,9},{9,8},{10,11... | collective-permute-start | bytes 393224 | tf_op jit(solution)/shard_map/ppermute | solution.py:156
  32.4 3.6 %collective-permute-start.19 = (f32[128,256]{1,0:T(8,128)S(1)}, f32[128,256]{1,0:T(8,128)S(1)}, u32[]{:S(2)}, u32[]{:S(2)}) collective-permute-start(f32[128,256]{1,0:T(8,128)S(1)} %get-tuple-element.58), channel_id=1, source_target_pairs={{0,1},{1,0},{2,3},{3,2},{4,5},{5,4},{6,7},{7,6},{8,9},{9,8},{10,11... | collective-permute-start | bytes 393224 | tf_op jit(solution)/shard_map/ppermute | solution.py:156
  (1 other events, 1.0 us)

commit v21 on v20

--- a/solution.py
+++ b/solution.py
@@ -174,7 +174,7 @@
     )
 
 
-def near_kernel(turns, near_ref, own_ref, first_ref, second_ref, *refs):
+def near_kernel(turns, near_ref, own_ref, second_ref, first_ref, *refs):
     base_refs, out_refs = refs[: -len(turns)], refs[-len(turns) :]
     count = lax.axis_size("tile")
     tile = lax.axis_index("tile")
@@ -256,7 +256,7 @@
     block, right, left = lax.optimization_barrier((block, right_bases, left_bases))
     (bases,) = kernel_call(join_kernel, [((2, *right_bases.shape[2:]), BF)], (right, left))
     across = list_swap(bases, 2)
-    beside = [block, tile_swap(block, 1), middle_swap(block)]
+    beside = [block, middle_swap(block), tile_swap(block, 1)]
     (own,) = kernel_call(
         coefficient_kernel,
         [((ranks // 2, probe_count), BF)],
@@ -284,10 +284,10 @@
     own = (own + list_swap(other, 1)).astype(BF)
     near_by, far = tile_swap(own[: ranks // 2], 1), far_swap(own)
     block = (keep + list_swap(send, 1) + crossed).astype(BF)
-    held, held_across, near_by, far, ready = lax.optimization_barrier(
+    held, held_across, near_by, far, _ = lax.optimization_barrier(
         (bases, across, near_by, far, block)
     )
-    beside = [block, tile_swap(block, 1), middle_swap(ready)]
+    beside = [block, middle_swap(block), tile_swap(block, 1)]
     left = list_swap(jnp.stack([held[1], held_across[1]]), 1)
 
     base = call(far_kernel, (3, 2, 1, 0), (*fixed, left, own, near_by, far), cost=0)

time: 36.8 us -> 36.8 us (level)
  starting transfers between devices: 18.5 us -> 16.3 us
  waiting for transfers between devices: 11.9 us -> 14.1 us
    ppermute x6, waiting for transfers between devices: 4.35 us -> 5.91 us  [tile_swap(): lax.ppermute(block, 'tile', [(i, i ^ turn) for i in range(lax.axis_size('...]
    ppermute x6, starting transfers between devices: 7.77 us -> 6.4 us  [tile_swap(): lax.ppermute(block, 'tile', [(i, i ^ turn) for i in range(lax.axis_size('...]
    ppermute x12, waiting for transfers between devices: 7.51 us -> 8.18 us  [list_swap(): lax.ppermute(block, 'list', [(i, i ^ bit) for i in range(lax.axis_size('l...]
    ppermute x12, starting transfers between devices: 8.1 us -> 7.62 us  [list_swap(): lax.ppermute(block, 'list', [(i, i ^ bit) for i in range(lax.axis_size('l...]
where the time goes in v21:
time: 36.8 us; the launch traced here: 36.7 us
  starting transfers between devices  16.3 us (44%)
  waiting for transfers between devices  14.1 us (38%)
  Pallas kernels  2.81 us (8%)
  between operations  1.53 us (4%)
  local copies, waits for them, and re-layouts  1.01 us (3%)
  other arithmetic  0.89 us (2%)
    ppermute x12, waiting for transfers between devices, list_swap(): lax.ppermute(block, 'list', [(i, i ^ bit) for i in range(lax.axis_size('l...  8.18 us
    ppermute x12, starting transfers between devices, list_swap(): lax.ppermute(block, 'list', [(i, i ^ bit) for i in range(lax.axis_size('l...  7.62 us
    ppermute x6, starting transfers between devices, tile_swap(): lax.ppermute(block, 'tile', [(i, i ^ turn) for i in range(lax.axis_size('...  6.4 us
    ppermute x6, waiting for transfers between devices, tile_swap(): lax.ppermute(block, 'tile', [(i, i ^ turn) for i in range(lax.axis_size('...  5.91 us
    pallas_call x10, Pallas kernels, kernel_call(): pl.pallas_call(kernel, out_shape=tuple((jax.ShapeDtypeStruct(shape, kind)...  2.81 us
    ppermute x1, starting transfers between devices, far_swap(): return lax.ppermute(block, ('tile', 'list'), route)  2.09 us
    unnamed x8, local copies, waits for them, and re-layouts  0.97 us
    add x1, other arithmetic, one_slot(): return keep + list_swap_in_pieces(send, 1, 2) + crossed  0.75 us
  transfers between devices with their start and end apart: 21, of which 9 were waited for; matrix products, arithmetic and copies ran while one was open for 0% of the time, Pallas kernels for 6%

profile of v21, /device:TPU:0, one launch (start us, length us, event | category | flops | bytes accessed | tf_op | source)
XLA Modules:
  0.0 36.7 jit_solution(13352124094117223699)
XLA Ops:
  0.0 1.0 %copy-done.3 = f32[256,256]{1,0:T(8,128)S(1)} copy-done((f32[256,256]{1,0:T(8,128)S(1)}, f32[256,256]{1,0:T(8,128)}, u32[]{:S(2)}) %copy-start.3) | copy-done | bytes 262168
  1.0 3.0 %collective-permute-start = (bf16[2,24,1024]{2,1,0:T(8,128)(2,1)S(1)}, bf16[2,24,1024]{2,1,0:T(8,128)(2,1)S(1)}, u32[]{:S(2)}, u32[]{:S(2)}) collective-permute-start(bf16[2,24,1024]{2,1,0:T(8,128)(2,1)S(1)} %shard_map.65.bases_ref), channel_id=1, source_target_pairs={{0,2},{1,3},{2,0},{3,1},{4,6},{5,7},{6,4},{7,5},{8,10},{9,11},{10,... | collective-permute-start | bytes 294920 | tf_op jit(solution)/shard_map/ppermute | solution.py:156
  4.0 1.6 %collective-permute-start.7 = (bf16[256,256]{1,0:T(8,128)(2,1)S(1)}, bf16[256,256]{1,0:T(8,128)(2,1)S(1)}, u32[]{:S(2)}, u32[]{:S(2)}) collective-permute-start(bf16[256,256]{1,0:T(8,128)(2,1)S(1)} %shard_map.64.block_ref.own_ref), channel_id=1, source_target_pairs={{0,4},{4,0},{8,12},{12,8},{1,5},{5,1},{9,13},{13,9},{2,6},{6,2},{1... | collective-permute-start | bytes 393224 | tf_op jit(solution)/shard_map/ppermute | solution.py:130
  6.5 0.3 collective-permute-done.across_ref
  7.1 4.0 %collective-permute-start.5 = (bf16[48,256]{1,0:T(8,128)(2,1)S(1)}, bf16[48,256]{1,0:T(8,128)(2,1)S(1)}, u32[]{:S(2)}, u32[]{:S(2)}) collective-permute-start(bf16[48,256]{1,0:T(8,128)(2,1)S(1)} %shard_map.66.refs_0_), channel_id=1, source_target_pairs={{0,12},{4,8},{8,4},{12,0},{1,13},{5,9},{9,5},{13,1},{2,14},{6,10},... | collective-permute-start | bytes 73736 | tf_op jit(solution)/shard_map/ppermute | solution.py:130
  11.3 0.5 %collective-permute-start.3 = (bf16[48,256]{1,0:T(8,128)(2,1)S(1)}, bf16[48,256]{1,0:T(8,128)(2,1)S(1)}, u32[]{:S(2)}, u32[]{:S(2)}) collective-permute-start(bf16[48,256]{1,0:T(8,128)(2,1)S(1)} %shard_map.66.refs_0_), channel_id=1, source_target_pairs={{0,4},{4,0},{8,12},{12,8},{1,5},{5,1},{9,13},{13,9},{2,6},{6,2},{1... | collective-permute-start | bytes 73736 | tf_op jit(solution)/shard_map/ppermute | solution.py:130
  12.4 0.6 %shard_map.67 = (f32[256,256]{1,0:T(8,128)S(1)}, f32[256,256]{1,0:T(8,128)S(1)}, f32[256,256]{1,0:T(8,128)S(1)}, f32[256,256]{1,0:T(8,128)S(1)}) custom-call(bf16[3,1024,256]{2,1,0:T(8,128)(2,1)S(1)} %bitcast.3, bf16[256,256]{1,0:T(8,128)(2,1)S(1)} %shard_map.64.block_ref.own_ref, bf16[256,256]{1,0:T(8,128)(2,1)S(1)} %collective-permute-done.6.second_ref, ...), custom_call_target="tpu_custom_call" | custom-call | tf_op jit(solution)/shard_map/pallas_call | solution.py:77
  13.0 2.8 %collective-permute-done.4.refs_2_ = bf16[48,256]{1,0:T(8,128)(2,1)S(1)} collective-permute-done((bf16[48,256]{1,0:T(8,128)(2,1)S(1)}, bf16[48,256]{1,0:T(8,128)(2,1)S(1)}, u32[]{:S(2)}, u32[]{:S(2)}) %collective-permute-start.4) | collective-permute-done | bytes 24608 | tf_op jit(solution)/shard_map/ppermute | solution.py:130
  16.2 0.5 %shard_map.69 = (f32[256,256]{1,0:T(8,128)S(1)}, f32[256,256]{1,0:T(8,128)S(1)}, f32[256,256]{1,0:T(8,128)S(1)}, f32[96,256]{1,0:T(8,128)S(1)}, f32[96,256]{1,0:T(8,128)S(1)}) custom-call(s32[1,1]{1,0:T(1,128)S(6)} %copy.8.columns_ref, bf16[2,24,1024]{2,1,0:T(8,128)(2,1)S(1)} %shard_map.65.bases_ref, ...), custom_call_target="tpu_custom_call" | custom-call | flops 301989888 | bytes 294912 | tf_op jit(solution)/shard_map/pallas_call | solution.py:77
  16.7 0.6 %collective-permute-start.13 = (f32[96,256]{1,0:T(8,128)S(1)}, f32[96,256]{1,0:T(8,128)S(1)}, u32[]{:S(2)}, u32[]{:S(2)}) collective-permute-start(f32[96,256]{1,0:T(8,128)S(1)} %get-tuple-element.42), channel_id=1, source_target_pairs={{0,1},{1,0},{2,3},{3,2},{4,5},{5,4},{6,7},{7,6},{8,9},{9,8},{10,11... | collective-permute-start | bytes 294920 | tf_op jit(solution)/shard_map/ppermute | solution.py:156
  17.3 0.3 collective-permute-done.9
  17.7 1.6 %collective-permute-start.10 = (bf16[256,256]{1,0:T(8,128)(2,1)S(1)}, bf16[256,256]{1,0:T(8,128)(2,1)S(1)}, u32[]{:S(2)}, u32[]{:S(2)}) collective-permute-start(bf16[256,256]{1,0:T(8,128)(2,1)S(1)} %add_convert_fusion.2), channel_id=1, source_target_pairs={{0,2},{1,3},{2,0},{3,1},{4,6},{5,7},{6,4},{7,5},{8,10},{9,11},{10,... | collective-permute-start | bytes 393224 | tf_op jit(solution)/shard_map/ppermute | solution.py:156
  19.3 2.1 %collective-permute-start.15 = (bf16[96,256]{1,0:T(8,128)(2,1)S(1)}, bf16[96,256]{1,0:T(8,128)(2,1)S(1)}, u32[]{:S(2)}, u32[]{:S(2)}) collective-permute-start(bf16[96,256]{1,0:T(8,128)(2,1)S(1)} %add_convert_fusion.3.refs_0_), channel_id=1, source_target_pairs={{0,8},{1,13},{2,10},{3,15},{4,12},{5,9},{6,14},{7,11},{8,0},{9,5},... | collective-permute-start | bytes 147464 | tf_op jit(solution)/shard_map/ppermute | solution.py:152
  21.4 1.9 %collective-permute-done.10 = bf16[256,256]{1,0:T(8,128)(2,1)S(1)} collective-permute-done((bf16[256,256]{1,0:T(8,128)(2,1)S(1)}, bf16[256,256]{1,0:T(8,128)(2,1)S(1)}, u32[]{:S(2)}, u32[]{:S(2)}) %collective-permute-start.10) | collective-permute-done | bytes 131104 | tf_op jit(solution)/shard_map/ppermute | solution.py:156
  23.6 1.7 %collective-permute-done.14.refs_1_ = bf16[48,256]{1,0:T(8,128)(2,1)S(1)} collective-permute-done((bf16[48,256]{1,0:T(8,128)(2,1)S(1)}, bf16[48,256]{1,0:T(8,128)(2,1)S(1)}, u32[]{:S(2)}, u32[]{:S(2)}) %collective-permute-start.14) | collective-permute-done | bytes 24608 | tf_op jit(solution)/shard_map/ppermute | solution.py:130
  25.4 1.3 %collective-permute-done.16.other_ref = bf16[2,24,1024]{2,1,0:T(8,128)(2,1)S(1)} collective-permute-done((bf16[2,24,1024]{2,1,0:T(8,128)(2,1)S(1)}, bf16[2,24,1024]{2,1,0:T(8,128)(2,1)S(1)}, u32[]{:S(2)}, u32[]{:S(2)}) %collective-permute-start.16) | collective-permute-done | bytes 98336 | tf_op jit(solution)/shard_map/ppermute | solution.py:156
  26.6 0.4 shard_map.70
  27.0 1.4 %collective-permute-done.12.first_ref = bf16[256,256]{1,0:T(8,128)(2,1)S(1)} collective-permute-done((bf16[256,256]{1,0:T(8,128)(2,1)S(1)}, bf16[256,256]{1,0:T(8,128)(2,1)S(1)}, u32[]{:S(2)}, u32[]{:S(2)}) %collective-permute-start.12) | collective-permute-done | bytes 131104 | tf_op jit(solution)/shard_map/ppermute | solution.py:130
  29.1 1.2 %collective-permute-done.17 = f32[256,256]{1,0:T(8,128)S(1)} collective-permute-done((f32[256,256]{1,0:T(8,128)S(1)}, f32[256,256]{1,0:T(8,128)S(1)}, u32[]{:S(2)}, u32[]{:S(2)}) %collective-permute-start.17) | collective-permute-done | bytes 262176 | tf_op jit(solution)/shard_map/ppermute | solution.py:156
  30.3 1.6 %collective-permute-start.20 = (bf16[256,256]{1,0:T(8,128)(2,1)S(1)}, bf16[256,256]{1,0:T(8,128)(2,1)S(1)}, u32[]{:S(2)}, u32[]{:S(2)}) collective-permute-start(bf16[256,256]{1,0:T(8,128)(2,1)S(1)} %add_convert_fusion), channel_id=1, source_target_pairs={{0,2},{1,3},{2,0},{3,1},{4,6},{5,7},{6,4},{7,5},{8,10},{9,11},{10,... | collective-permute-start | bytes 393224 | tf_op jit(solution)/shard_map/ppermute | solution.py:156
  31.9 0.4 shard_map.73
  32.4 0.5 %collective-permute-start.19 = (f32[128,256]{1,0:T(8,128)S(1)}, f32[128,256]{1,0:T(8,128)S(1)}, u32[]{:S(2)}, u32[]{:S(2)}) collective-permute-start(f32[128,256]{1,0:T(8,128)S(1)} %get-tuple-element.56), channel_id=1, source_target_pairs={{0,1},{1,0},{2,3},{3,2},{4,5},{5,4},{6,7},{7,6},{8,9},{9,8},{10,11... | collective-permute-start | bytes 393224 | tf_op jit(solution)/shard_map/ppermute | solution.py:156
  32.9 3.1 %collective-permute-done.20 = bf16[256,256]{1,0:T(8,128)(2,1)S(1)} collective-permute-done((bf16[256,256]{1,0:T(8,128)(2,1)S(1)}, bf16[256,256]{1,0:T(8,128)(2,1)S(1)}, u32[]{:S(2)}, u32[]{:S(2)}) %collective-permute-start.20) | collective-permute-done | bytes 131104 | tf_op jit(solution)/shard_map/ppermute | solution.py:156
  35.9 0.7 %fusion = f32[256,256]{1,0:T(8,128)} fusion(f32[256,256]{1,0:T(8,128)S(1)} %get-tuple-element.52, f32[128,256]{1,0:T(8,128)S(1)} %collective-permute-done.19, f32[128,256]{1,0:T(8,128)S(1)} %collective-permute-done.18, bf16[256,256]{1,0:T(8,128)(2,1)S(1)} %collective-permute-done.20), kind=kLoop, calls=%fused_computation.1 | loop fusion | flops 262144 | bytes 917504 | tf_op jit(solution)/shard_map/add | solution.py:301
  (49 shorter events, 2.2 us)
Async XLA Ops:
  0.0 1.0 %copy-start.2 = (bf16[1,1,24,1024]{3,2,1,0:T(8,128)(2,1)S(1)}, bf16[1,1,24,1024]{3,2,1,0:T(8,128)(2,1)}, u32[]{:S(2)}) copy-start(bf16[1,1,24,1024]{3,2,1,0:T(8,128)(2,1)} %left_ref) | copy-start | bytes 147460
  0.0 1.0 %copy-start.1 = (bf16[1,1,24,1024]{3,2,1,0:T(8,128)(2,1)S(1)}, bf16[1,1,24,1024]{3,2,1,0:T(8,128)(2,1)}, u32[]{:S(2)}) copy-start(bf16[1,1,24,1024]{3,2,1,0:T(8,128)(2,1)} %right_ref) | copy-start | bytes 147460
  1.0 5.8 %collective-permute-start = (bf16[2,24,1024]{2,1,0:T(8,128)(2,1)S(1)}, bf16[2,24,1024]{2,1,0:T(8,128)(2,1)S(1)}, u32[]{:S(2)}, u32[]{:S(2)}) collective-permute-start(bf16[2,24,1024]{2,1,0:T(8,128)(2,1)S(1)} %shard_map.65.bases_ref), channel_id=1, source_target_pairs={{0,2},{1,3},{2,0},{3,1},{4,6},{5,7},{6,4},{7,5},{8,10},{9,11},{10,... | collective-permute-start | bytes 294920 | tf_op jit(solution)/shard_map/ppermute | solution.py:156
  4.0 2.8 %collective-permute-start.1 = (bf16[256,256]{1,0:T(8,128)(2,1)S(1)}, bf16[256,256]{1,0:T(8,128)(2,1)S(1)}, u32[]{:S(2)}, u32[]{:S(2)}) collective-permute-start(bf16[256,256]{1,0:T(8,128)(2,1)S(1)} %shard_map.64.block_ref.own_ref), channel_id=1, source_target_pairs={{0,1},{1,0},{2,3},{3,2},{4,5},{5,4},{6,7},{7,6},{8,9},{9,8},{10,11... | collective-permute-start | bytes 393224 | tf_op jit(solution)/shard_map/ppermute | solution.py:156
  4.0 7.2 %collective-permute-start.7 = (bf16[256,256]{1,0:T(8,128)(2,1)S(1)}, bf16[256,256]{1,0:T(8,128)(2,1)S(1)}, u32[]{:S(2)}, u32[]{:S(2)}) collective-permute-start(bf16[256,256]{1,0:T(8,128)(2,1)S(1)} %shard_map.64.block_ref.own_ref), channel_id=1, source_target_pairs={{0,4},{4,0},{8,12},{12,8},{1,5},{5,1},{9,13},{13,9},{2,6},{6,2},{1... | collective-permute-start | bytes 393224 | tf_op jit(solution)/shard_map/ppermute | solution.py:130
  5.6 6.8 %collective-permute-start.6 = (bf16[256,256]{1,0:T(8,128)(2,1)S(1)}, bf16[256,256]{1,0:T(8,128)(2,1)S(1)}, u32[]{:S(2)}, u32[]{:S(2)}) collective-permute-start(bf16[256,256]{1,0:T(8,128)(2,1)S(1)} %shard_map.64.block_ref.own_ref), channel_id=1, source_target_pairs={{0,1},{1,0},{2,3},{3,2},{4,8},{5,9},{6,10},{7,11},{8,4},{9,5},{10,... | collective-permute-start | bytes 393224 | tf_op jit(solution)/shard_map/ppermute | solution.py:142
  6.8 5.6 %copy-start = (bf16[1,1024,3,256]{3,1,2,0:T(8,128)(2,1)S(1)}, bf16[1,1024,3,256]{3,1,2,0:T(8,128)(2,1)}, u32[]{:S(2)}) copy-start(bf16[1,1024,3,256]{3,1,2,0:T(8,128)(2,1)} %param.10) | copy-start | bytes 4718596
  7.0 8.8 %collective-permute-start.2 = (bf16[2,24,1024]{2,1,0:T(8,128)(2,1)S(1)}, bf16[2,24,1024]{2,1,0:T(8,128)(2,1)S(1)}, u32[]{:S(2)}, u32[]{:S(2)}) collective-permute-start(bf16[2,24,1024]{2,1,0:T(8,128)(2,1)S(1)} %pad_maximum_fusion), channel_id=1, source_target_pairs={{0,1},{1,0},{2,3},{3,2},{4,5},{5,4},{6,7},{7,6},{8,9},{9,8},{10,11... | collective-permute-start | bytes 294920 | tf_op jit(solution)/shard_map/ppermute | solution.py:156
  7.1 5.9 %collective-permute-start.5 = (bf16[48,256]{1,0:T(8,128)(2,1)S(1)}, bf16[48,256]{1,0:T(8,128)(2,1)S(1)}, u32[]{:S(2)}, u32[]{:S(2)}) collective-permute-start(bf16[48,256]{1,0:T(8,128)(2,1)S(1)} %shard_map.66.refs_0_), channel_id=1, source_target_pairs={{0,12},{4,8},{8,4},{12,0},{1,13},{5,9},{9,5},{13,1},{2,14},{6,10},... | collective-permute-start | bytes 73736 | tf_op jit(solution)/shard_map/ppermute | solution.py:130
  11.1 4.7 %collective-permute-start.4 = (bf16[48,256]{1,0:T(8,128)(2,1)S(1)}, bf16[48,256]{1,0:T(8,128)(2,1)S(1)}, u32[]{:S(2)}, u32[]{:S(2)}) collective-permute-start(bf16[48,256]{1,0:T(8,128)(2,1)S(1)} %shard_map.66.refs_0_), channel_id=1, source_target_pairs={{0,8},{4,12},{8,0},{12,4},{1,9},{5,13},{9,1},{13,5},{2,10},{6,14},... | collective-permute-start | bytes 73736 | tf_op jit(solution)/shard_map/ppermute | solution.py:130
  11.3 4.6 %collective-permute-start.3 = (bf16[48,256]{1,0:T(8,128)(2,1)S(1)}, bf16[48,256]{1,0:T(8,128)(2,1)S(1)}, u32[]{:S(2)}, u32[]{:S(2)}) collective-permute-start(bf16[48,256]{1,0:T(8,128)(2,1)S(1)} %shard_map.66.refs_0_), channel_id=1, source_target_pairs={{0,4},{4,0},{8,12},{12,8},{1,5},{5,1},{9,13},{13,9},{2,6},{6,2},{1... | collective-permute-start | bytes 73736 | tf_op jit(solution)/shard_map/ppermute | solution.py:130
  16.1 1.6 %collective-permute-start.9 = (f32[256,256]{1,0:T(8,128)S(1)}, f32[256,256]{1,0:T(8,128)S(1)}, u32[]{:S(2)}, u32[]{:S(2)}) collective-permute-start(f32[256,256]{1,0:T(8,128)S(1)} %shard_map.68.refs_7_), channel_id=1, source_target_pairs={{0,1},{1,0},{2,3},{3,2},{4,5},{5,4},{6,7},{7,6},{8,9},{9,8},{10,11... | collective-permute-start | bytes 786440 | tf_op jit(solution)/shard_map/ppermute | solution.py:156
  16.7 2.6 %collective-permute-start.13 = (f32[96,256]{1,0:T(8,128)S(1)}, f32[96,256]{1,0:T(8,128)S(1)}, u32[]{:S(2)}, u32[]{:S(2)}) collective-permute-start(f32[96,256]{1,0:T(8,128)S(1)} %get-tuple-element.42), channel_id=1, source_target_pairs={{0,1},{1,0},{2,3},{3,2},{4,5},{5,4},{6,7},{7,6},{8,9},{9,8},{10,11... | collective-permute-start | bytes 294920 | tf_op jit(solution)/shard_map/ppermute | solution.py:156
  17.3 4.1 %collective-permute-start.8 = (f32[256,256]{1,0:T(8,128)S(1)}, f32[256,256]{1,0:T(8,128)S(1)}, u32[]{:S(2)}, u32[]{:S(2)}) collective-permute-start(f32[256,256]{1,0:T(8,128)S(1)} %get-tuple-element.39), channel_id=1, source_target_pairs={{0,1},{1,0},{2,3},{3,2},{4,5},{5,4},{6,7},{7,6},{8,9},{9,8},{10,11... | collective-permute-start | bytes 786440 | tf_op jit(solution)/shard_map/ppermute | solution.py:156
  17.7 5.6 %collective-permute-start.10 = (bf16[256,256]{1,0:T(8,128)(2,1)S(1)}, bf16[256,256]{1,0:T(8,128)(2,1)S(1)}, u32[]{:S(2)}, u32[]{:S(2)}) collective-permute-start(bf16[256,256]{1,0:T(8,128)(2,1)S(1)} %add_convert_fusion.2), channel_id=1, source_target_pairs={{0,2},{1,3},{2,0},{3,1},{4,6},{5,7},{6,4},{7,5},{8,10},{9,11},{10,... | collective-permute-start | bytes 393224 | tf_op jit(solution)/shard_map/ppermute | solution.py:156
  19.3 5.9 %collective-permute-start.15 = (bf16[96,256]{1,0:T(8,128)(2,1)S(1)}, bf16[96,256]{1,0:T(8,128)(2,1)S(1)}, u32[]{:S(2)}, u32[]{:S(2)}) collective-permute-start(bf16[96,256]{1,0:T(8,128)(2,1)S(1)} %add_convert_fusion.3.refs_0_), channel_id=1, source_target_pairs={{0,8},{1,13},{2,10},{3,15},{4,12},{5,9},{6,14},{7,11},{8,0},{9,5},... | collective-permute-start | bytes 147464 | tf_op jit(solution)/shard_map/ppermute | solution.py:152
  21.4 3.8 %collective-permute-start.14 = (bf16[48,256]{1,0:T(8,128)(2,1)S(1)}, bf16[48,256]{1,0:T(8,128)(2,1)S(1)}, u32[]{:S(2)}, u32[]{:S(2)}) collective-permute-start(bf16[48,256]{1,0:T(8,128)(2,1)S(1)} %slice.22), channel_id=1, source_target_pairs={{0,4},{4,0},{8,12},{12,8},{1,5},{5,1},{9,13},{13,9},{2,6},{6,2},{1... | collective-permute-start | bytes 73736 | tf_op jit(solution)/shard_map/ppermute | solution.py:130
  23.4 5.0 %collective-permute-start.12 = (bf16[256,256]{1,0:T(8,128)(2,1)S(1)}, bf16[256,256]{1,0:T(8,128)(2,1)S(1)}, u32[]{:S(2)}, u32[]{:S(2)}) collective-permute-start(bf16[256,256]{1,0:T(8,128)(2,1)S(1)} %add_convert_fusion.1.own_ref), channel_id=1, source_target_pairs={{0,4},{4,0},{8,12},{12,8},{1,5},{5,1},{9,13},{13,9},{2,6},{6,2},{1... | collective-permute-start | bytes 393224 | tf_op jit(solution)/shard_map/ppermute | solution.py:130
  23.6 4.9 %collective-permute-start.11 = (bf16[256,256]{1,0:T(8,128)(2,1)S(1)}, bf16[256,256]{1,0:T(8,128)(2,1)S(1)}, u32[]{:S(2)}, u32[]{:S(2)}) collective-permute-start(bf16[256,256]{1,0:T(8,128)(2,1)S(1)} %add_convert_fusion.1.own_ref), channel_id=1, source_target_pairs={{0,1},{1,0},{2,3},{3,2},{4,8},{5,9},{6,10},{7,11},{8,4},{9,5},{10,... | collective-permute-start | bytes 393224 | tf_op jit(solution)/shard_map/ppermute | solution.py:142
  25.3 1.4 %collective-permute-start.16 = (bf16[2,24,1024]{2,1,0:T(8,128)(2,1)S(1)}, bf16[2,24,1024]{2,1,0:T(8,128)(2,1)S(1)}, u32[]{:S(2)}, u32[]{:S(2)}) collective-permute-start(bf16[2,24,1024]{2,1,0:T(8,128)(2,1)S(1)} %pad_maximum_fusion.1), channel_id=1, source_target_pairs={{0,1},{1,0},{2,3},{3,2},{4,5},{5,4},{6,7},{7,6},{8,9},{9,8},{10,11... | collective-permute-start | bytes 294920 | tf_op jit(solution)/shard_map/ppermute | solution.py:156
  28.7 1.6 %collective-permute-start.17 = (f32[256,256]{1,0:T(8,128)S(1)}, f32[256,256]{1,0:T(8,128)S(1)}, u32[]{:S(2)}, u32[]{:S(2)}) collective-permute-start(f32[256,256]{1,0:T(8,128)S(1)} %shard_map.72), channel_id=1, source_target_pairs={{0,1},{1,0},{2,3},{3,2},{4,5},{5,4},{6,7},{7,6},{8,9},{9,8},{10,11... | collective-permute-start | bytes 786440 | tf_op jit(solution)/shard_map/ppermute | solution.py:156
  30.3 5.6 %collective-permute-start.20 = (bf16[256,256]{1,0:T(8,128)(2,1)S(1)}, bf16[256,256]{1,0:T(8,128)(2,1)S(1)}, u32[]{:S(2)}, u32[]{:S(2)}) collective-permute-start(bf16[256,256]{1,0:T(8,128)(2,1)S(1)} %add_convert_fusion), channel_id=1, source_target_pairs={{0,2},{1,3},{2,0},{3,1},{4,6},{5,7},{6,4},{7,5},{8,10},{9,11},{10,... | collective-permute-start | bytes 393224 | tf_op jit(solution)/shard_map/ppermute | solution.py:156
  32.3 3.6 %collective-permute-start.18 = (f32[128,256]{1,0:T(8,128)S(1)}, f32[128,256]{1,0:T(8,128)S(1)}, u32[]{:S(2)}, u32[]{:S(2)}) collective-permute-start(f32[128,256]{1,0:T(8,128)S(1)} %get-tuple-element.55), channel_id=1, source_target_pairs={{0,1},{1,0},{2,3},{3,2},{4,5},{5,4},{6,7},{7,6},{8,9},{9,8},{10,11... | collective-permute-start | bytes 393224 | tf_op jit(solution)/shard_map/ppermute | solution.py:156
  32.4 3.6 %collective-permute-start.19 = (f32[128,256]{1,0:T(8,128)S(1)}, f32[128,256]{1,0:T(8,128)S(1)}, u32[]{:S(2)}, u32[]{:S(2)}) collective-permute-start(f32[128,256]{1,0:T(8,128)S(1)} %get-tuple-element.56), channel_id=1, source_target_pairs={{0,1},{1,0},{2,3},{3,2},{4,5},{5,4},{6,7},{7,6},{8,9},{9,8},{10,11... | collective-permute-start | bytes 393224 | tf_op jit(solution)/shard_map/ppermute | solution.py:156
  (1 other events, 1.0 us)
